TPU v7x, 768 devices: a whole 4x8x12 slice. The times are simulated.
768 devices in a mesh: dp: 96 (over x, z, core), mp: 8 (over y).
Axes of the slice: x: 4, y: 8, z: 12, core: 2. Of those that a mesh axis runs over, the one named last changes fastest.
Arguments:
- hidden_rows: bfloat16 [49152, 2048], P('dp'), may hold values from -8 to 8
- lengths: int32 [96], P('dp'), may hold values from 256 to 512, as said below
- pair_order: int32 [96], replicated, may hold values from 0 to 95, each once
- gain_attn: float32 [2048], replicated, may hold values from 0.1 to 1.9
- w_query: bfloat16 [2048, 2048], P(None, 'mp')
- key_weight: bfloat16 [2048, 512], P(None, 'mp'), may hold values from -0.125 to 0.125
- value_weight: bfloat16 [2048, 512], P(None, 'mp'), may hold values from -0.125 to 0.125
- w_out: bfloat16 [2048, 2048], P('mp'), may hold values from -0.125 to 0.125
- gain_final: float32 [2048], replicated, may hold values from 0.1 to 1.9
- w_head: float32 [2048], replicated, may hold values from -1.5 to 1.5
Outputs:
- loss: float32 [], replicated
- rewards: float32 [96], replicated
- grad_out_proj: float32 [2048, 2048], P(None, 'mp')
- grad_head: float32 [2048], P('mp')
- grad_gain: float32 [2048], P('mp')
Inputs may be any that keep to these rules, and one draw needn't show every extreme that they name: The one entry of `lengths` on a data shard is the length of the sequence packed from that shard's first row on. `pair_order`: entries 2p and 2p+1 name the chosen and the rejected sequence of pair p; every sequence is named once.
All inputs are finite; a program needn't handle non-finite values.
Results may differ from a plain program's by a relative error of at most 0.009.
The roundings to bfloat16 on the way count: a program that leaves them out, or rounds other values in their place, can miss the bound.
Values may be sent and summed in bfloat16 or wider, within the bound.
No kernel may reach another device: no remote copies, remote signals or barrier semaphores. Data moves between devices by JAX's collectives and lax.ppermute only.
A program may use at most 32 MiB of HBM per device.

v0:
```python
import jax
import jax.numpy as jnp
from jax import lax
from jax.sharding import PartitionSpec as P

QUERY_HEADS = 32
KEY_VALUE_HEADS = 8
HEAD_SIZE = 64


EPS = 1e-05
THETA = 500000.0


def positions_of(lens, rows):
    ends = jnp.cumsum(lens)
    starts = ends - lens
    row_ids = jnp.arange(rows, dtype=jnp.int32)
    inside = (row_ids[:, None] >= starts[None, :]) & (row_ids[:, None] < ends[None, :])
    member = inside.astype(jnp.int32)
    segment = jnp.sum((row_ids[:, None] >= ends[None, :]).astype(jnp.int32), axis=1)
    offset = jnp.sum(member * starts[None, :], axis=1) + (1 - jnp.sum(member, axis=1)) * ends[-1]
    return (segment, row_ids - offset, member)


def rope_tables(positions):
    half = HEAD_SIZE // 2
    freq = THETA ** (-jnp.arange(half, dtype=jnp.float32) * 2.0 / HEAD_SIZE)
    angle = positions.astype(jnp.float32)[:, None] * freq[None, :]
    return (jnp.cos(angle), jnp.sin(angle))


def rotate(vecs, cosine, sine):
    half = vecs.shape[-1] // 2
    first = vecs[..., :half]
    second = vecs[..., half:]
    cos_b = cosine[:, None, :]
    sin_b = sine[:, None, :]
    return jnp.concatenate(
        [first * cos_b - second * sin_b, second * cos_b + first * sin_b], axis=-1
    )


def body(
    hidden_rows,
    lengths,
    pair_order,
    gain_attn,
    w_query,
    key_weight,
    value_weight,
    w_out,
    gain_final,
    w_head,
):
    rows, width = hidden_rows.shape
    seqs = lengths.shape[0]
    q_heads = w_query.shape[1] // HEAD_SIZE
    kv_heads = key_weight.shape[1] // HEAD_SIZE
    head_group = QUERY_HEADS // KEY_VALUE_HEADS
    segment, positions, member_int = positions_of(lengths, rows)
    member = member_int.astype(jnp.float32)
    lens_f = lengths.astype(jnp.float32)
    x32 = hidden_rows.astype(jnp.float32)
    normalized_rows = (
        x32 * lax.rsqrt(jnp.mean(x32 * x32, axis=1, keepdims=True) + EPS) * gain_attn
    ).astype(jnp.bfloat16)
    cosine, sine = rope_tables(positions)
    query = jnp.dot(normalized_rows, w_query, preferred_element_type=jnp.float32).reshape(
        rows, q_heads, HEAD_SIZE
    )
    query = rotate(query, cosine, sine).astype(jnp.bfloat16)
    key_vectors = jnp.dot(normalized_rows, key_weight, preferred_element_type=jnp.float32).reshape(
        rows, kv_heads, HEAD_SIZE
    )
    key_vectors = rotate(key_vectors, cosine, sine).astype(jnp.bfloat16)
    value_rows = (
        jnp.dot(normalized_rows, value_weight, preferred_element_type=jnp.float32)
        .astype(jnp.bfloat16)
        .reshape(rows, kv_heads, HEAD_SIZE)
    )
    key_rep = jnp.repeat(key_vectors, head_group, axis=1)
    value_rep = jnp.repeat(value_rows, head_group, axis=1)
    row_ids = jnp.arange(rows, dtype=jnp.int32)
    block_rows = min(512, rows)
    num_blocks = rows // block_rows

    def attend_block(index):
        scores = jnp.einsum(
            "qhd,khd->hqk", query, key_rep, preferred_element_type=jnp.float32
        ) * HEAD_SIZE ** (-0.5)
        allowed = (segment[:, None] == segment[None, :]) & (row_ids[None, :] <= row_ids[:, None])
        scores = jnp.where(allowed[None], scores, -1e30)
        top = jnp.max(scores, axis=2, keepdims=True)
        weights = jnp.exp(scores - top)
        probs = (weights / jnp.sum(weights, axis=2, keepdims=True)).astype(jnp.bfloat16)
        out_block = jnp.einsum("hqk,khd->qhd", probs, value_rep, preferred_element_type=jnp.float32)
        return out_block.astype(jnp.bfloat16)

    mixed = lax.map(attend_block, jnp.arange(num_blocks, dtype=jnp.int32))
    mixed = mixed.reshape(rows, q_heads * HEAD_SIZE)
    my_part = lax.axis_index("mp")
    feat = width // lax.axis_size("mp")
    gain_share = lax.dynamic_slice_in_dim(gain_final, my_part * feat, feat, 0)
    head_share = lax.dynamic_slice_in_dim(w_head, my_part * feat, feat, 0)
    share = rows // lax.axis_size("mp")
    first = my_part * share
    attended = lax.psum_scatter(
        jnp.dot(mixed, w_out, preferred_element_type=jnp.float32).astype(jnp.bfloat16),
        "mp",
        scatter_dimension=0,
        tiled=True,
    ).astype(jnp.float32)
    resid = lax.dynamic_slice_in_dim(x32, first, share, 0) + attended
    scale = lax.rsqrt(jnp.mean(resid * resid, axis=1) + EPS)
    unit = resid * scale[:, None]
    member_share = lax.dynamic_slice_in_dim(member, first, share, 0)
    row_score = jnp.sum(unit * gain_final * w_head, axis=1)
    part_rewards = jnp.sum(member_share * row_score[:, None], axis=0) / lens_f
    my_rewards = lax.psum(part_rewards, "mp")
    rewards = lax.all_gather(my_rewards, "dp", axis=0, tiled=True)
    total_seqs = rewards.shape[0]
    picked = rewards[pair_order].reshape(total_seqs // 2, 2)
    margin = picked[:, 0] - picked[:, 1]
    loss = jnp.sum(jax.nn.softplus(-margin))
    sig = jax.nn.sigmoid(-margin)
    per_pos = jnp.stack([-sig, sig], axis=1).reshape(total_seqs)
    dreward = jnp.zeros((total_seqs,), jnp.float32).at[pair_order].set(per_pos)
    coef = lax.dynamic_slice_in_dim(dreward, lax.axis_index("dp") * seqs, seqs, 0) / lens_f
    row_coef = jnp.sum(member_share * coef[None, :], axis=1)
    dunit = row_coef[:, None] * (w_head * gain_final)[None, :]
    inner = jnp.mean(dunit * unit, axis=1)
    dresid = scale[:, None] * (dunit - unit * inner[:, None])
    pooled_part = jnp.sum(row_coef[:, None] * unit, axis=0)
    taken = mixed.astype(jnp.float32)
    grad_local = jnp.einsum(
        "rc,rd->cd",
        taken,
        lax.all_gather(dresid.astype(jnp.bfloat16), "mp", axis=0, tiled=True).astype(jnp.float32),
        preferred_element_type=jnp.float32,
        precision=lax.Precision.HIGHEST,
    )
    grad_summed = lax.psum(grad_local, "dp")
    pooled_all = lax.psum(pooled_part, ("dp", "mp"))
    grad_out_proj = lax.all_to_all(
        grad_summed.astype(jnp.bfloat16), "mp", split_axis=1, concat_axis=0, tiled=True
    ).astype(grad_summed.dtype)
    pooled = lax.dynamic_slice_in_dim(pooled_all, my_part * feat, feat, 0)
    return (loss, rewards, grad_out_proj, gain_share * pooled, head_share * pooled)


def solution(mesh):
    placed = (
        P("dp", None),
        P("dp"),
        P(),
        P(),
        P(None, "mp"),
        P(None, "mp"),
        P(None, "mp"),
        P("mp", None),
        P(),
        P(),
    )
    return jax.shard_map(
        body,
        mesh=mesh,
        in_specs=placed,
        out_specs=(P(), P(), P(None, "mp"), P("mp"), P("mp")),
        check_vma=False,
    )
```

profile of v0, /device:TPU:1, one launch (start us, length us, event | category | flops | bytes accessed | tf_op | source)
XLA Modules:
  0.0 860.7 jit_solution(17301593472988101105)
XLA Ops:
  8.1 2.1 multiply_reduce_fusion
  10.5 0.5 multiply_convert_fusion
  11.0 0.4 copy-done.3
  11.4 1.4 convolution_convert_fusion.1
  12.8 0.8 convolution_bitcast_fusion
  13.6 0.8 fusion.47
  15.0 0.6 pad_maximum_fusion.7
  15.6 0.7 subtract_convert_fusion
  16.3 4.5 fusion.42
  20.8 2.7 fusion.6
  23.5 2.1 convolution_convert_fusion
  25.7 2.5 convert_element_type.102
  28.2 48.1 %reduce-scatter.2.cloned.1.call-done = bf16[64,2048]{1,0:T(8,128)(2,1)} async-done(((bf16[512,2048]{1,0:T(8,128)(2,1)}), bf16[64,2048]{1,0:T(8,128)(2,1)}) %reduce-scatter.2.cloned.1.call-update) | async-done | bytes 262160 | tf_op jit(solution)/shard_map/reduce_scatter | solution.py:108
  76.3 1.3 multiply_reduce_fusion.3
  77.8 0.6 fusion.32
  79.1 1.3 dynamic-slice
  80.4 12.0 %psum.21 = f32[1]{0:T(128)} all-reduce(f32[1]{0:T(128)S(6)} %div.50), channel_id=1, replica_groups=mesh['dp'=96,'mp'=8] {'mp'}, use_global_device_ids=true, to_apply=%region_7.8 | all-reduce | flops 1 | bytes 8 | tf_op jit(solution)/shard_map/psum | solution.py:120
  92.4 1.4 dynamic-update-slice
  93.8 195.7 %all-reduce = f32[96]{0:T(128)S(1)} all-reduce(f32[96]{0:T(128)S(1)} %dynamic-update-slice), channel_id=1, replica_groups=mesh['dp'=96,'mp'=8] {'dp'}, use_global_device_ids=true, to_apply=%add | all-reduce | flops 96 | bytes 768
  289.5 1.2 gather_fusion
  291.2 0.9 scatter_custom_fusion
  292.1 0.6 dynamic_slice.20
  293.6 0.9 fusion.10
  294.5 32.1 %all-gather.2.cloned.1.call-done = bf16[512,2048]{1,0:T(8,128)(2,1)} async-done(((bf16[64,2048]{1,0:T(8,128)(2,1)}), bf16[512,2048]{1,0:T(8,128)(2,1)}) %all-gather.2.cloned.1.call-update) | async-done | bytes 2097168 | tf_op jit(solution)/shard_map/all_gather | solution.py:139
  326.6 2.3 fusion.48
  329.0 392.3 %all-reduce.2 = bf16[256,2048]{1,0:T(8,128)(2,1)} all-reduce(f32[256,2048]{1,0:T(8,128)S(1)} %fusion.48), channel_id=1, replica_groups=mesh['dp'=96,'mp'=8] {'dp'}, use_global_device_ids=true, to_apply=%region_11.12 | all-reduce | flops 524288 | bytes 3145728 | tf_op jit(solution)/shard_map/psum | solution.py:143
  721.2 2.3 copy.29
  723.5 4.0 all-to-all-start
  727.6 123.6 %psum.23 = f32[2048]{0:T(1024)S(1)} all-reduce(f32[2048]{0:T(1024)S(1)} %get-tuple-element.19), channel_id=1, replica_groups=mesh['dp'=96,'mp'=8] {'dp','mp'}, use_global_device_ids=true, to_apply=%region_13.14 | all-reduce | flops 2048 | bytes 16384 | tf_op jit(solution)/shard_map/psum | solution.py:144
  851.1 0.6 dynamic-slice_multiply_fusion
  851.8 0.6 fusion.31
  852.4 1.5 convert_element_type.120
  (44 shorter events, 2.1 us)
Async XLA Ops:
  7.2 16.4 %copy-start = (bf16[256,2048]{1,0:T(8,128)(2,1)S(1)}, bf16[256,2048]{1,0:T(8,128)(2,1)}, u32[]{:S(2)}) copy-start(bf16[256,2048]{1,0:T(8,128)(2,1)} %param.17) | copy-start | bytes 3145732
  7.2 3.2 copy-start.2
  7.2 3.2 copy-start.7
  7.2 69.1 %reduce-scatter.2.cloned.1.call-start = ((), (), s32[]{:S(2)}) async-start(), calls=%async_computation.2 | async-start | bytes 2359296 | tf_op jit(solution)/shard_map/reduce_scatter | solution.py:108
  10.4 1.0 copy-start.3
  11.4 1.4 copy-start.4
  11.4 2.2 copy-start.8
  25.6 301.0 %all-gather.2.cloned.1.call-start = ((), (), s32[]{:S(2)}) async-start(), calls=%async_computation.3 | async-start | bytes 2359296 | tf_op jit(solution)/shard_map/all_gather | solution.py:139
  25.7 2.5 copy-start.5
  25.7 2.5 copy-start.6
  25.7 2.5 copy-start.9
  289.5 39.5 %copy-start.1 = (f32[96]{0:T(128)}, f32[96]{0:T(128)S(1)}, u32[]{:S(2)}) copy-start(f32[96]{0:T(128)S(1)} %all-reduce) | copy-start | bytes 1156
  723.5 128.9 %all-to-all-start = ((bf16[256,8,256]{2,0,1:T(8,128)(2,1)}), bf16[256,8,256]{2,0,1:T(8,128)(2,1)S(1)}, u32[]{:S(2)}, u32[]{:S(2)}) async-start(bf16[256,8,256]{2,0,1:T(8,128)(2,1)} %bitcast.36), calls=%async_computation.1 | async-start | bytes 2097152 | tf_op jit(solution)/shard_map/all_to_all | solution.py:145
Sparse Core Ops, SparseCore 0:
  25.7 50.4 reduce-scatter.1
  294.7 31.9 all-gather.1
where the time goes:
time: 862 us; the launch traced here: 861 us
  blocking collectives  723 us (84%)
  waiting for transfers between devices  80.2 us (9%)
  between operations  16.4 us (2%)
  matrix products  14.5 us (2%)
  other arithmetic  13.7 us (2%)
    psum x1, blocking collectives, body(): grad_summed = lax.psum(grad_local, 'dp')  392 us
    unnamed x1, blocking collectives  196 us
    psum x1, blocking collectives, body(): pooled_all = lax.psum(pooled_part, ('dp', 'mp'))  124 us
    reduce_scatter x1, waiting for transfers between devices, body(): lax.psum_scatter(jnp.dot(mixed, w_out, preferred_element_type=jnp.float32...  48.1 us
    all_gather x1, waiting for transfers between devices, body(): lax.all_gather(dresid.astype(jnp.bfloat16), 'mp', axis=0, tiled=True)  32.1 us
  transfers between devices with their start and end apart: 3, of which 2 were waited for; matrix products, arithmetic and copies ran while one was open for 0% of the time, Pallas kernels for 0%

commit v1 on v0

v1 whole, which is shorter than its diff:
```python
import jax
import jax.numpy as jnp
from jax import lax
from jax.sharding import PartitionSpec as P

QUERY_HEADS = 32
KEY_VALUE_HEADS = 8
HEAD_SIZE = 64
NX, NZ, NCORE = 4, 12, 2


EPS = 1e-05
THETA = 500000.0


def positions_of(lens, rows):
    ends = jnp.cumsum(lens)
    starts = ends - lens
    row_ids = jnp.arange(rows, dtype=jnp.int32)
    inside = (row_ids[:, None] >= starts[None, :]) & (row_ids[:, None] < ends[None, :])
    member = inside.astype(jnp.int32)
    segment = jnp.sum((row_ids[:, None] >= ends[None, :]).astype(jnp.int32), axis=1)
    offset = jnp.sum(member * starts[None, :], axis=1) + (1 - jnp.sum(member, axis=1)) * ends[-1]
    return (segment, row_ids - offset, member)


def rope_tables(positions):
    half = HEAD_SIZE // 2
    freq = THETA ** (-jnp.arange(half, dtype=jnp.float32) * 2.0 / HEAD_SIZE)
    angle = positions.astype(jnp.float32)[:, None] * freq[None, :]
    return (jnp.cos(angle), jnp.sin(angle))


def rotate(vecs, cosine, sine):
    half = vecs.shape[-1] // 2
    first = vecs[..., :half]
    second = vecs[..., half:]
    cos_b = cosine[:, None, :]
    sin_b = sine[:, None, :]
    return jnp.concatenate(
        [first * cos_b - second * sin_b, second * cos_b + first * sin_b], axis=-1
    )


def dp_groups():
    near = [[(x * NZ + z) * NCORE + c for x in range(NX) for c in range(NCORE)] for z in range(NZ)]
    far = [[(x * NZ + z) * NCORE + c for z in range(NZ)] for x in range(NX) for c in range(NCORE)]
    return near, far


def swap(parts, groups):
    return lax.all_to_all(parts, "dp", 0, 0, tiled=True, axis_index_groups=groups)


def body(
    hidden_rows,
    lengths,
    pair_order,
    gain_attn,
    w_query,
    key_weight,
    value_weight,
    w_out,
    gain_final,
    w_head,
):
    rows, width = hidden_rows.shape
    q_heads = w_query.shape[1] // HEAD_SIZE
    kv_heads = key_weight.shape[1] // HEAD_SIZE
    head_group = QUERY_HEADS // KEY_VALUE_HEADS
    n_mp = lax.axis_size("mp")
    n_dp = lax.axis_size("dp")
    my_part = lax.axis_index("mp")
    feat = width // n_mp
    near, far = dp_groups()
    w_cols = lax.all_to_all(w_out, "mp", split_axis=1, concat_axis=0, tiled=True)
    segment, positions, member_int = positions_of(lengths, rows)
    member = member_int.astype(jnp.float32)[:, 0]
    lens_f = lengths.astype(jnp.float32)
    x32 = hidden_rows.astype(jnp.float32)
    normalized_rows = (
        x32 * lax.rsqrt(jnp.mean(x32 * x32, axis=1, keepdims=True) + EPS) * gain_attn
    ).astype(jnp.bfloat16)
    cosine, sine = rope_tables(positions)
    query = jnp.dot(normalized_rows, w_query, preferred_element_type=jnp.float32).reshape(
        rows, q_heads, HEAD_SIZE
    )
    query = rotate(query, cosine, sine).astype(jnp.bfloat16)
    key_vectors = jnp.dot(normalized_rows, key_weight, preferred_element_type=jnp.float32).reshape(
        rows, kv_heads, HEAD_SIZE
    )
    key_vectors = rotate(key_vectors, cosine, sine).astype(jnp.bfloat16)
    value_rows = (
        jnp.dot(normalized_rows, value_weight, preferred_element_type=jnp.float32)
        .astype(jnp.bfloat16)
        .reshape(rows, kv_heads, HEAD_SIZE)
    )
    key_rep = jnp.repeat(key_vectors, head_group, axis=1)
    value_rep = jnp.repeat(value_rows, head_group, axis=1)
    row_ids = jnp.arange(rows, dtype=jnp.int32)
    scores = jnp.einsum(
        "qhd,khd->hqk", query, key_rep, preferred_element_type=jnp.float32
    ) * HEAD_SIZE ** (-0.5)
    allowed = (segment[:, None] == segment[None, :]) & (row_ids[None, :] <= row_ids[:, None])
    scores = jnp.where(allowed[None], scores, -1e30)
    top = jnp.max(scores, axis=2, keepdims=True)
    weights = jnp.exp(scores - top)
    probs = (weights / jnp.sum(weights, axis=2, keepdims=True)).astype(jnp.bfloat16)
    mixed = jnp.einsum("hqk,khd->qhd", probs, value_rep, preferred_element_type=jnp.float32)
    mixed = mixed.astype(jnp.bfloat16).reshape(rows, q_heads * HEAD_SIZE)

    mixed_all = lax.all_gather(mixed, "mp", axis=0, tiled=False)
    partials = jnp.einsum(
        "grc,gcd->grd",
        mixed_all,
        w_cols.reshape(n_mp, q_heads * HEAD_SIZE, feat),
        preferred_element_type=jnp.float32,
    ).astype(jnp.bfloat16)
    attended = jnp.sum(partials.astype(jnp.float32), axis=0)
    x_cols = lax.dynamic_slice_in_dim(hidden_rows, my_part * feat, feat, 1).astype(jnp.float32)
    gain_share = lax.dynamic_slice_in_dim(gain_final, my_part * feat, feat, 0)
    head_share = lax.dynamic_slice_in_dim(w_head, my_part * feat, feat, 0)
    both = gain_share * head_share
    resid = x_cols + attended
    stats = jnp.stack([jnp.sum(resid * resid, axis=1), jnp.sum(resid * both, axis=1)])
    stats = lax.all_to_all(
        jnp.broadcast_to(stats[None], (n_mp,) + stats.shape), "mp", 0, 0, tiled=True
    )
    stats = jnp.sum(stats, axis=0)
    scale = lax.rsqrt(stats[0] / width + EPS)
    row_score = stats[1] * scale
    my_reward = jnp.sum(member * row_score) / lens_f[0]
    rewards = lax.all_to_all(
        jnp.broadcast_to(my_reward, (n_dp, 1, 128)), "dp", 0, 0, tiled=True
    )[:, 0, 0]

    unit = resid * scale[:, None]
    weight = member / lens_f[0]
    dresid = (weight * scale)[:, None] * (both[None, :] - unit * (row_score / width)[:, None])
    grad_block = jnp.einsum(
        "grc,rd->gcd", mixed_all, dresid.astype(jnp.bfloat16), preferred_element_type=jnp.float32
    ).reshape(width, feat)
    pooled_block = jnp.sum(weight[:, None] * unit, axis=0)
    near_n, far_n = NX * NCORE, NZ
    piece = -(-(width + 1) // (near_n * far_n * 8)) * 8
    total_rows = piece * near_n * far_n
    block = jnp.concatenate(
        [
            grad_block.astype(jnp.bfloat16),
            jnp.pad(pooled_block[None], ((0, total_rows - width - 1), (0, 0))).astype(jnp.bfloat16),
        ],
        axis=0,
    )
    got = swap(block.reshape(near_n, far_n * piece, feat), near)

    total_seqs = rewards.shape[0]
    picked = rewards[pair_order].reshape(total_seqs // 2, 2)
    margin = picked[:, 0] - picked[:, 1]
    loss = jnp.sum(jax.nn.softplus(-margin))
    sig = jax.nn.sigmoid(-margin)
    per_pos = jnp.stack([-sig, sig], axis=1).reshape(total_seqs)
    dreward = jnp.zeros((total_seqs,), jnp.float32).at[pair_order].set(per_pos)
    my_z = (lax.axis_index("dp") // NCORE) % NZ
    near_dreward = lax.dynamic_slice_in_dim(dreward.reshape(NX, NZ, NCORE), my_z, 1, 1).reshape(near_n)
    summed = jnp.sum(got.astype(jnp.float32) * near_dreward[:, None, None], axis=0)
    got = swap(summed.astype(jnp.bfloat16).reshape(far_n, piece, feat), far)
    mine = jnp.sum(got.astype(jnp.float32), axis=0).astype(jnp.bfloat16)
    got = swap(jnp.broadcast_to(mine[None], (far_n, piece, feat)), far)
    got = swap(jnp.broadcast_to(got.reshape(1, far_n * piece, feat), (near_n, far_n * piece, feat)), near)
    got = got.reshape(total_rows, feat).astype(jnp.float32)
    grad_out_proj = got[:width]
    pooled = got[width]
    return (loss, rewards, grad_out_proj, gain_share * pooled, head_share * pooled)


def solution(mesh):
    placed = (
        P("dp", None),
        P("dp"),
        P(),
        P(),
        P(None, "mp"),
        P(None, "mp"),
        P(None, "mp"),
        P("mp", None),
        P(),
        P(),
    )
    return jax.shard_map(
        body,
        mesh=mesh,
        in_specs=placed,
        out_specs=(P(), P(), P(None, "mp"), P("mp"), P("mp")),
        check_vma=False,
    )
```

time: 862 us -> 222 us (0.26)
  blocking collectives: 723 us -> 28.1 us
  starting transfers between devices: 4.12 us -> 45.4 us
  waiting for transfers between devices: 80.2 us -> 91.7 us
    psum x3 -> x0, blocking collectives: 528 us -> none  [the longest x1 392 us: body(): grad_summed = lax.psum(grad_local, 'dp')]
    unnamed x1 -> x0, blocking collectives: 196 us -> none
    all_to_all x1 -> x5, waiting for transfers between devices: 0.01 us -> 68.8 us  [the longest x2 28.7 us: swap(): lax.all_to_all(parts, 'dp', 0, 0, tiled=True, axis_index_groups=groups)]
    reduce_scatter x1 -> x0, waiting for transfers between devices: 48.1 us -> none  [body(): lax.psum_scatter(jnp.dot(mixed, w_out, preferred_element_type=jnp.float32...]
    all_to_all x1 -> x5, starting transfers between devices: 4.04 us -> 45.3 us  [the longest x1 22.1 us: body(): lax.all_to_all(jnp.broadcast_to(my_reward, (n_dp, 1, 128)), 'dp', 0, 0, t...]
    all_to_all x0 -> x2, blocking collectives: none -> 28.1 us  [swap(): lax.all_to_all(parts, 'dp', 0, 0, tiled=True, axis_index_groups=groups)]
    all_gather x1, waiting for transfers between devices: 32.1 us -> 22.9 us  [body(): mixed_all = lax.all_gather(mixed, 'mp', axis=0, tiled=False)]
  transfers between devices with their start and end apart: 3 -> 6, of which waited for: 2 -> 6; matrix products, arithmetic and copies ran while one was open for 0% -> 6% of each run, Pallas kernels for 0% -> 0%
where the time goes in v1:
time: 222 us
  waiting for transfers between devices  91.7 us (41%)
  starting transfers between devices  45.4 us (20%)
  blocking collectives  28.1 us (13%)
  between operations  15.7 us (7%)
  matrix products  15.4 us (7%)
  local copies, waits for them, and re-layouts  13.8 us (6%)
  other arithmetic  11.7 us (5%)
    all_to_all x2, waiting for transfers between devices, swap(): lax.all_to_all(parts, 'dp', 0, 0, tiled=True, axis_index_groups=groups)  28.7 us
    all_to_all x2, blocking collectives, swap(): lax.all_to_all(parts, 'dp', 0, 0, tiled=True, axis_index_groups=groups)  28.1 us
    all_to_all x1, waiting for transfers between devices, body(): lax.all_to_all(w_out, 'mp', split_axis=1, concat_axis=0, tiled=True)  24.8 us
    all_gather x1, waiting for transfers between devices, body(): mixed_all = lax.all_gather(mixed, 'mp', axis=0, tiled=False)  22.9 us
    all_to_all x1, starting transfers between devices, body(): lax.all_to_all(jnp.broadcast_to(my_reward, (n_dp, 1, 128)), 'dp', 0, 0, t...  22.1 us
    all_to_all x2, starting transfers between devices, swap(): lax.all_to_all(parts, 'dp', 0, 0, tiled=True, axis_index_groups=groups)  11 us
    all_to_all x1, waiting for transfers between devices, body(): lax.all_to_all(jnp.broadcast_to(my_reward, (n_dp, 1, 128)), 'dp', 0, 0, t...  8.4 us
    all_to_all x1, starting transfers between devices, body(): lax.all_to_all(w_out, 'mp', split_axis=1, concat_axis=0, tiled=True)  7.65 us
  transfers between devices with their start and end apart: 6, of which 6 were waited for; matrix products, arithmetic and copies ran while one was open for 6% of the time, Pallas kernels for 0%

profile of v1, /device:TPU:1, one launch (start us, length us, event | category | flops | bytes accessed | tf_op | source)
XLA Modules:
  0.0 221.7 jit_solution(12027507444053308240)
XLA Ops:
  8.1 2.1 fusion.1
  11.4 1.4 convolution_convert_fusion.1
  16.3 4.5 %fusion.58 = (f32[4,512]{1,0:T(4,128)S(1)}, f32[4,512,512]{1,2,0:T(8,128)}) fusion(pred[512,512]{0,1:T(8,128)(4,1)S(1)} %fusion.13, bf16[512,4,32]{0,2,1:T(8,128)(2,1)} %get-tuple-element.10, bf16[512,4,32]{0,2,1:T(8,128)(2,1)S(1)} %get-tuple-element.9, bf16[512,64]{0,1:T(8,128)(2,1)} %pad_maximum_fusion.7), kind=kOutput, calls=%fused_computation.101 | convolution fusion | flops 138936832 | bytes 4792320 | tf_op jit(solution)/shard_map/sub | solution.py:107
  20.8 2.7 %fusion.10 = bf16[4,64,512]{2,1,0:T(8,128)(2,1)S(1)} fusion(f32[4,512,512]{1,2,0:T(8,128)} %get-tuple-element.24, f32[4,512]{1,0:T(4,128)S(1)} %get-tuple-element.23, bf16[512,64]{0,1:T(8,128)(2,1)} %convolution_convert_fusion.1), kind=kOutput, calls=%fused_computation.21 | convolution fusion | flops 136445952 | bytes 4530176 | tf_op jit(solution)/shard_map/hqk,khd->qhd/dot_general | solution.py:109
  23.5 0.8 copy.45
  24.4 2.3 %copy.46 = bf16[256,2048]{0,1:T(8,128)(2,1)} copy(bf16[256,2048]{1,0:T(8,128)(2,1)} %param.17) | data formatting | bytes 2097152 | tf_op args[7]
  26.6 2.3 %copy.47 = bf16[256,8,256]{2,0,1:T(8,128)(2,1)} copy(bf16[256,8,256]{0,2,1:T(8,128)(2,1)} %bitcast.44) | data formatting | bytes 2097152 | tf_op jit(solution)/shard_map/all_to_all | solution.py:76
  28.9 7.7 %all-to-all-start = ((bf16[256,8,256]{2,0,1:T(8,128)(2,1)}), bf16[256,8,256]{2,0,1:T(8,128)(2,1)}, u32[]{:S(2)}, u32[]{:S(2)}) async-start(bf16[256,8,256]{2,0,1:T(8,128)(2,1)} %copy.47), calls=%async_computation | async-start | bytes 2097152 | tf_op jit(solution)/shard_map/all_to_all | solution.py:76
  36.6 0.8 dynamic-slice_multiply_fusion.1
  37.3 24.8 %all-to-all-done = bf16[256,8,256]{2,0,1:T(8,128)(2,1)} async-done(((bf16[256,8,256]{2,0,1:T(8,128)(2,1)}), bf16[256,8,256]{2,0,1:T(8,128)(2,1)}, u32[]{:S(2)}, u32[]{:S(2)}) %all-to-all-start) | async-done | bytes 1048608 | tf_op jit(solution)/shard_map/all_to_all | solution.py:76
  62.1 22.9 %all-gather.2.cloned.1.call-done = bf16[8,512,256]{2,1,0:T(8,128)(2,1)} async-done(((bf16[1,512,256]{2,1,0:T(8,128)(2,1)}), bf16[8,512,256]{2,1,0:T(8,128)(2,1)}) %all-gather.2.cloned.1.call-update) | async-done | bytes 2097168 | tf_op jit(solution)/shard_map/all_gather | solution.py:112
  85.0 2.6 %convert_reduce_fusion = f32[512,256]{1,0:T(8,128)S(1)} fusion(bf16[8,512,256]{2,1,0:T(8,128)(2,1)} %all-gather.2.cloned.1.call-done, bf16[256,8,256]{2,0,1:T(8,128)(2,1)} %all-to-all-done), kind=kOutput, calls=%fused_computation.8 | convolution fusion | flops 539885568 | bytes 3670016 | tf_op jit(solution)/shard_map/grc,gcd->grd/dot_general | solution.py:113
  87.6 0.8 copy-done.3
  89.2 4.5 %all-to-all-start.1 = ((f32[8,2,512]{2,1,0:T(2,128)}), f32[8,2,512]{2,1,0:T(2,128)S(1)}, u32[]{:S(2)}, u32[]{:S(2)}) async-start(f32[8,2,512]{2,1,0:T(2,128)} %broadcast_in_dim.31), calls=%async_computation.1 | async-start | bytes 65536 | tf_op jit(solution)/shard_map/all_to_all | solution.py:126
  93.8 6.9 %all-to-all-done.1 = f32[8,2,512]{2,1,0:T(2,128)S(1)} async-done(((f32[8,2,512]{2,1,0:T(2,128)}), f32[8,2,512]{2,1,0:T(2,128)S(1)}, u32[]{:S(2)}, u32[]{:S(2)}) %all-to-all-start.1) | async-done | bytes 32800 | tf_op jit(solution)/shard_map/all_to_all | solution.py:126
  100.7 1.3 multiply_reduce_fusion.1
  103.9 22.1 %all-to-all-start.2 = ((f32[96,1,128]{2,1,0:T(1,128)}), f32[96,1,128]{2,1,0:T(1,128)S(1)}, u32[]{:S(2)}, u32[]{:S(2)}) async-start(f32[96,1,128]{2,1,0:T(1,128)} %broadcast_in_dim.32), calls=%async_computation.2 | async-start | bytes 98304 | tf_op jit(solution)/shard_map/all_to_all | solution.py:133
  126.0 2.7 %convolution_convert_fusion = bf16[8,256,256]{2,1,0:T(8,128)(2,1)S(1)} fusion(bf16[8,512,256]{2,1,0:T(8,128)(2,1)} %all-gather.2.cloned.1.call-done, f32[512]{0:T(512)S(1)} %get-tuple-element.14, f32[512]{0:T(512)S(1)} %bitcast.52, f32[512]{0:T(512)S(1)} %get-tuple-element.20, f32[256]{0:T(256)S(1)} %dynamic-slice_multiply_fusion.1, ...), kind=kOutput, calls=%fused_computation.20 | convolution fusion | flops 538312704 | bytes 3939332 | tf_op jit(solution)/shard_map/grc,rd->gcd/dot_general | solution.py:140
  128.7 1.1 fusion.11
  129.8 8.4 %all-to-all-done.2 = f32[96,1,128]{2,1,0:T(1,128)S(1)} async-done(((f32[96,1,128]{2,1,0:T(1,128)}), f32[96,1,128]{2,1,0:T(1,128)S(1)}, u32[]{:S(2)}, u32[]{:S(2)}) %all-to-all-start.2) | async-done | bytes 49184 | tf_op jit(solution)/shard_map/all_to_all | solution.py:133
  138.2 4.4 %all-to-all-start.3 = ((bf16[8,288,256]{2,1,0:T(8,128)(2,1)}), bf16[8,288,256]{2,1,0:T(8,128)(2,1)S(1)}, u32[]{:S(2)}, u32[]{:S(2)}) async-start(bf16[8,288,256]{2,1,0:T(8,128)(2,1)} %bitcast.16), calls=%async_computation.3 | async-start | bytes 2359296 | tf_op jit(solution)/shard_map/all_to_all | solution.py:52
  142.6 0.8 slice_reduce_fusion
  143.4 1.2 gather_fusion
  145.2 0.9 scatter_custom_fusion
  146.3 12.8 %all-to-all-done.3 = bf16[8,288,256]{2,1,0:T(8,128)(2,1)S(1)} async-done(((bf16[8,288,256]{2,1,0:T(8,128)(2,1)}), bf16[8,288,256]{2,1,0:T(8,128)(2,1)S(1)}, u32[]{:S(2)}, u32[]{:S(2)}) %all-to-all-start.3) | async-done | bytes 1179680 | tf_op jit(solution)/shard_map/all_to_all | solution.py:52
  159.4 13.9 %all_to_all.46 = bf16[12,24,256]{2,1,0:T(8,128)(2,1)S(1)} all-to-all(bf16[12,24,256]{2,1,0:T(8,128)(2,1)S(1)} %bitcast.46), channel_id=1, replica_groups={{0,16,32,48,64,80,96,112,128,144,160,176},{8,24,40,56,72,88,104,120,136..., dimensions={0} | all-to-all | bytes 294912 | tf_op jit(solution)/shard_map/all_to_all | solution.py:52
  173.4 14.2 %all_to_all.47 = bf16[12,24,256]{2,1,0:T(8,128)(2,1)S(1)} all-to-all(bf16[12,24,256]{2,1,0:T(8,128)(2,1)S(1)} %broadcast_in_dim.36), channel_id=1, replica_groups={{0,16,32,48,64,80,96,112,128,144,160,176},{8,24,40,56,72,88,104,120,136..., dimensions={0} | all-to-all | bytes 294912 | tf_op jit(solution)/shard_map/all_to_all | solution.py:52
  187.5 1.1 broadcast_in_dim.38
  188.6 6.6 %all-to-all-start.6 = ((bf16[8,288,256]{2,1,0:T(8,128)(2,1)}), bf16[8,288,256]{2,1,0:T(8,128)(2,1)S(1)}, u32[]{:S(2)}, u32[]{:S(2)}) async-start(bf16[8,288,256]{2,1,0:T(8,128)(2,1)} %broadcast_in_dim.38), calls=%async_computation.6 | async-start | bytes 2359296 | tf_op jit(solution)/shard_map/all_to_all | solution.py:52
  195.9 15.9 %all-to-all-done.6 = bf16[8,288,256]{2,1,0:T(8,128)(2,1)S(1)} async-done(((bf16[8,288,256]{2,1,0:T(8,128)(2,1)}), bf16[8,288,256]{2,1,0:T(8,128)(2,1)S(1)}, u32[]{:S(2)}, u32[]{:S(2)}) %all-to-all-start.6) | async-done | bytes 1179680 | tf_op jit(solution)/shard_map/all_to_all | solution.py:52
  212.0 1.5 slice.55
  213.5 1.3 dynamic-slice_multiply_fusion
  (53 shorter events, 8.9 us)
Async XLA Ops:
  7.2 6.4 %copy-start = (bf16[2048,256]{1,0:T(8,128)(2,1)S(1)}, bf16[2048,256]{1,0:T(8,128)(2,1)}, u32[]{:S(2)}) copy-start(bf16[2048,256]{1,0:T(8,128)(2,1)} %param.14) | copy-start | bytes 3145732
  7.2 3.2 %copy-start.2 = (bf16[512,2048]{1,0:T(8,128)(2,1)S(1)}, bf16[512,2048]{1,0:T(8,128)(2,1)}, u32[]{:S(2)}) copy-start(bf16[512,2048]{1,0:T(8,128)(2,1)} %param.10) | copy-start | bytes 6291460
  7.2 3.2 %copy-start.6 = (f32[2048]{0:T(1024)S(1)}, f32[2048]{0:T(1024)}, u32[]{:S(2)}) copy-start(f32[2048]{0:T(1024)} %param.13) | copy-start | bytes 24580
  7.2 77.8 %all-gather.2.cloned.1.call-start = ((), (), s32[]{:S(2)}) async-start(), calls=%async_computation.7 | async-start | bytes 2359296 | tf_op jit(solution)/shard_map/all_gather | solution.py:112
  10.4 1.0 copy-start.4
  11.4 1.4 copy-start.5
  28.9 33.2 %all-to-all-start = ((bf16[256,8,256]{2,0,1:T(8,128)(2,1)}), bf16[256,8,256]{2,0,1:T(8,128)(2,1)}, u32[]{:S(2)}, u32[]{:S(2)}) async-start(bf16[256,8,256]{2,0,1:T(8,128)(2,1)} %copy.47), calls=%async_computation | async-start | bytes 2097152 | tf_op jit(solution)/shard_map/all_to_all | solution.py:76
  87.6 0.8 copy-start.3
  89.2 11.4 %all-to-all-start.1 = ((f32[8,2,512]{2,1,0:T(2,128)}), f32[8,2,512]{2,1,0:T(2,128)S(1)}, u32[]{:S(2)}, u32[]{:S(2)}) async-start(f32[8,2,512]{2,1,0:T(2,128)} %broadcast_in_dim.31), calls=%async_computation.1 | async-start | bytes 65536 | tf_op jit(solution)/shard_map/all_to_all | solution.py:126
  103.9 34.4 %all-to-all-start.2 = ((f32[96,1,128]{2,1,0:T(1,128)}), f32[96,1,128]{2,1,0:T(1,128)S(1)}, u32[]{:S(2)}, u32[]{:S(2)}) async-start(f32[96,1,128]{2,1,0:T(1,128)} %broadcast_in_dim.32), calls=%async_computation.2 | async-start | bytes 98304 | tf_op jit(solution)/shard_map/all_to_all | solution.py:133
  128.7 13.9 %copy-start.7 = (s32[96]{0:T(128)S(1)}, s32[96]{0:T(128)}, u32[]{:S(2)}) copy-start(s32[96]{0:T(128)} %param.12) | copy-start | bytes 1156
  138.2 20.9 %all-to-all-start.3 = ((bf16[8,288,256]{2,1,0:T(8,128)(2,1)}), bf16[8,288,256]{2,1,0:T(8,128)(2,1)S(1)}, u32[]{:S(2)}, u32[]{:S(2)}) async-start(bf16[8,288,256]{2,1,0:T(8,128)(2,1)} %bitcast.16), calls=%async_computation.3 | async-start | bytes 2359296 | tf_op jit(solution)/shard_map/all_to_all | solution.py:52
  143.4 45.2 %copy-start.1 = (f32[96]{0:T(128)}, f32[96]{0:T(128)S(1)}, u32[]{:S(2)}) copy-start(f32[96]{0:T(128)S(1)} %slice_reduce_fusion) | copy-start | bytes 1156
  188.6 23.2 %all-to-all-start.6 = ((bf16[8,288,256]{2,1,0:T(8,128)(2,1)}), bf16[8,288,256]{2,1,0:T(8,128)(2,1)S(1)}, u32[]{:S(2)}, u32[]{:S(2)}) async-start(bf16[8,288,256]{2,1,0:T(8,128)(2,1)} %broadcast_in_dim.38), calls=%async_computation.6 | async-start | bytes 2359296 | tf_op jit(solution)/shard_map/all_to_all | solution.py:52
Sparse Core Ops, SparseCore 0:
  24.5 60.4 all-gather.1

commit v2 on v1

--- a/solution.py
+++ b/solution.py
@@ -42,14 +42,23 @@
     )
 
 
+def device_of(x, z, core):
+    return (x * NZ + z) * NCORE + core
+
+
 def dp_groups():
-    near = [[(x * NZ + z) * NCORE + c for x in range(NX) for c in range(NCORE)] for z in range(NZ)]
-    far = [[(x * NZ + z) * NCORE + c for z in range(NZ)] for x in range(NX) for c in range(NCORE)]
-    return near, far
+    along_x = [[device_of(x, z, c) for x in range(NX)] for z in range(NZ) for c in range(NCORE)]
+    along_z = [[device_of(x, z, c) for z in range(NZ)] for x in range(NX) for c in range(NCORE)]
+    return along_x, along_z
 
 
 def swap(parts, groups):
     return lax.all_to_all(parts, "dp", 0, 0, tiled=True, axis_index_groups=groups)
+
+
+def to_sibling(x):
+    pairs = [(i, i ^ 1) for i in range(NX * NZ * NCORE)]
+    return lax.ppermute(x, "dp", pairs)
 
 
 def body(
@@ -72,8 +81,13 @@
     n_dp = lax.axis_size("dp")
     my_part = lax.axis_index("mp")
     feat = width // n_mp
-    near, far = dp_groups()
-    w_cols = lax.all_to_all(w_out, "mp", split_axis=1, concat_axis=0, tiled=True)
+    along_x, along_z = dp_groups()
+    core = lax.axis_index("dp") % NCORE
+    half_rows = w_out.shape[0] // NCORE
+    w_half = lax.dynamic_slice_in_dim(w_out, core * half_rows, half_rows, 0)
+    w_half = lax.all_to_all(
+        w_half.reshape(half_rows, n_mp, feat).swapaxes(0, 1), "mp", 0, 0, tiled=True
+    )
     segment, positions, member_int = positions_of(lengths, rows)
     member = member_int.astype(jnp.float32)[:, 0]
     lens_f = lengths.astype(jnp.float32)
@@ -109,11 +123,17 @@
     mixed = jnp.einsum("hqk,khd->qhd", probs, value_rep, preferred_element_type=jnp.float32)
     mixed = mixed.astype(jnp.bfloat16).reshape(rows, q_heads * HEAD_SIZE)
 
+    mixed, w_half = lax.optimization_barrier((mixed, w_half))
+    w_other = to_sibling(w_half)
+    w_cols = jnp.concatenate(
+        [jnp.where(core == 0, w_half, w_other), jnp.where(core == 0, w_other, w_half)], axis=1
+    )
+
     mixed_all = lax.all_gather(mixed, "mp", axis=0, tiled=False)
     partials = jnp.einsum(
         "grc,gcd->grd",
         mixed_all,
-        w_cols.reshape(n_mp, q_heads * HEAD_SIZE, feat),
+        w_cols,
         preferred_element_type=jnp.float32,
     ).astype(jnp.bfloat16)
     attended = jnp.sum(partials.astype(jnp.float32), axis=0)
@@ -141,17 +161,14 @@
         "grc,rd->gcd", mixed_all, dresid.astype(jnp.bfloat16), preferred_element_type=jnp.float32
     ).reshape(width, feat)
     pooled_block = jnp.sum(weight[:, None] * unit, axis=0)
-    near_n, far_n = NX * NCORE, NZ
-    piece = -(-(width + 1) // (near_n * far_n * 8)) * 8
-    total_rows = piece * near_n * far_n
-    block = jnp.concatenate(
-        [
-            grad_block.astype(jnp.bfloat16),
-            jnp.pad(pooled_block[None], ((0, total_rows - width - 1), (0, 0))).astype(jnp.bfloat16),
-        ],
-        axis=0,
-    )
-    got = swap(block.reshape(near_n, far_n * piece, feat), near)
+    half = width // NCORE
+    piece = -(-(half + 1) // (NX * NZ * 8)) * 8
+    half_ext = piece * NX * NZ
+    extra = jnp.pad(pooled_block[None], ((0, half_ext - half - 1), (0, 0))).astype(jnp.bfloat16)
+    grad_block = grad_block.astype(jnp.bfloat16).reshape(NCORE, half, feat)
+    keep = jnp.concatenate([lax.dynamic_index_in_dim(grad_block, core, 0, False), extra], axis=0)
+    send = jnp.concatenate([lax.dynamic_index_in_dim(grad_block, 1 - core, 0, False), extra], axis=0)
+    got = to_sibling(send)
 
     total_seqs = rewards.shape[0]
     picked = rewards[pair_order].reshape(total_seqs // 2, 2)
@@ -160,16 +177,22 @@
     sig = jax.nn.sigmoid(-margin)
     per_pos = jnp.stack([-sig, sig], axis=1).reshape(total_seqs)
     dreward = jnp.zeros((total_seqs,), jnp.float32).at[pair_order].set(per_pos)
-    my_z = (lax.axis_index("dp") // NCORE) % NZ
-    near_dreward = lax.dynamic_slice_in_dim(dreward.reshape(NX, NZ, NCORE), my_z, 1, 1).reshape(near_n)
-    summed = jnp.sum(got.astype(jnp.float32) * near_dreward[:, None, None], axis=0)
-    got = swap(summed.astype(jnp.bfloat16).reshape(far_n, piece, feat), far)
+    me = lax.axis_index("dp")
+    own = lax.dynamic_index_in_dim(dreward, me, 0, False)
+    sib = lax.dynamic_index_in_dim(dreward, me ^ 1, 0, False)
+    summed = keep.astype(jnp.float32) * own + got.astype(jnp.float32) * sib
+    got = swap(summed.astype(jnp.bfloat16).reshape(NX, NZ * piece, feat), along_x)
+    summed = jnp.sum(got.astype(jnp.float32), axis=0).astype(jnp.bfloat16)
+    got = swap(summed.reshape(NZ, piece, feat), along_z)
     mine = jnp.sum(got.astype(jnp.float32), axis=0).astype(jnp.bfloat16)
-    got = swap(jnp.broadcast_to(mine[None], (far_n, piece, feat)), far)
-    got = swap(jnp.broadcast_to(got.reshape(1, far_n * piece, feat), (near_n, far_n * piece, feat)), near)
-    got = got.reshape(total_rows, feat).astype(jnp.float32)
-    grad_out_proj = got[:width]
-    pooled = got[width]
+    got = swap(jnp.broadcast_to(mine[None], (NZ, piece, feat)), along_z)
+    got = swap(jnp.broadcast_to(got.reshape(1, NZ * piece, feat), (NX, NZ * piece, feat)), along_x)
+    got = got.reshape(half_ext, feat)
+    other = to_sibling(got)
+    lower = jnp.where(core == 0, got, other)
+    upper = jnp.where(core == 0, other, got)
+    grad_out_proj = jnp.concatenate([lower[:half], upper[:half]], axis=0).astype(jnp.float32)
+    pooled = got[half].astype(jnp.float32)
     return (loss, rewards, grad_out_proj, gain_share * pooled, head_share * pooled)
 
 

time: 222 us -> 216 us (0.973)
  waiting for transfers between devices: 91.7 us -> 51.3 us
  blocking collectives: 28.1 us -> 49.2 us
  starting transfers between devices: 45.4 us -> 50.5 us
  local copies, waits for them, and re-layouts: 13.8 us -> 17.3 us
  other arithmetic: 11.7 us -> 15 us
    all_to_all x3 -> x1, waiting for transfers between devices: 53.5 us -> 0.01 us  [body(): lax.all_to_all(w_half.reshape(half_rows, n_mp, feat).swapaxes(0, 1), 'mp'...]
    all_to_all x2 -> x4, blocking collectives: 28.1 us -> 49.2 us  [swap(): lax.all_to_all(parts, 'dp', 0, 0, tiled=True, axis_index_groups=groups)]
    ppermute x0 -> x3, starting transfers between devices: none -> 19.2 us  [to_sibling(): return lax.ppermute(x, 'dp', pairs)]
    all_gather x1, waiting for transfers between devices: 22.9 us -> 36.8 us  [body(): mixed_all = lax.all_gather(mixed, 'mp', axis=0, tiled=False)]
    all_to_all x3 -> x1, starting transfers between devices: 18.7 us -> 7.65 us  [body(): lax.all_to_all(w_half.reshape(half_rows, n_mp, feat).swapaxes(0, 1), 'mp'...]
    all_gather x0 -> x1, local copies, waits for them, and re-layouts: none -> 4.06 us  [body(): mixed_all = lax.all_gather(mixed, 'mp', axis=0, tiled=False)]
    convert_element_type x1 -> x3, other arithmetic: 0.25 us -> 4.08 us  [the longest x1 2.6 us: body(): summed.astype(jnp.bfloat16).reshape(NX, NZ * piece, feat)]
    all_to_all x1, starting transfers between devices: 22.1 us -> 19.5 us  [body(): lax.all_to_all(jnp.broadcast_to(my_reward, (n_dp, 1, 128)), 'dp', 0, 0, t...]
  transfers between devices with their start and end apart: 6 -> 7, of which waited for: 6 -> 4; matrix products, arithmetic and copies ran while one was open for 6% -> 12% of each run, Pallas kernels for 0% -> 0%
where the time goes in v2:
time: 216 us; the launch traced here: 215 us
  waiting for transfers between devices  51.3 us (24%)
  starting transfers between devices  50.5 us (23%)
  blocking collectives  49.2 us (23%)
  local copies, waits for them, and re-layouts  17.3 us (8%)
  matrix products  16.1 us (7%)
  between operations  15.7 us (7%)
  other arithmetic  15 us (7%)
    all_to_all x4, blocking collectives, swap(): lax.all_to_all(parts, 'dp', 0, 0, tiled=True, axis_index_groups=groups)  49.2 us
    all_gather x1, waiting for transfers between devices, body(): mixed_all = lax.all_gather(mixed, 'mp', axis=0, tiled=False)  36.8 us
    all_to_all x1, starting transfers between devices, body(): lax.all_to_all(jnp.broadcast_to(my_reward, (n_dp, 1, 128)), 'dp', 0, 0, t...  19.5 us
    ppermute x3, starting transfers between devices, to_sibling(): return lax.ppermute(x, 'dp', pairs)  19.2 us
    all_to_all x1, starting transfers between devices, body(): lax.all_to_all(w_half.reshape(half_rows, n_mp, feat).swapaxes(0, 1), 'mp'...  7.65 us
    all_to_all x1, waiting for transfers between devices, body(): lax.all_to_all(jnp.broadcast_to(stats[None], (n_mp,) + stats.shape), 'mp'...  6.87 us
    all_to_all x1, waiting for transfers between devices, body(): lax.all_to_all(jnp.broadcast_to(my_reward, (n_dp, 1, 128)), 'dp', 0, 0, t...  6.49 us
    unnamed x21, local copies, waits for them, and re-layouts  5.25 us
  transfers between devices with their start and end apart: 7, of which 4 were waited for; matrix products, arithmetic and copies ran while one was open for 12% of the time, Pallas kernels for 0%

profile of v2, /device:TPU:1, one launch (start us, length us, event | category | flops | bytes accessed | tf_op | source)
XLA Modules:
  0.0 214.9 jit_solution(5896992952816837503)
XLA Ops:
  7.2 1.2 copy-done
  8.4 0.8 constant_dynamic-slice_fusion
  9.2 2.0 copy.53
  11.3 2.1 copy.46
  13.3 7.7 %all-to-all-start = ((bf16[8,128,256]{2,1,0:T(8,128)(2,1)}), bf16[8,128,256]{2,1,0:T(8,128)(2,1)}, u32[]{:S(2)}, u32[]{:S(2)}) async-start(bf16[8,128,256]{2,1,0:T(8,128)(2,1)} %bitcast.53), calls=%async_computation | async-start | bytes 1048576 | tf_op jit(solution)/shard_map/all_to_all | solution.py:88
  23.4 1.4 convolution_convert_fusion.1
  28.3 4.5 %fusion.63 = (f32[4,512]{1,0:T(4,128)S(1)}, f32[4,512,512]{1,2,0:T(8,128)}) fusion(pred[512,512]{0,1:T(8,128)(4,1)S(1)} %fusion.14, bf16[512,4,32]{0,2,1:T(8,128)(2,1)} %get-tuple-element.20, bf16[512,4,32]{0,2,1:T(8,128)(2,1)S(1)} %get-tuple-element.19, bf16[512,64]{0,1:T(8,128)(2,1)} %pad_maximum_fusion.7), kind=kOutput, calls=%fused_computation.113 | convolution fusion | flops 138936832 | bytes 4792320 | tf_op jit(solution)/shard_map/sub | solution.py:121
  32.8 3.4 %fusion.9 = bf16[4,64,512]{2,1,0:T(8,128)(2,1)} fusion(f32[4,512,512]{1,2,0:T(8,128)} %get-tuple-element.36, f32[4,512]{1,0:T(4,128)S(1)} %get-tuple-element.35, bf16[512,64]{0,1:T(8,128)(2,1)} %convolution_convert_fusion.1), kind=kOutput, calls=%fused_computation.18 | convolution fusion | flops 136445952 | bytes 4530176 | tf_op jit(solution)/shard_map/hqk,khd->qhd/dot_general | solution.py:123
  36.2 8.9 %collective-permute-start = (bf16[8,128,256]{2,1,0:T(8,128)(2,1)}, bf16[8,128,256]{2,1,0:T(8,128)(2,1)}, u32[]{:S(2)}, u32[]{:S(2)}) collective-permute-start(bf16[8,128,256]{2,1,0:T(8,128)(2,1)} %all-to-all-done), channel_id=1, source_target_pairs={{0,8},{8,0},{16,24},{24,16},{32,40},{40,32},{48,56},{56,48},{64,72... | collective-permute-start | bytes 1572872 | tf_op jit(solution)/shard_map/ppermute | solution.py:61
  46.0 1.1 collective-permute-done
  47.0 2.3 %broadcast_select_fusion.3 = (bf16[8,128,256]{2,1,0:T(8,128)(2,1)}, bf16[8,128,256]{2,1,0:T(8,128)(2,1)}) fusion(bf16[8,128,256]{2,1,0:T(8,128)(2,1)} %all-to-all-done, bf16[8,128,256]{2,1,0:T(8,128)(2,1)} %collective-permute-done, pred[]{:T(512)S(6)} %eq.28), kind=kLoop, calls=%fused_computation.42 | loop fusion | flops 524288 | bytes 2097153 | tf_op jit(solution)/shard_map/jit(_where)/select_n | solution.py:129
  49.3 36.8 %all-gather.3.cloned.1.call-done = bf16[4096,256]{0,1:T(8,128)(2,1)} async-done(((bf16[512,256]{0,1:T(8,128)(2,1)}), bf16[4096,256]{0,1:T(8,128)(2,1)}) %all-gather.3.cloned.1.call-update) | async-done | bytes 2097168 | tf_op jit(solution)/shard_map/all_gather | solution.py:132
  86.1 4.1 %copy.47 = bf16[4096,256]{1,0:T(8,128)(2,1)} copy(bf16[4096,256]{0,1:T(8,128)(2,1)} %all-gather.3.cloned.1.call-done) | data formatting | bytes 4194304 | tf_op jit(solution)/shard_map/all_gather | solution.py:132
  90.2 2.6 %convert_reduce_fusion = f32[512,256]{1,0:T(8,128)S(1)} fusion(bf16[8,512,256]{2,1,0:T(8,128)(2,1)} %bitcast.51, bf16[8,128,256]{2,1,0:T(8,128)(2,1)} %get-tuple-element.18, bf16[8,128,256]{2,1,0:T(8,128)(2,1)} %get-tuple-element.17), kind=kOutput, calls=%fused_computation.8 | convolution fusion | flops 541982720 | bytes 3670016 | tf_op jit(solution)/shard_map/grc,gcd->grd/dot_general | solution.py:133
  94.4 4.0 %all-to-all-start.1 = ((f32[8,2,512]{2,1,0:T(2,128)}), f32[8,2,512]{2,1,0:T(2,128)S(1)}, u32[]{:S(2)}, u32[]{:S(2)}) async-start(f32[8,2,512]{2,1,0:T(2,128)} %broadcast_in_dim.31), calls=%async_computation.1 | async-start | bytes 65536 | tf_op jit(solution)/shard_map/all_to_all | solution.py:146
  98.5 6.9 %all-to-all-done.1 = f32[8,2,512]{2,1,0:T(2,128)S(1)} async-done(((f32[8,2,512]{2,1,0:T(2,128)}), f32[8,2,512]{2,1,0:T(2,128)S(1)}, u32[]{:S(2)}, u32[]{:S(2)}) %all-to-all-start.1) | async-done | bytes 32800 | tf_op jit(solution)/shard_map/all_to_all | solution.py:146
  105.4 1.3 multiply_reduce_fusion
  108.5 19.5 %all-to-all-start.2 = ((f32[96,1,128]{2,1,0:T(1,128)}), f32[96,1,128]{2,1,0:T(1,128)S(1)}, u32[]{:S(2)}, u32[]{:S(2)}) async-start(f32[96,1,128]{2,1,0:T(1,128)} %broadcast_in_dim.32), calls=%async_computation.2 | async-start | bytes 98304 | tf_op jit(solution)/shard_map/all_to_all | solution.py:153
  128.1 2.7 %convolution_convert_fusion = bf16[8,256,256]{2,1,0:T(8,128)(2,1)S(1)} fusion(bf16[8,512,256]{2,1,0:T(8,128)(2,1)} %bitcast.52, f32[512]{0:T(512)S(1)} %get-tuple-element.24, f32[512]{0:T(512)S(1)} %bitcast.62, f32[512]{0:T(512)S(1)} %get-tuple-element.30, f32[256]{0:T(256)S(1)} %dynamic-slice_multiply_fusion.1, f32[512,256]{1,0:T(8,128)} %copy-done.3, ...), kind=kOutput, calls=%fused_computation.17 | convolution fusion | flops 538312704 | bytes 3939332 | tf_op jit(solution)/shard_map/grc,rd->gcd/dot_general | solution.py:160
  130.9 2.8 %collective-permute-start.1 = (bf16[1152,256]{1,0:T(8,128)(2,1)S(1)}, bf16[1152,256]{1,0:T(8,128)(2,1)S(1)}, u32[]{:S(2)}, u32[]{:S(2)}) collective-permute-start(bf16[1152,256]{1,0:T(8,128)(2,1)S(1)} %fusion.16), channel_id=1, source_target_pairs={{0,8},{8,0},{16,24},{24,16},{32,40},{40,32},{48,56},{56,48},{64,72... | collective-permute-start | bytes 1769480 | tf_op jit(solution)/shard_map/ppermute | solution.py:61
  133.7 6.5 %all-to-all-done.2 = f32[96,1,128]{2,1,0:T(1,128)S(1)} async-done(((f32[96,1,128]{2,1,0:T(1,128)}), f32[96,1,128]{2,1,0:T(1,128)S(1)}, u32[]{:S(2)}, u32[]{:S(2)}) %all-to-all-start.2) | async-done | bytes 49184 | tf_op jit(solution)/shard_map/all_to_all | solution.py:153
  141.0 1.2 gather_fusion
  142.8 0.9 scatter_custom_fusion
  144.3 0.8 copy-done.4
  145.1 2.6 %add_convert_fusion = bf16[1152,256]{1,0:T(8,128)(2,1)S(1)} fusion(bf16[1152,256]{1,0:T(8,128)(2,1)} %copy-done.4, bf16[1,256]{1,0:T(2,128)(2,1)S(1)} %broadcast_in_dim.34, bf16[1024,256]{1,0:T(8,128)(2,1)S(1)} %get-tuple-element.15, f32[]{:T(128)} %bitcast.20, f32[]{:T(128)} %bitcast.18), kind=kLoop, calls=%fused_computation.20 | loop fusion | flops 3244032 | bytes 1704456 | tf_op jit(solution)/shard_map/convert_element_type | solution.py:184
  147.7 11.4 %all_to_all.35 = bf16[4,288,256]{2,1,0:T(8,128)(2,1)S(1)} all-to-all(bf16[4,288,256]{2,1,0:T(8,128)(2,1)S(1)} %bitcast.47), channel_id=1, replica_groups={{0,192,384,576},{8,200,392,584},{16,208,400,592},{24,216,408,600},{32,2..., dimensions={0} | all-to-all | bytes 1179648 | tf_op jit(solution)/shard_map/all_to_all | solution.py:56
  159.2 15.0 %all_to_all.36 = bf16[12,24,256]{2,1,0:T(8,128)(2,1)S(1)} all-to-all(bf16[12,24,256]{2,1,0:T(8,128)(2,1)S(1)} %bitcast.56), channel_id=1, replica_groups={{0,16,32,48,64,80,96,112,128,144,160,176},{8,24,40,56,72,88,104,120,136..., dimensions={0} | all-to-all | bytes 294912 | tf_op jit(solution)/shard_map/all_to_all | solution.py:56
  174.2 13.1 %all_to_all.37 = bf16[12,24,256]{2,1,0:T(8,128)(2,1)S(1)} all-to-all(bf16[12,24,256]{2,1,0:T(8,128)(2,1)S(1)} %broadcast_in_dim.36), channel_id=1, replica_groups={{0,16,32,48,64,80,96,112,128,144,160,176},{8,24,40,56,72,88,104,120,136..., dimensions={0} | all-to-all | bytes 294912 | tf_op jit(solution)/shard_map/all_to_all | solution.py:56
  187.4 9.7 %all_to_all.38 = bf16[4,288,256]{2,1,0:T(8,128)(2,1)S(1)} all-to-all(bf16[4,288,256]{2,1,0:T(8,128)(2,1)S(1)} %broadcast_in_dim.38), channel_id=1, replica_groups={{0,192,384,576},{8,200,392,584},{16,208,400,592},{24,216,408,600},{32,2..., dimensions={0} | all-to-all | bytes 1179648 | tf_op jit(solution)/shard_map/all_to_all | solution.py:56
  197.1 7.5 %collective-permute-start.2 = (bf16[1152,256]{1,0:T(8,128)(2,1)S(1)}, bf16[1152,256]{1,0:T(8,128)(2,1)S(1)}, u32[]{:S(2)}, u32[]{:S(2)}) collective-permute-start(bf16[1152,256]{1,0:T(8,128)(2,1)S(1)} %bitcast.48), channel_id=1, source_target_pairs={{0,8},{8,0},{16,24},{24,16},{32,40},{40,32},{48,56},{56,48},{64,72... | collective-permute-start | bytes 1769480 | tf_op jit(solution)/shard_map/ppermute | solution.py:61
  205.2 1.3 dynamic-slice_multiply_fusion
  206.6 1.5 maximum_convert_fusion
  (63 shorter events, 11.9 us)
Async XLA Ops:
  7.2 1.2 copy-start
  8.4 13.3 %copy-start.2 = (bf16[512,2048]{1,0:T(8,128)(2,1)S(1)}, bf16[512,2048]{1,0:T(8,128)(2,1)}, u32[]{:S(2)}) copy-start(bf16[512,2048]{1,0:T(8,128)(2,1)} %param.10) | copy-start | bytes 6291460
  11.3 11.2 %copy-start.7 = (f32[2048]{0:T(1024)S(1)}, f32[2048]{0:T(1024)}, u32[]{:S(2)}) copy-start(f32[2048]{0:T(1024)} %param.13) | copy-start | bytes 24580
  13.3 22.9 %all-to-all-start = ((bf16[8,128,256]{2,1,0:T(8,128)(2,1)}), bf16[8,128,256]{2,1,0:T(8,128)(2,1)}, u32[]{:S(2)}, u32[]{:S(2)}) async-start(bf16[8,128,256]{2,1,0:T(8,128)(2,1)} %bitcast.53), calls=%async_computation | async-start | bytes 1048576 | tf_op jit(solution)/shard_map/all_to_all | solution.py:88
  21.0 65.1 %all-gather.3.cloned.1.call-start = ((), (), s32[]{:S(2)}) async-start(), calls=%async_computation.7 | async-start | bytes 2359296 | tf_op jit(solution)/shard_map/all_gather | solution.py:132
  22.4 1.0 copy-start.5
  23.4 1.4 copy-start.6
  23.4 2.2 %copy-start.8 = (bf16[2048,256]{1,0:T(8,128)(2,1)S(1)}, bf16[2048,256]{1,0:T(8,128)(2,1)}, u32[]{:S(2)}) copy-start(bf16[2048,256]{1,0:T(8,128)(2,1)} %param.14) | copy-start | bytes 3145732
  36.2 10.8 %collective-permute-start = (bf16[8,128,256]{2,1,0:T(8,128)(2,1)}, bf16[8,128,256]{2,1,0:T(8,128)(2,1)}, u32[]{:S(2)}, u32[]{:S(2)}) collective-permute-start(bf16[8,128,256]{2,1,0:T(8,128)(2,1)} %all-to-all-done), channel_id=1, source_target_pairs={{0,8},{8,0},{16,24},{24,16},{32,40},{40,32},{48,56},{56,48},{64,72... | collective-permute-start | bytes 1572872 | tf_op jit(solution)/shard_map/ppermute | solution.py:61
  92.8 0.8 copy-start.3
  94.4 10.9 %all-to-all-start.1 = ((f32[8,2,512]{2,1,0:T(2,128)}), f32[8,2,512]{2,1,0:T(2,128)S(1)}, u32[]{:S(2)}, u32[]{:S(2)}) async-start(f32[8,2,512]{2,1,0:T(2,128)} %broadcast_in_dim.31), calls=%async_computation.1 | async-start | bytes 65536 | tf_op jit(solution)/shard_map/all_to_all | solution.py:146
  108.5 31.7 %all-to-all-start.2 = ((f32[96,1,128]{2,1,0:T(1,128)}), f32[96,1,128]{2,1,0:T(1,128)S(1)}, u32[]{:S(2)}, u32[]{:S(2)}) async-start(f32[96,1,128]{2,1,0:T(1,128)} %broadcast_in_dim.32), calls=%async_computation.2 | async-start | bytes 98304 | tf_op jit(solution)/shard_map/all_to_all | solution.py:153
  130.8 2.9 %copy-start.9 = (s32[96]{0:T(128)S(1)}, s32[96]{0:T(128)}, u32[]{:S(2)}) copy-start(s32[96]{0:T(128)} %param.12) | copy-start | bytes 1156
  130.9 13.3 %collective-permute-start.1 = (bf16[1152,256]{1,0:T(8,128)(2,1)S(1)}, bf16[1152,256]{1,0:T(8,128)(2,1)S(1)}, u32[]{:S(2)}, u32[]{:S(2)}) collective-permute-start(bf16[1152,256]{1,0:T(8,128)(2,1)S(1)} %fusion.16), channel_id=1, source_target_pairs={{0,8},{8,0},{16,24},{24,16},{32,40},{40,32},{48,56},{56,48},{64,72... | collective-permute-start | bytes 1769480 | tf_op jit(solution)/shard_map/ppermute | solution.py:61
  141.0 18.1 %copy-start.1 = (f32[96]{0:T(128)}, f32[96]{0:T(128)S(1)}, u32[]{:S(2)}) copy-start(f32[96]{0:T(128)S(1)} %slice_reduce_fusion) | copy-start | bytes 1156
  144.3 0.8 copy-start.4
  197.1 9.5 %collective-permute-start.2 = (bf16[1152,256]{1,0:T(8,128)(2,1)S(1)}, bf16[1152,256]{1,0:T(8,128)(2,1)S(1)}, u32[]{:S(2)}, u32[]{:S(2)}) collective-permute-start(bf16[1152,256]{1,0:T(8,128)(2,1)S(1)} %bitcast.48), channel_id=1, source_target_pairs={{0,8},{8,0},{16,24},{24,16},{32,40},{40,32},{48,56},{56,48},{64,72... | collective-permute-start | bytes 1769480 | tf_op jit(solution)/shard_map/ppermute | solution.py:61
Sparse Core Ops, SparseCore 0:
  36.3 49.7 all-gather.2

commit v3 on v2

v3 whole, which is shorter than its diff:
```python
import functools

import jax
import jax.numpy as jnp
from jax import lax
from jax.experimental import pallas as pl
from jax.experimental.pallas import tpu as pltpu
from jax.sharding import PartitionSpec as P

QUERY_HEADS = 32
KEY_VALUE_HEADS = 8
HEAD_SIZE = 64
NX, NZ, NCORE = 4, 12, 2
NEAR = NX * NCORE

EPS = 1e-05
THETA = 500000.0
LANES = 128
F32 = jnp.float32
BF16 = jnp.bfloat16


def device_of(x, z, core):
    return (x * NZ + z) * NCORE + core


def dp_groups():
    along_x = [[device_of(x, z, c) for x in range(NX)] for z in range(NZ) for c in range(NCORE)]
    along_z = [[device_of(x, z, c) for z in range(NZ)] for x in range(NX) for c in range(NCORE)]
    near = [[device_of(x, z, c) for x in range(NX) for c in range(NCORE)] for z in range(NZ)]
    return along_x, along_z, near


def swap(parts, groups):
    return lax.all_to_all(parts, "dp", 0, 0, tiled=True, axis_index_groups=groups)


def to_sibling(x):
    pairs = [(i, i ^ 1) for i in range(NX * NZ * NCORE)]
    return lax.ppermute(x, "dp", pairs)


def dot(a, b, a_dim, b_dim, precision=None):
    return lax.dot_general(
        a, b, (((a_dim,), (b_dim,)), ((), ())), preferred_element_type=F32, precision=precision
    )


def rope_tables(positions):
    half = HEAD_SIZE // 2
    freq = THETA ** (-jnp.arange(half, dtype=F32) * 2.0 / HEAD_SIZE)
    angle = positions.astype(F32)[:, None] * jnp.tile(freq, LANES // half)[None, :]
    sign = jnp.tile(jnp.repeat(jnp.array([-1.0, 1.0], F32), half), LANES // HEAD_SIZE)
    return jnp.cos(angle), jnp.sin(angle) * sign[None, :]


def front_kernel(lens, x_ref, gain_ref, wq_ref, wk_ref, wv_ref, cos_ref, sin_ref, out_ref, k_ref, v_ref):
    step = pl.program_id(0)
    rows = x_ref.shape[0]
    x = x_ref[...].astype(F32)
    inv = lax.rsqrt(jnp.mean(x * x, axis=1, keepdims=True) + EPS)
    normed = (x * inv * gain_ref[...]).astype(BF16)
    cosine, sine = cos_ref[...], sin_ref[...]
    lane = lax.broadcasted_iota(jnp.int32, (rows, LANES), 1)
    first_half = (lane % HEAD_SIZE) < HEAD_SIZE // 2
    low = lane < HEAD_SIZE

    def rotate(t):
        partner = jnp.where(
            first_half, pltpu.roll(t, LANES - HEAD_SIZE // 2, 1), pltpu.roll(t, HEAD_SIZE // 2, 1)
        )
        return t * cosine + partner * sine

    query = dot(normed, wq_ref[...], 1, 0)
    key = dot(normed, wk_ref[...], 1, 0)
    value = dot(normed, wv_ref[...], 1, 0)
    key = rotate(jnp.concatenate([key, key], axis=1))
    value = jnp.concatenate([value, value], axis=1)
    here = pl.ds(pl.multiple_of(step * rows, rows), rows)
    k_ref[0, here, :] = jnp.where(low, key, 0.0).astype(BF16)
    k_ref[1, here, :] = jnp.where(low, 0.0, key).astype(BF16)
    v_ref[0, here, :] = jnp.where(low, value, 0.0).astype(BF16)
    v_ref[1, here, :] = jnp.where(low, 0.0, value).astype(BF16)
    pairs = query.shape[1] // LANES
    turned = [rotate(query[:, p * LANES : (p + 1) * LANES]).astype(BF16) for p in range(pairs)]
    used = lens[0]

    def attend(first, cols):
        row = first + lax.broadcasted_iota(jnp.int32, (rows, cols), 0)
        col = lax.broadcasted_iota(jnp.int32, (rows, cols), 1)
        allowed = (col <= row) & ((row >= used) == (col >= used))
        for p in range(pairs):
            total = jnp.zeros((rows, LANES), F32)
            for e in range(LANES // HEAD_SIZE):
                scores = dot(turned[p], k_ref[e, :cols, :], 1, 1) * HEAD_SIZE ** (-0.5)
                scores = jnp.where(allowed, scores, -1e30)
                top = jnp.max(scores, axis=1, keepdims=True)
                weights = jnp.exp(scores - top)
                probs = weights * (1.0 / jnp.sum(weights, axis=1, keepdims=True))
                total = total + dot(probs.astype(BF16), v_ref[e, :cols, :], 1, 0)
            out_ref[:, p * LANES : (p + 1) * LANES] = total.astype(BF16)

    for s in range(k_ref.shape[1] // rows):
        @pl.when(step == s)
        def _(s=s):
            attend(s * rows, (s + 1) * rows)


def front(hidden_rows, lengths, gain_attn, w_query, key_weight, value_weight):
    rows, width = hidden_rows.shape
    row = jnp.arange(rows, dtype=jnp.int32)
    cosine, sine = rope_tables(row - jnp.where(row >= lengths[0], lengths[0], 0))
    block = rows // 2
    whole = lambda a: pl.BlockSpec(a.shape, lambda i, s: (0, 0))
    by_rows = lambda cols: pl.BlockSpec((block, cols), lambda i, s: (i, 0))
    gain = gain_attn[None]
    return pl.pallas_call(
        front_kernel,
        out_shape=jax.ShapeDtypeStruct((rows, w_query.shape[1]), BF16),
        grid_spec=pltpu.PrefetchScalarGridSpec(
            num_scalar_prefetch=1,
            grid=(rows // block,),
            in_specs=[
                by_rows(width),
                whole(gain),
                whole(w_query),
                whole(key_weight),
                whole(value_weight),
                by_rows(LANES),
                by_rows(LANES),
            ],
            out_specs=by_rows(w_query.shape[1]),
            scratch_shapes=[pltpu.VMEM((2, rows, LANES), BF16), pltpu.VMEM((2, rows, LANES), BF16)],
        ),
        compiler_params=pltpu.CompilerParams(vmem_limit_bytes=48 * 2**20),
        cost_estimate=pl.CostEstimate(flops=1500000000, bytes_accessed=4000000, transcendentals=800000),
        name="front",
    )(lengths, hidden_rows, gain, w_query, key_weight, value_weight, cosine, sine)


def project_kernel(place, mixed_ref, w_ref, x_ref, gain_ref, head_ref, resid_ref, stats_ref):
    step = pl.program_id(0)
    groups = mixed_ref.shape[0]
    rows, feat = resid_ref.shape

    @pl.when(step == 0)
    def _():
        resid_ref[...] = x_ref[...].astype(F32)

    total = jnp.zeros((rows, feat), F32)
    for g in range(groups):
        weight = w_ref[:, g].reshape(-1, feat)
        total = total + dot(mixed_ref[g], weight, 1, 0).astype(BF16).astype(F32)
    resid_ref[...] += total

    @pl.when(step == pl.num_programs(0) - 1)
    def _():
        resid = resid_ref[...]
        both = gain_ref[...] * head_ref[...]
        squares = dot(jnp.ones((8, feat), F32), resid * resid, 1, 1, lax.Precision.HIGHEST)
        scores = dot(jnp.broadcast_to(both, (8, feat)), resid, 1, 1, lax.Precision.HIGHEST)
        pair = jnp.concatenate([squares[:1], scores[:1]], axis=0)
        stats_ref[...] = jnp.broadcast_to(pair[None], stats_ref.shape)


def project(place, mixed_all, w_parts, hidden_rows, gain_final, w_head):
    n_mp, rows, heads = mixed_all.shape
    feat = w_parts.shape[-1]
    step = 2
    share = pl.BlockSpec((1, feat), lambda i, s: (0, s[0]))
    return pl.pallas_call(
        project_kernel,
        out_shape=(
            jax.ShapeDtypeStruct((rows, feat), F32),
            jax.ShapeDtypeStruct((n_mp, 2, rows), F32),
        ),
        grid_spec=pltpu.PrefetchScalarGridSpec(
            num_scalar_prefetch=1,
            grid=(n_mp // step,),
            in_specs=[
                pl.BlockSpec((step, rows, heads), lambda i, s: (i, 0, 0)),
                pl.BlockSpec(
                    (w_parts.shape[0], step, w_parts.shape[2], feat), lambda i, s: (0, i, 0, 0)
                ),
                pl.BlockSpec((rows, feat), lambda i, s: (0, s[0])),
                share,
                share,
            ],
            out_specs=(
                pl.BlockSpec((rows, feat), lambda i, s: (0, 0)),
                pl.BlockSpec((n_mp, 2, rows), lambda i, s: (0, 0, 0)),
            ),
        ),
        compiler_params=pltpu.CompilerParams(vmem_limit_bytes=48 * 2**20),
        cost_estimate=pl.CostEstimate(flops=550000000, bytes_accessed=4000000, transcendentals=0),
        name="project",
    )(place, mixed_all, w_parts, hidden_rows, gain_final[None], w_head[None])


def row_terms(stats, used, width):
    sums = stats[0]
    for part in range(1, stats.shape[0]):
        sums = sums + stats[part]
    scale = lax.rsqrt(sums[:1] / width + EPS)
    score = sums[1:2] * scale
    row = lax.broadcasted_iota(jnp.int32, scale.shape, 1)
    inside = row < used
    return scale, score, inside


def reward_kernel(width, lens, stats_ref, out_ref):
    _, score, inside = row_terms(stats_ref, lens[0], width)
    total = jnp.sum(jnp.where(inside, score, 0.0), axis=1, keepdims=True)
    reward = total / lens[0].astype(F32)
    out_ref[...] = jnp.broadcast_to(reward[None], out_ref.shape)


def reward_of(lengths, stats, width, n_dp):
    return pl.pallas_call(
        functools.partial(reward_kernel, width),
        out_shape=jax.ShapeDtypeStruct((n_dp, 1, LANES), F32),
        grid_spec=pltpu.PrefetchScalarGridSpec(
            num_scalar_prefetch=1,
            grid=(1,),
            in_specs=[pl.BlockSpec(stats.shape, lambda i, s: (0, 0, 0))],
            out_specs=pl.BlockSpec((n_dp, 1, LANES), lambda i, s: (0, 0, 0)),
        ),
        cost_estimate=pl.CostEstimate(flops=10000, bytes_accessed=90000, transcendentals=512),
        name="reward",
    )(lengths, stats)


def gradient_kernel(width, place, stats_ref, resid_ref, gain_ref, head_ref, mixed_ref, send_ref, keep_ref, d_ref, p_ref):
    step = pl.program_id(0)
    groups, rows, heads = mixed_ref.shape
    feat = resid_ref.shape[1]
    half = groups * heads

    @pl.when(step == 0)
    def _():
        used = place[2]
        scale, score, inside = row_terms(stats_ref, used, width)
        weight = jnp.where(inside, scale, 0.0) / used.astype(F32)
        minus = weight * scale * score * (1.0 / width)
        plus = jnp.broadcast_to(weight, (LANES, rows)).T
        minus = jnp.broadcast_to(minus, (LANES, rows)).T
        both = gain_ref[...] * head_ref[...]
        for part in range(feat // LANES):
            at = slice(part * LANES, (part + 1) * LANES)
            resid = resid_ref[:, at]
            d_ref[:, at] = (plus * both[:, at] - minus * resid).astype(BF16)
            pooled = jnp.sum(plus * resid, axis=0, keepdims=True)
            p_ref[:, at] = jnp.broadcast_to(pooled, (8, LANES))

    def fill(out_ref):
        for g in range(groups):
            out_ref[g * heads : (g + 1) * heads, :] = dot(mixed_ref[g], d_ref[...], 0, 0).astype(BF16)
        extra = out_ref.shape[0] - half
        first = lax.broadcasted_iota(jnp.int32, (extra, feat), 0) == 0
        out_ref[half:, :] = jnp.where(first, p_ref[:1, :], 0.0).astype(BF16)

    @pl.when(step == 0)
    def _():
        fill(send_ref)

    @pl.when(step == 1)
    def _():
        fill(keep_ref)


def gradient_halves(place, stats, resid, gain_final, w_head, mixed_all, half_ext):
    n_mp, rows, heads = mixed_all.shape
    feat = resid.shape[1]
    width = gain_final.shape[0]
    share = pl.BlockSpec((1, feat), lambda i, s: (0, s[0]))
    half = jax.ShapeDtypeStruct((half_ext, feat), BF16)
    half_spec = pl.BlockSpec((half_ext, feat), lambda i, s: (0, 0))
    return pl.pallas_call(
        functools.partial(gradient_kernel, width),
        out_shape=(half, half),
        grid_spec=pltpu.PrefetchScalarGridSpec(
            num_scalar_prefetch=1,
            grid=(NCORE,),
            in_specs=[
                pl.BlockSpec(stats.shape, lambda i, s: (0, 0, 0)),
                pl.BlockSpec(resid.shape, lambda i, s: (0, 0)),
                share,
                share,
                pl.BlockSpec((n_mp // NCORE, rows, heads), lambda i, s: (i * s[1] + (1 - i) * (1 - s[1]), 0, 0)),
            ],
            out_specs=(half_spec, half_spec),
            scratch_shapes=[pltpu.VMEM((rows, feat), BF16), pltpu.VMEM((8, feat), F32)],
        ),
        compiler_params=pltpu.CompilerParams(vmem_limit_bytes=48 * 2**20),
        cost_estimate=pl.CostEstimate(flops=550000000, bytes_accessed=4000000, transcendentals=0),
        name="gradient",
    )(place, stats, resid, gain_final[None], w_head[None], mixed_all)


def weigh_kernel(place, rewards_ref, order_ref, keep_ref, got_ref, out_ref, margin_ref):
    seqs = rewards_ref.shape[0]
    rewards = rewards_ref[...].reshape(seqs, LANES)
    order = order_ref[...]
    seq = lax.broadcasted_iota(jnp.int32, (seqs, LANES), 0)
    picked = jnp.sum(jnp.where(seq == order, rewards, 0.0), axis=0, keepdims=True)
    lane = lax.broadcasted_iota(jnp.int32, (1, LANES), 1)
    chosen = lane % 2 == 0
    partner = jnp.where(chosen, pltpu.roll(picked, LANES - 1, 1), pltpu.roll(picked, 1, 1))
    margin = jnp.where(chosen, picked - partner, partner - picked)
    sig = 1.0 / (1.0 + jnp.exp(margin))
    dreward = jnp.where(chosen, -sig, sig)
    me = place[3]
    own = jnp.sum(jnp.where(order == me, dreward, 0.0), axis=1, keepdims=True)
    sib = jnp.sum(jnp.where(order == (me ^ 1), dreward, 0.0), axis=1, keepdims=True)
    out_ref[...] = (keep_ref[...].astype(F32) * own + got_ref[...].astype(F32) * sib).astype(BF16)
    margin_ref[...] = margin


def weigh(place, rewards, order, keep, got):
    flat = lambda a: pl.BlockSpec(a.shape, lambda i, s: (0,) * len(a.shape))
    return pl.pallas_call(
        weigh_kernel,
        out_shape=(
            jax.ShapeDtypeStruct(keep.shape, BF16),
            jax.ShapeDtypeStruct((1, LANES), F32),
        ),
        grid_spec=pltpu.PrefetchScalarGridSpec(
            num_scalar_prefetch=1,
            grid=(1,),
            in_specs=[flat(rewards), flat(order), flat(keep), flat(got)],
            out_specs=(flat(keep), pl.BlockSpec((1, LANES), lambda i, s: (0, 0))),
        ),
        cost_estimate=pl.CostEstimate(flops=1000000, bytes_accessed=2000000, transcendentals=128),
        name="weigh",
    )(place, rewards, order, keep, got)


def finish_kernel(half, place, mine_ref, other_ref, gain_ref, head_ref, grad_ref, ghead_ref, ggain_ref):
    step = pl.program_id(0)

    @pl.when(step == place[1])
    def _():
        grad_ref[...] = mine_ref[:half, :].astype(F32)

    @pl.when(step != place[1])
    def _():
        grad_ref[...] = other_ref[:half, :].astype(F32)

    pooled = mine_ref[half : half + 16, :].astype(F32)[:1]
    ghead_ref[...] = gain_ref[...] * pooled
    ggain_ref[...] = head_ref[...] * pooled


def finish(place, mine, other, gain_final, w_head, half):
    feat = mine.shape[1]
    flat = pl.BlockSpec(mine.shape, lambda i, s: (0, 0))
    share = pl.BlockSpec((1, feat), lambda i, s: (0, s[0]))
    line = pl.BlockSpec((1, feat), lambda i, s: (0, 0))
    return pl.pallas_call(
        functools.partial(finish_kernel, half),
        out_shape=(
            jax.ShapeDtypeStruct((NCORE * half, feat), F32),
            jax.ShapeDtypeStruct((1, feat), F32),
            jax.ShapeDtypeStruct((1, feat), F32),
        ),
        grid_spec=pltpu.PrefetchScalarGridSpec(
            num_scalar_prefetch=1,
            grid=(NCORE,),
            in_specs=[flat, flat, share, share],
            out_specs=(pl.BlockSpec((half, feat), lambda i, s: (i, 0)), line, line),
        ),
        cost_estimate=pl.CostEstimate(flops=1000000, bytes_accessed=4000000, transcendentals=0),
        name="finish",
    )(place, mine, other, gain_final[None], w_head[None])


def body(
    hidden_rows,
    lengths,
    pair_order,
    gain_attn,
    w_query,
    key_weight,
    value_weight,
    w_out,
    gain_final,
    w_head,
):
    rows, width = hidden_rows.shape
    n_mp = lax.axis_size("mp")
    n_dp = lax.axis_size("dp")
    feat = width // n_mp
    me = lax.axis_index("dp").astype(jnp.int32)
    core = me % NCORE
    along_x, along_z, near = dp_groups()
    place = jnp.stack([lax.axis_index("mp").astype(jnp.int32), core, lengths[0], me])

    mixed = front(hidden_rows, lengths, gain_attn, w_query, key_weight, value_weight)

    mixed, w_out = lax.optimization_barrier((mixed, w_out))
    mixed_all = lax.all_gather(mixed, "mp", axis=0, tiled=False)
    piece_rows = w_out.shape[0] // NEAR
    my_near = (me // (NZ * NCORE)) * NCORE + core
    w_piece = lax.dynamic_slice_in_dim(w_out, my_near * piece_rows, piece_rows, 0)
    w_piece = w_piece.reshape(piece_rows, n_mp, feat).swapaxes(0, 1)
    w_piece = lax.all_to_all(w_piece, "mp", 0, 0, tiled=True)
    w_parts = swap(jnp.broadcast_to(w_piece[None], (NEAR,) + w_piece.shape), near)

    resid, stats = project(place, mixed_all, w_parts, hidden_rows, gain_final, w_head)
    stats = lax.all_to_all(stats, "mp", 0, 0, tiled=True)
    rewards = lax.all_to_all(reward_of(lengths, stats, width, n_dp), "dp", 0, 0, tiled=True)

    half = width // NCORE
    piece = -(-(half + 1) // (NX * NZ * 8)) * 8
    half_ext = piece * NX * NZ
    send, keep = gradient_halves(place, stats, resid, gain_final, w_head, mixed_all, half_ext)
    got = to_sibling(send)
    seqs = pair_order.shape[0]
    order = jnp.pad(pair_order, (0, LANES - seqs), constant_values=-1)[None]
    summed, margin = weigh(place, rewards, order, keep, got)
    loss = jnp.sum(jax.nn.softplus(-margin[0, :seqs:2]))

    got = swap(summed.reshape(NX, NZ * piece, feat), along_x)
    summed = jnp.sum(got.astype(F32), axis=0).astype(BF16)
    got = swap(summed.reshape(NZ, piece, feat), along_z)
    mine = jnp.sum(got.astype(F32), axis=0).astype(BF16)
    got = swap(jnp.broadcast_to(mine[None], (NZ, piece, feat)), along_z)
    got = swap(jnp.broadcast_to(got.reshape(1, NZ * piece, feat), (NX, NZ * piece, feat)), along_x)
    got = got.reshape(half_ext, feat)
    other = to_sibling(got)
    grad_out_proj, grad_head, grad_gain = finish(place, got, other, gain_final, w_head, half)
    return (loss, rewards[:, 0, 0], grad_out_proj, grad_head[0], grad_gain[0])


def solution(mesh):
    placed = (
        P("dp", None),
        P("dp"),
        P(),
        P(),
        P(None, "mp"),
        P(None, "mp"),
        P(None, "mp"),
        P("mp", None),
        P(),
        P(),
    )
    return jax.shard_map(
        body,
        mesh=mesh,
        in_specs=placed,
        out_specs=(P(), P(), P(None, "mp"), P("mp"), P("mp")),
        check_vma=False,
    )
```

time: 216 us -> 203 us (0.940)
  blocking collectives: 49.2 us -> 75.2 us
  Pallas kernels: 0 us -> 18.6 us
  matrix products: 16.1 us -> 0 us
  waiting for transfers between devices: 51.3 us -> 35.2 us
  other arithmetic: 15 us -> 1.83 us
  starting transfers between devices: 50.5 us -> 39.2 us
    all_gather x1, waiting for transfers between devices: 36.8 us -> 8.53 us  [body(): mixed_all = lax.all_gather(mixed, 'mp', axis=0, tiled=False)]
    all_to_all x0 -> x2, blocking collectives: none -> 26.2 us  [the longest x1 15.4 us: body(): w_piece = lax.all_to_all(w_piece, 'mp', 0, 0, tiled=True)]
    pallas_call x0 -> x6, Pallas kernels: none -> 18.6 us  [the longest x1 5.69 us: front(): pl.pallas_call(front_kernel, out_shape=jax.ShapeDtypeStruct((rows, w_quer...]
    all_to_all x3 -> x2, waiting for transfers between devices: 13.4 us -> 26.7 us  [the longest x1 15 us: swap(): lax.all_to_all(parts, 'dp', 0, 0, tiled=True, axis_index_groups=groups)]
    dot_general x6 -> x0, matrix products: 11.6 us -> none  [the longest x1 3.42 us: body(): jnp.einsum('hqk,khd->qhd', probs, value_rep, preferred_element_type=jnp.f...]
    unnamed x21 -> x45, local copies, waits for them, and re-layouts: 5.25 us -> 13 us
    all_to_all x3 -> x2, starting transfers between devices: 31.2 us -> 23.7 us  [the longest x1 13.6 us: body(): lax.all_to_all(reward_of(lengths, stats, width, n_dp), 'dp', 0, 0, tiled=...]
    convert_element_type x6 -> x1, other arithmetic: 4.63 us -> 0.01 us  [rope_tables(): positions.astype(F32)[:, None] * jnp.tile(freq, LANES // half)[None, :]]
  transfers between devices with their start and end apart: 7 -> 5, of which waited for: 4 -> 3; matrix products, arithmetic and copies ran while one was open for 12% -> 2% of each run, Pallas kernels for 0% -> 1%
where the time goes in v3:
time: 203 us; the launch traced here: 202 us
  blocking collectives  75.2 us (37%)
  starting transfers between devices  39.2 us (19%)
  waiting for transfers between devices  35.2 us (17%)
  Pallas kernels  18.6 us (9%)
  local copies, waits for them, and re-layouts  17.1 us (8%)
  between operations  15.1 us (7%)
    all_to_all x4, blocking collectives, swap(): lax.all_to_all(parts, 'dp', 0, 0, tiled=True, axis_index_groups=groups)  48.9 us
    ppermute x2, starting transfers between devices, to_sibling(): return lax.ppermute(x, 'dp', pairs)  15.5 us
    all_to_all x1, blocking collectives, body(): w_piece = lax.all_to_all(w_piece, 'mp', 0, 0, tiled=True)  15.4 us
    all_to_all x1, waiting for transfers between devices, swap(): lax.all_to_all(parts, 'dp', 0, 0, tiled=True, axis_index_groups=groups)  15 us
    all_to_all x1, starting transfers between devices, body(): lax.all_to_all(reward_of(lengths, stats, width, n_dp), 'dp', 0, 0, tiled=...  13.6 us
    unnamed x45, local copies, waits for them, and re-layouts  13 us
    all_to_all x1, waiting for transfers between devices, body(): lax.all_to_all(reward_of(lengths, stats, width, n_dp), 'dp', 0, 0, tiled=...  11.6 us
    all_to_all x1, blocking collectives, body(): stats = lax.all_to_all(stats, 'mp', 0, 0, tiled=True)  10.8 us
  transfers between devices with their start and end apart: 5, of which 3 were waited for; matrix products, arithmetic and copies ran while one was open for 2% of the time, Pallas kernels for 1%

profile of v3, /device:TPU:1, one launch (start us, length us, event | category | flops | bytes accessed | tf_op | source)
XLA Modules:
  0.0 202.3 jit_solution(15891968733057043727)
XLA Ops:
  8.2 0.7 broadcast_in_dim.47
  9.1 2.0 copy.24.wk_ref
  11.0 2.0 copy.25.wv_ref
  13.0 1.0 fusion
  14.0 1.0 copy-done.6
  15.0 1.0 copy-done.7
  16.1 1.2 copy-done.12
  17.3 5.7 %front.1 = bf16[512,256]{1,0:T(8,128)(2,1)} custom-call(s32[1]{0:T(128)} %copy.28.lens, bf16[512,2048]{1,0:T(8,128)(2,1)S(1)} %copy-done.3, f32[1,2048]{1,0:T(1,128)S(1)} %bitcast.45, bf16[2048,256]{1,0:T(8,128)(2,1)S(1)} %copy-done.12, bf16[2048,64]{1,0:T(8,128)(2,1)S(1)} %copy-done.6, bf16[2048,64]{1,0:T(8,128)(2,1)S(1)} %copy-done.7, ...), custom_call_target="tpu_custom_call" | custom-call | flops 1500000000 | bytes 4000000 | tf_op jit(solution)/shard_map/front/pallas_call | solution.py:117
  23.2 15.4 %all_to_all.40 = bf16[8,32,256]{2,1,0:T(8,128)(2,1)S(1)} all-to-all(bf16[8,32,256]{2,1,0:T(8,128)(2,1)S(1)} %copy.26), channel_id=1, replica_groups=mesh['dp'=96,'mp'=8] {'mp'}, dimensions={0} | all-to-all | bytes 262144 | tf_op jit(solution)/shard_map/all_to_all | solution.py:406
  38.6 1.1 broadcast_in_dim.48
  39.7 10.1 %all-to-all-start.1 = ((bf16[8,8,32,256]{3,2,1,0:T(8,128)(2,1)}), bf16[8,8,32,256]{3,2,1,0:T(8,128)(2,1)S(1)}, u32[]{:S(2)}, u32[]{:S(2)}) async-start(bf16[8,8,32,256]{3,2,1,0:T(8,128)(2,1)} %broadcast_in_dim.48), calls=%async_computation.1 | async-start | bytes 2097152 | tf_op jit(solution)/shard_map/all_to_all | solution.py:35
  49.8 15.0 %all-to-all-done.1.w_ref = bf16[8,8,32,256]{3,2,1,0:T(8,128)(2,1)S(1)} async-done(((bf16[8,8,32,256]{3,2,1,0:T(8,128)(2,1)}), bf16[8,8,32,256]{3,2,1,0:T(8,128)(2,1)S(1)}, u32[]{:S(2)}, u32[]{:S(2)}) %all-to-all-start.1) | async-done | bytes 1048608 | tf_op jit(solution)/shard_map/all_to_all | solution.py:35
  64.9 8.5 %all-gather.3.cloned.1.call-done = bf16[4096,256]{1,0:T(8,128)(2,1)} async-done(((bf16[512,256]{1,0:T(8,128)(2,1)}), bf16[4096,256]{1,0:T(8,128)(2,1)}) %all-gather.3.cloned.1.call-update) | async-done | bytes 2097168 | tf_op jit(solution)/shard_map/all_gather | solution.py:401
  73.4 1.6 copy-done.1
  75.0 1.6 copy-done.4
  76.6 2.9 %project.1 = (f32[512,256]{1,0:T(8,128)S(1)}, f32[8,2,512]{2,1,0:T(2,128)S(1)}) custom-call(s32[4]{0:T(128)S(1)} %pad_add_fusion.place, bf16[8,512,256]{2,1,0:T(8,128)(2,1)S(1)} %bitcast.37, bf16[8,8,32,256]{3,2,1,0:T(8,128)(2,1)S(1)} %all-to-all-done.1.w_ref, bf16[512,2048]{1,0:T(8,128)(2,1)S(1)} %copy-done.4, f32[1,2048]{1,0:T(1,128)S(1)} %bitcast.40, ...), custom_call_target="tpu_custom_call" | custom-call | flops 550000000 | bytes 4000000 | tf_op jit(solution)/shard_map/project/pallas_call | solution.py:171
  79.5 10.8 %all_to_all.41.stats_ref = f32[8,2,512]{2,1,0:T(2,128)S(1)} all-to-all(f32[8,2,512]{2,1,0:T(2,128)S(1)} %get-tuple-element.18), channel_id=1, replica_groups=mesh['dp'=96,'mp'=8] {'mp'}, dimensions={0} | all-to-all | bytes 65536 | tf_op jit(solution)/shard_map/all_to_all | solution.py:410
  90.4 1.9 gradient.1
  92.2 0.8 copy-done.5
  93.0 7.9 %collective-permute-start = (bf16[1152,256]{1,0:T(8,128)(2,1)S(1)}, bf16[1152,256]{1,0:T(8,128)(2,1)S(1)}, u32[]{:S(2)}, u32[]{:S(2)}) collective-permute-start(bf16[1152,256]{1,0:T(8,128)(2,1)S(1)} %get-tuple-element.21), channel_id=1, source_target_pairs={{0,8},{8,0},{16,24},{24,16},{32,40},{40,32},{48,56},{56,48},{64,72... | collective-permute-start | bytes 1769480 | tf_op jit(solution)/shard_map/ppermute | solution.py:40
  101.0 1.5 reward.1
  102.5 13.6 %all-to-all-start.3 = ((f32[96,1,128]{2,1,0:T(1,128)}), f32[96,1,128]{2,1,0:T(1,128)S(1)}, u32[]{:S(2)}, u32[]{:S(2)}) async-start(f32[96,1,128]{2,1,0:T(1,128)} %reward.1), calls=%async_computation.3 | async-start | bytes 98304 | tf_op jit(solution)/shard_map/all_to_all | solution.py:411
  116.7 11.6 %all-to-all-done.3.rewards_ref = f32[96,1,128]{2,1,0:T(1,128)S(1)} async-done(((f32[96,1,128]{2,1,0:T(1,128)}), f32[96,1,128]{2,1,0:T(1,128)S(1)}, u32[]{:S(2)}, u32[]{:S(2)}) %all-to-all-start.3) | async-done | bytes 49184 | tf_op jit(solution)/shard_map/all_to_all | solution.py:411
  129.2 3.3 %weigh.1 = (bf16[1152,256]{1,0:T(8,128)(2,1)}, f32[1,128]{1,0:T(1,128)}) custom-call(s32[4]{0:T(128)} %copy-done.11, f32[96,1,128]{2,1,0:T(1,128)} %copy-done.17, s32[1,128]{1,0:T(1,128)} %pad_bitcast_fusion.order_ref, bf16[1152,256]{1,0:T(8,128)(2,1)} %copy-done.5, bf16[1152,256]{1,0:T(8,128)(2,1)} %copy-done.16), custom_call_target="tpu_custom_call" | custom-call | flops 1000000 | bytes 2000000 | tf_op jit(solution)/shard_map/weigh/pallas_call | solution.py:321
  132.5 12.5 %all_to_all.42 = bf16[4,288,256]{2,1,0:T(8,128)(2,1)S(1)} all-to-all(bf16[4,288,256]{2,1,0:T(8,128)(2,1)} %bitcast.49), channel_id=1, replica_groups={{0,192,384,576},{8,200,392,584},{16,208,400,592},{24,216,408,600},{32,2..., dimensions={0} | all-to-all | bytes 1179648 | tf_op jit(solution)/shard_map/all_to_all | solution.py:35
  145.1 13.6 %all_to_all.43 = bf16[12,24,256]{2,1,0:T(8,128)(2,1)S(1)} all-to-all(bf16[12,24,256]{2,1,0:T(8,128)(2,1)S(1)} %bitcast.48), channel_id=1, replica_groups={{0,16,32,48,64,80,96,112,128,144,160,176},{8,24,40,56,72,88,104,120,136..., dimensions={0} | all-to-all | bytes 294912 | tf_op jit(solution)/shard_map/all_to_all | solution.py:35
  158.8 13.1 %all_to_all.44 = bf16[12,24,256]{2,1,0:T(8,128)(2,1)S(1)} all-to-all(bf16[12,24,256]{2,1,0:T(8,128)(2,1)S(1)} %broadcast_in_dim.52), channel_id=1, replica_groups={{0,16,32,48,64,80,96,112,128,144,160,176},{8,24,40,56,72,88,104,120,136..., dimensions={0} | all-to-all | bytes 294912 | tf_op jit(solution)/shard_map/all_to_all | solution.py:35
  171.9 9.7 %all_to_all.45 = bf16[4,288,256]{2,1,0:T(8,128)(2,1)S(1)} all-to-all(bf16[4,288,256]{2,1,0:T(8,128)(2,1)S(1)} %broadcast_in_dim.54), channel_id=1, replica_groups={{0,192,384,576},{8,200,392,584},{16,208,400,592},{24,216,408,600},{32,2..., dimensions={0} | all-to-all | bytes 1179648 | tf_op jit(solution)/shard_map/all_to_all | solution.py:35
  181.6 7.5 %collective-permute-start.1 = (bf16[1152,256]{1,0:T(8,128)(2,1)S(1)}, bf16[1152,256]{1,0:T(8,128)(2,1)S(1)}, u32[]{:S(2)}, u32[]{:S(2)}) collective-permute-start(bf16[1152,256]{1,0:T(8,128)(2,1)S(1)} %bitcast.46), channel_id=1, source_target_pairs={{0,8},{8,0},{16,24},{24,16},{32,40},{40,32},{48,56},{56,48},{64,72... | collective-permute-start | bytes 1769480 | tf_op jit(solution)/shard_map/ppermute | solution.py:40
  189.2 1.3 slice_reduce_fusion
  191.2 0.8 copy-done.15
  192.1 3.3 %finish.1 = (f32[2048,256]{1,0:T(8,128)}, f32[1,256]{1,0:T(1,128)}, f32[1,256]{1,0:T(1,128)}) custom-call(s32[4]{0:T(128)} %copy-done.11, bf16[1152,256]{1,0:T(8,128)(2,1)} %bitcast.47, bf16[1152,256]{1,0:T(8,128)(2,1)} %copy-done.15, f32[1,2048]{1,0:T(1,128)} %bitcast.39, f32[1,2048]{1,0:T(1,128)} %bitcast.42), custom_call_target="tpu_custom_call" | custom-call | flops 1000000 | bytes 4000000 | tf_op jit(solution)/shard_map/finish/pallas_call | solution.py:359
  (57 shorter events, 2.9 us)
Async XLA Ops:
  7.2 15.9 %copy-start = (bf16[256,2048]{1,0:T(8,128)(2,1)S(1)}, bf16[256,2048]{1,0:T(8,128)(2,1)}, u32[]{:S(2)}) copy-start(bf16[256,2048]{1,0:T(8,128)(2,1)} %param.18) | copy-start | bytes 3145732
  7.2 6.8 %copy-start.13 = (f32[2048]{0:T(1024)S(1)}, f32[2048]{0:T(1024)}, u32[]{:S(2)}) copy-start(f32[2048]{0:T(1024)} %param.14) | copy-start | bytes 24580
  7.2 6.8 %copy-start.3 = (bf16[512,2048]{1,0:T(8,128)(2,1)S(1)}, bf16[512,2048]{1,0:T(8,128)(2,1)}, u32[]{:S(2)}) copy-start(bf16[512,2048]{1,0:T(8,128)(2,1)} %x_ref.3) | copy-start | bytes 6291460
  7.2 66.2 %all-gather.3.cloned.1.call-start = ((), (), s32[]{:S(2)}) async-start(), calls=%async_computation.8 | async-start | bytes 2359296 | tf_op jit(solution)/shard_map/all_gather | solution.py:401
  14.0 1.0 copy-start.6
  15.0 1.0 copy-start.7
  16.1 1.2 copy-start.12
  23.1 50.3 %copy-start.9 = (f32[2048]{0:T(1024)S(1)}, f32[2048]{0:T(1024)}, u32[]{:S(2)}) copy-start(f32[2048]{0:T(1024)} %param.19) | copy-start | bytes 24580
  23.1 50.3 %copy-start.10 = (f32[2048]{0:T(1024)S(1)}, f32[2048]{0:T(1024)}, u32[]{:S(2)}) copy-start(f32[2048]{0:T(1024)} %param.20) | copy-start | bytes 24580
  39.7 25.2 %all-to-all-start.1 = ((bf16[8,8,32,256]{3,2,1,0:T(8,128)(2,1)}), bf16[8,8,32,256]{3,2,1,0:T(8,128)(2,1)S(1)}, u32[]{:S(2)}, u32[]{:S(2)}) async-start(bf16[8,8,32,256]{3,2,1,0:T(8,128)(2,1)} %broadcast_in_dim.48), calls=%async_computation.1 | async-start | bytes 2097152 | tf_op jit(solution)/shard_map/all_to_all | solution.py:35
  49.8 40.5 %copy-start.11 = (s32[4]{0:T(128)}, s32[4]{0:T(128)S(1)}, u32[]{:S(2)}) copy-start(s32[4]{0:T(128)S(1)} %pad_add_fusion.place) | copy-start | bytes 52
  73.4 1.6 copy-start.1
  75.0 1.6 copy-start.4
  76.6 13.8 %copy-start.2 = (bf16[4096,256]{1,0:T(8,128)(2,1)S(1)}, bf16[4096,256]{1,0:T(8,128)(2,1)}, u32[]{:S(2)}) copy-start(bf16[4096,256]{1,0:T(8,128)(2,1)} %all-gather.3.cloned.1.call-done) | copy-start | bytes 6291460
  79.5 36.6 %copy-start.19 = (s32[96]{0:T(128)S(1)}, s32[96]{0:T(128)}, u32[]{:S(2)}) copy-start(s32[96]{0:T(128)} %param.13) | copy-start | bytes 1156
  90.4 10.6 %copy-start.8 = (f32[8,2,512]{2,1,0:T(2,128)}, f32[8,2,512]{2,1,0:T(2,128)S(1)}, u32[]{:S(2)}) copy-start(f32[8,2,512]{2,1,0:T(2,128)S(1)} %all_to_all.41.stats_ref) | copy-start | bytes 98308
  92.2 0.8 copy-start.5
  93.0 35.3 %collective-permute-start = (bf16[1152,256]{1,0:T(8,128)(2,1)S(1)}, bf16[1152,256]{1,0:T(8,128)(2,1)S(1)}, u32[]{:S(2)}, u32[]{:S(2)}) collective-permute-start(bf16[1152,256]{1,0:T(8,128)(2,1)S(1)} %get-tuple-element.21), channel_id=1, source_target_pairs={{0,8},{8,0},{16,24},{24,16},{32,40},{40,32},{48,56},{56,48},{64,72... | collective-permute-start | bytes 1769480 | tf_op jit(solution)/shard_map/ppermute | solution.py:40
  102.5 25.8 %all-to-all-start.3 = ((f32[96,1,128]{2,1,0:T(1,128)}), f32[96,1,128]{2,1,0:T(1,128)S(1)}, u32[]{:S(2)}, u32[]{:S(2)}) async-start(f32[96,1,128]{2,1,0:T(1,128)} %reward.1), calls=%async_computation.3 | async-start | bytes 98304 | tf_op jit(solution)/shard_map/all_to_all | solution.py:411
  128.3 0.6 copy-start.17
  128.3 0.9 copy-start.16
  132.5 56.7 %copy-start.18 = (f32[96,1,128]{2,1,0:T(1,128)S(1)}, f32[96,1,128]{2,1,0:T(1,128)}, u32[]{:S(2)}) copy-start(f32[96,1,128]{2,1,0:T(1,128)} %copy-done.17) | copy-start | bytes 147460
  145.0 45.4 %copy-start.20 = (f32[1,128]{1,0:T(1,128)S(1)}, f32[1,128]{1,0:T(1,128)}, u32[]{:S(2)}) copy-start(f32[1,128]{1,0:T(1,128)} %get-tuple-element.22) | copy-start | bytes 1540
  181.6 9.6 %copy-start.14 = (bf16[4,288,256]{2,1,0:T(8,128)(2,1)}, bf16[4,288,256]{2,1,0:T(8,128)(2,1)S(1)}, u32[]{:S(2)}) copy-start(bf16[4,288,256]{2,1,0:T(8,128)(2,1)S(1)} %all_to_all.45) | copy-start | bytes 1769476
  181.6 9.6 %collective-permute-start.1 = (bf16[1152,256]{1,0:T(8,128)(2,1)S(1)}, bf16[1152,256]{1,0:T(8,128)(2,1)S(1)}, u32[]{:S(2)}, u32[]{:S(2)}) collective-permute-start(bf16[1152,256]{1,0:T(8,128)(2,1)S(1)} %bitcast.46), channel_id=1, source_target_pairs={{0,8},{8,0},{16,24},{24,16},{32,40},{40,32},{48,56},{56,48},{64,72... | collective-permute-start | bytes 1769480 | tf_op jit(solution)/shard_map/ppermute | solution.py:40
  191.2 0.8 copy-start.15
Sparse Core Ops, SparseCore 0:
  23.1 50.2 all-gather.2

commit v4 on v3

--- a/solution.py
+++ b/solution.py
@@ -2,6 +2,7 @@
 
 import jax
 import jax.numpy as jnp
+import numpy as np
 from jax import lax
 from jax.experimental import pallas as pl
 from jax.experimental.pallas import tpu as pltpu
@@ -48,9 +49,9 @@
 
 def rope_tables(positions):
     half = HEAD_SIZE // 2
-    freq = THETA ** (-jnp.arange(half, dtype=F32) * 2.0 / HEAD_SIZE)
-    angle = positions.astype(F32)[:, None] * jnp.tile(freq, LANES // half)[None, :]
-    sign = jnp.tile(jnp.repeat(jnp.array([-1.0, 1.0], F32), half), LANES // HEAD_SIZE)
+    freq = np.tile(THETA ** (-np.arange(half) * 2.0 / HEAD_SIZE), LANES // half).astype(np.float32)
+    sign = np.tile(np.repeat([-1.0, 1.0], half), LANES // HEAD_SIZE).astype(np.float32)
+    angle = positions.astype(F32)[:, None] * freq[None, :]
     return jnp.cos(angle), jnp.sin(angle) * sign[None, :]
 
 
@@ -72,8 +73,8 @@
         return t * cosine + partner * sine
 
     query = dot(normed, wq_ref[...], 1, 0)
-    key = dot(normed, wk_ref[...], 1, 0)
-    value = dot(normed, wv_ref[...], 1, 0)
+    key = dot(normed, wk_ref[...], 1, 1)
+    value = dot(normed, wv_ref[...], 1, 1)
     key = rotate(jnp.concatenate([key, key], axis=1))
     value = jnp.concatenate([value, value], axis=1)
     here = pl.ds(pl.multiple_of(step * rows, rows), rows)
@@ -114,6 +115,7 @@
     whole = lambda a: pl.BlockSpec(a.shape, lambda i, s: (0, 0))
     by_rows = lambda cols: pl.BlockSpec((block, cols), lambda i, s: (i, 0))
     gain = gain_attn[None]
+    key_weight, value_weight = key_weight.T, value_weight.T
     return pl.pallas_call(
         front_kernel,
         out_shape=jax.ShapeDtypeStruct((rows, w_query.shape[1]), BF16),
@@ -132,7 +134,7 @@
             out_specs=by_rows(w_query.shape[1]),
             scratch_shapes=[pltpu.VMEM((2, rows, LANES), BF16), pltpu.VMEM((2, rows, LANES), BF16)],
         ),
-        compiler_params=pltpu.CompilerParams(vmem_limit_bytes=48 * 2**20),
+        compiler_params=pltpu.CompilerParams(vmem_limit_bytes=58 * 2**20),
         cost_estimate=pl.CostEstimate(flops=1500000000, bytes_accessed=4000000, transcendentals=800000),
         name="front",
     )(lengths, hidden_rows, gain, w_query, key_weight, value_weight, cosine, sine)
@@ -191,7 +193,7 @@
                 pl.BlockSpec((n_mp, 2, rows), lambda i, s: (0, 0, 0)),
             ),
         ),
-        compiler_params=pltpu.CompilerParams(vmem_limit_bytes=48 * 2**20),
+        compiler_params=pltpu.CompilerParams(vmem_limit_bytes=58 * 2**20),
         cost_estimate=pl.CostEstimate(flops=550000000, bytes_accessed=4000000, transcendentals=0),
         name="project",
     )(place, mixed_all, w_parts, hidden_rows, gain_final[None], w_head[None])
@@ -225,6 +227,7 @@
             in_specs=[pl.BlockSpec(stats.shape, lambda i, s: (0, 0, 0))],
             out_specs=pl.BlockSpec((n_dp, 1, LANES), lambda i, s: (0, 0, 0)),
         ),
+        compiler_params=pltpu.CompilerParams(vmem_limit_bytes=16 * 2**20),
         cost_estimate=pl.CostEstimate(flops=10000, bytes_accessed=90000, transcendentals=512),
         name="reward",
     )(lengths, stats)
@@ -297,7 +300,7 @@
     )(place, stats, resid, gain_final[None], w_head[None], mixed_all)
 
 
-def weigh_kernel(place, rewards_ref, order_ref, keep_ref, got_ref, out_ref, margin_ref):
+def weigh_kernel(place, rewards_ref, order_ref, keep_ref, got_ref, out_ref, margin_ref, row_ref):
     seqs = rewards_ref.shape[0]
     rewards = rewards_ref[...].reshape(seqs, LANES)
     order = order_ref[...]
@@ -314,6 +317,8 @@
     sib = jnp.sum(jnp.where(order == (me ^ 1), dreward, 0.0), axis=1, keepdims=True)
     out_ref[...] = (keep_ref[...].astype(F32) * own + got_ref[...].astype(F32) * sib).astype(BF16)
     margin_ref[...] = margin
+    at = lax.broadcasted_iota(jnp.int32, (seqs, LANES), 1)
+    row_ref[...] = jnp.sum(jnp.where(seq == at, rewards, 0.0), axis=0, keepdims=True)
 
 
 def weigh(place, rewards, order, keep, got):
@@ -323,13 +328,15 @@
         out_shape=(
             jax.ShapeDtypeStruct(keep.shape, BF16),
             jax.ShapeDtypeStruct((1, LANES), F32),
+            jax.ShapeDtypeStruct((1, LANES), F32),
         ),
         grid_spec=pltpu.PrefetchScalarGridSpec(
             num_scalar_prefetch=1,
             grid=(1,),
             in_specs=[flat(rewards), flat(order), flat(keep), flat(got)],
-            out_specs=(flat(keep), pl.BlockSpec((1, LANES), lambda i, s: (0, 0))),
-        ),
+            out_specs=(flat(keep),) + (pl.BlockSpec((1, LANES), lambda i, s: (0, 0)),) * 2,
+        ),
+        compiler_params=pltpu.CompilerParams(vmem_limit_bytes=16 * 2**20),
         cost_estimate=pl.CostEstimate(flops=1000000, bytes_accessed=2000000, transcendentals=128),
         name="weigh",
     )(place, rewards, order, keep, got)
@@ -369,6 +376,7 @@
             in_specs=[flat, flat, share, share],
             out_specs=(pl.BlockSpec((half, feat), lambda i, s: (i, 0)), line, line),
         ),
+        compiler_params=pltpu.CompilerParams(vmem_limit_bytes=16 * 2**20),
         cost_estimate=pl.CostEstimate(flops=1000000, bytes_accessed=4000000, transcendentals=0),
         name="finish",
     )(place, mine, other, gain_final[None], w_head[None])
@@ -408,7 +416,8 @@
 
     resid, stats = project(place, mixed_all, w_parts, hidden_rows, gain_final, w_head)
     stats = lax.all_to_all(stats, "mp", 0, 0, tiled=True)
-    rewards = lax.all_to_all(reward_of(lengths, stats, width, n_dp), "dp", 0, 0, tiled=True)
+    reward, stats = lax.optimization_barrier((reward_of(lengths, stats, width, n_dp), stats))
+    rewards = lax.all_to_all(reward, "dp", 0, 0, tiled=True)
 
     half = width // NCORE
     piece = -(-(half + 1) // (NX * NZ * 8)) * 8
@@ -417,7 +426,7 @@
     got = to_sibling(send)
     seqs = pair_order.shape[0]
     order = jnp.pad(pair_order, (0, LANES - seqs), constant_values=-1)[None]
-    summed, margin = weigh(place, rewards, order, keep, got)
+    summed, margin, reward_row = weigh(place, rewards, order, keep, got)
     loss = jnp.sum(jax.nn.softplus(-margin[0, :seqs:2]))
 
     got = swap(summed.reshape(NX, NZ * piece, feat), along_x)
@@ -429,7 +438,7 @@
     got = got.reshape(half_ext, feat)
     other = to_sibling(got)
     grad_out_proj, grad_head, grad_gain = finish(place, got, other, gain_final, w_head, half)
-    return (loss, rewards[:, 0, 0], grad_out_proj, grad_head[0], grad_gain[0])
+    return (loss, reward_row[0, :seqs], grad_out_proj, grad_head[0], grad_gain[0])
 
 
 def solution(mesh):

time: 203 us -> 190 us (0.936)
  local copies, waits for them, and re-layouts: 17.1 us -> 2.93 us
  other arithmetic: 1.83 us -> 3.9 us
    unnamed x45 -> x17, local copies, waits for them, and re-layouts: 13 us -> 1.09 us
    pallas_call x1, Pallas kernels: 2.92 us -> 5.98 us  [project(): pl.pallas_call(project_kernel, out_shape=(jax.ShapeDtypeStruct((rows, fea...]
    pallas_call x1, Pallas kernels: 3.32 us -> 1.1 us  [weigh(): pl.pallas_call(weigh_kernel, out_shape=(jax.ShapeDtypeStruct(keep.shape,...]
  transfers between devices with their start and end apart: 5 -> 5, of which waited for: 3 -> 4; matrix products, arithmetic and copies ran while one was open for 2% -> 2% of each run, Pallas kernels for 1% -> 0%
where the time goes in v4:
time: 190 us
  blocking collectives  74.3 us (39%)
  starting transfers between devices  39.1 us (21%)
  waiting for transfers between devices  35.5 us (19%)
  Pallas kernels  19.2 us (10%)
  between operations  14.9 us (8%)
  other arithmetic  3.9 us (2%)
  local copies, waits for them, and re-layouts  2.93 us (2%)
    all_to_all x4, blocking collectives, swap(): lax.all_to_all(parts, 'dp', 0, 0, tiled=True, axis_index_groups=groups)  47.8 us
    all_to_all x1, blocking collectives, body(): w_piece = lax.all_to_all(w_piece, 'mp', 0, 0, tiled=True)  15.4 us
    ppermute x2, starting transfers between devices, to_sibling(): return lax.ppermute(x, 'dp', pairs)  15.3 us
    all_to_all x1, waiting for transfers between devices, swap(): lax.all_to_all(parts, 'dp', 0, 0, tiled=True, axis_index_groups=groups)  14.5 us
    all_to_all x1, starting transfers between devices, body(): rewards = lax.all_to_all(reward, 'dp', 0, 0, tiled=True)  13.6 us
    all_to_all x1, waiting for transfers between devices, body(): rewards = lax.all_to_all(reward, 'dp', 0, 0, tiled=True)  12.1 us
    all_to_all x1, blocking collectives, body(): stats = lax.all_to_all(stats, 'mp', 0, 0, tiled=True)  11 us
    all_to_all x1, starting transfers between devices, swap(): lax.all_to_all(parts, 'dp', 0, 0, tiled=True, axis_index_groups=groups)  10.1 us
  transfers between devices with their start and end apart: 5, of which 4 were waited for; matrix products, arithmetic and copies ran while one was open for 2% of the time, Pallas kernels for 0%

profile of v4, /device:TPU:1, one launch (start us, length us, event | category | flops | bytes accessed | tf_op | source)
XLA Modules:
  0.0 189.8 jit_solution(7423961166145553660)
XLA Ops:
  7.2 0.0 copy-start
  7.2 0.0 all-gather.3.cloned.1.call-start
  8.0 2.5 %fusion = (f32[512,128]{1,0:T(8,128)}, f32[512,128]{1,0:T(8,128)}) fusion(f32[128]{0:T(128)} %constant.54, f32[128]{0:T(128)} %constant.53, f32[512]{0:T(512)S(1)} %subtract_convert_fusion), kind=kLoop, calls=%fused_computation.2 | loop fusion | flops 131072 | bytes 527360 | tf_op jit(solution)/shard_map/mul | solution.py:55
  10.5 7.6 %front.1 = bf16[512,256]{1,0:T(8,128)(2,1)} custom-call(s32[1]{0:T(128)} %copy.21.lens, bf16[512,2048]{1,0:T(8,128)(2,1)} %x_ref.3, f32[1,2048]{1,0:T(1,128)} %bitcast.58, bf16[2048,256]{1,0:T(8,128)(2,1)} %wq_ref.1, bf16[64,2048]{1,0:T(8,128)(2,1)} %bitcast.56, bf16[64,2048]{1,0:T(8,128)(2,1)} %bitcast.57, f32[512,128]{1,0:T(8,128)} %get-tuple-element.34.cos_ref, ...), custom_call_target="tpu_custom_call" | custom-call | flops 1500000000 | bytes 4000000 | tf_op jit(solution)/shard_map/front/pallas_call | solution.py:119
  18.0 0.0 all-gather.3.cloned.1.call-update
  18.2 15.4 %all_to_all.40 = bf16[8,32,256]{2,1,0:T(8,128)(2,1)S(1)} all-to-all(bf16[8,32,256]{2,1,0:T(8,128)(2,1)S(1)} %copy.19), channel_id=1, replica_groups=mesh['dp'=96,'mp'=8] {'mp'}, dimensions={0} | all-to-all | bytes 262144 | tf_op jit(solution)/shard_map/all_to_all | solution.py:414
  33.6 1.1 broadcast_in_dim.44
  34.7 10.1 %all-to-all-start.1 = ((bf16[8,8,32,256]{3,2,1,0:T(8,128)(2,1)}), bf16[8,8,32,256]{3,2,1,0:T(8,128)(2,1)S(1)}, u32[]{:S(2)}, u32[]{:S(2)}) async-start(bf16[8,8,32,256]{3,2,1,0:T(8,128)(2,1)} %broadcast_in_dim.44), calls=%async_computation.1 | async-start | bytes 2097152 | tf_op jit(solution)/shard_map/all_to_all | solution.py:36
  44.8 0.7 pad_add_fusion.place
  45.4 14.5 %all-to-all-done.1.w_ref = bf16[8,8,32,256]{3,2,1,0:T(8,128)(2,1)S(1)} async-done(((bf16[8,8,32,256]{3,2,1,0:T(8,128)(2,1)}), bf16[8,8,32,256]{3,2,1,0:T(8,128)(2,1)S(1)}, u32[]{:S(2)}, u32[]{:S(2)}) %all-to-all-start.1) | async-done | bytes 1048608 | tf_op jit(solution)/shard_map/all_to_all | solution.py:36
  59.9 8.6 %all-gather.3.cloned.1.call-done = bf16[4096,256]{1,0:T(8,128)(2,1)} async-done(((bf16[512,256]{1,0:T(8,128)(2,1)}), bf16[4096,256]{1,0:T(8,128)(2,1)}) %all-gather.3.cloned.1.call-update) | async-done | bytes 2097168 | tf_op jit(solution)/shard_map/all_gather | solution.py:409
  68.5 6.0 %project.1 = (f32[512,256]{1,0:T(8,128)}, f32[8,2,512]{2,1,0:T(2,128)}) custom-call(s32[4]{0:T(128)} %pad_add_fusion.place, bf16[8,512,256]{2,1,0:T(8,128)(2,1)} %bitcast.41, bf16[8,8,32,256]{3,2,1,0:T(8,128)(2,1)} %copy-done.6, bf16[512,2048]{1,0:T(8,128)(2,1)} %x_ref.3, f32[1,2048]{1,0:T(1,128)} %bitcast.46, f32[1,2048]{1,0:T(1,128)} %bitcast.49), custom_call_target="tpu_custom_call" | custom-call | flops 550000000 | bytes 4000000 | tf_op jit(solution)/shard_map/project/pallas_call | solution.py:173
  74.4 11.0 %all_to_all.41.stats_ref = f32[8,2,512]{2,1,0:T(2,128)S(1)} all-to-all(f32[8,2,512]{2,1,0:T(2,128)} %get-tuple-element.21), channel_id=1, replica_groups=mesh['dp'=96,'mp'=8] {'mp'}, dimensions={0} | all-to-all | bytes 65536 | tf_op jit(solution)/shard_map/all_to_all | solution.py:418
  85.5 0.7 reward.1
  86.2 1.0 copy-done.2
  87.3 1.9 gradient.1
  89.1 7.9 %collective-permute-start = (bf16[1152,256]{1,0:T(8,128)(2,1)S(1)}, bf16[1152,256]{1,0:T(8,128)(2,1)S(1)}, u32[]{:S(2)}, u32[]{:S(2)}) collective-permute-start(bf16[1152,256]{1,0:T(8,128)(2,1)S(1)} %get-tuple-element.26), channel_id=1, source_target_pairs={{0,8},{8,0},{16,24},{24,16},{32,40},{40,32},{48,56},{56,48},{64,72... | collective-permute-start | bytes 1769480 | tf_op jit(solution)/shard_map/ppermute | solution.py:41
  97.1 13.6 %all-to-all-start.3 = ((f32[96,1,128]{2,1,0:T(1,128)}), f32[96,1,128]{2,1,0:T(1,128)S(1)}, u32[]{:S(2)}, u32[]{:S(2)}) async-start(f32[96,1,128]{2,1,0:T(1,128)} %reward.1), calls=%async_computation.3 | async-start | bytes 98304 | tf_op jit(solution)/shard_map/all_to_all | solution.py:420
  110.7 12.1 %all-to-all-done.3.rewards_ref = f32[96,1,128]{2,1,0:T(1,128)S(1)} async-done(((f32[96,1,128]{2,1,0:T(1,128)}), f32[96,1,128]{2,1,0:T(1,128)S(1)}, u32[]{:S(2)}, u32[]{:S(2)}) %all-to-all-start.3) | async-done | bytes 49184 | tf_op jit(solution)/shard_map/all_to_all | solution.py:420
  122.8 0.0 collective-permute-done.got_ref
  122.8 1.1 weigh.1
  123.9 11.4 %all_to_all.42 = bf16[4,288,256]{2,1,0:T(8,128)(2,1)S(1)} all-to-all(bf16[4,288,256]{2,1,0:T(8,128)(2,1)S(1)} %bitcast.45), channel_id=1, replica_groups={{0,192,384,576},{8,200,392,584},{16,208,400,592},{24,216,408,600},{32,2..., dimensions={0} | all-to-all | bytes 1179648 | tf_op jit(solution)/shard_map/all_to_all | solution.py:36
  135.3 0.1 reduce_sum.34
  135.4 13.4 %all_to_all.43 = bf16[12,24,256]{2,1,0:T(8,128)(2,1)S(1)} all-to-all(bf16[12,24,256]{2,1,0:T(8,128)(2,1)S(1)} %bitcast.52), channel_id=1, replica_groups={{0,16,32,48,64,80,96,112,128,144,160,176},{8,24,40,56,72,88,104,120,136..., dimensions={0} | all-to-all | bytes 294912 | tf_op jit(solution)/shard_map/all_to_all | solution.py:36
  148.8 13.4 %all_to_all.44 = bf16[12,24,256]{2,1,0:T(8,128)(2,1)S(1)} all-to-all(bf16[12,24,256]{2,1,0:T(8,128)(2,1)S(1)} %broadcast_in_dim.48), channel_id=1, replica_groups={{0,16,32,48,64,80,96,112,128,144,160,176},{8,24,40,56,72,88,104,120,136..., dimensions={0} | all-to-all | bytes 294912 | tf_op jit(solution)/shard_map/all_to_all | solution.py:36
  162.3 9.7 %all_to_all.45 = bf16[4,288,256]{2,1,0:T(8,128)(2,1)S(1)} all-to-all(bf16[4,288,256]{2,1,0:T(8,128)(2,1)S(1)} %broadcast_in_dim.50), channel_id=1, replica_groups={{0,192,384,576},{8,200,392,584},{16,208,400,592},{24,216,408,600},{32,2..., dimensions={0} | all-to-all | bytes 1179648 | tf_op jit(solution)/shard_map/all_to_all | solution.py:36
  172.0 7.4 %collective-permute-start.1 = (bf16[1152,256]{1,0:T(8,128)(2,1)S(1)}, bf16[1152,256]{1,0:T(8,128)(2,1)S(1)}, u32[]{:S(2)}, u32[]{:S(2)}) collective-permute-start(bf16[1152,256]{1,0:T(8,128)(2,1)S(1)} %bitcast.43), channel_id=1, source_target_pairs={{0,8},{8,0},{16,24},{24,16},{32,40},{40,32},{48,56},{56,48},{64,72... | collective-permute-start | bytes 1769480 | tf_op jit(solution)/shard_map/ppermute | solution.py:41
  179.3 0.1 slice.6
  179.5 0.6 fusion.1
  180.1 0.5 slice_bitcast_fusion
  180.6 0.3 collective-permute-done.1.other_ref
  181.0 2.0 %finish.1 = (f32[2048,256]{1,0:T(8,128)}, f32[1,256]{1,0:T(1,128)}, f32[1,256]{1,0:T(1,128)}) custom-call(s32[4]{0:T(128)S(1)} %copy-done.5, bf16[1152,256]{1,0:T(8,128)(2,1)S(1)} %bitcast.44, bf16[1152,256]{1,0:T(8,128)(2,1)S(1)} %collective-permute-done.1.other_ref, f32[1,2048]{1,0:T(1,128)S(1)} %bitcast.48, f32[1,2048]{1,0:T(1,128)S(1)} %bitcast.51), custom_call_target="tpu_custom_call" | custom-call | flops 1000000 | bytes 4000000 | tf_op jit(solution)/shard_map/finish/pallas_call | solution.py:366
  (22 shorter events, 0.2 us)
Async XLA Ops:
  7.2 10.9 %copy-start = (bf16[256,2048]{1,0:T(8,128)(2,1)S(1)}, bf16[256,2048]{1,0:T(8,128)(2,1)}, u32[]{:S(2)}) copy-start(bf16[256,2048]{1,0:T(8,128)(2,1)} %param.19) | copy-start | bytes 3145732
  7.2 61.3 %all-gather.3.cloned.1.call-start = ((), (), s32[]{:S(2)}) async-start(), calls=%async_computation.8 | async-start | bytes 2359296 | tf_op jit(solution)/shard_map/all_gather | solution.py:409
  34.7 25.2 %all-to-all-start.1 = ((bf16[8,8,32,256]{3,2,1,0:T(8,128)(2,1)}), bf16[8,8,32,256]{3,2,1,0:T(8,128)(2,1)S(1)}, u32[]{:S(2)}, u32[]{:S(2)}) async-start(bf16[8,8,32,256]{3,2,1,0:T(8,128)(2,1)} %broadcast_in_dim.44), calls=%async_computation.1 | async-start | bytes 2097152 | tf_op jit(solution)/shard_map/all_to_all | solution.py:36
  59.9 8.6 %copy-start.6 = (bf16[8,8,32,256]{3,2,1,0:T(8,128)(2,1)}, bf16[8,8,32,256]{3,2,1,0:T(8,128)(2,1)S(1)}, u32[]{:S(2)}) copy-start(bf16[8,8,32,256]{3,2,1,0:T(8,128)(2,1)S(1)} %all-to-all-done.1.w_ref) | copy-start | bytes 3145732
  68.4 17.8 %copy-start.1 = (bf16[4096,256]{1,0:T(8,128)(2,1)S(1)}, bf16[4096,256]{1,0:T(8,128)(2,1)}, u32[]{:S(2)}) copy-start(bf16[4096,256]{1,0:T(8,128)(2,1)} %all-gather.3.cloned.1.call-done) | copy-start | bytes 6291460
  68.4 17.8 %copy-start.3 = (f32[2048]{0:T(1024)S(1)}, f32[2048]{0:T(1024)}, u32[]{:S(2)}) copy-start(f32[2048]{0:T(1024)} %param.20) | copy-start | bytes 24580
  68.4 17.8 %copy-start.4 = (f32[2048]{0:T(1024)S(1)}, f32[2048]{0:T(1024)}, u32[]{:S(2)}) copy-start(f32[2048]{0:T(1024)} %param.21) | copy-start | bytes 24580
  68.4 17.8 %copy-start.5 = (s32[4]{0:T(128)S(1)}, s32[4]{0:T(128)}, u32[]{:S(2)}) copy-start(s32[4]{0:T(128)} %pad_add_fusion.place) | copy-start | bytes 52
  74.4 36.3 %copy-start.7 = (s32[96]{0:T(128)S(1)}, s32[96]{0:T(128)}, u32[]{:S(2)}) copy-start(s32[96]{0:T(128)} %param.14) | copy-start | bytes 1156
  86.2 1.0 copy-start.2
  89.1 33.7 %collective-permute-start = (bf16[1152,256]{1,0:T(8,128)(2,1)S(1)}, bf16[1152,256]{1,0:T(8,128)(2,1)S(1)}, u32[]{:S(2)}, u32[]{:S(2)}) collective-permute-start(bf16[1152,256]{1,0:T(8,128)(2,1)S(1)} %get-tuple-element.26), channel_id=1, source_target_pairs={{0,8},{8,0},{16,24},{24,16},{32,40},{40,32},{48,56},{56,48},{64,72... | collective-permute-start | bytes 1769480 | tf_op jit(solution)/shard_map/ppermute | solution.py:41
  97.1 25.8 %all-to-all-start.3 = ((f32[96,1,128]{2,1,0:T(1,128)}), f32[96,1,128]{2,1,0:T(1,128)S(1)}, u32[]{:S(2)}, u32[]{:S(2)}) async-start(f32[96,1,128]{2,1,0:T(1,128)} %reward.1), calls=%async_computation.3 | async-start | bytes 98304 | tf_op jit(solution)/shard_map/all_to_all | solution.py:420
  172.0 9.0 %collective-permute-start.1 = (bf16[1152,256]{1,0:T(8,128)(2,1)S(1)}, bf16[1152,256]{1,0:T(8,128)(2,1)S(1)}, u32[]{:S(2)}, u32[]{:S(2)}) collective-permute-start(bf16[1152,256]{1,0:T(8,128)(2,1)S(1)} %bitcast.43), channel_id=1, source_target_pairs={{0,8},{8,0},{16,24},{24,16},{32,40},{40,32},{48,56},{56,48},{64,72... | collective-permute-start | bytes 1769480 | tf_op jit(solution)/shard_map/ppermute | solution.py:41
Sparse Core Ops, SparseCore 0:
  18.2 50.2 all-gather.2

commit v5 on v4

--- a/solution.py
+++ b/solution.py
@@ -134,42 +134,36 @@
             out_specs=by_rows(w_query.shape[1]),
             scratch_shapes=[pltpu.VMEM((2, rows, LANES), BF16), pltpu.VMEM((2, rows, LANES), BF16)],
         ),
-        compiler_params=pltpu.CompilerParams(vmem_limit_bytes=58 * 2**20),
+        compiler_params=pltpu.CompilerParams(vmem_limit_bytes=48 * 2**20),
         cost_estimate=pl.CostEstimate(flops=1500000000, bytes_accessed=4000000, transcendentals=800000),
         name="front",
     )(lengths, hidden_rows, gain, w_query, key_weight, value_weight, cosine, sine)
 
 
-def project_kernel(place, mixed_ref, w_ref, x_ref, gain_ref, head_ref, resid_ref, stats_ref):
-    step = pl.program_id(0)
+def project_kernel(place, mixed_hbm, w_ref, x_ref, gain_ref, head_ref, resid_ref, stats_ref, mixed_ref, sems):
     groups = mixed_ref.shape[0]
     rows, feat = resid_ref.shape
-
-    @pl.when(step == 0)
-    def _():
-        resid_ref[...] = x_ref[...].astype(F32)
-
-    total = jnp.zeros((rows, feat), F32)
+    copies = [pltpu.make_async_copy(mixed_hbm.at[g], mixed_ref.at[g], sems.at[g]) for g in range(groups)]
+    for copy in copies:
+        copy.start()
+    resid_ref[...] = x_ref[...].astype(F32)
     for g in range(groups):
+        copies[g].wait()
         weight = w_ref[:, g].reshape(-1, feat)
-        total = total + dot(mixed_ref[g], weight, 1, 0).astype(BF16).astype(F32)
-    resid_ref[...] += total
-
-    @pl.when(step == pl.num_programs(0) - 1)
-    def _():
-        resid = resid_ref[...]
-        both = gain_ref[...] * head_ref[...]
-        squares = dot(jnp.ones((8, feat), F32), resid * resid, 1, 1, lax.Precision.HIGHEST)
-        scores = dot(jnp.broadcast_to(both, (8, feat)), resid, 1, 1, lax.Precision.HIGHEST)
-        pair = jnp.concatenate([squares[:1], scores[:1]], axis=0)
-        stats_ref[...] = jnp.broadcast_to(pair[None], stats_ref.shape)
-
-
-def project(place, mixed_all, w_parts, hidden_rows, gain_final, w_head):
+        resid_ref[...] += dot(mixed_ref[g], weight, 1, 0).astype(BF16).astype(F32)
+    resid = resid_ref[...]
+    both = gain_ref[...] * head_ref[...]
+    squares = dot(jnp.ones((8, feat), F32), resid * resid, 1, 1, lax.Precision.HIGHEST)
+    scores = dot(jnp.broadcast_to(both, (8, feat)), resid, 1, 1, lax.Precision.HIGHEST)
+    pair = jnp.concatenate([squares[:1], scores[:1]], axis=0)
+    stats_ref[...] = jnp.broadcast_to(pair[None], stats_ref.shape)
+
+
+def project(place, mixed_all, w_parts, x_cols, gain_final, w_head):
     n_mp, rows, heads = mixed_all.shape
     feat = w_parts.shape[-1]
-    step = 2
     share = pl.BlockSpec((1, feat), lambda i, s: (0, s[0]))
+    flat = lambda a: pl.BlockSpec(a.shape, lambda i, s: (0,) * len(a.shape))
     return pl.pallas_call(
         project_kernel,
         out_shape=(
@@ -178,13 +172,11 @@
         ),
         grid_spec=pltpu.PrefetchScalarGridSpec(
             num_scalar_prefetch=1,
-            grid=(n_mp // step,),
+            grid=(1,),
             in_specs=[
-                pl.BlockSpec((step, rows, heads), lambda i, s: (i, 0, 0)),
-                pl.BlockSpec(
-                    (w_parts.shape[0], step, w_parts.shape[2], feat), lambda i, s: (0, i, 0, 0)
-                ),
-                pl.BlockSpec((rows, feat), lambda i, s: (0, s[0])),
+                pl.BlockSpec(memory_space=pltpu.HBM),
+                flat(w_parts),
+                flat(x_cols),
                 share,
                 share,
             ],
@@ -192,11 +184,15 @@
                 pl.BlockSpec((rows, feat), lambda i, s: (0, 0)),
                 pl.BlockSpec((n_mp, 2, rows), lambda i, s: (0, 0, 0)),
             ),
-        ),
-        compiler_params=pltpu.CompilerParams(vmem_limit_bytes=58 * 2**20),
+            scratch_shapes=[
+                pltpu.VMEM(mixed_all.shape, BF16),
+                pltpu.SemaphoreType.DMA((n_mp,)),
+            ],
+        ),
+        compiler_params=pltpu.CompilerParams(vmem_limit_bytes=32 * 2**20),
         cost_estimate=pl.CostEstimate(flops=550000000, bytes_accessed=4000000, transcendentals=0),
         name="project",
-    )(place, mixed_all, w_parts, hidden_rows, gain_final[None], w_head[None])
+    )(place, mixed_all, w_parts, x_cols, gain_final[None], w_head[None])
 
 
 def row_terms(stats, used, width):
@@ -294,13 +290,13 @@
             out_specs=(half_spec, half_spec),
             scratch_shapes=[pltpu.VMEM((rows, feat), BF16), pltpu.VMEM((8, feat), F32)],
         ),
-        compiler_params=pltpu.CompilerParams(vmem_limit_bytes=48 * 2**20),
+        compiler_params=pltpu.CompilerParams(vmem_limit_bytes=58 * 2**20),
         cost_estimate=pl.CostEstimate(flops=550000000, bytes_accessed=4000000, transcendentals=0),
         name="gradient",
     )(place, stats, resid, gain_final[None], w_head[None], mixed_all)
 
 
-def weigh_kernel(place, rewards_ref, order_ref, keep_ref, got_ref, out_ref, margin_ref, row_ref):
+def pairs_kernel(place, rewards_ref, order_ref, coef_ref, margin_ref, row_ref):
     seqs = rewards_ref.shape[0]
     rewards = rewards_ref[...].reshape(seqs, LANES)
     order = order_ref[...]
@@ -315,31 +311,45 @@
     me = place[3]
     own = jnp.sum(jnp.where(order == me, dreward, 0.0), axis=1, keepdims=True)
     sib = jnp.sum(jnp.where(order == (me ^ 1), dreward, 0.0), axis=1, keepdims=True)
-    out_ref[...] = (keep_ref[...].astype(F32) * own + got_ref[...].astype(F32) * sib).astype(BF16)
+    row = lax.broadcasted_iota(jnp.int32, coef_ref.shape, 0)
+    coef_ref[...] = jnp.where(row == 0, own, sib)
     margin_ref[...] = margin
     at = lax.broadcasted_iota(jnp.int32, (seqs, LANES), 1)
     row_ref[...] = jnp.sum(jnp.where(seq == at, rewards, 0.0), axis=0, keepdims=True)
 
 
-def weigh(place, rewards, order, keep, got):
-    flat = lambda a: pl.BlockSpec(a.shape, lambda i, s: (0,) * len(a.shape))
+def pair_weights(place, rewards, order):
+    flat = lambda shape: pl.BlockSpec(shape, lambda i, s: (0,) * len(shape))
+    line = jax.ShapeDtypeStruct((1, LANES), F32)
+    return pl.pallas_call(
+        pairs_kernel,
+        out_shape=(jax.ShapeDtypeStruct((8, LANES), F32), line, line),
+        grid_spec=pltpu.PrefetchScalarGridSpec(
+            num_scalar_prefetch=1,
+            grid=(1,),
+            in_specs=[flat(rewards.shape), flat(order.shape)],
+            out_specs=(flat((8, LANES)), flat((1, LANES)), flat((1, LANES))),
+        ),
+        compiler_params=pltpu.CompilerParams(vmem_limit_bytes=16 * 2**20),
+        cost_estimate=pl.CostEstimate(flops=1000000, bytes_accessed=60000000, transcendentals=128),
+        name="pairs",
+    )(place, rewards, order)
+
+
+def weigh_kernel(coef_ref, keep_ref, got_ref, out_ref):
+    own = coef_ref[0:1, 0:1]
+    sib = coef_ref[1:2, 0:1]
+    out_ref[...] = (keep_ref[...].astype(F32) * own + got_ref[...].astype(F32) * sib).astype(BF16)
+
+
+def weigh(coef, keep, got):
     return pl.pallas_call(
         weigh_kernel,
-        out_shape=(
-            jax.ShapeDtypeStruct(keep.shape, BF16),
-            jax.ShapeDtypeStruct((1, LANES), F32),
-            jax.ShapeDtypeStruct((1, LANES), F32),
-        ),
-        grid_spec=pltpu.PrefetchScalarGridSpec(
-            num_scalar_prefetch=1,
-            grid=(1,),
-            in_specs=[flat(rewards), flat(order), flat(keep), flat(got)],
-            out_specs=(flat(keep),) + (pl.BlockSpec((1, LANES), lambda i, s: (0, 0)),) * 2,
-        ),
+        out_shape=jax.ShapeDtypeStruct(keep.shape, BF16),
         compiler_params=pltpu.CompilerParams(vmem_limit_bytes=16 * 2**20),
-        cost_estimate=pl.CostEstimate(flops=1000000, bytes_accessed=2000000, transcendentals=128),
+        cost_estimate=pl.CostEstimate(flops=1000000, bytes_accessed=2000000, transcendentals=0),
         name="weigh",
-    )(place, rewards, order, keep, got)
+    )(coef, keep, got)
 
 
 def finish_kernel(half, place, mine_ref, other_ref, gain_ref, head_ref, grad_ref, ghead_ref, ggain_ref):
@@ -405,7 +415,7 @@
 
     mixed = front(hidden_rows, lengths, gain_attn, w_query, key_weight, value_weight)
 
-    mixed, w_out = lax.optimization_barrier((mixed, w_out))
+    mixed, w_out, hidden_rows = lax.optimization_barrier((mixed, w_out, hidden_rows))
     mixed_all = lax.all_gather(mixed, "mp", axis=0, tiled=False)
     piece_rows = w_out.shape[0] // NEAR
     my_near = (me // (NZ * NCORE)) * NCORE + core
@@ -414,7 +424,8 @@
     w_piece = lax.all_to_all(w_piece, "mp", 0, 0, tiled=True)
     w_parts = swap(jnp.broadcast_to(w_piece[None], (NEAR,) + w_piece.shape), near)
 
-    resid, stats = project(place, mixed_all, w_parts, hidden_rows, gain_final, w_head)
+    x_cols = lax.dynamic_slice_in_dim(hidden_rows, place[0] * feat, feat, 1)
+    resid, stats = project(place, mixed_all, w_parts, x_cols, gain_final, w_head)
     stats = lax.all_to_all(stats, "mp", 0, 0, tiled=True)
     reward, stats = lax.optimization_barrier((reward_of(lengths, stats, width, n_dp), stats))
     rewards = lax.all_to_all(reward, "dp", 0, 0, tiled=True)
@@ -423,10 +434,12 @@
     piece = -(-(half + 1) // (NX * NZ * 8)) * 8
     half_ext = piece * NX * NZ
     send, keep = gradient_halves(place, stats, resid, gain_final, w_head, mixed_all, half_ext)
+    send, rewards = lax.optimization_barrier((send, rewards))
     got = to_sibling(send)
     seqs = pair_order.shape[0]
     order = jnp.pad(pair_order, (0, LANES - seqs), constant_values=-1)[None]
-    summed, margin, reward_row = weigh(place, rewards, order, keep, got)
+    coef, margin, reward_row = pair_weights(place, rewards, order)
+    summed = weigh(coef, keep, got)
     loss = jnp.sum(jax.nn.softplus(-margin[0, :seqs:2]))
 
     got = swap(summed.reshape(NX, NZ * piece, feat), along_x)

time: 190 us -> 194 us (1.021)
  local copies, waits for them, and re-layouts: 2.93 us -> 11.7 us
  waiting for transfers between devices: 35.5 us -> 31.7 us
    unnamed x17 -> x35, local copies, waits for them, and re-layouts: 1.09 us -> 8.93 us
    all_to_all x1, starting transfers between devices: 13.6 us -> 19.5 us  [body(): rewards = lax.all_to_all(reward, 'dp', 0, 0, tiled=True)]
    ppermute x2, starting transfers between devices: 15.3 us -> 9.64 us  [to_sibling(): return lax.ppermute(x, 'dp', pairs)]
    all_to_all x1, waiting for transfers between devices: 12.1 us -> 7.73 us  [body(): rewards = lax.all_to_all(reward, 'dp', 0, 0, tiled=True)]
    pallas_call x1, Pallas kernels: 1.86 us -> 4.44 us  [gradient_halves(): pl.pallas_call(functools.partial(gradient_kernel, width), out_shape=(half...]
    pallas_call x1, Pallas kernels: 5.98 us -> 3.98 us  [project(): pl.pallas_call(project_kernel, out_shape=(jax.ShapeDtypeStruct((rows, fea...]
  transfers between devices with their start and end apart: 5 -> 5, of which waited for: 4 -> 5; matrix products, arithmetic and copies ran while one was open for 2% -> 2% of each run, Pallas kernels for 0% -> 3%
where the time goes in v5:
time: 194 us; the launch traced here: 193 us
  blocking collectives  74.7 us (39%)
  starting transfers between devices  39.3 us (20%)
  waiting for transfers between devices  31.7 us (16%)
  Pallas kernels  18 us (9%)
  between operations  15 us (8%)
  local copies, waits for them, and re-layouts  11.7 us (6%)
  other arithmetic  2.49 us (1%)
    all_to_all x4, blocking collectives, swap(): lax.all_to_all(parts, 'dp', 0, 0, tiled=True, axis_index_groups=groups)  48.5 us
    all_to_all x1, starting transfers between devices, body(): rewards = lax.all_to_all(reward, 'dp', 0, 0, tiled=True)  19.5 us
    all_to_all x1, blocking collectives, body(): w_piece = lax.all_to_all(w_piece, 'mp', 0, 0, tiled=True)  15.4 us
    all_to_all x1, waiting for transfers between devices, swap(): lax.all_to_all(parts, 'dp', 0, 0, tiled=True, axis_index_groups=groups)  14.1 us
    all_to_all x1, blocking collectives, body(): stats = lax.all_to_all(stats, 'mp', 0, 0, tiled=True)  10.8 us
    all_to_all x1, starting transfers between devices, swap(): lax.all_to_all(parts, 'dp', 0, 0, tiled=True, axis_index_groups=groups)  10.1 us
    ppermute x2, starting transfers between devices, to_sibling(): return lax.ppermute(x, 'dp', pairs)  9.64 us
    unnamed x35, local copies, waits for them, and re-layouts  8.93 us
  transfers between devices with their start and end apart: 5, of which 5 were waited for; matrix products, arithmetic and copies ran while one was open for 2% of the time, Pallas kernels for 3%

profile of v5, /device:TPU:1, one launch (start us, length us, event | category | flops | bytes accessed | tf_op | source)
XLA Modules:
  0.0 193.0 jit_solution(12913139855142267979)
XLA Ops:
  8.0 1.7 fusion
  9.6 1.6 copy-done.9
  11.2 1.2 copy-done.12
  12.5 0.9 copy-done.13
  13.4 0.9 copy-done.14
  14.4 0.7 copy-done.15
  15.1 5.7 %front.1 = bf16[512,256]{1,0:T(8,128)(2,1)} custom-call(s32[1]{0:T(128)} %copy.21.lens, bf16[512,2048]{1,0:T(8,128)(2,1)S(1)} %copy-done.9, f32[1,2048]{1,0:T(1,128)S(1)} %bitcast.54, bf16[2048,256]{1,0:T(8,128)(2,1)S(1)} %copy-done.12, bf16[64,2048]{1,0:T(8,128)(2,1)S(1)} %bitcast.52, bf16[64,2048]{1,0:T(8,128)(2,1)S(1)} %bitcast.53, ...), custom_call_target="tpu_custom_call" | custom-call | flops 1500000000 | bytes 4000000 | tf_op jit(solution)/shard_map/front/pallas_call | solution.py:119
  20.9 15.4 %all_to_all.40 = bf16[8,32,256]{2,1,0:T(8,128)(2,1)S(1)} all-to-all(bf16[8,32,256]{2,1,0:T(8,128)(2,1)S(1)} %copy.19), channel_id=1, replica_groups=mesh['dp'=96,'mp'=8] {'mp'}, dimensions={0} | all-to-all | bytes 262144 | tf_op jit(solution)/shard_map/all_to_all | solution.py:424
  36.3 1.1 broadcast_in_dim.44
  37.4 10.1 %all-to-all-start.1 = ((bf16[8,8,32,256]{3,2,1,0:T(8,128)(2,1)}), bf16[8,8,32,256]{3,2,1,0:T(8,128)(2,1)S(1)}, u32[]{:S(2)}, u32[]{:S(2)}) async-start(bf16[8,8,32,256]{3,2,1,0:T(8,128)(2,1)} %broadcast_in_dim.44), calls=%async_computation.1 | async-start | bytes 2097152 | tf_op jit(solution)/shard_map/all_to_all | solution.py:36
  47.6 1.0 constant_dynamic-slice_fusion.x_ref
  48.5 14.1 %all-to-all-done.1.w_ref = bf16[8,8,32,256]{3,2,1,0:T(8,128)(2,1)S(1)} async-done(((bf16[8,8,32,256]{3,2,1,0:T(8,128)(2,1)}), bf16[8,8,32,256]{3,2,1,0:T(8,128)(2,1)S(1)}, u32[]{:S(2)}, u32[]{:S(2)}) %all-to-all-start.1) | async-done | bytes 1048608 | tf_op jit(solution)/shard_map/all_to_all | solution.py:36
  62.6 8.5 %all-gather.3.cloned.1.call-done = bf16[4096,256]{1,0:T(8,128)(2,1)} async-done(((bf16[512,256]{1,0:T(8,128)(2,1)}), bf16[4096,256]{1,0:T(8,128)(2,1)}) %all-gather.3.cloned.1.call-update) | async-done | bytes 2097168 | tf_op jit(solution)/shard_map/all_gather | solution.py:419
  71.2 1.6 copy-done.1
  72.7 4.0 %project.1 = (f32[512,256]{1,0:T(8,128)S(1)}, f32[8,2,512]{2,1,0:T(2,128)S(1)}) custom-call(s32[4]{0:T(128)S(1)} %pad_add_fusion.place, bf16[8,512,256]{2,1,0:T(8,128)(2,1)S(1)} %bitcast.42, bf16[8,8,32,256]{3,2,1,0:T(8,128)(2,1)S(1)} %all-to-all-done.1.w_ref, bf16[512,256]{1,0:T(8,128)(2,1)S(1)} %constant_dynamic-slice_fusion.x_ref, ...), custom_call_target="tpu_custom_call" | custom-call | flops 550000000 | bytes 4000000 | tf_op jit(solution)/shard_map/project/pallas_call | solution.py:167
  76.7 0.8 copy-done.3
  77.5 10.8 %all_to_all.41.stats_ref = f32[8,2,512]{2,1,0:T(2,128)S(1)} all-to-all(f32[8,2,512]{2,1,0:T(2,128)S(1)} %get-tuple-element.25), channel_id=1, replica_groups=mesh['dp'=96,'mp'=8] {'mp'}, dimensions={0} | all-to-all | bytes 65536 | tf_op jit(solution)/shard_map/all_to_all | solution.py:429
  88.3 0.7 reward.1
  89.1 19.5 %all-to-all-start.3 = ((f32[96,1,128]{2,1,0:T(1,128)}), f32[96,1,128]{2,1,0:T(1,128)S(1)}, u32[]{:S(2)}, u32[]{:S(2)}) async-start(f32[96,1,128]{2,1,0:T(1,128)} %reward.1), calls=%async_computation.3 | async-start | bytes 98304 | tf_op jit(solution)/shard_map/all_to_all | solution.py:431
  108.6 4.4 %gradient.1 = (bf16[1152,256]{1,0:T(8,128)(2,1)}, bf16[1152,256]{1,0:T(8,128)(2,1)}) custom-call(s32[4]{0:T(128)} %copy-done.10, f32[8,2,512]{2,1,0:T(2,128)} %copy-done.4, f32[512,256]{1,0:T(8,128)} %copy-done.3, f32[1,2048]{1,0:T(1,128)} %bitcast.46, f32[1,2048]{1,0:T(1,128)} %bitcast.49, bf16[8,512,256]{2,1,0:T(8,128)(2,1)} %bitcast.41), custom_call_target="tpu_custom_call" | custom-call | flops 550000000 | bytes 4000000 | tf_op jit(solution)/shard_map/gradient/pallas_call | solution.py:277
  113.1 7.7 %all-to-all-done.3.rewards_ref = f32[96,1,128]{2,1,0:T(1,128)S(1)} async-done(((f32[96,1,128]{2,1,0:T(1,128)}), f32[96,1,128]{2,1,0:T(1,128)S(1)}, u32[]{:S(2)}, u32[]{:S(2)}) %all-to-all-start.3) | async-done | bytes 49184 | tf_op jit(solution)/shard_map/all_to_all | solution.py:431
  120.8 2.8 %collective-permute-start = (bf16[1152,256]{1,0:T(8,128)(2,1)}, bf16[1152,256]{1,0:T(8,128)(2,1)S(1)}, u32[]{:S(2)}, u32[]{:S(2)}) collective-permute-start(bf16[1152,256]{1,0:T(8,128)(2,1)} %get-tuple-element.35), channel_id=1, source_target_pairs={{0,8},{8,0},{16,24},{24,16},{32,40},{40,32},{48,56},{56,48},{64,72... | collective-permute-start | bytes 1769480 | tf_op jit(solution)/shard_map/ppermute | solution.py:41
  123.7 0.8 pairs.1
  124.4 1.0 collective-permute-done.got_ref
  125.5 1.1 copy-done.2
  127.0 12.0 %all_to_all.42 = bf16[4,288,256]{2,1,0:T(8,128)(2,1)S(1)} all-to-all(bf16[4,288,256]{2,1,0:T(8,128)(2,1)S(1)} %bitcast.43), channel_id=1, replica_groups={{0,192,384,576},{8,200,392,584},{16,208,400,592},{24,216,408,600},{32,2..., dimensions={0} | all-to-all | bytes 1179648 | tf_op jit(solution)/shard_map/all_to_all | solution.py:36
  139.1 13.0 %all_to_all.43 = bf16[12,24,256]{2,1,0:T(8,128)(2,1)S(1)} all-to-all(bf16[12,24,256]{2,1,0:T(8,128)(2,1)S(1)} %bitcast.55), channel_id=1, replica_groups={{0,16,32,48,64,80,96,112,128,144,160,176},{8,24,40,56,72,88,104,120,136..., dimensions={0} | all-to-all | bytes 294912 | tf_op jit(solution)/shard_map/all_to_all | solution.py:36
  152.2 13.8 %all_to_all.44 = bf16[12,24,256]{2,1,0:T(8,128)(2,1)S(1)} all-to-all(bf16[12,24,256]{2,1,0:T(8,128)(2,1)S(1)} %broadcast_in_dim.48), channel_id=1, replica_groups={{0,16,32,48,64,80,96,112,128,144,160,176},{8,24,40,56,72,88,104,120,136..., dimensions={0} | all-to-all | bytes 294912 | tf_op jit(solution)/shard_map/all_to_all | solution.py:36
  166.1 9.7 %all_to_all.45 = bf16[4,288,256]{2,1,0:T(8,128)(2,1)S(1)} all-to-all(bf16[4,288,256]{2,1,0:T(8,128)(2,1)S(1)} %broadcast_in_dim.50), channel_id=1, replica_groups={{0,192,384,576},{8,200,392,584},{16,208,400,592},{24,216,408,600},{32,2..., dimensions={0} | all-to-all | bytes 1179648 | tf_op jit(solution)/shard_map/all_to_all | solution.py:36
  175.7 6.8 %collective-permute-start.1 = (bf16[1152,256]{1,0:T(8,128)(2,1)S(1)}, bf16[1152,256]{1,0:T(8,128)(2,1)S(1)}, u32[]{:S(2)}, u32[]{:S(2)}) collective-permute-start(bf16[1152,256]{1,0:T(8,128)(2,1)S(1)} %bitcast.44), channel_id=1, source_target_pairs={{0,8},{8,0},{16,24},{24,16},{32,40},{40,32},{48,56},{56,48},{64,72... | collective-permute-start | bytes 1769480 | tf_op jit(solution)/shard_map/ppermute | solution.py:41
  182.7 0.6 fusion.1
  184.2 2.0 %finish.1 = (f32[2048,256]{1,0:T(8,128)}, f32[1,256]{1,0:T(1,128)}, f32[1,256]{1,0:T(1,128)}) custom-call(s32[4]{0:T(128)S(1)} %copy-done.11, bf16[1152,256]{1,0:T(8,128)(2,1)S(1)} %bitcast.45, bf16[1152,256]{1,0:T(8,128)(2,1)S(1)} %collective-permute-done.1.other_ref, f32[1,2048]{1,0:T(1,128)S(1)} %bitcast.48, f32[1,2048]{1,0:T(1,128)S(1)} %bitcast.51), custom_call_target="tpu_custom_call" | custom-call | flops 1000000 | bytes 4000000 | tf_op jit(solution)/shard_map/finish/pallas_call | solution.py:376
  (42 shorter events, 1.9 us)
Async XLA Ops:
  7.2 13.7 %copy-start = (bf16[256,2048]{1,0:T(8,128)(2,1)S(1)}, bf16[256,2048]{1,0:T(8,128)(2,1)}, u32[]{:S(2)}) copy-start(bf16[256,2048]{1,0:T(8,128)(2,1)} %param.19) | copy-start | bytes 3145732
  7.2 64.0 %all-gather.3.cloned.1.call-start = ((), (), s32[]{:S(2)}) async-start(), calls=%async_computation.8 | async-start | bytes 2359296 | tf_op jit(solution)/shard_map/all_gather | solution.py:419
  9.6 1.6 copy-start.9
  11.2 1.2 copy-start.12
  12.5 0.9 copy-start.13
  13.4 0.9 copy-start.14
  14.4 0.7 copy-start.15
  20.9 50.2 %copy-start.5 = (f32[2048]{0:T(1024)S(1)}, f32[2048]{0:T(1024)}, u32[]{:S(2)}) copy-start(f32[2048]{0:T(1024)} %param.20) | copy-start | bytes 24580
  20.9 50.2 %copy-start.7 = (f32[2048]{0:T(1024)S(1)}, f32[2048]{0:T(1024)}, u32[]{:S(2)}) copy-start(f32[2048]{0:T(1024)} %param.21) | copy-start | bytes 24580
  37.4 25.2 %all-to-all-start.1 = ((bf16[8,8,32,256]{3,2,1,0:T(8,128)(2,1)}), bf16[8,8,32,256]{3,2,1,0:T(8,128)(2,1)S(1)}, u32[]{:S(2)}, u32[]{:S(2)}) async-start(bf16[8,8,32,256]{3,2,1,0:T(8,128)(2,1)} %broadcast_in_dim.44), calls=%async_computation.1 | async-start | bytes 2097152 | tf_op jit(solution)/shard_map/all_to_all | solution.py:36
  47.6 41.5 %copy-start.10 = (s32[4]{0:T(128)}, s32[4]{0:T(128)S(1)}, u32[]{:S(2)}) copy-start(s32[4]{0:T(128)S(1)} %pad_add_fusion.place) | copy-start | bytes 52
  71.1 1.6 copy-start.1
  76.7 0.8 copy-start.3
  77.5 46.1 %copy-start.16 = (s32[96]{0:T(128)S(1)}, s32[96]{0:T(128)}, u32[]{:S(2)}) copy-start(s32[96]{0:T(128)} %param.14) | copy-start | bytes 1156
  88.3 20.3 %copy-start.4 = (f32[8,2,512]{2,1,0:T(2,128)}, f32[8,2,512]{2,1,0:T(2,128)S(1)}, u32[]{:S(2)}) copy-start(f32[8,2,512]{2,1,0:T(2,128)S(1)} %all_to_all.41.stats_ref) | copy-start | bytes 98308
  89.1 31.7 %all-to-all-start.3 = ((f32[96,1,128]{2,1,0:T(1,128)}), f32[96,1,128]{2,1,0:T(1,128)S(1)}, u32[]{:S(2)}, u32[]{:S(2)}) async-start(f32[96,1,128]{2,1,0:T(1,128)} %reward.1), calls=%async_computation.3 | async-start | bytes 98304 | tf_op jit(solution)/shard_map/all_to_all | solution.py:431
  108.6 15.1 %copy-start.11 = (s32[4]{0:T(128)S(1)}, s32[4]{0:T(128)}, u32[]{:S(2)}) copy-start(s32[4]{0:T(128)} %copy-done.10) | copy-start | bytes 52
  120.8 4.7 %collective-permute-start = (bf16[1152,256]{1,0:T(8,128)(2,1)}, bf16[1152,256]{1,0:T(8,128)(2,1)S(1)}, u32[]{:S(2)}, u32[]{:S(2)}) collective-permute-start(bf16[1152,256]{1,0:T(8,128)(2,1)} %get-tuple-element.35), channel_id=1, source_target_pairs={{0,8},{8,0},{16,24},{24,16},{32,40},{40,32},{48,56},{56,48},{64,72... | collective-permute-start | bytes 1769480 | tf_op jit(solution)/shard_map/ppermute | solution.py:41
  125.5 1.1 copy-start.2
  127.0 57.2 %copy-start.6 = (f32[2048]{0:T(1024)S(1)}, f32[2048]{0:T(1024)}, u32[]{:S(2)}) copy-start(f32[2048]{0:T(1024)} %param.20) | copy-start | bytes 24580
  127.0 57.2 %copy-start.8 = (f32[2048]{0:T(1024)S(1)}, f32[2048]{0:T(1024)}, u32[]{:S(2)}) copy-start(f32[2048]{0:T(1024)} %param.21) | copy-start | bytes 24580
  175.7 8.4 %collective-permute-start.1 = (bf16[1152,256]{1,0:T(8,128)(2,1)S(1)}, bf16[1152,256]{1,0:T(8,128)(2,1)S(1)}, u32[]{:S(2)}, u32[]{:S(2)}) collective-permute-start(bf16[1152,256]{1,0:T(8,128)(2,1)S(1)} %bitcast.44), channel_id=1, source_target_pairs={{0,8},{8,0},{16,24},{24,16},{32,40},{40,32},{48,56},{56,48},{64,72... | collective-permute-start | bytes 1769480 | tf_op jit(solution)/shard_map/ppermute | solution.py:41
Sparse Core Ops, SparseCore 0:
  20.9 50.2 all-gather.2

commit v6 on v4

--- a/solution.py
+++ b/solution.py
@@ -13,6 +13,7 @@
 HEAD_SIZE = 64
 NX, NZ, NCORE = 4, 12, 2
 NEAR = NX * NCORE
+ZB = 4
 
 EPS = 1e-05
 THETA = 500000.0
@@ -27,9 +28,11 @@
 
 def dp_groups():
     along_x = [[device_of(x, z, c) for x in range(NX)] for z in range(NZ) for c in range(NCORE)]
-    along_z = [[device_of(x, z, c) for z in range(NZ)] for x in range(NX) for c in range(NCORE)]
+    columns = [(x, c) for x in range(NX) for c in range(NCORE)]
+    close_z = [[device_of(x, b * ZB + z, c) for z in range(ZB)] for x, c in columns for b in range(NZ // ZB)]
+    far_z = [[device_of(x, b * ZB + z, c) for b in range(NZ // ZB)] for x, c in columns for z in range(ZB)]
     near = [[device_of(x, z, c) for x in range(NX) for c in range(NCORE)] for z in range(NZ)]
-    return along_x, along_z, near
+    return along_x, close_z, far_z, near
 
 
 def swap(parts, groups):
@@ -47,129 +50,144 @@
     )
 
 
-def rope_tables(positions):
-    half = HEAD_SIZE // 2
-    freq = np.tile(THETA ** (-np.arange(half) * 2.0 / HEAD_SIZE), LANES // half).astype(np.float32)
-    sign = np.tile(np.repeat([-1.0, 1.0], half), LANES // HEAD_SIZE).astype(np.float32)
-    angle = positions.astype(F32)[:, None] * freq[None, :]
-    return jnp.cos(angle), jnp.sin(angle) * sign[None, :]
-
-
-def front_kernel(lens, x_ref, gain_ref, wq_ref, wk_ref, wv_ref, cos_ref, sin_ref, out_ref, k_ref, v_ref):
-    step = pl.program_id(0)
-    rows = x_ref.shape[0]
-    x = x_ref[...].astype(F32)
-    inv = lax.rsqrt(jnp.mean(x * x, axis=1, keepdims=True) + EPS)
-    normed = (x * inv * gain_ref[...]).astype(BF16)
-    cosine, sine = cos_ref[...], sin_ref[...]
+def front_kernel(lens, x_hbm, gain_ref, wq_hbm, wk_hbm, wv_hbm, freq_ref, out_ref, x_ref, wq_ref, wk_ref, wv_ref, k_ref, v_ref, sems):
+    total_rows = x_ref.shape[0]
+    blocks = 2
+    rows = total_rows // blocks
+    copies = [
+        pltpu.make_async_copy(x_hbm.at[pl.ds(0, rows)], x_ref.at[pl.ds(0, rows)], sems.at[0]),
+        pltpu.make_async_copy(wq_hbm, wq_ref, sems.at[1]),
+        pltpu.make_async_copy(wk_hbm, wk_ref, sems.at[2]),
+        pltpu.make_async_copy(wv_hbm, wv_ref, sems.at[3]),
+        pltpu.make_async_copy(x_hbm.at[pl.ds(rows, rows)], x_ref.at[pl.ds(rows, rows)], sems.at[4]),
+    ]
+    for copy in copies:
+        copy.start()
+    used = lens[0]
     lane = lax.broadcasted_iota(jnp.int32, (rows, LANES), 1)
     first_half = (lane % HEAD_SIZE) < HEAD_SIZE // 2
     low = lane < HEAD_SIZE
-
-    def rotate(t):
+    gain = gain_ref[...]
+
+    def tables(first):
+        row = first + lax.broadcasted_iota(jnp.int32, (rows, LANES), 0)
+        position = row - jnp.where(row >= used, used, 0)
+        angle = position.astype(F32) * freq_ref[...]
+        sine = jnp.sin(angle)
+        return jnp.cos(angle), jnp.where(first_half, -sine, sine)
+
+    turns = [tables(i * rows) for i in range(blocks)]
+
+    def rotate(t, turn):
         partner = jnp.where(
             first_half, pltpu.roll(t, LANES - HEAD_SIZE // 2, 1), pltpu.roll(t, HEAD_SIZE // 2, 1)
         )
-        return t * cosine + partner * sine
-
-    query = dot(normed, wq_ref[...], 1, 0)
-    key = dot(normed, wk_ref[...], 1, 1)
-    value = dot(normed, wv_ref[...], 1, 1)
-    key = rotate(jnp.concatenate([key, key], axis=1))
-    value = jnp.concatenate([value, value], axis=1)
-    here = pl.ds(pl.multiple_of(step * rows, rows), rows)
-    k_ref[0, here, :] = jnp.where(low, key, 0.0).astype(BF16)
-    k_ref[1, here, :] = jnp.where(low, 0.0, key).astype(BF16)
-    v_ref[0, here, :] = jnp.where(low, value, 0.0).astype(BF16)
-    v_ref[1, here, :] = jnp.where(low, 0.0, value).astype(BF16)
-    pairs = query.shape[1] // LANES
-    turned = [rotate(query[:, p * LANES : (p + 1) * LANES]).astype(BF16) for p in range(pairs)]
-    used = lens[0]
-
-    def attend(first, cols):
+        return t * turn[0] + partner * turn[1]
+
+    def norm(i):
+        x = x_ref[i * rows : (i + 1) * rows, :].astype(F32)
+        return (x * lax.rsqrt(jnp.mean(x * x, axis=1, keepdims=True) + EPS) * gain).astype(BF16)
+
+    def attend(query, first, cols):
         row = first + lax.broadcasted_iota(jnp.int32, (rows, cols), 0)
         col = lax.broadcasted_iota(jnp.int32, (rows, cols), 1)
         allowed = (col <= row) & ((row >= used) == (col >= used))
-        for p in range(pairs):
+        for p in range(len(query)):
             total = jnp.zeros((rows, LANES), F32)
             for e in range(LANES // HEAD_SIZE):
-                scores = dot(turned[p], k_ref[e, :cols, :], 1, 1) * HEAD_SIZE ** (-0.5)
+                scores = dot(query[p], k_ref[e, :cols, :], 1, 1) * HEAD_SIZE ** (-0.5)
                 scores = jnp.where(allowed, scores, -1e30)
                 top = jnp.max(scores, axis=1, keepdims=True)
                 weights = jnp.exp(scores - top)
                 probs = weights * (1.0 / jnp.sum(weights, axis=1, keepdims=True))
                 total = total + dot(probs.astype(BF16), v_ref[e, :cols, :], 1, 0)
-            out_ref[:, p * LANES : (p + 1) * LANES] = total.astype(BF16)
-
-    for s in range(k_ref.shape[1] // rows):
-        @pl.when(step == s)
-        def _(s=s):
-            attend(s * rows, (s + 1) * rows)
+            out_ref[first : first + rows, p * LANES : (p + 1) * LANES] = total.astype(BF16)
+
+    copies[0].wait()
+    for i in range(blocks):
+        if i == 1:
+            copies[4].wait()
+        normed = norm(i)
+        if i == 0:
+            for copy in copies[1:4]:
+                copy.wait()
+        query = dot(normed, wq_ref[...], 1, 0)
+        key = dot(normed, wk_ref[...], 1, 1)
+        value = dot(normed, wv_ref[...], 1, 1)
+        key = rotate(jnp.concatenate([key, key], axis=1), turns[i])
+        value = jnp.concatenate([value, value], axis=1)
+        here = slice(i * rows, (i + 1) * rows)
+        k_ref[0, here, :] = jnp.where(low, key, 0.0).astype(BF16)
+        k_ref[1, here, :] = jnp.where(low, 0.0, key).astype(BF16)
+        v_ref[0, here, :] = jnp.where(low, value, 0.0).astype(BF16)
+        v_ref[1, here, :] = jnp.where(low, 0.0, value).astype(BF16)
+        turned = [
+            rotate(query[:, p * LANES : (p + 1) * LANES], turns[i]).astype(BF16)
+            for p in range(query.shape[1] // LANES)
+        ]
+        attend(turned, i * rows, (i + 1) * rows)
 
 
 def front(hidden_rows, lengths, gain_attn, w_query, key_weight, value_weight):
     rows, width = hidden_rows.shape
-    row = jnp.arange(rows, dtype=jnp.int32)
-    cosine, sine = rope_tables(row - jnp.where(row >= lengths[0], lengths[0], 0))
-    block = rows // 2
+    key_weight, value_weight = key_weight.T, value_weight.T
+    gain = gain_attn[None]
+    half = HEAD_SIZE // 2
+    freq = np.tile(THETA ** (-np.arange(half) * 2.0 / HEAD_SIZE), LANES // half).astype(np.float32)[None]
     whole = lambda a: pl.BlockSpec(a.shape, lambda i, s: (0, 0))
-    by_rows = lambda cols: pl.BlockSpec((block, cols), lambda i, s: (i, 0))
-    gain = gain_attn[None]
-    key_weight, value_weight = key_weight.T, value_weight.T
+    far = pl.BlockSpec(memory_space=pl.ANY)
     return pl.pallas_call(
         front_kernel,
         out_shape=jax.ShapeDtypeStruct((rows, w_query.shape[1]), BF16),
         grid_spec=pltpu.PrefetchScalarGridSpec(
             num_scalar_prefetch=1,
-            grid=(rows // block,),
-            in_specs=[
-                by_rows(width),
-                whole(gain),
-                whole(w_query),
-                whole(key_weight),
-                whole(value_weight),
-                by_rows(LANES),
-                by_rows(LANES),
+            grid=(1,),
+            in_specs=[far, whole(gain), far, far, far, whole(freq)],
+            out_specs=pl.BlockSpec((rows, w_query.shape[1]), lambda i, s: (0, 0)),
+            scratch_shapes=[
+                pltpu.VMEM(hidden_rows.shape, BF16),
+                pltpu.VMEM(w_query.shape, BF16),
+                pltpu.VMEM(key_weight.shape, BF16),
+                pltpu.VMEM(value_weight.shape, BF16),
+                pltpu.VMEM((2, rows, LANES), BF16),
+                pltpu.VMEM((2, rows, LANES), BF16),
+                pltpu.SemaphoreType.DMA((5,)),
             ],
-            out_specs=by_rows(w_query.shape[1]),
-            scratch_shapes=[pltpu.VMEM((2, rows, LANES), BF16), pltpu.VMEM((2, rows, LANES), BF16)],
         ),
         compiler_params=pltpu.CompilerParams(vmem_limit_bytes=58 * 2**20),
-        cost_estimate=pl.CostEstimate(flops=1500000000, bytes_accessed=4000000, transcendentals=800000),
+        cost_estimate=pl.CostEstimate(flops=1500000000, bytes_accessed=4000000, transcendentals=900000),
         name="front",
-    )(lengths, hidden_rows, gain, w_query, key_weight, value_weight, cosine, sine)
-
-
-def project_kernel(place, mixed_ref, w_ref, x_ref, gain_ref, head_ref, resid_ref, stats_ref):
-    step = pl.program_id(0)
+    )(lengths, hidden_rows, gain, w_query, key_weight, value_weight, jnp.asarray(freq))
+
+
+def project_kernel(place, mixed_hbm, w_hbm, x_ref, gain_ref, head_ref, resid_ref, stats_ref, mixed_ref, w_ref, sems):
     groups = mixed_ref.shape[0]
     rows, feat = resid_ref.shape
-
-    @pl.when(step == 0)
-    def _():
-        resid_ref[...] = x_ref[...].astype(F32)
-
-    total = jnp.zeros((rows, feat), F32)
+    copies = [pltpu.make_async_copy(mixed_hbm.at[g], mixed_ref.at[g], sems.at[g]) for g in range(groups)]
+    weights = pltpu.make_async_copy(w_hbm, w_ref, sems.at[groups])
+    copies[0].start()
+    weights.start()
+    for copy in copies[1:]:
+        copy.start()
+    resid_ref[...] = x_ref[...].astype(F32)
+    weights.wait()
     for g in range(groups):
+        copies[g].wait()
         weight = w_ref[:, g].reshape(-1, feat)
-        total = total + dot(mixed_ref[g], weight, 1, 0).astype(BF16).astype(F32)
-    resid_ref[...] += total
-
-    @pl.when(step == pl.num_programs(0) - 1)
-    def _():
-        resid = resid_ref[...]
-        both = gain_ref[...] * head_ref[...]
-        squares = dot(jnp.ones((8, feat), F32), resid * resid, 1, 1, lax.Precision.HIGHEST)
-        scores = dot(jnp.broadcast_to(both, (8, feat)), resid, 1, 1, lax.Precision.HIGHEST)
-        pair = jnp.concatenate([squares[:1], scores[:1]], axis=0)
-        stats_ref[...] = jnp.broadcast_to(pair[None], stats_ref.shape)
-
-
-def project(place, mixed_all, w_parts, hidden_rows, gain_final, w_head):
+        resid_ref[...] += dot(mixed_ref[g], weight, 1, 0).astype(BF16).astype(F32)
+    resid = resid_ref[...]
+    both = gain_ref[...] * head_ref[...]
+    squares = dot(jnp.ones((8, feat), F32), resid * resid, 1, 1, lax.Precision.HIGHEST)
+    scores = dot(jnp.broadcast_to(both, (8, feat)), resid, 1, 1, lax.Precision.HIGHEST)
+    pair = jnp.concatenate([squares[:1], scores[:1]], axis=0)
+    stats_ref[...] = jnp.broadcast_to(pair[None], stats_ref.shape)
+
+
+def project(place, mixed_all, w_parts, x_cols, gain_final, w_head):
     n_mp, rows, heads = mixed_all.shape
     feat = w_parts.shape[-1]
-    step = 2
     share = pl.BlockSpec((1, feat), lambda i, s: (0, s[0]))
+    flat = lambda a: pl.BlockSpec(a.shape, lambda i, s: (0,) * len(a.shape))
     return pl.pallas_call(
         project_kernel,
         out_shape=(
@@ -178,13 +196,11 @@
         ),
         grid_spec=pltpu.PrefetchScalarGridSpec(
             num_scalar_prefetch=1,
-            grid=(n_mp // step,),
+            grid=(1,),
             in_specs=[
-                pl.BlockSpec((step, rows, heads), lambda i, s: (i, 0, 0)),
-                pl.BlockSpec(
-                    (w_parts.shape[0], step, w_parts.shape[2], feat), lambda i, s: (0, i, 0, 0)
-                ),
-                pl.BlockSpec((rows, feat), lambda i, s: (0, s[0])),
+                pl.BlockSpec(memory_space=pl.ANY),
+                pl.BlockSpec(memory_space=pl.ANY),
+                flat(x_cols),
                 share,
                 share,
             ],
@@ -192,11 +208,16 @@
                 pl.BlockSpec((rows, feat), lambda i, s: (0, 0)),
                 pl.BlockSpec((n_mp, 2, rows), lambda i, s: (0, 0, 0)),
             ),
+            scratch_shapes=[
+                pltpu.VMEM(mixed_all.shape, BF16),
+                pltpu.VMEM(w_parts.shape, BF16),
+                pltpu.SemaphoreType.DMA((n_mp + 1,)),
+            ],
         ),
         compiler_params=pltpu.CompilerParams(vmem_limit_bytes=58 * 2**20),
         cost_estimate=pl.CostEstimate(flops=550000000, bytes_accessed=4000000, transcendentals=0),
         name="project",
-    )(place, mixed_all, w_parts, hidden_rows, gain_final[None], w_head[None])
+    )(place, mixed_all, w_parts, x_cols, gain_final[None], w_head[None])
 
 
 def row_terms(stats, used, width):
@@ -400,12 +421,12 @@
     feat = width // n_mp
     me = lax.axis_index("dp").astype(jnp.int32)
     core = me % NCORE
-    along_x, along_z, near = dp_groups()
+    along_x, close_z, far_z, near = dp_groups()
     place = jnp.stack([lax.axis_index("mp").astype(jnp.int32), core, lengths[0], me])
 
     mixed = front(hidden_rows, lengths, gain_attn, w_query, key_weight, value_weight)
 
-    mixed, w_out = lax.optimization_barrier((mixed, w_out))
+    mixed, w_out, hidden_rows = lax.optimization_barrier((mixed, w_out, hidden_rows))
     mixed_all = lax.all_gather(mixed, "mp", axis=0, tiled=False)
     piece_rows = w_out.shape[0] // NEAR
     my_near = (me // (NZ * NCORE)) * NCORE + core
@@ -414,14 +435,15 @@
     w_piece = lax.all_to_all(w_piece, "mp", 0, 0, tiled=True)
     w_parts = swap(jnp.broadcast_to(w_piece[None], (NEAR,) + w_piece.shape), near)
 
-    resid, stats = project(place, mixed_all, w_parts, hidden_rows, gain_final, w_head)
+    x_cols = lax.dynamic_slice_in_dim(hidden_rows, place[0] * feat, feat, 1)
+    resid, stats = project(place, mixed_all, w_parts, x_cols, gain_final, w_head)
     stats = lax.all_to_all(stats, "mp", 0, 0, tiled=True)
     reward, stats = lax.optimization_barrier((reward_of(lengths, stats, width, n_dp), stats))
     rewards = lax.all_to_all(reward, "dp", 0, 0, tiled=True)
 
     half = width // NCORE
-    piece = -(-(half + 1) // (NX * NZ * 8)) * 8
-    half_ext = piece * NX * NZ
+    piece = -(-(half + 16) // (NX * ZB * 8)) * 8
+    half_ext = piece * NX * ZB
     send, keep = gradient_halves(place, stats, resid, gain_final, w_head, mixed_all, half_ext)
     got = to_sibling(send)
     seqs = pair_order.shape[0]
@@ -429,12 +451,14 @@
     summed, margin, reward_row = weigh(place, rewards, order, keep, got)
     loss = jnp.sum(jax.nn.softplus(-margin[0, :seqs:2]))
 
-    got = swap(summed.reshape(NX, NZ * piece, feat), along_x)
+    got = swap(summed.reshape(NX, ZB * piece, feat), along_x)
     summed = jnp.sum(got.astype(F32), axis=0).astype(BF16)
-    got = swap(summed.reshape(NZ, piece, feat), along_z)
-    mine = jnp.sum(got.astype(F32), axis=0).astype(BF16)
-    got = swap(jnp.broadcast_to(mine[None], (NZ, piece, feat)), along_z)
-    got = swap(jnp.broadcast_to(got.reshape(1, NZ * piece, feat), (NX, NZ * piece, feat)), along_x)
+    got = swap(summed.reshape(ZB, piece, feat), close_z)
+    summed = jnp.sum(got.astype(F32), axis=0).astype(BF16)
+    got = swap(jnp.broadcast_to(summed[None], (NZ // ZB, piece, feat)), far_z)
+    summed = jnp.sum(got.astype(F32), axis=0).astype(BF16)
+    got = swap(jnp.broadcast_to(summed[None], (ZB, piece, feat)), close_z)
+    got = swap(jnp.broadcast_to(got.reshape(1, ZB * piece, feat), (NX, ZB * piece, feat)), along_x)
     got = got.reshape(half_ext, feat)
     other = to_sibling(got)
     grad_out_proj, grad_head, grad_gain = finish(place, got, other, gain_final, w_head, half)

time: 190 us -> 192 us (1.011)
  other arithmetic: 3.9 us -> 1.35 us
    mul x1 -> x0, other arithmetic: 2.5 us -> none  [rope_tables(): return (jnp.cos(angle), jnp.sin(angle) * sign[None, :])]
    all_to_all x4 -> x5, blocking collectives: 47.8 us -> 48.1 us  [swap(): lax.all_to_all(parts, 'dp', 0, 0, tiled=True, axis_index_groups=groups)]
where the time goes in v6:
time: 192 us; the launch traced here: 191 us
  blocking collectives  74.3 us (39%)
  starting transfers between devices  40.9 us (21%)
  waiting for transfers between devices  33.8 us (18%)
  Pallas kernels  20.9 us (11%)
  between operations  15 us (8%)
  local copies, waits for them, and re-layouts  4.63 us (2%)
    all_to_all x5, blocking collectives, swap(): lax.all_to_all(parts, 'dp', 0, 0, tiled=True, axis_index_groups=groups)  48.1 us
    ppermute x2, starting transfers between devices, to_sibling(): return lax.ppermute(x, 'dp', pairs)  17.1 us
    all_to_all x1, blocking collectives, body(): w_piece = lax.all_to_all(w_piece, 'mp', 0, 0, tiled=True)  15.4 us
    all_to_all x1, starting transfers between devices, body(): rewards = lax.all_to_all(reward, 'dp', 0, 0, tiled=True)  13.6 us
    all_to_all x1, waiting for transfers between devices, swap(): lax.all_to_all(parts, 'dp', 0, 0, tiled=True, axis_index_groups=groups)  12.8 us
    all_to_all x1, waiting for transfers between devices, body(): rewards = lax.all_to_all(reward, 'dp', 0, 0, tiled=True)  12.1 us
    all_to_all x1, blocking collectives, body(): stats = lax.all_to_all(stats, 'mp', 0, 0, tiled=True)  10.9 us
    all_to_all x1, starting transfers between devices, swap(): lax.all_to_all(parts, 'dp', 0, 0, tiled=True, axis_index_groups=groups)  10.1 us
  transfers between devices with their start and end apart: 5, of which 4 were waited for; matrix products, arithmetic and copies ran while one was open for 2% of the time, Pallas kernels for 0%

profile of v6, /device:TPU:1, one launch (start us, length us, event | category | flops | bytes accessed | tf_op | source)
XLA Modules:
  0.0 190.8 jit_solution(1497110416321906553)
XLA Ops:
  7.2 0.0 copy-start
  7.2 0.0 all-gather.3.cloned.1.call-start
  8.0 8.3 %front.1 = bf16[512,256]{1,0:T(8,128)(2,1)} custom-call(s32[1]{0:T(128)S(6)} %copy.20.lens, bf16[512,2048]{1,0:T(8,128)(2,1)} %x_hbm.1, f32[1,2048]{1,0:T(1,128)} %bitcast.56, bf16[2048,256]{1,0:T(8,128)(2,1)} %wq_hbm.1, bf16[64,2048]{1,0:T(8,128)(2,1)} %bitcast.54, bf16[64,2048]{1,0:T(8,128)(2,1)} %bitcast.55, f32[1,128]{1,0:T(1,128)} %constant.48.clone.freq_ref), custom_call_target="tpu_custom_call" | custom-call | flops 1500000000 | bytes 4000000 | tf_op jit(solution)/shard_map/front/pallas_call | solution.py:139
  16.2 0.0 all-gather.3.cloned.1.call-update
  16.4 15.4 %all_to_all.45 = bf16[8,32,256]{2,1,0:T(8,128)(2,1)S(1)} all-to-all(bf16[8,32,256]{2,1,0:T(8,128)(2,1)S(1)} %copy.18), channel_id=1, replica_groups=mesh['dp'=96,'mp'=8] {'mp'}, dimensions={0} | all-to-all | bytes 262144 | tf_op jit(solution)/shard_map/all_to_all | solution.py:435
  31.8 1.1 broadcast_in_dim.19
  32.9 10.1 %all-to-all-start.1 = ((bf16[8,8,32,256]{3,2,1,0:T(8,128)(2,1)}), bf16[8,8,32,256]{3,2,1,0:T(8,128)(2,1)S(1)}, u32[]{:S(2)}, u32[]{:S(2)}) async-start(bf16[8,8,32,256]{3,2,1,0:T(8,128)(2,1)} %broadcast_in_dim.19), calls=%async_computation.1 | async-start | bytes 2097152 | tf_op jit(solution)/shard_map/all_to_all | solution.py:39
  42.9 0.6 pad_add_fusion.place
  43.5 1.7 constant_dynamic-slice_fusion.x_ref
  45.2 12.8 %all-to-all-done.1.w_hbm = bf16[8,8,32,256]{3,2,1,0:T(8,128)(2,1)S(1)} async-done(((bf16[8,8,32,256]{3,2,1,0:T(8,128)(2,1)}), bf16[8,8,32,256]{3,2,1,0:T(8,128)(2,1)S(1)}, u32[]{:S(2)}, u32[]{:S(2)}) %all-to-all-start.1) | async-done | bytes 1048608 | tf_op jit(solution)/shard_map/all_to_all | solution.py:39
  58.1 8.6 %all-gather.3.cloned.1.call-done = bf16[4096,256]{1,0:T(8,128)(2,1)} async-done(((bf16[512,256]{1,0:T(8,128)(2,1)}), bf16[4096,256]{1,0:T(8,128)(2,1)}) %all-gather.3.cloned.1.call-update) | async-done | bytes 2097168 | tf_op jit(solution)/shard_map/all_gather | solution.py:430
  66.6 6.9 %project.1 = (f32[512,256]{1,0:T(8,128)}, f32[8,2,512]{2,1,0:T(2,128)}) custom-call(s32[4]{0:T(128)} %pad_add_fusion.place, bf16[8,512,256]{2,1,0:T(8,128)(2,1)} %bitcast.39, bf16[8,8,32,256]{3,2,1,0:T(8,128)(2,1)} %copy-done.6, bf16[512,256]{1,0:T(8,128)(2,1)} %constant_dynamic-slice_fusion.x_ref, f32[1,2048]{1,0:T(1,128)} %bitcast.44, f32[1,2048]{1,0:T(1,128)} %bitcast.47), custom_call_target="tpu_custom_call" | custom-call | flops 550000000 | bytes 4000000 | tf_op jit(solution)/shard_map/project/pallas_call | solution.py:191
  73.6 10.9 %all_to_all.46.stats_ref = f32[8,2,512]{2,1,0:T(2,128)S(1)} all-to-all(f32[8,2,512]{2,1,0:T(2,128)} %get-tuple-element.23), channel_id=1, replica_groups=mesh['dp'=96,'mp'=8] {'mp'}, dimensions={0} | all-to-all | bytes 65536 | tf_op jit(solution)/shard_map/all_to_all | solution.py:440
  84.5 0.7 reward.1
  85.3 1.0 copy-done.2
  86.3 1.9 gradient.1
  88.1 8.0 %collective-permute-start = (bf16[1152,256]{1,0:T(8,128)(2,1)S(1)}, bf16[1152,256]{1,0:T(8,128)(2,1)S(1)}, u32[]{:S(2)}, u32[]{:S(2)}) collective-permute-start(bf16[1152,256]{1,0:T(8,128)(2,1)S(1)} %get-tuple-element.28), channel_id=1, source_target_pairs={{0,8},{8,0},{16,24},{24,16},{32,40},{40,32},{48,56},{56,48},{64,72... | collective-permute-start | bytes 1769480 | tf_op jit(solution)/shard_map/ppermute | solution.py:44
  96.1 13.6 %all-to-all-start.3 = ((f32[96,1,128]{2,1,0:T(1,128)}), f32[96,1,128]{2,1,0:T(1,128)S(1)}, u32[]{:S(2)}, u32[]{:S(2)}) async-start(f32[96,1,128]{2,1,0:T(1,128)} %reward.1), calls=%async_computation.3 | async-start | bytes 98304 | tf_op jit(solution)/shard_map/all_to_all | solution.py:442
  109.8 12.1 %all-to-all-done.3.rewards_ref = f32[96,1,128]{2,1,0:T(1,128)S(1)} async-done(((f32[96,1,128]{2,1,0:T(1,128)}), f32[96,1,128]{2,1,0:T(1,128)S(1)}, u32[]{:S(2)}, u32[]{:S(2)}) %all-to-all-start.3) | async-done | bytes 49184 | tf_op jit(solution)/shard_map/all_to_all | solution.py:442
  121.9 1.1 weigh.1
  123.0 11.4 %all_to_all.47 = bf16[4,288,256]{2,1,0:T(8,128)(2,1)S(1)} all-to-all(bf16[4,288,256]{2,1,0:T(8,128)(2,1)S(1)} %bitcast.43), channel_id=1, replica_groups={{0,192,384,576},{8,200,392,584},{16,208,400,592},{24,216,408,600},{32,2..., dimensions={0} | all-to-all | bytes 1179648 | tf_op jit(solution)/shard_map/all_to_all | solution.py:39
  134.3 0.1 reduce_sum.46
  134.4 8.0 %all_to_all.48 = bf16[4,72,256]{2,1,0:T(8,128)(2,1)S(1)} all-to-all(bf16[4,72,256]{2,1,0:T(8,128)(2,1)S(1)} %bitcast.50), channel_id=1, replica_groups={{0,16,32,48},{64,80,96,112},{128,144,160,176},{8,24,40,56},{72,88,104,1..., dimensions={0} | all-to-all | bytes 294912 | tf_op jit(solution)/shard_map/all_to_all | solution.py:39
  142.4 11.2 %all_to_all.49 = bf16[3,72,256]{2,1,0:T(8,128)(2,1)S(1)} all-to-all(bf16[3,72,256]{2,1,0:T(8,128)(2,1)S(1)} %broadcast_in_dim.46), channel_id=1, replica_groups={{0,64,128},{16,80,144},{32,96,160},{48,112,176},{8,72,136},{24,88,152},..., dimensions={0} | all-to-all | bytes 221184 | tf_op jit(solution)/shard_map/all_to_all | solution.py:39
  153.7 7.9 %all_to_all.50 = bf16[4,72,256]{2,1,0:T(8,128)(2,1)S(1)} all-to-all(bf16[4,72,256]{2,1,0:T(8,128)(2,1)S(1)} %broadcast_in_dim.47), channel_id=1, replica_groups={{0,16,32,48},{64,80,96,112},{128,144,160,176},{8,24,40,56},{72,88,104,1..., dimensions={0} | all-to-all | bytes 294912 | tf_op jit(solution)/shard_map/all_to_all | solution.py:39
  161.6 9.7 %all_to_all.51 = bf16[4,288,256]{2,1,0:T(8,128)(2,1)S(1)} all-to-all(bf16[4,288,256]{2,1,0:T(8,128)(2,1)S(1)} %broadcast_in_dim.49), channel_id=1, replica_groups={{0,192,384,576},{8,200,392,584},{16,208,400,592},{24,216,408,600},{32,2..., dimensions={0} | all-to-all | bytes 1179648 | tf_op jit(solution)/shard_map/all_to_all | solution.py:39
  171.2 9.2 %collective-permute-start.1 = (bf16[1152,256]{1,0:T(8,128)(2,1)S(1)}, bf16[1152,256]{1,0:T(8,128)(2,1)S(1)}, u32[]{:S(2)}, u32[]{:S(2)}) collective-permute-start(bf16[1152,256]{1,0:T(8,128)(2,1)S(1)} %bitcast.41), channel_id=1, source_target_pairs={{0,8},{8,0},{16,24},{24,16},{32,40},{40,32},{48,56},{56,48},{64,72... | collective-permute-start | bytes 1769480 | tf_op jit(solution)/shard_map/ppermute | solution.py:44
  180.4 0.1 slice.6
  180.6 0.6 fusion
  181.2 0.5 slice_bitcast_fusion
  181.7 0.3 collective-permute-done.1.other_ref
  182.0 2.0 %finish.1 = (f32[2048,256]{1,0:T(8,128)}, f32[1,256]{1,0:T(1,128)}, f32[1,256]{1,0:T(1,128)}) custom-call(s32[4]{0:T(128)S(1)} %copy-done.5, bf16[1152,256]{1,0:T(8,128)(2,1)S(1)} %bitcast.42, bf16[1152,256]{1,0:T(8,128)(2,1)S(1)} %collective-permute-done.1.other_ref, f32[1,2048]{1,0:T(1,128)S(1)} %bitcast.46, f32[1,2048]{1,0:T(1,128)S(1)} %bitcast.49), custom_call_target="tpu_custom_call" | custom-call | flops 1000000 | bytes 4000000 | tf_op jit(solution)/shard_map/finish/pallas_call | solution.py:387
  (24 shorter events, 0.2 us)
Async XLA Ops:
  7.2 9.1 %copy-start = (bf16[256,2048]{1,0:T(8,128)(2,1)S(1)}, bf16[256,2048]{1,0:T(8,128)(2,1)}, u32[]{:S(2)}) copy-start(bf16[256,2048]{1,0:T(8,128)(2,1)} %param.18) | copy-start | bytes 3145732
  7.2 59.5 %all-gather.3.cloned.1.call-start = ((), (), s32[]{:S(2)}) async-start(), calls=%async_computation.9 | async-start | bytes 2359296 | tf_op jit(solution)/shard_map/all_gather | solution.py:430
  32.9 25.2 %all-to-all-start.1 = ((bf16[8,8,32,256]{3,2,1,0:T(8,128)(2,1)}), bf16[8,8,32,256]{3,2,1,0:T(8,128)(2,1)S(1)}, u32[]{:S(2)}, u32[]{:S(2)}) async-start(bf16[8,8,32,256]{3,2,1,0:T(8,128)(2,1)} %broadcast_in_dim.19), calls=%async_computation.1 | async-start | bytes 2097152 | tf_op jit(solution)/shard_map/all_to_all | solution.py:39
  42.9 42.3 %copy-start.3 = (f32[2048]{0:T(1024)S(1)}, f32[2048]{0:T(1024)}, u32[]{:S(2)}) copy-start(f32[2048]{0:T(1024)} %param.19) | copy-start | bytes 24580
  42.9 42.3 %copy-start.4 = (f32[2048]{0:T(1024)S(1)}, f32[2048]{0:T(1024)}, u32[]{:S(2)}) copy-start(f32[2048]{0:T(1024)} %param.20) | copy-start | bytes 24580
  43.5 41.7 %copy-start.5 = (s32[4]{0:T(128)S(1)}, s32[4]{0:T(128)}, u32[]{:S(2)}) copy-start(s32[4]{0:T(128)} %pad_add_fusion.place) | copy-start | bytes 52
  58.1 8.6 %copy-start.6 = (bf16[8,8,32,256]{3,2,1,0:T(8,128)(2,1)}, bf16[8,8,32,256]{3,2,1,0:T(8,128)(2,1)S(1)}, u32[]{:S(2)}) copy-start(bf16[8,8,32,256]{3,2,1,0:T(8,128)(2,1)S(1)} %all-to-all-done.1.w_hbm) | copy-start | bytes 3145732
  66.6 18.6 %copy-start.1 = (bf16[4096,256]{1,0:T(8,128)(2,1)S(1)}, bf16[4096,256]{1,0:T(8,128)(2,1)}, u32[]{:S(2)}) copy-start(bf16[4096,256]{1,0:T(8,128)(2,1)} %all-gather.3.cloned.1.call-done) | copy-start | bytes 6291460
  73.6 36.2 %copy-start.7 = (s32[96]{0:T(128)S(1)}, s32[96]{0:T(128)}, u32[]{:S(2)}) copy-start(s32[96]{0:T(128)} %param.13) | copy-start | bytes 1156
  85.2 1.0 copy-start.2
  88.1 33.7 %collective-permute-start = (bf16[1152,256]{1,0:T(8,128)(2,1)S(1)}, bf16[1152,256]{1,0:T(8,128)(2,1)S(1)}, u32[]{:S(2)}, u32[]{:S(2)}) collective-permute-start(bf16[1152,256]{1,0:T(8,128)(2,1)S(1)} %get-tuple-element.28), channel_id=1, source_target_pairs={{0,8},{8,0},{16,24},{24,16},{32,40},{40,32},{48,56},{56,48},{64,72... | collective-permute-start | bytes 1769480 | tf_op jit(solution)/shard_map/ppermute | solution.py:44
  96.1 25.7 %all-to-all-start.3 = ((f32[96,1,128]{2,1,0:T(1,128)}), f32[96,1,128]{2,1,0:T(1,128)S(1)}, u32[]{:S(2)}, u32[]{:S(2)}) async-start(f32[96,1,128]{2,1,0:T(1,128)} %reward.1), calls=%async_computation.3 | async-start | bytes 98304 | tf_op jit(solution)/shard_map/all_to_all | solution.py:442
  171.2 10.8 %collective-permute-start.1 = (bf16[1152,256]{1,0:T(8,128)(2,1)S(1)}, bf16[1152,256]{1,0:T(8,128)(2,1)S(1)}, u32[]{:S(2)}, u32[]{:S(2)}) collective-permute-start(bf16[1152,256]{1,0:T(8,128)(2,1)S(1)} %bitcast.41), channel_id=1, source_target_pairs={{0,8},{8,0},{16,24},{24,16},{32,40},{40,32},{48,56},{56,48},{64,72... | collective-permute-start | bytes 1769480 | tf_op jit(solution)/shard_map/ppermute | solution.py:44
Sparse Core Ops, SparseCore 0:
  16.4 50.2 all-gather.2

commit v7 on v6

--- a/solution.py
+++ b/solution.py
@@ -13,7 +13,6 @@
 HEAD_SIZE = 64
 NX, NZ, NCORE = 4, 12, 2
 NEAR = NX * NCORE
-ZB = 4
 
 EPS = 1e-05
 THETA = 500000.0
@@ -28,11 +27,9 @@
 
 def dp_groups():
     along_x = [[device_of(x, z, c) for x in range(NX)] for z in range(NZ) for c in range(NCORE)]
-    columns = [(x, c) for x in range(NX) for c in range(NCORE)]
-    close_z = [[device_of(x, b * ZB + z, c) for z in range(ZB)] for x, c in columns for b in range(NZ // ZB)]
-    far_z = [[device_of(x, b * ZB + z, c) for b in range(NZ // ZB)] for x, c in columns for z in range(ZB)]
+    along_z = [[device_of(x, z, c) for z in range(NZ)] for x in range(NX) for c in range(NCORE)]
     near = [[device_of(x, z, c) for x in range(NX) for c in range(NCORE)] for z in range(NZ)]
-    return along_x, close_z, far_z, near
+    return along_x, along_z, near
 
 
 def swap(parts, groups):
@@ -160,64 +157,36 @@
     )(lengths, hidden_rows, gain, w_query, key_weight, value_weight, jnp.asarray(freq))
 
 
-def project_kernel(place, mixed_hbm, w_hbm, x_ref, gain_ref, head_ref, resid_ref, stats_ref, mixed_ref, w_ref, sems):
+def project_kernel(mixed_ref, w_ref, x_ref, both_ref, resid_ref, stats_ref):
     groups = mixed_ref.shape[0]
     rows, feat = resid_ref.shape
-    copies = [pltpu.make_async_copy(mixed_hbm.at[g], mixed_ref.at[g], sems.at[g]) for g in range(groups)]
-    weights = pltpu.make_async_copy(w_hbm, w_ref, sems.at[groups])
-    copies[0].start()
-    weights.start()
-    for copy in copies[1:]:
-        copy.start()
-    resid_ref[...] = x_ref[...].astype(F32)
-    weights.wait()
+    resid = x_ref[...].astype(F32)
     for g in range(groups):
-        copies[g].wait()
         weight = w_ref[:, g].reshape(-1, feat)
-        resid_ref[...] += dot(mixed_ref[g], weight, 1, 0).astype(BF16).astype(F32)
-    resid = resid_ref[...]
-    both = gain_ref[...] * head_ref[...]
+        resid = resid + dot(mixed_ref[g], weight, 1, 0).astype(BF16).astype(F32)
+    resid_ref[...] = resid
     squares = dot(jnp.ones((8, feat), F32), resid * resid, 1, 1, lax.Precision.HIGHEST)
-    scores = dot(jnp.broadcast_to(both, (8, feat)), resid, 1, 1, lax.Precision.HIGHEST)
+    scores = dot(jnp.broadcast_to(both_ref[...], (8, feat)), resid, 1, 1, lax.Precision.HIGHEST)
     pair = jnp.concatenate([squares[:1], scores[:1]], axis=0)
     stats_ref[...] = jnp.broadcast_to(pair[None], stats_ref.shape)
 
 
-def project(place, mixed_all, w_parts, x_cols, gain_final, w_head):
+def project(mixed_all, w_parts, x_cols, both):
     n_mp, rows, heads = mixed_all.shape
     feat = w_parts.shape[-1]
-    share = pl.BlockSpec((1, feat), lambda i, s: (0, s[0]))
-    flat = lambda a: pl.BlockSpec(a.shape, lambda i, s: (0,) * len(a.shape))
+    here = pl.BlockSpec(memory_space=pltpu.VMEM)
     return pl.pallas_call(
         project_kernel,
         out_shape=(
             jax.ShapeDtypeStruct((rows, feat), F32),
             jax.ShapeDtypeStruct((n_mp, 2, rows), F32),
         ),
-        grid_spec=pltpu.PrefetchScalarGridSpec(
-            num_scalar_prefetch=1,
-            grid=(1,),
-            in_specs=[
-                pl.BlockSpec(memory_space=pl.ANY),
-                pl.BlockSpec(memory_space=pl.ANY),
-                flat(x_cols),
-                share,
-                share,
-            ],
-            out_specs=(
-                pl.BlockSpec((rows, feat), lambda i, s: (0, 0)),
-                pl.BlockSpec((n_mp, 2, rows), lambda i, s: (0, 0, 0)),
-            ),
-            scratch_shapes=[
-                pltpu.VMEM(mixed_all.shape, BF16),
-                pltpu.VMEM(w_parts.shape, BF16),
-                pltpu.SemaphoreType.DMA((n_mp + 1,)),
-            ],
-        ),
-        compiler_params=pltpu.CompilerParams(vmem_limit_bytes=58 * 2**20),
+        in_specs=[here] * 4,
+        out_specs=(here, here),
+        compiler_params=pltpu.CompilerParams(vmem_limit_bytes=32 * 2**20),
         cost_estimate=pl.CostEstimate(flops=550000000, bytes_accessed=4000000, transcendentals=0),
         name="project",
-    )(place, mixed_all, w_parts, x_cols, gain_final[None], w_head[None])
+    )(mixed_all, w_parts, x_cols, both)
 
 
 def row_terms(stats, used, width):
@@ -254,76 +223,69 @@
     )(lengths, stats)
 
 
-def gradient_kernel(width, place, stats_ref, resid_ref, gain_ref, head_ref, mixed_ref, send_ref, keep_ref, d_ref, p_ref):
-    step = pl.program_id(0)
-    groups, rows, heads = mixed_ref.shape
-    feat = resid_ref.shape[1]
+def gradient_kernel(width, place, stats_ref, resid_ref, both_ref, mixed_hbm, send_ref, keep_ref, d_ref, mixed_ref, sems):
+    rows, feat = resid_ref.shape
+    heads = mixed_ref.shape[2]
+    order = []
+    for which in (1 - place[1], place[1]):
+        for g in range(mixed_ref.shape[0] // NCORE):
+            order.append(which * (mixed_ref.shape[0] // NCORE) + g)
+    copies = [
+        pltpu.make_async_copy(mixed_hbm.at[at], mixed_ref.at[i], sems.at[i]) for i, at in enumerate(order)
+    ]
+    for copy in copies:
+        copy.start()
+    groups = mixed_ref.shape[0] // NCORE
+    used = place[2]
+    scale, score, inside = row_terms(stats_ref, used, width)
+    weight = jnp.where(inside, scale, 0.0) / used.astype(F32)
+    minus = weight * scale * score * (1.0 / width)
+    plus = jnp.broadcast_to(weight, (LANES, rows)).T
+    minus = jnp.broadcast_to(minus, (LANES, rows)).T
+    both = both_ref[...]
+    pooled = []
+    for part in range(feat // LANES):
+        at = slice(part * LANES, (part + 1) * LANES)
+        resid = resid_ref[:, at]
+        d_ref[:, at] = (plus * both[:, at] - minus * resid).astype(BF16)
+        pooled.append(jnp.sum(plus * resid, axis=0, keepdims=True))
+    pooled = jnp.concatenate(pooled, axis=1)
     half = groups * heads
-
-    @pl.when(step == 0)
-    def _():
-        used = place[2]
-        scale, score, inside = row_terms(stats_ref, used, width)
-        weight = jnp.where(inside, scale, 0.0) / used.astype(F32)
-        minus = weight * scale * score * (1.0 / width)
-        plus = jnp.broadcast_to(weight, (LANES, rows)).T
-        minus = jnp.broadcast_to(minus, (LANES, rows)).T
-        both = gain_ref[...] * head_ref[...]
-        for part in range(feat // LANES):
-            at = slice(part * LANES, (part + 1) * LANES)
-            resid = resid_ref[:, at]
-            d_ref[:, at] = (plus * both[:, at] - minus * resid).astype(BF16)
-            pooled = jnp.sum(plus * resid, axis=0, keepdims=True)
-            p_ref[:, at] = jnp.broadcast_to(pooled, (8, LANES))
-
-    def fill(out_ref):
+    extra = send_ref.shape[0] - half
+    first = lax.broadcasted_iota(jnp.int32, (extra, feat), 0) == 0
+    pooled = jnp.where(first, pooled, 0.0).astype(BF16)
+    for part, out_ref in enumerate((send_ref, keep_ref)):
         for g in range(groups):
-            out_ref[g * heads : (g + 1) * heads, :] = dot(mixed_ref[g], d_ref[...], 0, 0).astype(BF16)
-        extra = out_ref.shape[0] - half
-        first = lax.broadcasted_iota(jnp.int32, (extra, feat), 0) == 0
-        out_ref[half:, :] = jnp.where(first, p_ref[:1, :], 0.0).astype(BF16)
-
-    @pl.when(step == 0)
-    def _():
-        fill(send_ref)
-
-    @pl.when(step == 1)
-    def _():
-        fill(keep_ref)
-
-
-def gradient_halves(place, stats, resid, gain_final, w_head, mixed_all, half_ext):
+            copies[part * groups + g].wait()
+            mixed = mixed_ref[part * groups + g]
+            out_ref[g * heads : (g + 1) * heads, :] = dot(mixed, d_ref[...], 0, 0).astype(BF16)
+        out_ref[half:, :] = pooled
+
+
+def gradient_halves(place, stats, resid, both, mixed_all, half_ext, width):
     n_mp, rows, heads = mixed_all.shape
     feat = resid.shape[1]
-    width = gain_final.shape[0]
-    share = pl.BlockSpec((1, feat), lambda i, s: (0, s[0]))
+    here = pl.BlockSpec(memory_space=pltpu.VMEM)
     half = jax.ShapeDtypeStruct((half_ext, feat), BF16)
-    half_spec = pl.BlockSpec((half_ext, feat), lambda i, s: (0, 0))
     return pl.pallas_call(
         functools.partial(gradient_kernel, width),
         out_shape=(half, half),
-        grid_spec=pltpu.PrefetchScalarGridSpec(
-            num_scalar_prefetch=1,
-            grid=(NCORE,),
-            in_specs=[
-                pl.BlockSpec(stats.shape, lambda i, s: (0, 0, 0)),
-                pl.BlockSpec(resid.shape, lambda i, s: (0, 0)),
-                share,
-                share,
-                pl.BlockSpec((n_mp // NCORE, rows, heads), lambda i, s: (i * s[1] + (1 - i) * (1 - s[1]), 0, 0)),
-            ],
-            out_specs=(half_spec, half_spec),
-            scratch_shapes=[pltpu.VMEM((rows, feat), BF16), pltpu.VMEM((8, feat), F32)],
-        ),
-        compiler_params=pltpu.CompilerParams(vmem_limit_bytes=48 * 2**20),
+        in_specs=[pl.BlockSpec(memory_space=pltpu.SMEM)] + [here] * 3 + [pl.BlockSpec(memory_space=pl.ANY)],
+        out_specs=(here, here),
+        scratch_shapes=[
+            pltpu.VMEM((rows, feat), BF16),
+            pltpu.VMEM(mixed_all.shape, BF16),
+            pltpu.SemaphoreType.DMA((n_mp,)),
+        ],
+        compiler_params=pltpu.CompilerParams(vmem_limit_bytes=60 * 2**20),
         cost_estimate=pl.CostEstimate(flops=550000000, bytes_accessed=4000000, transcendentals=0),
         name="gradient",
-    )(place, stats, resid, gain_final[None], w_head[None], mixed_all)
-
-
-def weigh_kernel(place, rewards_ref, order_ref, keep_ref, got_ref, out_ref, margin_ref, row_ref):
-    seqs = rewards_ref.shape[0]
-    rewards = rewards_ref[...].reshape(seqs, LANES)
+    )(place, stats, resid, both, mixed_all)
+
+
+def weigh_kernel(place, costs_ref, order_ref, keep_ref, got_ref, out_ref, margin_ref, row_ref):
+    seqs = costs_ref.shape[0]
+    rewards = -costs_ref[...].reshape(seqs, LANES)
     order = order_ref[...]
     seq = lax.broadcasted_iota(jnp.int32, (seqs, LANES), 0)
     picked = jnp.sum(jnp.where(seq == order, rewards, 0.0), axis=0, keepdims=True)
@@ -342,7 +304,7 @@
     row_ref[...] = jnp.sum(jnp.where(seq == at, rewards, 0.0), axis=0, keepdims=True)
 
 
-def weigh(place, rewards, order, keep, got):
+def weigh(place, costs, order, keep, got):
     flat = lambda a: pl.BlockSpec(a.shape, lambda i, s: (0,) * len(a.shape))
     return pl.pallas_call(
         weigh_kernel,
@@ -354,13 +316,13 @@
         grid_spec=pltpu.PrefetchScalarGridSpec(
             num_scalar_prefetch=1,
             grid=(1,),
-            in_specs=[flat(rewards), flat(order), flat(keep), flat(got)],
+            in_specs=[flat(costs), flat(order), flat(keep), flat(got)],
             out_specs=(flat(keep),) + (pl.BlockSpec((1, LANES), lambda i, s: (0, 0)),) * 2,
         ),
         compiler_params=pltpu.CompilerParams(vmem_limit_bytes=16 * 2**20),
         cost_estimate=pl.CostEstimate(flops=1000000, bytes_accessed=2000000, transcendentals=128),
         name="weigh",
-    )(place, rewards, order, keep, got)
+    )(place, costs, order, keep, got)
 
 
 def finish_kernel(half, place, mine_ref, other_ref, gain_ref, head_ref, grad_ref, ghead_ref, ggain_ref):
@@ -421,12 +383,14 @@
     feat = width // n_mp
     me = lax.axis_index("dp").astype(jnp.int32)
     core = me % NCORE
-    along_x, close_z, far_z, near = dp_groups()
+    along_x, along_z, near = dp_groups()
     place = jnp.stack([lax.axis_index("mp").astype(jnp.int32), core, lengths[0], me])
 
     mixed = front(hidden_rows, lengths, gain_attn, w_query, key_weight, value_weight)
 
-    mixed, w_out, hidden_rows = lax.optimization_barrier((mixed, w_out, hidden_rows))
+    mixed, w_out, hidden_rows, gain_final, w_head = lax.optimization_barrier(
+        (mixed, w_out, hidden_rows, gain_final, w_head)
+    )
     mixed_all = lax.all_gather(mixed, "mp", axis=0, tiled=False)
     piece_rows = w_out.shape[0] // NEAR
     my_near = (me // (NZ * NCORE)) * NCORE + core
@@ -436,29 +400,30 @@
     w_parts = swap(jnp.broadcast_to(w_piece[None], (NEAR,) + w_piece.shape), near)
 
     x_cols = lax.dynamic_slice_in_dim(hidden_rows, place[0] * feat, feat, 1)
-    resid, stats = project(place, mixed_all, w_parts, x_cols, gain_final, w_head)
+    both = lax.dynamic_slice_in_dim(gain_final * w_head, place[0] * feat, feat, 0)[None]
+    resid, stats = project(mixed_all, w_parts, x_cols, both)
     stats = lax.all_to_all(stats, "mp", 0, 0, tiled=True)
     reward, stats = lax.optimization_barrier((reward_of(lengths, stats, width, n_dp), stats))
-    rewards = lax.all_to_all(reward, "dp", 0, 0, tiled=True)
+    costs = -lax.all_to_all(reward, "dp", 0, 0, tiled=True)
+    costs = jnp.maximum(lax.optimization_barrier(costs), jnp.finfo(F32).min)
+    costs = jnp.minimum(lax.optimization_barrier(costs), jnp.finfo(F32).max)
 
     half = width // NCORE
-    piece = -(-(half + 16) // (NX * ZB * 8)) * 8
-    half_ext = piece * NX * ZB
-    send, keep = gradient_halves(place, stats, resid, gain_final, w_head, mixed_all, half_ext)
+    piece = -(-(half + 16) // (NX * NZ * 8)) * 8
+    half_ext = piece * NX * NZ
+    send, keep = gradient_halves(place, stats, resid, both, mixed_all, half_ext, width)
     got = to_sibling(send)
     seqs = pair_order.shape[0]
     order = jnp.pad(pair_order, (0, LANES - seqs), constant_values=-1)[None]
-    summed, margin, reward_row = weigh(place, rewards, order, keep, got)
+    summed, margin, reward_row = weigh(place, costs, order, keep, got)
     loss = jnp.sum(jax.nn.softplus(-margin[0, :seqs:2]))
 
-    got = swap(summed.reshape(NX, ZB * piece, feat), along_x)
+    got = swap(summed.reshape(NX, NZ * piece, feat), along_x)
     summed = jnp.sum(got.astype(F32), axis=0).astype(BF16)
-    got = swap(summed.reshape(ZB, piece, feat), close_z)
-    summed = jnp.sum(got.astype(F32), axis=0).astype(BF16)
-    got = swap(jnp.broadcast_to(summed[None], (NZ // ZB, piece, feat)), far_z)
-    summed = jnp.sum(got.astype(F32), axis=0).astype(BF16)
-    got = swap(jnp.broadcast_to(summed[None], (ZB, piece, feat)), close_z)
-    got = swap(jnp.broadcast_to(got.reshape(1, ZB * piece, feat), (NX, ZB * piece, feat)), along_x)
+    got = swap(summed.reshape(NZ, piece, feat), along_z)
+    mine = jnp.sum(got.astype(F32), axis=0).astype(BF16)
+    got = swap(jnp.broadcast_to(mine[None], (NZ, piece, feat)), along_z)
+    got = swap(jnp.broadcast_to(got.reshape(1, NZ * piece, feat), (NX, NZ * piece, feat)), along_x)
     got = got.reshape(half_ext, feat)
     other = to_sibling(got)
     grad_out_proj, grad_head, grad_gain = finish(place, got, other, gain_final, w_head, half)

time: 192 us -> 189 us (0.984)
  blocking collectives: 74.3 us -> 68.5 us
  starting transfers between devices: 40.9 us -> 43.9 us
    all_to_all x1 -> x0, blocking collectives: 10.9 us -> none  [body(): stats = lax.all_to_all(stats, 'mp', 0, 0, tiled=True)]
    all_to_all x1 -> x2, starting transfers between devices: 13.6 us -> 23.7 us  [the longest x1 19.5 us: body(): costs = -lax.all_to_all(reward, 'dp', 0, 0, tiled=True)]
    ppermute x2, starting transfers between devices: 17.1 us -> 10.1 us  [to_sibling(): return lax.ppermute(x, 'dp', pairs)]
    all_to_all x5 -> x4, blocking collectives: 48.1 us -> 53.2 us  [swap(): lax.all_to_all(parts, 'dp', 0, 0, tiled=True, axis_index_groups=groups)]
    pallas_call x1, Pallas kernels: 6.93 us -> 2.26 us  [project(): pl.pallas_call(project_kernel, out_shape=(jax.ShapeDtypeStruct((rows, fea...]
    pallas_call x1, Pallas kernels: 1.86 us -> 5.35 us  [gradient_halves(): pl.pallas_call(functools.partial(gradient_kernel, width), out_shape=(half...]
    unnamed x17 -> x21, local copies, waits for them, and re-layouts: 1.09 us -> 3.51 us
    all_to_all x1 -> x2, waiting for transfers between devices: 12.1 us -> 10.5 us  [the longest x1 6.32 us: body(): stats = lax.all_to_all(stats, 'mp', 0, 0, tiled=True)]
  transfers between devices with their start and end apart: 5 -> 6, of which waited for: 4 -> 5; matrix products, arithmetic and copies ran while one was open for 2% -> 2% of each run, Pallas kernels for 0% -> 3%
where the time goes in v7:
time: 189 us; the launch traced here: 188 us
  blocking collectives  68.5 us (36%)
  starting transfers between devices  43.9 us (23%)
  waiting for transfers between devices  33.4 us (18%)
  Pallas kernels  19.7 us (10%)
  between operations  15 us (8%)
  local copies, waits for them, and re-layouts  6.32 us (3%)
    all_to_all x4, blocking collectives, swap(): lax.all_to_all(parts, 'dp', 0, 0, tiled=True, axis_index_groups=groups)  53.2 us
    all_to_all x1, starting transfers between devices, body(): costs = -lax.all_to_all(reward, 'dp', 0, 0, tiled=True)  19.5 us
    all_to_all x1, blocking collectives, body(): w_piece = lax.all_to_all(w_piece, 'mp', 0, 0, tiled=True)  15.4 us
    all_to_all x1, waiting for transfers between devices, swap(): lax.all_to_all(parts, 'dp', 0, 0, tiled=True, axis_index_groups=groups)  14.1 us
    ppermute x2, starting transfers between devices, to_sibling(): return lax.ppermute(x, 'dp', pairs)  10.1 us
    all_to_all x1, starting transfers between devices, swap(): lax.all_to_all(parts, 'dp', 0, 0, tiled=True, axis_index_groups=groups)  10.1 us
    all_gather x1, waiting for transfers between devices, body(): mixed_all = lax.all_gather(mixed, 'mp', axis=0, tiled=False)  8.54 us
    pallas_call x1, Pallas kernels, front(): pl.pallas_call(front_kernel, out_shape=jax.ShapeDtypeStruct((rows, w_quer...  8.29 us
  transfers between devices with their start and end apart: 6, of which 5 were waited for; matrix products, arithmetic and copies ran while one was open for 2% of the time, Pallas kernels for 3%

profile of v7, /device:TPU:1, one launch (start us, length us, event | category | flops | bytes accessed | tf_op | source)
XLA Modules:
  0.0 188.4 jit_solution(9292444747194237551)
XLA Ops:
  8.0 8.3 %front.1 = bf16[512,256]{1,0:T(8,128)(2,1)} custom-call(s32[1]{0:T(128)S(6)} %copy.20.lens, bf16[512,2048]{1,0:T(8,128)(2,1)} %x_hbm.1, f32[1,2048]{1,0:T(1,128)} %bitcast.55, bf16[2048,256]{1,0:T(8,128)(2,1)} %wq_hbm.1, bf16[64,2048]{1,0:T(8,128)(2,1)} %bitcast.53, bf16[64,2048]{1,0:T(8,128)(2,1)} %bitcast.54, f32[1,128]{1,0:T(1,128)} %constant.51.clone.freq_ref), custom_call_target="tpu_custom_call" | custom-call | flops 1500000000 | bytes 4000000 | tf_op jit(solution)/shard_map/front/pallas_call | solution.py:136
  16.4 15.4 %all_to_all.40 = bf16[8,32,256]{2,1,0:T(8,128)(2,1)S(1)} all-to-all(bf16[8,32,256]{2,1,0:T(8,128)(2,1)S(1)} %copy.18), channel_id=1, replica_groups=mesh['dp'=96,'mp'=8] {'mp'}, dimensions={0} | all-to-all | bytes 262144 | tf_op jit(solution)/shard_map/all_to_all | solution.py:399
  31.8 1.1 broadcast_in_dim.35
  32.9 10.1 %all-to-all-start.1 = ((bf16[8,8,32,256]{3,2,1,0:T(8,128)(2,1)}), bf16[8,8,32,256]{3,2,1,0:T(8,128)(2,1)S(1)}, u32[]{:S(2)}, u32[]{:S(2)}) async-start(bf16[8,8,32,256]{3,2,1,0:T(8,128)(2,1)} %broadcast_in_dim.35), calls=%async_computation.1 | async-start | bytes 2097152 | tf_op jit(solution)/shard_map/all_to_all | solution.py:36
  43.0 0.1 dynamic-slice_multiply_fusion
  43.1 1.0 constant_dynamic-slice_fusion.x_ref
  44.0 14.1 %all-to-all-done.1.w_ref = bf16[8,8,32,256]{3,2,1,0:T(8,128)(2,1)S(1)} async-done(((bf16[8,8,32,256]{3,2,1,0:T(8,128)(2,1)}), bf16[8,8,32,256]{3,2,1,0:T(8,128)(2,1)S(1)}, u32[]{:S(2)}, u32[]{:S(2)}) %all-to-all-start.1) | async-done | bytes 1048608 | tf_op jit(solution)/shard_map/all_to_all | solution.py:36
  58.1 8.5 %all-gather.3.cloned.1.call-done = bf16[4096,256]{1,0:T(8,128)(2,1)} async-done(((bf16[512,256]{1,0:T(8,128)(2,1)}), bf16[4096,256]{1,0:T(8,128)(2,1)}) %all-gather.3.cloned.1.call-update) | async-done | bytes 2097168 | tf_op jit(solution)/shard_map/all_gather | solution.py:394
  66.7 1.6 copy-done.1
  68.2 2.3 %project.1 = (f32[512,256]{1,0:T(8,128)S(1)}, f32[8,2,512]{2,1,0:T(2,128)}) custom-call(bf16[8,512,256]{2,1,0:T(8,128)(2,1)S(1)} %bitcast.41, bf16[8,8,32,256]{3,2,1,0:T(8,128)(2,1)S(1)} %all-to-all-done.1.w_ref, bf16[512,256]{1,0:T(8,128)(2,1)S(1)} %constant_dynamic-slice_fusion.x_ref, f32[1,256]{1,0:T(1,128)S(1)} %bitcast.47), custom_call_target="tpu_custom_call" | custom-call | flops 550000000 | bytes 4000000 | tf_op jit(solution)/shard_map/project/pallas_call | solution.py:178
  70.5 0.8 copy-done.3
  71.3 4.2 %all-to-all-start.2 = ((f32[8,2,512]{2,1,0:T(2,128)}), f32[8,2,512]{2,1,0:T(2,128)S(1)}, u32[]{:S(2)}, u32[]{:S(2)}) async-start(f32[8,2,512]{2,1,0:T(2,128)} %get-tuple-element.27), calls=%async_computation.2 | async-start | bytes 65536 | tf_op jit(solution)/shard_map/all_to_all | solution.py:405
  75.5 0.6 pad_add_fusion.place
  76.0 6.3 %all-to-all-done.2.stats_ref = f32[8,2,512]{2,1,0:T(2,128)S(1)} async-done(((f32[8,2,512]{2,1,0:T(2,128)}), f32[8,2,512]{2,1,0:T(2,128)S(1)}, u32[]{:S(2)}, u32[]{:S(2)}) %all-to-all-start.2) | async-done | bytes 32800 | tf_op jit(solution)/shard_map/all_to_all | solution.py:405
  82.3 0.7 reward.1
  83.1 19.5 %all-to-all-start.3 = ((f32[96,1,128]{2,1,0:T(1,128)}), f32[96,1,128]{2,1,0:T(1,128)S(1)}, u32[]{:S(2)}, u32[]{:S(2)}) async-start(f32[96,1,128]{2,1,0:T(1,128)} %reward.1), calls=%async_computation.3 | async-start | bytes 98304 | tf_op jit(solution)/shard_map/all_to_all | solution.py:407
  102.6 5.4 %gradient.1 = (bf16[1152,256]{1,0:T(8,128)(2,1)}, bf16[1152,256]{1,0:T(8,128)(2,1)}) custom-call(s32[4]{0:T(128)} %pad_add_fusion.place, f32[8,2,512]{2,1,0:T(2,128)} %copy-done.4, f32[512,256]{1,0:T(8,128)} %copy-done.3, f32[1,256]{1,0:T(1,128)} %bitcast.48, bf16[8,512,256]{2,1,0:T(8,128)(2,1)} %bitcast.40), custom_call_target="tpu_custom_call" | custom-call | flops 550000000 | bytes 4000000 | tf_op jit(solution)/shard_map/gradient/pallas_call | solution.py:270
  108.0 2.6 %collective-permute-start = (bf16[1152,256]{1,0:T(8,128)(2,1)}, bf16[1152,256]{1,0:T(8,128)(2,1)S(1)}, u32[]{:S(2)}, u32[]{:S(2)}) collective-permute-start(bf16[1152,256]{1,0:T(8,128)(2,1)} %get-tuple-element.32), channel_id=1, source_target_pairs={{0,8},{8,0},{16,24},{24,16},{32,40},{40,32},{48,56},{56,48},{64,72... | collective-permute-start | bytes 1769480 | tf_op jit(solution)/shard_map/ppermute | solution.py:41
  110.6 4.2 %all-to-all-done.3 = f32[96,1,128]{2,1,0:T(1,128)S(1)} async-done(((f32[96,1,128]{2,1,0:T(1,128)}), f32[96,1,128]{2,1,0:T(1,128)S(1)}, u32[]{:S(2)}, u32[]{:S(2)}) %all-to-all-start.3) | async-done | bytes 49184 | tf_op jit(solution)/shard_map/all_to_all | solution.py:407
  115.0 1.1 copy-done.2
  116.0 1.1 weigh.1
  117.1 11.4 %all_to_all.41 = bf16[4,288,256]{2,1,0:T(8,128)(2,1)S(1)} all-to-all(bf16[4,288,256]{2,1,0:T(8,128)(2,1)S(1)} %bitcast.44), channel_id=1, replica_groups={{0,192,384,576},{8,200,392,584},{16,208,400,592},{24,216,408,600},{32,2..., dimensions={0} | all-to-all | bytes 1179648 | tf_op jit(solution)/shard_map/all_to_all | solution.py:36
  128.5 0.1 reduce_sum.34
  128.6 19.0 %all_to_all.42 = bf16[12,24,256]{2,1,0:T(8,128)(2,1)S(1)} all-to-all(bf16[12,24,256]{2,1,0:T(8,128)(2,1)S(1)} %bitcast.49), channel_id=1, replica_groups={{0,16,32,48,64,80,96,112,128,144,160,176},{8,24,40,56,72,88,104,120,136..., dimensions={0} | all-to-all | bytes 294912 | tf_op jit(solution)/shard_map/all_to_all | solution.py:36
  147.7 13.1 %all_to_all.43 = bf16[12,24,256]{2,1,0:T(8,128)(2,1)S(1)} all-to-all(bf16[12,24,256]{2,1,0:T(8,128)(2,1)S(1)} %broadcast_in_dim.38), channel_id=1, replica_groups={{0,16,32,48,64,80,96,112,128,144,160,176},{8,24,40,56,72,88,104,120,136..., dimensions={0} | all-to-all | bytes 294912 | tf_op jit(solution)/shard_map/all_to_all | solution.py:36
  160.8 9.7 %all_to_all.44 = bf16[4,288,256]{2,1,0:T(8,128)(2,1)S(1)} all-to-all(bf16[4,288,256]{2,1,0:T(8,128)(2,1)S(1)} %broadcast_in_dim.40), channel_id=1, replica_groups={{0,192,384,576},{8,200,392,584},{16,208,400,592},{24,216,408,600},{32,2..., dimensions={0} | all-to-all | bytes 1179648 | tf_op jit(solution)/shard_map/all_to_all | solution.py:36
  170.5 7.5 %collective-permute-start.1 = (bf16[1152,256]{1,0:T(8,128)(2,1)S(1)}, bf16[1152,256]{1,0:T(8,128)(2,1)S(1)}, u32[]{:S(2)}, u32[]{:S(2)}) collective-permute-start(bf16[1152,256]{1,0:T(8,128)(2,1)S(1)} %bitcast.42), channel_id=1, source_target_pairs={{0,8},{8,0},{16,24},{24,16},{32,40},{40,32},{48,56},{56,48},{64,72... | collective-permute-start | bytes 1769480 | tf_op jit(solution)/shard_map/ppermute | solution.py:41
  178.0 0.1 slice.6
  178.1 0.6 fusion
  178.8 0.5 slice_bitcast_fusion
  179.3 0.3 collective-permute-done.1.other_ref
  179.6 2.0 %finish.1 = (f32[2048,256]{1,0:T(8,128)}, f32[1,256]{1,0:T(1,128)}, f32[1,256]{1,0:T(1,128)}) custom-call(s32[4]{0:T(128)S(1)} %copy-done.8, bf16[1152,256]{1,0:T(8,128)(2,1)S(1)} %bitcast.43, bf16[1152,256]{1,0:T(8,128)(2,1)S(1)} %collective-permute-done.1.other_ref, f32[1,2048]{1,0:T(1,128)S(1)} %bitcast.46, f32[1,2048]{1,0:T(1,128)S(1)} %bitcast.45), custom_call_target="tpu_custom_call" | custom-call | flops 1000000 | bytes 4000000 | tf_op jit(solution)/shard_map/finish/pallas_call | solution.py:349
  (30 shorter events, 0.4 us)
Async XLA Ops:
  7.2 9.2 %copy-start = (bf16[256,2048]{1,0:T(8,128)(2,1)S(1)}, bf16[256,2048]{1,0:T(8,128)(2,1)}, u32[]{:S(2)}) copy-start(bf16[256,2048]{1,0:T(8,128)(2,1)} %param.18) | copy-start | bytes 3145732
  7.2 59.5 %all-gather.3.cloned.1.call-start = ((), (), s32[]{:S(2)}) async-start(), calls=%async_computation.8 | async-start | bytes 2359296 | tf_op jit(solution)/shard_map/all_gather | solution.py:394
  16.4 26.6 %copy-start.5 = (f32[2048]{0:T(1024)S(1)}, f32[2048]{0:T(1024)}, u32[]{:S(2)}) copy-start(f32[2048]{0:T(1024)} %param.20) | copy-start | bytes 24580
  16.4 26.6 %copy-start.6 = (f32[2048]{0:T(1024)S(1)}, f32[2048]{0:T(1024)}, u32[]{:S(2)}) copy-start(f32[2048]{0:T(1024)} %param.19) | copy-start | bytes 24580
  32.9 25.2 %all-to-all-start.1 = ((bf16[8,8,32,256]{3,2,1,0:T(8,128)(2,1)}), bf16[8,8,32,256]{3,2,1,0:T(8,128)(2,1)S(1)}, u32[]{:S(2)}, u32[]{:S(2)}) async-start(bf16[8,8,32,256]{3,2,1,0:T(8,128)(2,1)} %broadcast_in_dim.35), calls=%async_computation.1 | async-start | bytes 2097152 | tf_op jit(solution)/shard_map/all_to_all | solution.py:36
  43.1 59.5 %copy-start.7 = (f32[256]{0:T(256)}, f32[256]{0:T(256)S(1)}, u32[]{:S(2)}) copy-start(f32[256]{0:T(256)S(1)} %dynamic-slice_multiply_fusion) | copy-start | bytes 3076
  66.7 1.6 copy-start.1
  70.5 0.8 copy-start.3
  71.3 39.3 %copy-start.9 = (s32[96]{0:T(128)S(1)}, s32[96]{0:T(128)}, u32[]{:S(2)}) copy-start(s32[96]{0:T(128)} %param.13) | copy-start | bytes 1156
  71.3 11.0 %all-to-all-start.2 = ((f32[8,2,512]{2,1,0:T(2,128)}), f32[8,2,512]{2,1,0:T(2,128)S(1)}, u32[]{:S(2)}, u32[]{:S(2)}) async-start(f32[8,2,512]{2,1,0:T(2,128)} %get-tuple-element.27), calls=%async_computation.2 | async-start | bytes 65536 | tf_op jit(solution)/shard_map/all_to_all | solution.py:405
  76.0 38.9 %copy-start.8 = (s32[4]{0:T(128)S(1)}, s32[4]{0:T(128)}, u32[]{:S(2)}) copy-start(s32[4]{0:T(128)} %pad_add_fusion.place) | copy-start | bytes 52
  82.3 20.3 %copy-start.4 = (f32[8,2,512]{2,1,0:T(2,128)}, f32[8,2,512]{2,1,0:T(2,128)S(1)}, u32[]{:S(2)}) copy-start(f32[8,2,512]{2,1,0:T(2,128)S(1)} %all-to-all-done.2.stats_ref) | copy-start | bytes 98308
  83.1 31.7 %all-to-all-start.3 = ((f32[96,1,128]{2,1,0:T(1,128)}), f32[96,1,128]{2,1,0:T(1,128)S(1)}, u32[]{:S(2)}, u32[]{:S(2)}) async-start(f32[96,1,128]{2,1,0:T(1,128)} %reward.1), calls=%async_computation.3 | async-start | bytes 98304 | tf_op jit(solution)/shard_map/all_to_all | solution.py:407
  108.0 6.9 %collective-permute-start = (bf16[1152,256]{1,0:T(8,128)(2,1)}, bf16[1152,256]{1,0:T(8,128)(2,1)S(1)}, u32[]{:S(2)}, u32[]{:S(2)}) collective-permute-start(bf16[1152,256]{1,0:T(8,128)(2,1)} %get-tuple-element.32), channel_id=1, source_target_pairs={{0,8},{8,0},{16,24},{24,16},{32,40},{40,32},{48,56},{56,48},{64,72... | collective-permute-start | bytes 1769480 | tf_op jit(solution)/shard_map/ppermute | solution.py:41
  115.0 1.1 copy-start.2
  170.5 9.1 %collective-permute-start.1 = (bf16[1152,256]{1,0:T(8,128)(2,1)S(1)}, bf16[1152,256]{1,0:T(8,128)(2,1)S(1)}, u32[]{:S(2)}, u32[]{:S(2)}) collective-permute-start(bf16[1152,256]{1,0:T(8,128)(2,1)S(1)} %bitcast.42), channel_id=1, source_target_pairs={{0,8},{8,0},{16,24},{24,16},{32,40},{40,32},{48,56},{56,48},{64,72... | collective-permute-start | bytes 1769480 | tf_op jit(solution)/shard_map/ppermute | solution.py:41
Sparse Core Ops, SparseCore 0:
  16.4 50.2 all-gather.2

commit v8 on v7

--- a/solution.py
+++ b/solution.py
@@ -12,7 +12,6 @@
 KEY_VALUE_HEADS = 8
 HEAD_SIZE = 64
 NX, NZ, NCORE = 4, 12, 2
-NEAR = NX * NCORE
 
 EPS = 1e-05
 THETA = 500000.0
@@ -28,8 +27,7 @@
 def dp_groups():
     along_x = [[device_of(x, z, c) for x in range(NX)] for z in range(NZ) for c in range(NCORE)]
     along_z = [[device_of(x, z, c) for z in range(NZ)] for x in range(NX) for c in range(NCORE)]
-    near = [[device_of(x, z, c) for x in range(NX) for c in range(NCORE)] for z in range(NZ)]
-    return along_x, along_z, near
+    return along_x, along_z
 
 
 def swap(parts, groups):
@@ -157,13 +155,69 @@
     )(lengths, hidden_rows, gain, w_query, key_weight, value_weight, jnp.asarray(freq))
 
 
-def project_kernel(mixed_ref, w_ref, x_ref, both_ref, resid_ref, stats_ref):
-    groups = mixed_ref.shape[0]
-    rows, feat = resid_ref.shape
+def ring(x):
+    n = lax.axis_size("mp")
+    up = [(i, (i + 1) % n) for i in range(n)]
+    down = [(i, (i - 1) % n) for i in range(n)]
+    parts, below, above = [(0, x)], x, x
+    for step in range(1, n // 2):
+        below, above = lax.ppermute(below, "mp", up), lax.ppermute(above, "mp", down)
+        parts += [(-step, below), (step, above)]
+    half = x.shape[0] // 2
+    first = lax.ppermute(below[:half], "mp", up)
+    second = lax.ppermute(above[half:], "mp", down)
+    return parts + [(n // 2, (first, second))]
+
+
+def flatten(parts):
+    return [p for _, part in parts for p in (part if isinstance(part, tuple) else (part,))]
+
+
+def shard_of(refs, i):
+    if i < len(refs) - 2:
+        return refs[i][...]
+    return jnp.concatenate([refs[-2][...], refs[-1][...]], axis=0)
+
+
+def cut_kernel(place, w_hbm, out_ref, sems):
+    parts, rows, cols = out_ref.shape
+    mine = pl.ds(pl.multiple_of(place[1] * rows, rows), rows)
+    copies = [
+        pltpu.make_async_copy(w_hbm.at[mine, pl.ds(g * cols, cols)], out_ref.at[g], sems.at[g])
+        for g in range(parts)
+    ]
+    for copy in copies:
+        copy.start()
+    for copy in copies:
+        copy.wait()
+
+
+def cut(place, w_out, n_mp):
+    shape = (n_mp, w_out.shape[0] // NCORE, w_out.shape[1] // n_mp)
+    return pl.pallas_call(
+        cut_kernel,
+        out_shape=jax.ShapeDtypeStruct(shape, BF16),
+        in_specs=[pl.BlockSpec(memory_space=pltpu.SMEM), pl.BlockSpec(memory_space=pl.ANY)],
+        out_specs=pl.BlockSpec(memory_space=pltpu.VMEM),
+        scratch_shapes=[pltpu.SemaphoreType.DMA((n_mp,))],
+        compiler_params=pltpu.CompilerParams(vmem_limit_bytes=58 * 2**20),
+        cost_estimate=pl.CostEstimate(flops=0, bytes_accessed=1000000, transcendentals=0),
+        name="cut",
+    )(place, w_out)
+
+
+def project_kernel(distances, place, *refs):
+    count = len(distances) + 1
+    shards = refs[:count]
+    mine_ref, other_ref, x_ref, both_ref, resid_ref, stats_ref, w_ref = refs[count:]
+    groups, half, feat = mine_ref.shape
+    core = place[1]
+    w_ref[:, pl.ds(pl.multiple_of(core * half, half), half), :] = mine_ref[...]
+    w_ref[:, pl.ds(pl.multiple_of((1 - core) * half, half), half), :] = other_ref[...]
     resid = x_ref[...].astype(F32)
-    for g in range(groups):
-        weight = w_ref[:, g].reshape(-1, feat)
-        resid = resid + dot(mixed_ref[g], weight, 1, 0).astype(BF16).astype(F32)
+    for i, distance in enumerate(distances):
+        group = lax.rem(place[0] + (distance + groups), groups)
+        resid = resid + dot(shard_of(shards, i), w_ref[group], 1, 0).astype(BF16).astype(F32)
     resid_ref[...] = resid
     squares = dot(jnp.ones((8, feat), F32), resid * resid, 1, 1, lax.Precision.HIGHEST)
     scores = dot(jnp.broadcast_to(both_ref[...], (8, feat)), resid, 1, 1, lax.Precision.HIGHEST)
@@ -171,22 +225,24 @@
     stats_ref[...] = jnp.broadcast_to(pair[None], stats_ref.shape)
 
 
-def project(mixed_all, w_parts, x_cols, both):
-    n_mp, rows, heads = mixed_all.shape
-    feat = w_parts.shape[-1]
+def project(place, parts, w_mine, w_other, x_cols, both):
+    n_mp, half, feat = w_mine.shape
+    rows = x_cols.shape[0]
+    shards = flatten(parts)
     here = pl.BlockSpec(memory_space=pltpu.VMEM)
     return pl.pallas_call(
-        project_kernel,
+        functools.partial(project_kernel, [d for d, _ in parts]),
         out_shape=(
             jax.ShapeDtypeStruct((rows, feat), F32),
             jax.ShapeDtypeStruct((n_mp, 2, rows), F32),
         ),
-        in_specs=[here] * 4,
+        in_specs=[pl.BlockSpec(memory_space=pltpu.SMEM)] + [here] * (len(shards) + 4),
         out_specs=(here, here),
+        scratch_shapes=[pltpu.VMEM((n_mp, NCORE * half, feat), BF16)],
         compiler_params=pltpu.CompilerParams(vmem_limit_bytes=32 * 2**20),
         cost_estimate=pl.CostEstimate(flops=550000000, bytes_accessed=4000000, transcendentals=0),
         name="project",
-    )(mixed_all, w_parts, x_cols, both)
+    )(place, *shards, w_mine, w_other, x_cols, both)
 
 
 def row_terms(stats, used, width):
@@ -223,19 +279,13 @@
     )(lengths, stats)
 
 
-def gradient_kernel(width, place, stats_ref, resid_ref, both_ref, mixed_hbm, send_ref, keep_ref, d_ref, mixed_ref, sems):
+def gradient_kernel(width, distances, place, stats_ref, resid_ref, both_ref, *refs):
+    count = len(distances) + 1
+    shards = refs[:count]
+    send_ref, keep_ref, d_ref = refs[count:]
     rows, feat = resid_ref.shape
-    heads = mixed_ref.shape[2]
-    order = []
-    for which in (1 - place[1], place[1]):
-        for g in range(mixed_ref.shape[0] // NCORE):
-            order.append(which * (mixed_ref.shape[0] // NCORE) + g)
-    copies = [
-        pltpu.make_async_copy(mixed_hbm.at[at], mixed_ref.at[i], sems.at[i]) for i, at in enumerate(order)
-    ]
-    for copy in copies:
-        copy.start()
-    groups = mixed_ref.shape[0] // NCORE
+    heads = shards[0].shape[1]
+    groups = width // heads
     used = place[2]
     scale, score, inside = row_terms(stats_ref, used, width)
     weight = jnp.where(inside, scale, 0.0) / used.astype(F32)
@@ -250,37 +300,42 @@
         d_ref[:, at] = (plus * both[:, at] - minus * resid).astype(BF16)
         pooled.append(jnp.sum(plus * resid, axis=0, keepdims=True))
     pooled = jnp.concatenate(pooled, axis=1)
-    half = groups * heads
+    half = width // NCORE
     extra = send_ref.shape[0] - half
     first = lax.broadcasted_iota(jnp.int32, (extra, feat), 0) == 0
     pooled = jnp.where(first, pooled, 0.0).astype(BF16)
-    for part, out_ref in enumerate((send_ref, keep_ref)):
-        for g in range(groups):
-            copies[part * groups + g].wait()
-            mixed = mixed_ref[part * groups + g]
-            out_ref[g * heads : (g + 1) * heads, :] = dot(mixed, d_ref[...], 0, 0).astype(BF16)
-        out_ref[half:, :] = pooled
-
-
-def gradient_halves(place, stats, resid, both, mixed_all, half_ext, width):
-    n_mp, rows, heads = mixed_all.shape
-    feat = resid.shape[1]
+    send_ref[half:, :] = pooled
+    keep_ref[half:, :] = pooled
+    for i, distance in enumerate(distances):
+        group = lax.rem(place[0] + (distance + groups), groups)
+        at = pl.ds(pl.multiple_of(lax.rem(group, groups // NCORE) * heads, heads), heads)
+        block = dot(shard_of(shards, i), d_ref[...], 0, 0).astype(BF16)
+        stays = lax.div(group, groups // NCORE) == place[1]
+
+        @pl.when(stays)
+        def _(block=block, at=at):
+            keep_ref[at, :] = block
+
+        @pl.when(jnp.logical_not(stays))
+        def _(block=block, at=at):
+            send_ref[at, :] = block
+
+
+def gradient_halves(place, stats, resid, both, parts, half_ext, width):
+    rows, feat = resid.shape
+    shards = flatten(parts)
     here = pl.BlockSpec(memory_space=pltpu.VMEM)
     half = jax.ShapeDtypeStruct((half_ext, feat), BF16)
     return pl.pallas_call(
-        functools.partial(gradient_kernel, width),
+        functools.partial(gradient_kernel, width, [d for d, _ in parts]),
         out_shape=(half, half),
-        in_specs=[pl.BlockSpec(memory_space=pltpu.SMEM)] + [here] * 3 + [pl.BlockSpec(memory_space=pl.ANY)],
+        in_specs=[pl.BlockSpec(memory_space=pltpu.SMEM)] + [here] * (len(shards) + 3),
         out_specs=(here, here),
-        scratch_shapes=[
-            pltpu.VMEM((rows, feat), BF16),
-            pltpu.VMEM(mixed_all.shape, BF16),
-            pltpu.SemaphoreType.DMA((n_mp,)),
-        ],
-        compiler_params=pltpu.CompilerParams(vmem_limit_bytes=60 * 2**20),
+        scratch_shapes=[pltpu.VMEM((rows, feat), BF16)],
+        compiler_params=pltpu.CompilerParams(vmem_limit_bytes=32 * 2**20),
         cost_estimate=pl.CostEstimate(flops=550000000, bytes_accessed=4000000, transcendentals=0),
         name="gradient",
-    )(place, stats, resid, both, mixed_all)
+    )(place, stats, resid, both, *shards)
 
 
 def weigh_kernel(place, costs_ref, order_ref, keep_ref, got_ref, out_ref, margin_ref, row_ref):
@@ -383,25 +438,20 @@
     feat = width // n_mp
     me = lax.axis_index("dp").astype(jnp.int32)
     core = me % NCORE
-    along_x, along_z, near = dp_groups()
+    along_x, along_z = dp_groups()
     place = jnp.stack([lax.axis_index("mp").astype(jnp.int32), core, lengths[0], me])
 
+    w_mine = lax.all_to_all(cut(place, w_out, n_mp), "mp", 0, 0, tiled=True)
     mixed = front(hidden_rows, lengths, gain_attn, w_query, key_weight, value_weight)
-
-    mixed, w_out, hidden_rows, gain_final, w_head = lax.optimization_barrier(
-        (mixed, w_out, hidden_rows, gain_final, w_head)
+    mixed, w_mine, hidden_rows, gain_final, w_head = lax.optimization_barrier(
+        (mixed, w_mine, hidden_rows, gain_final, w_head)
     )
-    mixed_all = lax.all_gather(mixed, "mp", axis=0, tiled=False)
-    piece_rows = w_out.shape[0] // NEAR
-    my_near = (me // (NZ * NCORE)) * NCORE + core
-    w_piece = lax.dynamic_slice_in_dim(w_out, my_near * piece_rows, piece_rows, 0)
-    w_piece = w_piece.reshape(piece_rows, n_mp, feat).swapaxes(0, 1)
-    w_piece = lax.all_to_all(w_piece, "mp", 0, 0, tiled=True)
-    w_parts = swap(jnp.broadcast_to(w_piece[None], (NEAR,) + w_piece.shape), near)
-
+    w_other = to_sibling(w_mine)
+
+    parts = ring(mixed)
     x_cols = lax.dynamic_slice_in_dim(hidden_rows, place[0] * feat, feat, 1)
     both = lax.dynamic_slice_in_dim(gain_final * w_head, place[0] * feat, feat, 0)[None]
-    resid, stats = project(mixed_all, w_parts, x_cols, both)
+    resid, stats = project(place, parts, w_mine, w_other, x_cols, both)
     stats = lax.all_to_all(stats, "mp", 0, 0, tiled=True)
     reward, stats = lax.optimization_barrier((reward_of(lengths, stats, width, n_dp), stats))
     costs = -lax.all_to_all(reward, "dp", 0, 0, tiled=True)
@@ -411,7 +461,7 @@
     half = width // NCORE
     piece = -(-(half + 16) // (NX * NZ * 8)) * 8
     half_ext = piece * NX * NZ
-    send, keep = gradient_halves(place, stats, resid, both, mixed_all, half_ext, width)
+    send, keep = gradient_halves(place, stats, resid, both, parts, half_ext, width)
     got = to_sibling(send)
     seqs = pair_order.shape[0]
     order = jnp.pad(pair_order, (0, LANES - seqs), constant_values=-1)[None]

time: 189 us -> 187 us (0.989)
  starting transfers between devices: 43.9 us -> 77.2 us
  waiting for transfers between devices: 33.4 us -> 15.7 us
  between operations: 15 us -> 1.65 us
  blocking collectives: 68.5 us -> 64.7 us
    ppermute x0 -> x8, starting transfers between devices: none -> 26.1 us  [the longest x3 13.4 us: ring(): lax.ppermute(above, 'mp', down)]
    all_to_all x2 -> x1, waiting for transfers between devices: 20.4 us -> 3.92 us  [body(): w_mine = lax.all_to_all(cut(place, w_out, n_mp), 'mp', 0, 0, tiled=True)]
    ppermute x2 -> x3, starting transfers between devices: 10.1 us -> 23.9 us  [to_sibling(): return lax.ppermute(x, 'dp', pairs)]
    all_gather x1 -> x0, waiting for transfers between devices: 8.54 us -> none  [body(): mixed_all = lax.all_gather(mixed, 'mp', axis=0, tiled=False)]
    ppermute x0 -> x8, waiting for transfers between devices: none -> 7.84 us  [the longest x3 7.01 us: ring(): lax.ppermute(below, 'mp', up)]
    all_to_all x2 -> x1, starting transfers between devices: 14.2 us -> 7.66 us  [body(): w_mine = lax.all_to_all(cut(place, w_out, n_mp), 'mp', 0, 0, tiled=True)]
    all_to_all x1, blocking collectives: 15.4 us -> 11 us  [body(): stats = lax.all_to_all(stats, 'mp', 0, 0, tiled=True)]
    pallas_call x2 -> x3, Pallas kernels: 7.62 us -> 8.91 us  [the longest x1 4.1 us: gradient_halves(): pl.pallas_call(functools.partial(gradient_kernel, width, [d for d, _ in p...]
  transfers between devices with their start and end apart: 6 -> 13, of which waited for: 5 -> 6; matrix products, arithmetic and copies ran while one was open for 2% -> 1% of each run, Pallas kernels for 3% -> 7%
where the time goes in v8:
time: 187 us; the launch traced here: 186 us
  starting transfers between devices  77.2 us (41%)
  blocking collectives  64.7 us (35%)
  Pallas kernels  21 us (11%)
  waiting for transfers between devices  15.7 us (8%)
  local copies, waits for them, and re-layouts  4.53 us (2%)
    all_to_all x4, blocking collectives, swap(): lax.all_to_all(parts, 'dp', 0, 0, tiled=True, axis_index_groups=groups)  53.7 us
    ppermute x3, starting transfers between devices, to_sibling(): return lax.ppermute(x, 'dp', pairs)  23.9 us
    all_to_all x1, starting transfers between devices, body(): costs = -lax.all_to_all(reward, 'dp', 0, 0, tiled=True)  19.5 us
    ppermute x3, starting transfers between devices, ring(): lax.ppermute(above, 'mp', down)  13.4 us
    all_to_all x1, blocking collectives, body(): stats = lax.all_to_all(stats, 'mp', 0, 0, tiled=True)  11 us
    pallas_call x1, Pallas kernels, front(): pl.pallas_call(front_kernel, out_shape=jax.ShapeDtypeStruct((rows, w_quer...  8.29 us
    all_to_all x1, starting transfers between devices, body(): w_mine = lax.all_to_all(cut(place, w_out, n_mp), 'mp', 0, 0, tiled=True)  7.66 us
    ppermute x3, waiting for transfers between devices, ring(): lax.ppermute(below, 'mp', up)  7.01 us
  transfers between devices with their start and end apart: 13, of which 6 were waited for; matrix products, arithmetic and copies ran while one was open for 1% of the time, Pallas kernels for 7%

profile of v8, /device:TPU:1, one launch (start us, length us, event | category | flops | bytes accessed | tf_op | source)
XLA Modules:
  0.0 186.4 jit_solution(7834344526338843786)
XLA Ops:
  1.9 2.6 %cut.1 = bf16[8,128,256]{2,1,0:T(8,128)(2,1)} custom-call(s32[4]{0:T(128)} %pad_add_fusion.place, bf16[256,2048]{1,0:T(8,128)(2,1)} %w_hbm.1), custom_call_target="tpu_custom_call" | custom-call | bytes 1000000 | tf_op jit(solution)/shard_map/cut/pallas_call | solution.py:197
  4.5 7.7 %all-to-all-start = ((bf16[8,128,256]{2,1,0:T(8,128)(2,1)}), bf16[8,128,256]{2,1,0:T(8,128)(2,1)S(1)}, u32[]{:S(2)}, u32[]{:S(2)}) async-start(bf16[8,128,256]{2,1,0:T(8,128)(2,1)} %cut.1), calls=%async_computation | async-start | bytes 1048576 | tf_op jit(solution)/shard_map/all_to_all | solution.py:444
  12.2 8.3 %front.1.refs_0_ = bf16[512,256]{1,0:T(8,128)(2,1)} custom-call(s32[1]{0:T(128)S(6)} %copy.16.lens, bf16[512,2048]{1,0:T(8,128)(2,1)} %x_hbm.1, f32[1,2048]{1,0:T(1,128)} %bitcast.46, bf16[2048,256]{1,0:T(8,128)(2,1)} %wq_hbm.1, bf16[64,2048]{1,0:T(8,128)(2,1)} %bitcast.44, bf16[64,2048]{1,0:T(8,128)(2,1)} %bitcast.45, f32[1,128]{1,0:T(1,128)} %constant.41.clone.freq_ref), custom_call_target="tpu_custom_call" | custom-call | flops 1500000000 | bytes 4000000 | tf_op jit(solution)/shard_map/front/pallas_call | solution.py:134
  20.5 3.9 %all-to-all-done.refs_9_ = bf16[8,128,256]{2,1,0:T(8,128)(2,1)S(1)} async-done(((bf16[8,128,256]{2,1,0:T(8,128)(2,1)}), bf16[8,128,256]{2,1,0:T(8,128)(2,1)S(1)}, u32[]{:S(2)}, u32[]{:S(2)}) %all-to-all-start) | async-done | bytes 524320 | tf_op jit(solution)/shard_map/all_to_all | solution.py:444
  24.4 2.2 %collective-permute-start = (bf16[512,256]{1,0:T(8,128)(2,1)}, bf16[512,256]{1,0:T(8,128)(2,1)S(1)}, u32[]{:S(2)}, u32[]{:S(2)}) collective-permute-start(bf16[512,256]{1,0:T(8,128)(2,1)} %front.1.refs_0_), channel_id=1, source_target_pairs={{0,1},{1,2},{2,3},{3,4},{4,5},{5,6},{6,7},{7,0},{8,9},{9,10},{10,1... | collective-permute-start | bytes 786440 | tf_op jit(solution)/shard_map/ppermute | solution.py:164
  26.6 4.3 %collective-permute-start.1 = (bf16[512,256]{1,0:T(8,128)(2,1)}, bf16[512,256]{1,0:T(8,128)(2,1)S(1)}, u32[]{:S(2)}, u32[]{:S(2)}) collective-permute-start(bf16[512,256]{1,0:T(8,128)(2,1)} %front.1.refs_0_), channel_id=1, source_target_pairs={{0,7},{1,0},{2,1},{3,2},{4,3},{5,4},{6,5},{7,6},{8,15},{9,8},{10,9... | collective-permute-start | bytes 786440 | tf_op jit(solution)/shard_map/ppermute | solution.py:164
  30.9 2.7 %collective-permute-done.refs_1_ = bf16[512,256]{1,0:T(8,128)(2,1)S(1)} collective-permute-done((bf16[512,256]{1,0:T(8,128)(2,1)}, bf16[512,256]{1,0:T(8,128)(2,1)S(1)}, u32[]{:S(2)}, u32[]{:S(2)}) %collective-permute-start) | collective-permute-done | bytes 262176 | tf_op jit(solution)/shard_map/ppermute | solution.py:164
  33.6 1.9 %collective-permute-start.2 = (bf16[512,256]{1,0:T(8,128)(2,1)S(1)}, bf16[512,256]{1,0:T(8,128)(2,1)S(1)}, u32[]{:S(2)}, u32[]{:S(2)}) collective-permute-start(bf16[512,256]{1,0:T(8,128)(2,1)S(1)} %collective-permute-done.refs_1_), channel_id=1, source_target_pairs={{0,1},{1,2},{2,3},{3,4},{4,5},{5,6},{6,7},{7,0},{8,9},{9,10},{10,1... | collective-permute-start | bytes 786440 | tf_op jit(solution)/shard_map/ppermute | solution.py:164
  35.5 4.6 %collective-permute-start.3 = (bf16[512,256]{1,0:T(8,128)(2,1)S(1)}, bf16[512,256]{1,0:T(8,128)(2,1)S(1)}, u32[]{:S(2)}, u32[]{:S(2)}) collective-permute-start(bf16[512,256]{1,0:T(8,128)(2,1)S(1)} %collective-permute-done.1.refs_2_), channel_id=1, source_target_pairs={{0,7},{1,0},{2,1},{3,2},{4,3},{5,4},{6,5},{7,6},{8,15},{9,8},{10,9... | collective-permute-start | bytes 786440 | tf_op jit(solution)/shard_map/ppermute | solution.py:164
  40.1 13.9 %collective-permute-start.8 = (bf16[8,128,256]{2,1,0:T(8,128)(2,1)S(1)}, bf16[8,128,256]{2,1,0:T(8,128)(2,1)S(1)}, u32[]{:S(2)}, u32[]{:S(2)}) collective-permute-start(bf16[8,128,256]{2,1,0:T(8,128)(2,1)S(1)} %all-to-all-done.refs_9_), channel_id=1, source_target_pairs={{0,8},{8,0},{16,24},{24,16},{32,40},{40,32},{48,56},{56,48},{64,72... | collective-permute-start | bytes 1572872 | tf_op jit(solution)/shard_map/ppermute | solution.py:39
  54.0 1.9 %collective-permute-start.4 = (bf16[512,256]{1,0:T(8,128)(2,1)S(1)}, bf16[512,256]{1,0:T(8,128)(2,1)S(1)}, u32[]{:S(2)}, u32[]{:S(2)}) collective-permute-start(bf16[512,256]{1,0:T(8,128)(2,1)S(1)} %collective-permute-done.2.refs_3_), channel_id=1, source_target_pairs={{0,1},{1,2},{2,3},{3,4},{4,5},{5,6},{6,7},{7,0},{8,9},{9,10},{10,1... | collective-permute-start | bytes 786440 | tf_op jit(solution)/shard_map/ppermute | solution.py:164
  55.9 4.6 %collective-permute-start.5 = (bf16[512,256]{1,0:T(8,128)(2,1)S(1)}, bf16[512,256]{1,0:T(8,128)(2,1)S(1)}, u32[]{:S(2)}, u32[]{:S(2)}) collective-permute-start(bf16[512,256]{1,0:T(8,128)(2,1)S(1)} %collective-permute-done.3.refs_4_), channel_id=1, source_target_pairs={{0,7},{1,0},{2,1},{3,2},{4,3},{5,4},{6,5},{7,6},{8,15},{9,8},{10,9... | collective-permute-start | bytes 786440 | tf_op jit(solution)/shard_map/ppermute | solution.py:164
  60.5 4.3 %collective-permute-done.4.refs_5_ = bf16[512,256]{1,0:T(8,128)(2,1)S(1)} collective-permute-done((bf16[512,256]{1,0:T(8,128)(2,1)S(1)}, bf16[512,256]{1,0:T(8,128)(2,1)S(1)}, u32[]{:S(2)}, u32[]{:S(2)}) %collective-permute-start.4) | collective-permute-done | bytes 262176 | tf_op jit(solution)/shard_map/ppermute | solution.py:164
  64.8 1.9 %collective-permute-start.6 = (bf16[256,256]{1,0:T(8,128)(2,1)S(1)}, bf16[256,256]{1,0:T(8,128)(2,1)S(1)}, u32[]{:S(2)}, u32[]{:S(2)}) collective-permute-start(bf16[256,256]{1,0:T(8,128)(2,1)S(1)} %slice.16), channel_id=1, source_target_pairs={{0,1},{1,2},{2,3},{3,4},{4,5},{5,6},{6,7},{7,0},{8,9},{9,10},{10,1... | collective-permute-start | bytes 393224 | tf_op jit(solution)/shard_map/ppermute | solution.py:167
  66.8 4.7 %collective-permute-start.7 = (bf16[256,256]{1,0:T(8,128)(2,1)S(1)}, bf16[256,256]{1,0:T(8,128)(2,1)S(1)}, u32[]{:S(2)}, u32[]{:S(2)}) collective-permute-start(bf16[256,256]{1,0:T(8,128)(2,1)S(1)} %slice.17), channel_id=1, source_target_pairs={{0,7},{1,0},{2,1},{3,2},{4,3},{5,4},{6,5},{7,6},{8,15},{9,8},{10,9... | collective-permute-start | bytes 393224 | tf_op jit(solution)/shard_map/ppermute | solution.py:168
  71.6 1.0 constant_dynamic-slice_fusion.refs_11_
  73.4 1.0 copy-done
  74.4 2.2 %project.1 = (f32[512,256]{1,0:T(8,128)S(1)}, f32[8,2,512]{2,1,0:T(2,128)S(1)}) custom-call(s32[4]{0:T(128)S(1)} %copy-done.6, bf16[512,256]{1,0:T(8,128)(2,1)S(1)} %copy-done, bf16[512,256]{1,0:T(8,128)(2,1)S(1)} %collective-permute-done.refs_1_, bf16[512,256]{1,0:T(8,128)(2,1)S(1)} %collective-permute-done.1.refs_2_, ...), custom_call_target="tpu_custom_call" | custom-call | flops 550000000 | bytes 4000000 | tf_op jit(solution)/shard_map/project/pallas_call | solution.py:233
  76.7 11.0 %all_to_all.35.stats_ref = f32[8,2,512]{2,1,0:T(2,128)S(1)} all-to-all(f32[8,2,512]{2,1,0:T(2,128)S(1)} %get-tuple-element.27), channel_id=1, replica_groups=mesh['dp'=96,'mp'=8] {'mp'}, dimensions={0} | all-to-all | bytes 65536 | tf_op jit(solution)/shard_map/all_to_all | solution.py:455
  88.5 19.5 %all-to-all-start.2 = ((f32[96,1,128]{2,1,0:T(1,128)}), f32[96,1,128]{2,1,0:T(1,128)S(1)}, u32[]{:S(2)}, u32[]{:S(2)}) async-start(f32[96,1,128]{2,1,0:T(1,128)} %reward.1), calls=%async_computation.2 | async-start | bytes 98304 | tf_op jit(solution)/shard_map/all_to_all | solution.py:457
  108.0 0.9 copy-done.3
  108.9 0.9 copy-done.5
  109.8 4.1 %gradient.1 = (bf16[1152,256]{1,0:T(8,128)(2,1)}, bf16[1152,256]{1,0:T(8,128)(2,1)S(1)}) custom-call(s32[4]{0:T(128)S(1)} %copy-done.6, f32[8,2,512]{2,1,0:T(2,128)S(1)} %all_to_all.35.stats_ref, f32[512,256]{1,0:T(8,128)S(1)} %get-tuple-element.30.resid_ref, f32[1,256]{1,0:T(1,128)S(1)} %bitcast.41, bf16[512,256]{1,0:T(8,128)(2,1)S(1)} %copy-done.1, ...), custom_call_target="tpu_custom_call" | custom-call | flops 550000000 | bytes 4000000 | tf_op jit(solution)/shard_map/gradient/pallas_call | solution.py:329
  113.9 2.6 %collective-permute-start.9 = (bf16[1152,256]{1,0:T(8,128)(2,1)}, bf16[1152,256]{1,0:T(8,128)(2,1)S(1)}, u32[]{:S(2)}, u32[]{:S(2)}) collective-permute-start(bf16[1152,256]{1,0:T(8,128)(2,1)} %get-tuple-element.32), channel_id=1, source_target_pairs={{0,8},{8,0},{16,24},{24,16},{32,40},{40,32},{48,56},{56,48},{64,72... | collective-permute-start | bytes 1769480 | tf_op jit(solution)/shard_map/ppermute | solution.py:39
  116.5 3.6 %all-to-all-done.2 = f32[96,1,128]{2,1,0:T(1,128)S(1)} async-done(((f32[96,1,128]{2,1,0:T(1,128)}), f32[96,1,128]{2,1,0:T(1,128)S(1)}, u32[]{:S(2)}, u32[]{:S(2)}) %all-to-all-start.2) | async-done | bytes 49184 | tf_op jit(solution)/shard_map/all_to_all | solution.py:457
  120.3 1.1 weigh.1
  121.4 11.4 %all_to_all.36 = bf16[4,288,256]{2,1,0:T(8,128)(2,1)S(1)} all-to-all(bf16[4,288,256]{2,1,0:T(8,128)(2,1)S(1)} %bitcast.37), channel_id=1, replica_groups={{0,192,384,576},{8,200,392,584},{16,208,400,592},{24,216,408,600},{32,2..., dimensions={0} | all-to-all | bytes 1179648 | tf_op jit(solution)/shard_map/all_to_all | solution.py:34
  132.9 19.5 %all_to_all.37 = bf16[12,24,256]{2,1,0:T(8,128)(2,1)S(1)} all-to-all(bf16[12,24,256]{2,1,0:T(8,128)(2,1)S(1)} %bitcast.42), channel_id=1, replica_groups={{0,16,32,48,64,80,96,112,128,144,160,176},{8,24,40,56,72,88,104,120,136..., dimensions={0} | all-to-all | bytes 294912 | tf_op jit(solution)/shard_map/all_to_all | solution.py:34
  152.5 13.1 %all_to_all.38 = bf16[12,24,256]{2,1,0:T(8,128)(2,1)S(1)} all-to-all(bf16[12,24,256]{2,1,0:T(8,128)(2,1)S(1)} %broadcast_in_dim.31), channel_id=1, replica_groups={{0,16,32,48,64,80,96,112,128,144,160,176},{8,24,40,56,72,88,104,120,136..., dimensions={0} | all-to-all | bytes 294912 | tf_op jit(solution)/shard_map/all_to_all | solution.py:34
  165.7 9.7 %all_to_all.39 = bf16[4,288,256]{2,1,0:T(8,128)(2,1)S(1)} all-to-all(bf16[4,288,256]{2,1,0:T(8,128)(2,1)S(1)} %broadcast_in_dim.33), channel_id=1, replica_groups={{0,192,384,576},{8,200,392,584},{16,208,400,592},{24,216,408,600},{32,2..., dimensions={0} | all-to-all | bytes 1179648 | tf_op jit(solution)/shard_map/all_to_all | solution.py:34
  175.3 7.5 %collective-permute-start.10 = (bf16[1152,256]{1,0:T(8,128)(2,1)S(1)}, bf16[1152,256]{1,0:T(8,128)(2,1)S(1)}, u32[]{:S(2)}, u32[]{:S(2)}) collective-permute-start(bf16[1152,256]{1,0:T(8,128)(2,1)S(1)} %bitcast.35), channel_id=1, source_target_pairs={{0,8},{8,0},{16,24},{24,16},{32,40},{40,32},{48,56},{56,48},{64,72... | collective-permute-start | bytes 1769480 | tf_op jit(solution)/shard_map/ppermute | solution.py:39
  184.5 2.0 %finish.1 = (f32[2048,256]{1,0:T(8,128)}, f32[1,256]{1,0:T(1,128)}, f32[1,256]{1,0:T(1,128)}) custom-call(s32[4]{0:T(128)S(1)} %copy-done.6, bf16[1152,256]{1,0:T(8,128)(2,1)S(1)} %bitcast.36, bf16[1152,256]{1,0:T(8,128)(2,1)S(1)} %collective-permute-done.10.other_ref, f32[1,2048]{1,0:T(1,128)S(1)} %bitcast.39, f32[1,2048]{1,0:T(1,128)S(1)} %bitcast.38), custom_call_target="tpu_custom_call" | custom-call | flops 1000000 | bytes 4000000 | tf_op jit(solution)/shard_map/finish/pallas_call | solution.py:404
  (42 shorter events, 4.2 us)
Async XLA Ops:
  4.5 19.9 %all-to-all-start = ((bf16[8,128,256]{2,1,0:T(8,128)(2,1)}), bf16[8,128,256]{2,1,0:T(8,128)(2,1)S(1)}, u32[]{:S(2)}, u32[]{:S(2)}) async-start(bf16[8,128,256]{2,1,0:T(8,128)(2,1)} %cut.1), calls=%async_computation | async-start | bytes 1048576 | tf_op jit(solution)/shard_map/all_to_all | solution.py:444
  12.1 59.4 %copy-start.7 = (f32[2048]{0:T(1024)S(1)}, f32[2048]{0:T(1024)}, u32[]{:S(2)}) copy-start(f32[2048]{0:T(1024)} %param.20) | copy-start | bytes 24580
  12.2 59.4 %copy-start.8 = (f32[2048]{0:T(1024)S(1)}, f32[2048]{0:T(1024)}, u32[]{:S(2)}) copy-start(f32[2048]{0:T(1024)} %param.19) | copy-start | bytes 24580
  12.2 61.3 %copy-start.6 = (s32[4]{0:T(128)S(1)}, s32[4]{0:T(128)}, u32[]{:S(2)}) copy-start(s32[4]{0:T(128)} %pad_add_fusion.place) | copy-start | bytes 52
  24.4 9.2 %collective-permute-start = (bf16[512,256]{1,0:T(8,128)(2,1)}, bf16[512,256]{1,0:T(8,128)(2,1)S(1)}, u32[]{:S(2)}, u32[]{:S(2)}) collective-permute-start(bf16[512,256]{1,0:T(8,128)(2,1)} %front.1.refs_0_), channel_id=1, source_target_pairs={{0,1},{1,2},{2,3},{3,4},{4,5},{5,6},{6,7},{7,0},{8,9},{9,10},{10,1... | collective-permute-start | bytes 786440 | tf_op jit(solution)/shard_map/ppermute | solution.py:164
  26.6 8.9 %collective-permute-start.1 = (bf16[512,256]{1,0:T(8,128)(2,1)}, bf16[512,256]{1,0:T(8,128)(2,1)S(1)}, u32[]{:S(2)}, u32[]{:S(2)}) collective-permute-start(bf16[512,256]{1,0:T(8,128)(2,1)} %front.1.refs_0_), channel_id=1, source_target_pairs={{0,7},{1,0},{2,1},{3,2},{4,3},{5,4},{6,5},{7,6},{8,15},{9,8},{10,9... | collective-permute-start | bytes 786440 | tf_op jit(solution)/shard_map/ppermute | solution.py:164
  33.6 20.4 %collective-permute-start.2 = (bf16[512,256]{1,0:T(8,128)(2,1)S(1)}, bf16[512,256]{1,0:T(8,128)(2,1)S(1)}, u32[]{:S(2)}, u32[]{:S(2)}) collective-permute-start(bf16[512,256]{1,0:T(8,128)(2,1)S(1)} %collective-permute-done.refs_1_), channel_id=1, source_target_pairs={{0,1},{1,2},{2,3},{3,4},{4,5},{5,6},{6,7},{7,0},{8,9},{9,10},{10,1... | collective-permute-start | bytes 786440 | tf_op jit(solution)/shard_map/ppermute | solution.py:164
  35.5 20.4 %collective-permute-start.3 = (bf16[512,256]{1,0:T(8,128)(2,1)S(1)}, bf16[512,256]{1,0:T(8,128)(2,1)S(1)}, u32[]{:S(2)}, u32[]{:S(2)}) collective-permute-start(bf16[512,256]{1,0:T(8,128)(2,1)S(1)} %collective-permute-done.1.refs_2_), channel_id=1, source_target_pairs={{0,7},{1,0},{2,1},{3,2},{4,3},{5,4},{6,5},{7,6},{8,15},{9,8},{10,9... | collective-permute-start | bytes 786440 | tf_op jit(solution)/shard_map/ppermute | solution.py:164
  40.1 32.5 %collective-permute-start.8 = (bf16[8,128,256]{2,1,0:T(8,128)(2,1)S(1)}, bf16[8,128,256]{2,1,0:T(8,128)(2,1)S(1)}, u32[]{:S(2)}, u32[]{:S(2)}) collective-permute-start(bf16[8,128,256]{2,1,0:T(8,128)(2,1)S(1)} %all-to-all-done.refs_9_), channel_id=1, source_target_pairs={{0,8},{8,0},{16,24},{24,16},{32,40},{40,32},{48,56},{56,48},{64,72... | collective-permute-start | bytes 1572872 | tf_op jit(solution)/shard_map/ppermute | solution.py:39
  54.0 10.8 %collective-permute-start.4 = (bf16[512,256]{1,0:T(8,128)(2,1)S(1)}, bf16[512,256]{1,0:T(8,128)(2,1)S(1)}, u32[]{:S(2)}, u32[]{:S(2)}) collective-permute-start(bf16[512,256]{1,0:T(8,128)(2,1)S(1)} %collective-permute-done.2.refs_3_), channel_id=1, source_target_pairs={{0,1},{1,2},{2,3},{3,4},{4,5},{5,6},{6,7},{7,0},{8,9},{9,10},{10,1... | collective-permute-start | bytes 786440 | tf_op jit(solution)/shard_map/ppermute | solution.py:164
  55.9 10.8 %collective-permute-start.5 = (bf16[512,256]{1,0:T(8,128)(2,1)S(1)}, bf16[512,256]{1,0:T(8,128)(2,1)S(1)}, u32[]{:S(2)}, u32[]{:S(2)}) collective-permute-start(bf16[512,256]{1,0:T(8,128)(2,1)S(1)} %collective-permute-done.3.refs_4_), channel_id=1, source_target_pairs={{0,7},{1,0},{2,1},{3,2},{4,3},{5,4},{6,5},{7,6},{8,15},{9,8},{10,9... | collective-permute-start | bytes 786440 | tf_op jit(solution)/shard_map/ppermute | solution.py:164
  64.8 7.8 %collective-permute-start.6 = (bf16[256,256]{1,0:T(8,128)(2,1)S(1)}, bf16[256,256]{1,0:T(8,128)(2,1)S(1)}, u32[]{:S(2)}, u32[]{:S(2)}) collective-permute-start(bf16[256,256]{1,0:T(8,128)(2,1)S(1)} %slice.16), channel_id=1, source_target_pairs={{0,1},{1,2},{2,3},{3,4},{4,5},{5,6},{6,7},{7,0},{8,9},{9,10},{10,1... | collective-permute-start | bytes 393224 | tf_op jit(solution)/shard_map/ppermute | solution.py:167
  66.8 41.2 %copy-start.1 = (bf16[512,256]{1,0:T(8,128)(2,1)S(1)}, bf16[512,256]{1,0:T(8,128)(2,1)}, u32[]{:S(2)}) copy-start(bf16[512,256]{1,0:T(8,128)(2,1)} %front.1.refs_0_) | copy-start | bytes 786436
  66.8 6.6 %collective-permute-start.7 = (bf16[256,256]{1,0:T(8,128)(2,1)S(1)}, bf16[256,256]{1,0:T(8,128)(2,1)S(1)}, u32[]{:S(2)}, u32[]{:S(2)}) collective-permute-start(bf16[256,256]{1,0:T(8,128)(2,1)S(1)} %slice.17), channel_id=1, source_target_pairs={{0,7},{1,0},{2,1},{3,2},{4,3},{5,4},{6,5},{7,6},{8,15},{9,8},{10,9... | collective-permute-start | bytes 393224 | tf_op jit(solution)/shard_map/ppermute | solution.py:168
  72.6 4.1 %copy-start.2 = (bf16[256,256]{1,0:T(8,128)(2,1)}, bf16[256,256]{1,0:T(8,128)(2,1)S(1)}, u32[]{:S(2)}) copy-start(bf16[256,256]{1,0:T(8,128)(2,1)S(1)} %collective-permute-done.6.refs_7_) | copy-start | bytes 393220
  73.4 3.3 %copy-start.4 = (bf16[256,256]{1,0:T(8,128)(2,1)}, bf16[256,256]{1,0:T(8,128)(2,1)S(1)}, u32[]{:S(2)}) copy-start(bf16[256,256]{1,0:T(8,128)(2,1)S(1)} %collective-permute-done.7.refs_8_) | copy-start | bytes 393220
  73.4 1.0 copy-start
  76.7 39.8 %copy-start.9 = (s32[96]{0:T(128)S(1)}, s32[96]{0:T(128)}, u32[]{:S(2)}) copy-start(s32[96]{0:T(128)} %param.13) | copy-start | bytes 1156
  88.5 31.7 %all-to-all-start.2 = ((f32[96,1,128]{2,1,0:T(1,128)}), f32[96,1,128]{2,1,0:T(1,128)S(1)}, u32[]{:S(2)}, u32[]{:S(2)}) async-start(f32[96,1,128]{2,1,0:T(1,128)} %reward.1), calls=%async_computation.2 | async-start | bytes 98304 | tf_op jit(solution)/shard_map/all_to_all | solution.py:457
  108.0 0.9 copy-start.3
  108.9 0.9 copy-start.5
  113.9 6.4 %collective-permute-start.9 = (bf16[1152,256]{1,0:T(8,128)(2,1)}, bf16[1152,256]{1,0:T(8,128)(2,1)S(1)}, u32[]{:S(2)}, u32[]{:S(2)}) collective-permute-start(bf16[1152,256]{1,0:T(8,128)(2,1)} %get-tuple-element.32), channel_id=1, source_target_pairs={{0,8},{8,0},{16,24},{24,16},{32,40},{40,32},{48,56},{56,48},{64,72... | collective-permute-start | bytes 1769480 | tf_op jit(solution)/shard_map/ppermute | solution.py:39
  175.3 9.1 %collective-permute-start.10 = (bf16[1152,256]{1,0:T(8,128)(2,1)S(1)}, bf16[1152,256]{1,0:T(8,128)(2,1)S(1)}, u32[]{:S(2)}, u32[]{:S(2)}) collective-permute-start(bf16[1152,256]{1,0:T(8,128)(2,1)S(1)} %bitcast.35), channel_id=1, source_target_pairs={{0,8},{8,0},{16,24},{24,16},{32,40},{40,32},{48,56},{56,48},{64,72... | collective-permute-start | bytes 1769480 | tf_op jit(solution)/shard_map/ppermute | solution.py:39

commit v9 on v8

--- a/solution.py
+++ b/solution.py
@@ -12,6 +12,7 @@
 KEY_VALUE_HEADS = 8
 HEAD_SIZE = 64
 NX, NZ, NCORE = 4, 12, 2
+NEAR = NX * NCORE
 
 EPS = 1e-05
 THETA = 500000.0
@@ -27,7 +28,8 @@
 def dp_groups():
     along_x = [[device_of(x, z, c) for x in range(NX)] for z in range(NZ) for c in range(NCORE)]
     along_z = [[device_of(x, z, c) for z in range(NZ)] for x in range(NX) for c in range(NCORE)]
-    return along_x, along_z
+    near = [[device_of(x, z, c) for x in range(NX) for c in range(NCORE)] for z in range(NZ)]
+    return along_x, along_z, near
 
 
 def swap(parts, groups):
@@ -179,45 +181,16 @@
     return jnp.concatenate([refs[-2][...], refs[-1][...]], axis=0)
 
 
-def cut_kernel(place, w_hbm, out_ref, sems):
-    parts, rows, cols = out_ref.shape
-    mine = pl.ds(pl.multiple_of(place[1] * rows, rows), rows)
-    copies = [
-        pltpu.make_async_copy(w_hbm.at[mine, pl.ds(g * cols, cols)], out_ref.at[g], sems.at[g])
-        for g in range(parts)
-    ]
-    for copy in copies:
-        copy.start()
-    for copy in copies:
-        copy.wait()
-
-
-def cut(place, w_out, n_mp):
-    shape = (n_mp, w_out.shape[0] // NCORE, w_out.shape[1] // n_mp)
-    return pl.pallas_call(
-        cut_kernel,
-        out_shape=jax.ShapeDtypeStruct(shape, BF16),
-        in_specs=[pl.BlockSpec(memory_space=pltpu.SMEM), pl.BlockSpec(memory_space=pl.ANY)],
-        out_specs=pl.BlockSpec(memory_space=pltpu.VMEM),
-        scratch_shapes=[pltpu.SemaphoreType.DMA((n_mp,))],
-        compiler_params=pltpu.CompilerParams(vmem_limit_bytes=58 * 2**20),
-        cost_estimate=pl.CostEstimate(flops=0, bytes_accessed=1000000, transcendentals=0),
-        name="cut",
-    )(place, w_out)
-
-
 def project_kernel(distances, place, *refs):
     count = len(distances) + 1
     shards = refs[:count]
-    mine_ref, other_ref, x_ref, both_ref, resid_ref, stats_ref, w_ref = refs[count:]
-    groups, half, feat = mine_ref.shape
-    core = place[1]
-    w_ref[:, pl.ds(pl.multiple_of(core * half, half), half), :] = mine_ref[...]
-    w_ref[:, pl.ds(pl.multiple_of((1 - core) * half, half), half), :] = other_ref[...]
+    w_ref, x_ref, both_ref, resid_ref, stats_ref = refs[count:]
+    groups, feat = w_ref.shape[1], w_ref.shape[3]
     resid = x_ref[...].astype(F32)
     for i, distance in enumerate(distances):
         group = lax.rem(place[0] + (distance + groups), groups)
-        resid = resid + dot(shard_of(shards, i), w_ref[group], 1, 0).astype(BF16).astype(F32)
+        weight = w_ref[:, pl.ds(group, 1)].reshape(-1, feat)
+        resid = resid + dot(shard_of(shards, i), weight, 1, 0).astype(BF16).astype(F32)
     resid_ref[...] = resid
     squares = dot(jnp.ones((8, feat), F32), resid * resid, 1, 1, lax.Precision.HIGHEST)
     scores = dot(jnp.broadcast_to(both_ref[...], (8, feat)), resid, 1, 1, lax.Precision.HIGHEST)
@@ -225,8 +198,8 @@
     stats_ref[...] = jnp.broadcast_to(pair[None], stats_ref.shape)
 
 
-def project(place, parts, w_mine, w_other, x_cols, both):
-    n_mp, half, feat = w_mine.shape
+def project(place, parts, w_parts, x_cols, both):
+    n_mp, feat = w_parts.shape[1], w_parts.shape[3]
     rows = x_cols.shape[0]
     shards = flatten(parts)
     here = pl.BlockSpec(memory_space=pltpu.VMEM)
@@ -236,13 +209,12 @@
             jax.ShapeDtypeStruct((rows, feat), F32),
             jax.ShapeDtypeStruct((n_mp, 2, rows), F32),
         ),
-        in_specs=[pl.BlockSpec(memory_space=pltpu.SMEM)] + [here] * (len(shards) + 4),
+        in_specs=[pl.BlockSpec(memory_space=pltpu.SMEM)] + [here] * (len(shards) + 3),
         out_specs=(here, here),
-        scratch_shapes=[pltpu.VMEM((n_mp, NCORE * half, feat), BF16)],
         compiler_params=pltpu.CompilerParams(vmem_limit_bytes=32 * 2**20),
         cost_estimate=pl.CostEstimate(flops=550000000, bytes_accessed=4000000, transcendentals=0),
         name="project",
-    )(place, *shards, w_mine, w_other, x_cols, both)
+    )(place, *shards, w_parts, x_cols, both)
 
 
 def row_terms(stats, used, width):
@@ -438,20 +410,24 @@
     feat = width // n_mp
     me = lax.axis_index("dp").astype(jnp.int32)
     core = me % NCORE
-    along_x, along_z = dp_groups()
+    along_x, along_z, near = dp_groups()
     place = jnp.stack([lax.axis_index("mp").astype(jnp.int32), core, lengths[0], me])
 
-    w_mine = lax.all_to_all(cut(place, w_out, n_mp), "mp", 0, 0, tiled=True)
     mixed = front(hidden_rows, lengths, gain_attn, w_query, key_weight, value_weight)
-    mixed, w_mine, hidden_rows, gain_final, w_head = lax.optimization_barrier(
-        (mixed, w_mine, hidden_rows, gain_final, w_head)
+    mixed, w_out, hidden_rows, gain_final, w_head = lax.optimization_barrier(
+        (mixed, w_out, hidden_rows, gain_final, w_head)
     )
-    w_other = to_sibling(w_mine)
+    piece_rows = w_out.shape[0] // NEAR
+    my_near = (me // (NZ * NCORE)) * NCORE + core
+    w_piece = lax.dynamic_slice_in_dim(w_out, my_near * piece_rows, piece_rows, 0)
+    w_piece = w_piece.reshape(piece_rows, n_mp, feat).swapaxes(0, 1)
+    w_piece = lax.all_to_all(w_piece, "mp", 0, 0, tiled=True)
+    w_parts = swap(jnp.broadcast_to(w_piece[None], (NEAR,) + w_piece.shape), near)
 
     parts = ring(mixed)
     x_cols = lax.dynamic_slice_in_dim(hidden_rows, place[0] * feat, feat, 1)
     both = lax.dynamic_slice_in_dim(gain_final * w_head, place[0] * feat, feat, 0)[None]
-    resid, stats = project(place, parts, w_mine, w_other, x_cols, both)
+    resid, stats = project(place, parts, w_parts, x_cols, both)
     stats = lax.all_to_all(stats, "mp", 0, 0, tiled=True)
     reward, stats = lax.optimization_barrier((reward_of(lengths, stats, width, n_dp), stats))
     costs = -lax.all_to_all(reward, "dp", 0, 0, tiled=True)

time: 187 us -> 188 us (level)
  local copies, waits for them, and re-layouts: 4.53 us -> 12.3 us
  waiting for transfers between devices: 15.7 us -> 10.6 us
  starting transfers between devices: 77.2 us -> 72.9 us
  blocking collectives: 64.7 us -> 68.6 us
    ppermute x3 -> x2, starting transfers between devices: 23.9 us -> 10.1 us  [to_sibling(): return lax.ppermute(x, 'dp', pairs)]
    all_to_all x1 -> x2, starting transfers between devices: 7.66 us -> 17.9 us  [the longest x1 10.3 us: swap(): lax.all_to_all(parts, 'dp', 0, 0, tiled=True, axis_index_groups=groups)]
    unnamed x20 -> x33, local copies, waits for them, and re-layouts: 2.84 us -> 8.84 us
    ppermute x3, starting transfers between devices: 6.02 us -> 8.95 us  [ring(): lax.ppermute(below, 'mp', up)]
    ppermute x3, starting transfers between devices: 13.4 us -> 10.6 us  [ring(): lax.ppermute(above, 'mp', down)]
    pallas_call x1 -> x0, Pallas kernels: 2.59 us -> none  [cut(): pl.pallas_call(cut_kernel, out_shape=jax.ShapeDtypeStruct(shape, BF16), i...]
    all_to_all x1 -> x2, waiting for transfers between devices: 3.92 us -> 1.41 us  [the longest x1 1.4 us: body(): w_piece = lax.all_to_all(w_piece, 'mp', 0, 0, tiled=True)]
    all_to_all x1, waiting for transfers between devices: 3.62 us -> 1.16 us  [body(): costs = -lax.all_to_all(reward, 'dp', 0, 0, tiled=True)]
  transfers between devices with their start and end apart: 13 -> 13, of which waited for: 6 -> 7; matrix products, arithmetic and copies ran while one was open for 1% -> 2% of each run, Pallas kernels for 7% -> 2%
where the time goes in v9:
time: 188 us; the launch traced here: 187 us
  starting transfers between devices  72.9 us (39%)
  blocking collectives  68.6 us (36%)
  Pallas kernels  19.2 us (10%)
  local copies, waits for them, and re-layouts  12.3 us (7%)
  waiting for transfers between devices  10.6 us (6%)
    all_to_all x4, blocking collectives, swap(): lax.all_to_all(parts, 'dp', 0, 0, tiled=True, axis_index_groups=groups)  55.7 us
    all_to_all x1, starting transfers between devices, body(): costs = -lax.all_to_all(reward, 'dp', 0, 0, tiled=True)  18.8 us
    all_to_all x1, blocking collectives, body(): stats = lax.all_to_all(stats, 'mp', 0, 0, tiled=True)  12.9 us
    ppermute x3, starting transfers between devices, ring(): lax.ppermute(above, 'mp', down)  10.6 us
    all_to_all x1, starting transfers between devices, swap(): lax.all_to_all(parts, 'dp', 0, 0, tiled=True, axis_index_groups=groups)  10.3 us
    ppermute x2, starting transfers between devices, to_sibling(): return lax.ppermute(x, 'dp', pairs)  10.1 us
    ppermute x3, starting transfers between devices, ring(): lax.ppermute(below, 'mp', up)  8.95 us
    unnamed x33, local copies, waits for them, and re-layouts  8.84 us
  transfers between devices with their start and end apart: 13, of which 7 were waited for; matrix products, arithmetic and copies ran while one was open for 2% of the time, Pallas kernels for 2%

profile of v9, /device:TPU:1, one launch (start us, length us, event | category | flops | bytes accessed | tf_op | source)
XLA Modules:
  0.0 187.1 jit_solution(17672493164561067067)
XLA Ops:
  1.4 8.3 %front.1.refs_0_ = bf16[512,256]{1,0:T(8,128)(2,1)} custom-call(s32[1]{0:T(128)S(6)} %copy.20.lens, bf16[512,2048]{1,0:T(8,128)(2,1)} %x_hbm.1, f32[1,2048]{1,0:T(1,128)} %bitcast.52, bf16[2048,256]{1,0:T(8,128)(2,1)} %wq_hbm.1, bf16[64,2048]{1,0:T(8,128)(2,1)} %bitcast.50, bf16[64,2048]{1,0:T(8,128)(2,1)} %bitcast.51, f32[1,128]{1,0:T(1,128)} %constant.51.clone.freq_ref), custom_call_target="tpu_custom_call" | custom-call | flops 1500000000 | bytes 4000000 | tf_op jit(solution)/shard_map/front/pallas_call | solution.py:136
  10.5 7.6 %all-to-all-start = ((bf16[8,32,256]{2,1,0:T(8,128)(2,1)}), bf16[8,32,256]{2,1,0:T(8,128)(2,1)S(1)}, u32[]{:S(2)}, u32[]{:S(2)}) async-start(bf16[8,32,256]{2,1,0:T(8,128)(2,1)} %copy.18), calls=%async_computation | async-start | bytes 262144 | tf_op jit(solution)/shard_map/all_to_all | solution.py:424
  18.1 3.5 %collective-permute-start = (bf16[512,256]{1,0:T(8,128)(2,1)}, bf16[512,256]{1,0:T(8,128)(2,1)S(1)}, u32[]{:S(2)}, u32[]{:S(2)}) collective-permute-start(bf16[512,256]{1,0:T(8,128)(2,1)} %front.1.refs_0_), channel_id=1, source_target_pairs={{0,1},{1,2},{2,3},{3,4},{4,5},{5,6},{6,7},{7,0},{8,9},{9,10},{10,1... | collective-permute-start | bytes 786440 | tf_op jit(solution)/shard_map/ppermute | solution.py:166
  21.6 3.1 %collective-permute-start.1 = (bf16[512,256]{1,0:T(8,128)(2,1)}, bf16[512,256]{1,0:T(8,128)(2,1)S(1)}, u32[]{:S(2)}, u32[]{:S(2)}) collective-permute-start(bf16[512,256]{1,0:T(8,128)(2,1)} %front.1.refs_0_), channel_id=1, source_target_pairs={{0,7},{1,0},{2,1},{3,2},{4,3},{5,4},{6,5},{7,6},{8,15},{9,8},{10,9... | collective-permute-start | bytes 786440 | tf_op jit(solution)/shard_map/ppermute | solution.py:166
  24.8 1.4 all-to-all-done
  26.2 1.1 broadcast_in_dim.35
  27.3 10.3 %all-to-all-start.1 = ((bf16[8,8,32,256]{3,2,1,0:T(8,128)(2,1)}), bf16[8,8,32,256]{3,2,1,0:T(8,128)(2,1)S(1)}, u32[]{:S(2)}, u32[]{:S(2)}) async-start(bf16[8,8,32,256]{3,2,1,0:T(8,128)(2,1)} %broadcast_in_dim.35), calls=%async_computation.1 | async-start | bytes 2097152 | tf_op jit(solution)/shard_map/all_to_all | solution.py:36
  37.6 3.3 %collective-permute-start.2 = (bf16[512,256]{1,0:T(8,128)(2,1)S(1)}, bf16[512,256]{1,0:T(8,128)(2,1)S(1)}, u32[]{:S(2)}, u32[]{:S(2)}) collective-permute-start(bf16[512,256]{1,0:T(8,128)(2,1)S(1)} %collective-permute-done.refs_1_), channel_id=1, source_target_pairs={{0,1},{1,2},{2,3},{3,4},{4,5},{5,6},{6,7},{7,0},{8,9},{9,10},{10,1... | collective-permute-start | bytes 786440 | tf_op jit(solution)/shard_map/ppermute | solution.py:166
  40.9 3.2 %collective-permute-start.3 = (bf16[512,256]{1,0:T(8,128)(2,1)S(1)}, bf16[512,256]{1,0:T(8,128)(2,1)}, u32[]{:S(2)}, u32[]{:S(2)}) collective-permute-start(bf16[512,256]{1,0:T(8,128)(2,1)S(1)} %collective-permute-done.1.refs_2_), channel_id=1, source_target_pairs={{0,7},{1,0},{2,1},{3,2},{4,3},{5,4},{6,5},{7,6},{8,15},{9,8},{10,9... | collective-permute-start | bytes 786440 | tf_op jit(solution)/shard_map/ppermute | solution.py:166
  44.8 3.7 %collective-permute-done.2.refs_3_ = bf16[512,256]{1,0:T(8,128)(2,1)S(1)} collective-permute-done((bf16[512,256]{1,0:T(8,128)(2,1)S(1)}, bf16[512,256]{1,0:T(8,128)(2,1)S(1)}, u32[]{:S(2)}, u32[]{:S(2)}) %collective-permute-start.2) | collective-permute-done | bytes 262176 | tf_op jit(solution)/shard_map/ppermute | solution.py:166
  48.4 2.2 %collective-permute-start.4 = (bf16[512,256]{1,0:T(8,128)(2,1)S(1)}, bf16[512,256]{1,0:T(8,128)(2,1)S(1)}, u32[]{:S(2)}, u32[]{:S(2)}) collective-permute-start(bf16[512,256]{1,0:T(8,128)(2,1)S(1)} %collective-permute-done.2.refs_3_), channel_id=1, source_target_pairs={{0,1},{1,2},{2,3},{3,4},{4,5},{5,6},{6,7},{7,0},{8,9},{9,10},{10,1... | collective-permute-start | bytes 786440 | tf_op jit(solution)/shard_map/ppermute | solution.py:166
  50.6 4.3 %collective-permute-start.5 = (bf16[512,256]{1,0:T(8,128)(2,1)}, bf16[512,256]{1,0:T(8,128)(2,1)S(1)}, u32[]{:S(2)}, u32[]{:S(2)}) collective-permute-start(bf16[512,256]{1,0:T(8,128)(2,1)} %collective-permute-done.3.refs_4_), channel_id=1, source_target_pairs={{0,7},{1,0},{2,1},{3,2},{4,3},{5,4},{6,5},{7,6},{8,15},{9,8},{10,9... | collective-permute-start | bytes 786440 | tf_op jit(solution)/shard_map/ppermute | solution.py:166
  55.7 2.7 %collective-permute-done.4.refs_5_ = bf16[512,256]{1,0:T(8,128)(2,1)S(1)} collective-permute-done((bf16[512,256]{1,0:T(8,128)(2,1)S(1)}, bf16[512,256]{1,0:T(8,128)(2,1)S(1)}, u32[]{:S(2)}, u32[]{:S(2)}) %collective-permute-start.4) | collective-permute-done | bytes 262176 | tf_op jit(solution)/shard_map/ppermute | solution.py:166
  58.4 1.9 %collective-permute-start.6 = (bf16[256,256]{1,0:T(8,128)(2,1)S(1)}, bf16[256,256]{1,0:T(8,128)(2,1)S(1)}, u32[]{:S(2)}, u32[]{:S(2)}) collective-permute-start(bf16[256,256]{1,0:T(8,128)(2,1)S(1)} %slice.16), channel_id=1, source_target_pairs={{0,1},{1,2},{2,3},{3,4},{4,5},{5,6},{6,7},{7,0},{8,9},{9,10},{10,1... | collective-permute-start | bytes 393224 | tf_op jit(solution)/shard_map/ppermute | solution.py:169
  60.4 4.6 %collective-permute-start.7 = (bf16[256,256]{1,0:T(8,128)(2,1)S(1)}, bf16[256,256]{1,0:T(8,128)(2,1)S(1)}, u32[]{:S(2)}, u32[]{:S(2)}) collective-permute-start(bf16[256,256]{1,0:T(8,128)(2,1)S(1)} %slice.17), channel_id=1, source_target_pairs={{0,7},{1,0},{2,1},{3,2},{4,3},{5,4},{6,5},{7,6},{8,15},{9,8},{10,9... | collective-permute-start | bytes 393224 | tf_op jit(solution)/shard_map/ppermute | solution.py:170
  65.0 1.0 constant_dynamic-slice_fusion.refs_10_
  67.5 0.9 copy-done.3
  68.5 0.9 copy-done.6
  70.3 2.6 %project.1 = (f32[512,256]{1,0:T(8,128)S(1)}, f32[8,2,512]{2,1,0:T(2,128)S(1)}) custom-call(s32[4]{0:T(128)S(1)} %pad_add_fusion.place, bf16[512,256]{1,0:T(8,128)(2,1)S(1)} %copy-done.1, bf16[512,256]{1,0:T(8,128)(2,1)S(1)} %collective-permute-done.refs_1_, bf16[512,256]{1,0:T(8,128)(2,1)S(1)} %copy-done.3, bf16[512,256]{1,0:T(8,128)(2,1)S(1)} %copy-done.6, ...), custom_call_target="tpu_custom_call" | custom-call | flops 550000000 | bytes 4000000 | tf_op jit(solution)/shard_map/project/pallas_call | solution.py:206
  73.8 12.9 %all_to_all.40.stats_ref = f32[8,2,512]{2,1,0:T(2,128)S(1)} all-to-all(f32[8,2,512]{2,1,0:T(2,128)S(1)} %get-tuple-element.27), channel_id=1, replica_groups=mesh['dp'=96,'mp'=8] {'mp'}, dimensions={0} | all-to-all | bytes 65536 | tf_op jit(solution)/shard_map/all_to_all | solution.py:431
  87.4 18.8 %all-to-all-start.3 = ((f32[96,1,128]{2,1,0:T(1,128)}), f32[96,1,128]{2,1,0:T(1,128)S(1)}, u32[]{:S(2)}, u32[]{:S(2)}) async-start(f32[96,1,128]{2,1,0:T(1,128)} %reward.1), calls=%async_computation.3 | async-start | bytes 98304 | tf_op jit(solution)/shard_map/all_to_all | solution.py:433
  108.1 1.0 copy-done.9
  110.0 4.6 %gradient.1 = (bf16[1152,256]{1,0:T(8,128)(2,1)}, bf16[1152,256]{1,0:T(8,128)(2,1)S(1)}) custom-call(s32[4]{0:T(128)S(1)} %pad_add_fusion.place, f32[8,2,512]{2,1,0:T(2,128)S(1)} %all_to_all.40.stats_ref, f32[512,256]{1,0:T(8,128)S(1)} %copy-done.9, f32[1,256]{1,0:T(1,128)S(1)} %bitcast.45, bf16[512,256]{1,0:T(8,128)(2,1)S(1)} %copy-done.1, ...), custom_call_target="tpu_custom_call" | custom-call | flops 550000000 | bytes 4000000 | tf_op jit(solution)/shard_map/gradient/pallas_call | solution.py:301
  114.6 2.6 %collective-permute-start.8 = (bf16[1152,256]{1,0:T(8,128)(2,1)}, bf16[1152,256]{1,0:T(8,128)(2,1)S(1)}, u32[]{:S(2)}, u32[]{:S(2)}) collective-permute-start(bf16[1152,256]{1,0:T(8,128)(2,1)} %get-tuple-element.32), channel_id=1, source_target_pairs={{0,8},{8,0},{16,24},{24,16},{32,40},{40,32},{48,56},{56,48},{64,72... | collective-permute-start | bytes 1769480 | tf_op jit(solution)/shard_map/ppermute | solution.py:41
  117.2 1.2 all-to-all-done.3
  119.0 1.1 weigh.1
  120.1 13.5 %all_to_all.41 = bf16[4,288,256]{2,1,0:T(8,128)(2,1)S(1)} all-to-all(bf16[4,288,256]{2,1,0:T(8,128)(2,1)S(1)} %bitcast.41), channel_id=1, replica_groups={{0,192,384,576},{8,200,392,584},{16,208,400,592},{24,216,408,600},{32,2..., dimensions={0} | all-to-all | bytes 1179648 | tf_op jit(solution)/shard_map/all_to_all | solution.py:36
  133.7 19.4 %all_to_all.42 = bf16[12,24,256]{2,1,0:T(8,128)(2,1)S(1)} all-to-all(bf16[12,24,256]{2,1,0:T(8,128)(2,1)S(1)} %bitcast.46), channel_id=1, replica_groups={{0,16,32,48,64,80,96,112,128,144,160,176},{8,24,40,56,72,88,104,120,136..., dimensions={0} | all-to-all | bytes 294912 | tf_op jit(solution)/shard_map/all_to_all | solution.py:36
  153.2 13.1 %all_to_all.43 = bf16[12,24,256]{2,1,0:T(8,128)(2,1)S(1)} all-to-all(bf16[12,24,256]{2,1,0:T(8,128)(2,1)S(1)} %broadcast_in_dim.38), channel_id=1, replica_groups={{0,16,32,48,64,80,96,112,128,144,160,176},{8,24,40,56,72,88,104,120,136..., dimensions={0} | all-to-all | bytes 294912 | tf_op jit(solution)/shard_map/all_to_all | solution.py:36
  166.3 9.7 %all_to_all.44 = bf16[4,288,256]{2,1,0:T(8,128)(2,1)S(1)} all-to-all(bf16[4,288,256]{2,1,0:T(8,128)(2,1)S(1)} %broadcast_in_dim.40), channel_id=1, replica_groups={{0,192,384,576},{8,200,392,584},{16,208,400,592},{24,216,408,600},{32,2..., dimensions={0} | all-to-all | bytes 1179648 | tf_op jit(solution)/shard_map/all_to_all | solution.py:36
  176.0 7.5 %collective-permute-start.9 = (bf16[1152,256]{1,0:T(8,128)(2,1)S(1)}, bf16[1152,256]{1,0:T(8,128)(2,1)S(1)}, u32[]{:S(2)}, u32[]{:S(2)}) collective-permute-start(bf16[1152,256]{1,0:T(8,128)(2,1)S(1)} %bitcast.39), channel_id=1, source_target_pairs={{0,8},{8,0},{16,24},{24,16},{32,40},{40,32},{48,56},{56,48},{64,72... | collective-permute-start | bytes 1769480 | tf_op jit(solution)/shard_map/ppermute | solution.py:41
  185.1 2.0 %finish.1 = (f32[2048,256]{1,0:T(8,128)}, f32[1,256]{1,0:T(1,128)}, f32[1,256]{1,0:T(1,128)}) custom-call(s32[4]{0:T(128)S(1)} %pad_add_fusion.place, bf16[1152,256]{1,0:T(8,128)(2,1)S(1)} %bitcast.40, bf16[1152,256]{1,0:T(8,128)(2,1)S(1)} %collective-permute-done.9.other_ref, f32[1,2048]{1,0:T(1,128)S(1)} %bitcast.43, f32[1,2048]{1,0:T(1,128)S(1)} %bitcast.42), custom_call_target="tpu_custom_call" | custom-call | flops 1000000 | bytes 4000000 | tf_op jit(solution)/shard_map/finish/pallas_call | solution.py:376
  (57 shorter events, 11.5 us)
Async XLA Ops:
  0.6 9.1 %copy-start = (bf16[256,2048]{1,0:T(8,128)(2,1)S(1)}, bf16[256,2048]{1,0:T(8,128)(2,1)}, u32[]{:S(2)}) copy-start(bf16[256,2048]{1,0:T(8,128)(2,1)} %param.18) | copy-start | bytes 3145732
  9.7 45.2 %copy-start.13 = (f32[2048]{0:T(1024)S(1)}, f32[2048]{0:T(1024)}, u32[]{:S(2)}) copy-start(f32[2048]{0:T(1024)} %param.20) | copy-start | bytes 24580
  10.5 15.7 %all-to-all-start = ((bf16[8,32,256]{2,1,0:T(8,128)(2,1)}), bf16[8,32,256]{2,1,0:T(8,128)(2,1)S(1)}, u32[]{:S(2)}, u32[]{:S(2)}) async-start(bf16[8,32,256]{2,1,0:T(8,128)(2,1)} %copy.18), calls=%async_computation | async-start | bytes 262144 | tf_op jit(solution)/shard_map/all_to_all | solution.py:424
  18.1 49.4 %copy-start.1 = (bf16[512,256]{1,0:T(8,128)(2,1)S(1)}, bf16[512,256]{1,0:T(8,128)(2,1)}, u32[]{:S(2)}) copy-start(bf16[512,256]{1,0:T(8,128)(2,1)} %front.1.refs_0_) | copy-start | bytes 786436
  18.1 19.4 %collective-permute-start = (bf16[512,256]{1,0:T(8,128)(2,1)}, bf16[512,256]{1,0:T(8,128)(2,1)S(1)}, u32[]{:S(2)}, u32[]{:S(2)}) collective-permute-start(bf16[512,256]{1,0:T(8,128)(2,1)} %front.1.refs_0_), channel_id=1, source_target_pairs={{0,1},{1,2},{2,3},{3,4},{4,5},{5,6},{6,7},{7,0},{8,9},{9,10},{10,1... | collective-permute-start | bytes 786440 | tf_op jit(solution)/shard_map/ppermute | solution.py:166
  21.6 19.2 %collective-permute-start.1 = (bf16[512,256]{1,0:T(8,128)(2,1)}, bf16[512,256]{1,0:T(8,128)(2,1)S(1)}, u32[]{:S(2)}, u32[]{:S(2)}) collective-permute-start(bf16[512,256]{1,0:T(8,128)(2,1)} %front.1.refs_0_), channel_id=1, source_target_pairs={{0,7},{1,0},{2,1},{3,2},{4,3},{5,4},{6,5},{7,6},{8,15},{9,8},{10,9... | collective-permute-start | bytes 786440 | tf_op jit(solution)/shard_map/ppermute | solution.py:166
  27.3 40.3 %all-to-all-start.1 = ((bf16[8,8,32,256]{3,2,1,0:T(8,128)(2,1)}), bf16[8,8,32,256]{3,2,1,0:T(8,128)(2,1)S(1)}, u32[]{:S(2)}, u32[]{:S(2)}) async-start(bf16[8,8,32,256]{3,2,1,0:T(8,128)(2,1)} %broadcast_in_dim.35), calls=%async_computation.1 | async-start | bytes 2097152 | tf_op jit(solution)/shard_map/all_to_all | solution.py:36
  37.6 10.9 %collective-permute-start.2 = (bf16[512,256]{1,0:T(8,128)(2,1)S(1)}, bf16[512,256]{1,0:T(8,128)(2,1)S(1)}, u32[]{:S(2)}, u32[]{:S(2)}) collective-permute-start(bf16[512,256]{1,0:T(8,128)(2,1)S(1)} %collective-permute-done.refs_1_), channel_id=1, source_target_pairs={{0,1},{1,2},{2,3},{3,4},{4,5},{5,6},{6,7},{7,0},{8,9},{9,10},{10,1... | collective-permute-start | bytes 786440 | tf_op jit(solution)/shard_map/ppermute | solution.py:166
  40.9 9.8 %collective-permute-start.3 = (bf16[512,256]{1,0:T(8,128)(2,1)S(1)}, bf16[512,256]{1,0:T(8,128)(2,1)}, u32[]{:S(2)}, u32[]{:S(2)}) collective-permute-start(bf16[512,256]{1,0:T(8,128)(2,1)S(1)} %collective-permute-done.1.refs_2_), channel_id=1, source_target_pairs={{0,7},{1,0},{2,1},{3,2},{4,3},{5,4},{6,5},{7,6},{8,15},{9,8},{10,9... | collective-permute-start | bytes 786440 | tf_op jit(solution)/shard_map/ppermute | solution.py:166
  44.1 0.7 copy-start.2
  48.4 16.5 %copy-start.5 = (bf16[512,256]{1,0:T(8,128)(2,1)}, bf16[512,256]{1,0:T(8,128)(2,1)S(1)}, u32[]{:S(2)}) copy-start(bf16[512,256]{1,0:T(8,128)(2,1)S(1)} %collective-permute-done.2.refs_3_) | copy-start | bytes 786436
  48.4 10.0 %collective-permute-start.4 = (bf16[512,256]{1,0:T(8,128)(2,1)S(1)}, bf16[512,256]{1,0:T(8,128)(2,1)S(1)}, u32[]{:S(2)}, u32[]{:S(2)}) collective-permute-start(bf16[512,256]{1,0:T(8,128)(2,1)S(1)} %collective-permute-done.2.refs_3_), channel_id=1, source_target_pairs={{0,1},{1,2},{2,3},{3,4},{4,5},{5,6},{6,7},{7,0},{8,9},{9,10},{10,1... | collective-permute-start | bytes 786440 | tf_op jit(solution)/shard_map/ppermute | solution.py:166
  50.6 9.7 %collective-permute-start.5 = (bf16[512,256]{1,0:T(8,128)(2,1)}, bf16[512,256]{1,0:T(8,128)(2,1)S(1)}, u32[]{:S(2)}, u32[]{:S(2)}) collective-permute-start(bf16[512,256]{1,0:T(8,128)(2,1)} %collective-permute-done.3.refs_4_), channel_id=1, source_target_pairs={{0,7},{1,0},{2,1},{3,2},{4,3},{5,4},{6,5},{7,6},{8,15},{9,8},{10,9... | collective-permute-start | bytes 786440 | tf_op jit(solution)/shard_map/ppermute | solution.py:166
  58.4 7.6 %collective-permute-start.6 = (bf16[256,256]{1,0:T(8,128)(2,1)S(1)}, bf16[256,256]{1,0:T(8,128)(2,1)S(1)}, u32[]{:S(2)}, u32[]{:S(2)}) collective-permute-start(bf16[256,256]{1,0:T(8,128)(2,1)S(1)} %slice.16), channel_id=1, source_target_pairs={{0,1},{1,2},{2,3},{3,4},{4,5},{5,6},{6,7},{7,0},{8,9},{9,10},{10,1... | collective-permute-start | bytes 393224 | tf_op jit(solution)/shard_map/ppermute | solution.py:169
  60.4 6.5 %collective-permute-start.7 = (bf16[256,256]{1,0:T(8,128)(2,1)S(1)}, bf16[256,256]{1,0:T(8,128)(2,1)S(1)}, u32[]{:S(2)}, u32[]{:S(2)}) collective-permute-start(bf16[256,256]{1,0:T(8,128)(2,1)S(1)} %slice.17), channel_id=1, source_target_pairs={{0,7},{1,0},{2,1},{3,2},{4,3},{5,4},{6,5},{7,6},{8,15},{9,8},{10,9... | collective-permute-start | bytes 393224 | tf_op jit(solution)/shard_map/ppermute | solution.py:170
  66.9 0.6 copy-start.10
  67.5 1.0 copy-start.3
  68.5 0.9 copy-start.6
  69.4 0.9 copy-start.11
  72.9 0.8 copy-start.8
  73.8 43.4 %copy-start.15 = (s32[96]{0:T(128)S(1)}, s32[96]{0:T(128)}, u32[]{:S(2)}) copy-start(s32[96]{0:T(128)} %param.13) | copy-start | bytes 1156
  87.4 30.9 %all-to-all-start.3 = ((f32[96,1,128]{2,1,0:T(1,128)}), f32[96,1,128]{2,1,0:T(1,128)S(1)}, u32[]{:S(2)}, u32[]{:S(2)}) async-start(f32[96,1,128]{2,1,0:T(1,128)} %reward.1), calls=%async_computation.3 | async-start | bytes 98304 | tf_op jit(solution)/shard_map/all_to_all | solution.py:433
  106.2 1.0 copy-start.4
  107.1 0.9 copy-start.7
  108.1 1.0 copy-start.9
  109.1 0.9 copy-start.12
  114.6 4.4 %collective-permute-start.8 = (bf16[1152,256]{1,0:T(8,128)(2,1)}, bf16[1152,256]{1,0:T(8,128)(2,1)S(1)}, u32[]{:S(2)}, u32[]{:S(2)}) collective-permute-start(bf16[1152,256]{1,0:T(8,128)(2,1)} %get-tuple-element.32), channel_id=1, source_target_pairs={{0,8},{8,0},{16,24},{24,16},{32,40},{40,32},{48,56},{56,48},{64,72... | collective-permute-start | bytes 1769480 | tf_op jit(solution)/shard_map/ppermute | solution.py:41
  120.1 65.0 %copy-start.14 = (f32[2048]{0:T(1024)S(1)}, f32[2048]{0:T(1024)}, u32[]{:S(2)}) copy-start(f32[2048]{0:T(1024)} %param.19) | copy-start | bytes 24580
  176.0 9.1 %collective-permute-start.9 = (bf16[1152,256]{1,0:T(8,128)(2,1)S(1)}, bf16[1152,256]{1,0:T(8,128)(2,1)S(1)}, u32[]{:S(2)}, u32[]{:S(2)}) collective-permute-start(bf16[1152,256]{1,0:T(8,128)(2,1)S(1)} %bitcast.39), channel_id=1, source_target_pairs={{0,8},{8,0},{16,24},{24,16},{32,40},{40,32},{48,56},{56,48},{64,72... | collective-permute-start | bytes 1769480 | tf_op jit(solution)/shard_map/ppermute | solution.py:41

commit v10 on v9

--- a/solution.py
+++ b/solution.py
@@ -28,8 +28,7 @@
 def dp_groups():
     along_x = [[device_of(x, z, c) for x in range(NX)] for z in range(NZ) for c in range(NCORE)]
     along_z = [[device_of(x, z, c) for z in range(NZ)] for x in range(NX) for c in range(NCORE)]
-    near = [[device_of(x, z, c) for x in range(NX) for c in range(NCORE)] for z in range(NZ)]
-    return along_x, along_z, near
+    return along_x, along_z
 
 
 def swap(parts, groups):
@@ -184,12 +183,16 @@
 def project_kernel(distances, place, *refs):
     count = len(distances) + 1
     shards = refs[:count]
-    w_ref, x_ref, both_ref, resid_ref, stats_ref = refs[count:]
-    groups, feat = w_ref.shape[1], w_ref.shape[3]
+    mine_ref, other_ref, x_ref, both_ref, resid_ref, stats_ref, w_ref = refs[count:]
+    groups, feat = mine_ref.shape[1], mine_ref.shape[3]
+    for x in range(NX):
+        for g in range(groups):
+            w_ref[g, NCORE * x + place[1]] = mine_ref[x, g]
+            w_ref[g, NCORE * x + 1 - place[1]] = other_ref[x, g]
     resid = x_ref[...].astype(F32)
     for i, distance in enumerate(distances):
         group = lax.rem(place[0] + (distance + groups), groups)
-        weight = w_ref[:, pl.ds(group, 1)].reshape(-1, feat)
+        weight = w_ref[group].reshape(-1, feat)
         resid = resid + dot(shard_of(shards, i), weight, 1, 0).astype(BF16).astype(F32)
     resid_ref[...] = resid
     squares = dot(jnp.ones((8, feat), F32), resid * resid, 1, 1, lax.Precision.HIGHEST)
@@ -198,8 +201,8 @@
     stats_ref[...] = jnp.broadcast_to(pair[None], stats_ref.shape)
 
 
-def project(place, parts, w_parts, x_cols, both):
-    n_mp, feat = w_parts.shape[1], w_parts.shape[3]
+def project(place, parts, w_mine, w_other, x_cols, both):
+    _, n_mp, piece_rows, feat = w_mine.shape
     rows = x_cols.shape[0]
     shards = flatten(parts)
     here = pl.BlockSpec(memory_space=pltpu.VMEM)
@@ -209,12 +212,13 @@
             jax.ShapeDtypeStruct((rows, feat), F32),
             jax.ShapeDtypeStruct((n_mp, 2, rows), F32),
         ),
-        in_specs=[pl.BlockSpec(memory_space=pltpu.SMEM)] + [here] * (len(shards) + 3),
+        in_specs=[pl.BlockSpec(memory_space=pltpu.SMEM)] + [here] * (len(shards) + 4),
         out_specs=(here, here),
+        scratch_shapes=[pltpu.VMEM((n_mp, NEAR, piece_rows, feat), BF16)],
         compiler_params=pltpu.CompilerParams(vmem_limit_bytes=32 * 2**20),
         cost_estimate=pl.CostEstimate(flops=550000000, bytes_accessed=4000000, transcendentals=0),
         name="project",
-    )(place, *shards, w_parts, x_cols, both)
+    )(place, *shards, w_mine, w_other, x_cols, both)
 
 
 def row_terms(stats, used, width):
@@ -254,7 +258,7 @@
 def gradient_kernel(width, distances, place, stats_ref, resid_ref, both_ref, *refs):
     count = len(distances) + 1
     shards = refs[:count]
-    send_ref, keep_ref, d_ref = refs[count:]
+    send_ref, keep_ref, d_ref, both_halves = refs[count:]
     rows, feat = resid_ref.shape
     heads = shards[0].shape[1]
     groups = width // heads
@@ -280,17 +284,12 @@
     keep_ref[half:, :] = pooled
     for i, distance in enumerate(distances):
         group = lax.rem(place[0] + (distance + groups), groups)
-        at = pl.ds(pl.multiple_of(lax.rem(group, groups // NCORE) * heads, heads), heads)
+        stays = (lax.div(group, groups // NCORE) == place[1]).astype(jnp.int32)
+        at = stays * half + lax.rem(group, groups // NCORE) * heads
         block = dot(shard_of(shards, i), d_ref[...], 0, 0).astype(BF16)
-        stays = lax.div(group, groups // NCORE) == place[1]
-
-        @pl.when(stays)
-        def _(block=block, at=at):
-            keep_ref[at, :] = block
-
-        @pl.when(jnp.logical_not(stays))
-        def _(block=block, at=at):
-            send_ref[at, :] = block
+        both_halves[pl.ds(pl.multiple_of(at, heads), heads), :] = block
+    send_ref[:half, :] = both_halves[:half, :]
+    keep_ref[:half, :] = both_halves[half:, :]
 
 
 def gradient_halves(place, stats, resid, both, parts, half_ext, width):
@@ -303,7 +302,7 @@
         out_shape=(half, half),
         in_specs=[pl.BlockSpec(memory_space=pltpu.SMEM)] + [here] * (len(shards) + 3),
         out_specs=(here, here),
-        scratch_shapes=[pltpu.VMEM((rows, feat), BF16)],
+        scratch_shapes=[pltpu.VMEM((rows, feat), BF16), pltpu.VMEM((width, feat), BF16)],
         compiler_params=pltpu.CompilerParams(vmem_limit_bytes=32 * 2**20),
         cost_estimate=pl.CostEstimate(flops=550000000, bytes_accessed=4000000, transcendentals=0),
         name="gradient",
@@ -410,7 +409,7 @@
     feat = width // n_mp
     me = lax.axis_index("dp").astype(jnp.int32)
     core = me % NCORE
-    along_x, along_z, near = dp_groups()
+    along_x, along_z = dp_groups()
     place = jnp.stack([lax.axis_index("mp").astype(jnp.int32), core, lengths[0], me])
 
     mixed = front(hidden_rows, lengths, gain_attn, w_query, key_weight, value_weight)
@@ -422,12 +421,13 @@
     w_piece = lax.dynamic_slice_in_dim(w_out, my_near * piece_rows, piece_rows, 0)
     w_piece = w_piece.reshape(piece_rows, n_mp, feat).swapaxes(0, 1)
     w_piece = lax.all_to_all(w_piece, "mp", 0, 0, tiled=True)
-    w_parts = swap(jnp.broadcast_to(w_piece[None], (NEAR,) + w_piece.shape), near)
+    w_mine = swap(jnp.broadcast_to(w_piece[None], (NX,) + w_piece.shape), along_x)
+    w_other = to_sibling(w_mine)
 
     parts = ring(mixed)
     x_cols = lax.dynamic_slice_in_dim(hidden_rows, place[0] * feat, feat, 1)
     both = lax.dynamic_slice_in_dim(gain_final * w_head, place[0] * feat, feat, 0)[None]
-    resid, stats = project(place, parts, w_parts, x_cols, both)
+    resid, stats = project(place, parts, w_mine, w_other, x_cols, both)
     stats = lax.all_to_all(stats, "mp", 0, 0, tiled=True)
     reward, stats = lax.optimization_barrier((reward_of(lengths, stats, width, n_dp), stats))
     costs = -lax.all_to_all(reward, "dp", 0, 0, tiled=True)

time: 188 us -> 182 us (0.968)
  local copies, waits for them, and re-layouts: 12.3 us -> 7.95 us
  blocking collectives: 68.6 us -> 65.2 us
  Pallas kernels: 19.2 us -> 17.3 us
    ppermute x2 -> x3, starting transfers between devices: 10.1 us -> 19.7 us  [to_sibling(): return lax.ppermute(x, 'dp', pairs)]
    all_to_all x1, starting transfers between devices: 10.3 us -> 3.78 us  [swap(): lax.all_to_all(parts, 'dp', 0, 0, tiled=True, axis_index_groups=groups)]
    unnamed x33 -> x23, local copies, waits for them, and re-layouts: 8.84 us -> 4.71 us
    all_to_all x4, blocking collectives: 55.7 us -> 52.4 us  [swap(): lax.all_to_all(parts, 'dp', 0, 0, tiled=True, axis_index_groups=groups)]
    all_to_all x1, waiting for transfers between devices: 1.16 us -> 4.09 us  [body(): costs = -lax.all_to_all(reward, 'dp', 0, 0, tiled=True)]
    ppermute x3, waiting for transfers between devices: 6.32 us -> 3.74 us  [ring(): lax.ppermute(below, 'mp', up)]
    pallas_call x1, Pallas kernels: 4.57 us -> 2.45 us  [gradient_halves(): pl.pallas_call(functools.partial(gradient_kernel, width, [d for d, _ in p...]
  transfers between devices with their start and end apart: 13 -> 14, of which waited for: 7 -> 6; matrix products, arithmetic and copies ran while one was open for 2% -> 3% of each run, Pallas kernels for 2% -> 1%
where the time goes in v10:
time: 182 us; the launch traced here: 180 us
  starting transfers between devices  74.7 us (41%)
  blocking collectives  65.2 us (36%)
  Pallas kernels  17.3 us (10%)
  waiting for transfers between devices  11 us (6%)
  local copies, waits for them, and re-layouts  7.95 us (4%)
  other arithmetic  2.54 us (1%)
    all_to_all x4, blocking collectives, swap(): lax.all_to_all(parts, 'dp', 0, 0, tiled=True, axis_index_groups=groups)  52.4 us
    ppermute x3, starting transfers between devices, to_sibling(): return lax.ppermute(x, 'dp', pairs)  19.7 us
    all_to_all x1, starting transfers between devices, body(): costs = -lax.all_to_all(reward, 'dp', 0, 0, tiled=True)  17.6 us
    all_to_all x1, blocking collectives, body(): stats = lax.all_to_all(stats, 'mp', 0, 0, tiled=True)  12.8 us
    ppermute x3, starting transfers between devices, ring(): lax.ppermute(above, 'mp', down)  10.5 us
    ppermute x3, starting transfers between devices, ring(): lax.ppermute(below, 'mp', up)  8.96 us
    pallas_call x1, Pallas kernels, front(): pl.pallas_call(front_kernel, out_shape=jax.ShapeDtypeStruct((rows, w_quer...  8.27 us
    all_to_all x1, starting transfers between devices, body(): w_piece = lax.all_to_all(w_piece, 'mp', 0, 0, tiled=True)  7.65 us
  transfers between devices with their start and end apart: 14, of which 6 were waited for; matrix products, arithmetic and copies ran while one was open for 3% of the time, Pallas kernels for 1%

profile of v10, /device:TPU:1, one launch (start us, length us, event | category | flops | bytes accessed | tf_op | source)
XLA Modules:
  0.0 180.4 jit_solution(11923229192018188028)
XLA Ops:
  1.4 8.3 %front.1.refs_0_ = bf16[512,256]{1,0:T(8,128)(2,1)} custom-call(s32[1]{0:T(128)S(6)} %copy.20.lens, bf16[512,2048]{1,0:T(8,128)(2,1)} %x_hbm.1, f32[1,2048]{1,0:T(1,128)} %bitcast.52, bf16[2048,256]{1,0:T(8,128)(2,1)} %wq_hbm.1, bf16[64,2048]{1,0:T(8,128)(2,1)} %bitcast.50, bf16[64,2048]{1,0:T(8,128)(2,1)} %bitcast.51, f32[1,128]{1,0:T(1,128)} %constant.51.clone.freq_ref), custom_call_target="tpu_custom_call" | custom-call | flops 1500000000 | bytes 4000000 | tf_op jit(solution)/shard_map/front/pallas_call | solution.py:135
  10.5 7.6 %all-to-all-start = ((bf16[8,32,256]{2,1,0:T(8,128)(2,1)}), bf16[8,32,256]{2,1,0:T(8,128)(2,1)S(1)}, u32[]{:S(2)}, u32[]{:S(2)}) async-start(bf16[8,32,256]{2,1,0:T(8,128)(2,1)} %copy.18), calls=%async_computation | async-start | bytes 262144 | tf_op jit(solution)/shard_map/all_to_all | solution.py:423
  18.1 3.4 %collective-permute-start = (bf16[512,256]{1,0:T(8,128)(2,1)}, bf16[512,256]{1,0:T(8,128)(2,1)S(1)}, u32[]{:S(2)}, u32[]{:S(2)}) collective-permute-start(bf16[512,256]{1,0:T(8,128)(2,1)} %front.1.refs_0_), channel_id=1, source_target_pairs={{0,1},{1,2},{2,3},{3,4},{4,5},{5,6},{6,7},{7,0},{8,9},{9,10},{10,1... | collective-permute-start | bytes 786440 | tf_op jit(solution)/shard_map/ppermute | solution.py:165
  21.5 3.1 %collective-permute-start.1 = (bf16[512,256]{1,0:T(8,128)(2,1)}, bf16[512,256]{1,0:T(8,128)(2,1)S(1)}, u32[]{:S(2)}, u32[]{:S(2)}) collective-permute-start(bf16[512,256]{1,0:T(8,128)(2,1)} %front.1.refs_0_), channel_id=1, source_target_pairs={{0,7},{1,0},{2,1},{3,2},{4,3},{5,4},{6,5},{7,6},{8,15},{9,8},{10,9... | collective-permute-start | bytes 786440 | tf_op jit(solution)/shard_map/ppermute | solution.py:165
  24.6 1.5 all-to-all-done
  27.0 3.8 %all-to-all-start.1 = ((bf16[4,8,32,256]{3,2,1,0:T(8,128)(2,1)}), bf16[4,8,32,256]{3,2,1,0:T(8,128)(2,1)S(1)}, u32[]{:S(2)}, u32[]{:S(2)}) async-start(bf16[4,8,32,256]{3,2,1,0:T(8,128)(2,1)} %broadcast_in_dim.35), calls=%async_computation.1 | async-start | bytes 1048576 | tf_op jit(solution)/shard_map/all_to_all | solution.py:35
  30.8 2.3 %collective-permute-start.2 = (bf16[512,256]{1,0:T(8,128)(2,1)S(1)}, bf16[512,256]{1,0:T(8,128)(2,1)S(1)}, u32[]{:S(2)}, u32[]{:S(2)}) collective-permute-start(bf16[512,256]{1,0:T(8,128)(2,1)S(1)} %collective-permute-done.refs_1_), channel_id=1, source_target_pairs={{0,1},{1,2},{2,3},{3,4},{4,5},{5,6},{6,7},{7,0},{8,9},{9,10},{10,1... | collective-permute-start | bytes 786440 | tf_op jit(solution)/shard_map/ppermute | solution.py:165
  33.1 4.2 %collective-permute-start.3 = (bf16[512,256]{1,0:T(8,128)(2,1)S(1)}, bf16[512,256]{1,0:T(8,128)(2,1)S(1)}, u32[]{:S(2)}, u32[]{:S(2)}) collective-permute-start(bf16[512,256]{1,0:T(8,128)(2,1)S(1)} %collective-permute-done.1.refs_2_), channel_id=1, source_target_pairs={{0,7},{1,0},{2,1},{3,2},{4,3},{5,4},{6,5},{7,6},{8,15},{9,8},{10,9... | collective-permute-start | bytes 786440 | tf_op jit(solution)/shard_map/ppermute | solution.py:165
  37.7 9.6 %collective-permute-start.8 = (bf16[4,8,32,256]{3,2,1,0:T(8,128)(2,1)S(1)}, bf16[4,8,32,256]{3,2,1,0:T(8,128)(2,1)}, u32[]{:S(2)}, u32[]{:S(2)}) collective-permute-start(bf16[4,8,32,256]{3,2,1,0:T(8,128)(2,1)S(1)} %all-to-all-done.1.refs_9_), channel_id=1, source_target_pairs={{0,8},{8,0},{16,24},{24,16},{32,40},{40,32},{48,56},{56,48},{64,72... | collective-permute-start | bytes 1572872 | tf_op jit(solution)/shard_map/ppermute | solution.py:40
  47.3 3.3 %collective-permute-start.4 = (bf16[512,256]{1,0:T(8,128)(2,1)S(1)}, bf16[512,256]{1,0:T(8,128)(2,1)S(1)}, u32[]{:S(2)}, u32[]{:S(2)}) collective-permute-start(bf16[512,256]{1,0:T(8,128)(2,1)S(1)} %collective-permute-done.2.refs_3_), channel_id=1, source_target_pairs={{0,1},{1,2},{2,3},{3,4},{4,5},{5,6},{6,7},{7,0},{8,9},{9,10},{10,1... | collective-permute-start | bytes 786440 | tf_op jit(solution)/shard_map/ppermute | solution.py:165
  50.6 3.2 %collective-permute-start.5 = (bf16[512,256]{1,0:T(8,128)(2,1)S(1)}, bf16[512,256]{1,0:T(8,128)(2,1)S(1)}, u32[]{:S(2)}, u32[]{:S(2)}) collective-permute-start(bf16[512,256]{1,0:T(8,128)(2,1)S(1)} %collective-permute-done.3.refs_4_), channel_id=1, source_target_pairs={{0,7},{1,0},{2,1},{3,2},{4,3},{5,4},{6,5},{7,6},{8,15},{9,8},{10,9... | collective-permute-start | bytes 786440 | tf_op jit(solution)/shard_map/ppermute | solution.py:165
  54.6 3.7 %collective-permute-done.4.refs_5_ = bf16[512,256]{1,0:T(8,128)(2,1)S(1)} collective-permute-done((bf16[512,256]{1,0:T(8,128)(2,1)S(1)}, bf16[512,256]{1,0:T(8,128)(2,1)S(1)}, u32[]{:S(2)}, u32[]{:S(2)}) %collective-permute-start.4) | collective-permute-done | bytes 262176 | tf_op jit(solution)/shard_map/ppermute | solution.py:165
  58.4 2.1 %collective-permute-start.6 = (bf16[256,256]{1,0:T(8,128)(2,1)S(1)}, bf16[256,256]{1,0:T(8,128)(2,1)S(1)}, u32[]{:S(2)}, u32[]{:S(2)}) collective-permute-start(bf16[256,256]{1,0:T(8,128)(2,1)S(1)} %slice.16), channel_id=1, source_target_pairs={{0,1},{1,2},{2,3},{3,4},{4,5},{5,6},{6,7},{7,0},{8,9},{9,10},{10,1... | collective-permute-start | bytes 393224 | tf_op jit(solution)/shard_map/ppermute | solution.py:168
  60.5 4.4 %collective-permute-start.7 = (bf16[256,256]{1,0:T(8,128)(2,1)S(1)}, bf16[256,256]{1,0:T(8,128)(2,1)S(1)}, u32[]{:S(2)}, u32[]{:S(2)}) collective-permute-start(bf16[256,256]{1,0:T(8,128)(2,1)S(1)} %slice.17), channel_id=1, source_target_pairs={{0,7},{1,0},{2,1},{3,2},{4,3},{5,4},{6,5},{7,6},{8,15},{9,8},{10,9... | collective-permute-start | bytes 393224 | tf_op jit(solution)/shard_map/ppermute | solution.py:169
  65.0 1.0 constant_dynamic-slice_fusion.refs_11_
  66.0 0.9 collective-permute-done.7.refs_8_
  66.8 2.8 %project.1 = (f32[512,256]{1,0:T(8,128)S(1)}, f32[8,2,512]{2,1,0:T(2,128)S(1)}) custom-call(s32[4]{0:T(128)S(1)} %pad_add_fusion.place, bf16[512,256]{1,0:T(8,128)(2,1)S(1)} %copy-done.1, bf16[512,256]{1,0:T(8,128)(2,1)S(1)} %collective-permute-done.refs_1_, bf16[512,256]{1,0:T(8,128)(2,1)S(1)} %collective-permute-done.1.refs_2_, ...), custom_call_target="tpu_custom_call" | custom-call | flops 550000000 | bytes 4000000 | tf_op jit(solution)/shard_map/project/pallas_call | solution.py:209
  70.5 12.8 %all_to_all.40.stats_ref = f32[8,2,512]{2,1,0:T(2,128)S(1)} all-to-all(f32[8,2,512]{2,1,0:T(2,128)S(1)} %get-tuple-element.27), channel_id=1, replica_groups=mesh['dp'=96,'mp'=8] {'mp'}, dimensions={0} | all-to-all | bytes 65536 | tf_op jit(solution)/shard_map/all_to_all | solution.py:431
  84.0 17.6 %all-to-all-start.3 = ((f32[96,1,128]{2,1,0:T(1,128)}), f32[96,1,128]{2,1,0:T(1,128)}, u32[]{:S(2)}, u32[]{:S(2)}) async-start(f32[96,1,128]{2,1,0:T(1,128)} %reward.1), calls=%async_computation.3 | async-start | bytes 98304 | tf_op jit(solution)/shard_map/all_to_all | solution.py:433
  101.6 1.0 copy-done.5
  102.6 0.9 copy-done.7
  103.5 2.4 %gradient.1 = (bf16[1152,256]{1,0:T(8,128)(2,1)}, bf16[1152,256]{1,0:T(8,128)(2,1)S(1)}) custom-call(s32[4]{0:T(128)S(1)} %pad_add_fusion.place, f32[8,2,512]{2,1,0:T(2,128)S(1)} %all_to_all.40.stats_ref, f32[512,256]{1,0:T(8,128)S(1)} %copy-done.5, f32[1,256]{1,0:T(1,128)S(1)} %bitcast.45, bf16[512,256]{1,0:T(8,128)(2,1)S(1)} %copy-done.1, ...), custom_call_target="tpu_custom_call" | custom-call | flops 550000000 | bytes 4000000 | tf_op jit(solution)/shard_map/gradient/pallas_call | solution.py:300
  106.8 2.6 %collective-permute-start.9 = (bf16[1152,256]{1,0:T(8,128)(2,1)}, bf16[1152,256]{1,0:T(8,128)(2,1)S(1)}, u32[]{:S(2)}, u32[]{:S(2)}) collective-permute-start(bf16[1152,256]{1,0:T(8,128)(2,1)} %get-tuple-element.32), channel_id=1, source_target_pairs={{0,8},{8,0},{16,24},{24,16},{32,40},{40,32},{48,56},{56,48},{64,72... | collective-permute-start | bytes 1769480 | tf_op jit(solution)/shard_map/ppermute | solution.py:40
  109.5 4.1 %all-to-all-done.3 = f32[96,1,128]{2,1,0:T(1,128)} async-done(((f32[96,1,128]{2,1,0:T(1,128)}), f32[96,1,128]{2,1,0:T(1,128)}, u32[]{:S(2)}, u32[]{:S(2)}) %all-to-all-start.3) | async-done | bytes 49184 | tf_op jit(solution)/shard_map/all_to_all | solution.py:433
  114.6 1.1 copy-done.3
  115.6 1.1 weigh.1
  116.8 11.9 %all_to_all.41 = bf16[4,288,256]{2,1,0:T(8,128)(2,1)S(1)} all-to-all(bf16[4,288,256]{2,1,0:T(8,128)(2,1)S(1)} %bitcast.41), channel_id=1, replica_groups={{0,192,384,576},{8,200,392,584},{16,208,400,592},{24,216,408,600},{32,2..., dimensions={0} | all-to-all | bytes 1179648 | tf_op jit(solution)/shard_map/all_to_all | solution.py:35
  128.7 17.7 %all_to_all.42 = bf16[12,24,256]{2,1,0:T(8,128)(2,1)S(1)} all-to-all(bf16[12,24,256]{2,1,0:T(8,128)(2,1)S(1)} %bitcast.46), channel_id=1, replica_groups={{0,16,32,48,64,80,96,112,128,144,160,176},{8,24,40,56,72,88,104,120,136..., dimensions={0} | all-to-all | bytes 294912 | tf_op jit(solution)/shard_map/all_to_all | solution.py:35
  146.5 13.1 %all_to_all.43 = bf16[12,24,256]{2,1,0:T(8,128)(2,1)S(1)} all-to-all(bf16[12,24,256]{2,1,0:T(8,128)(2,1)S(1)} %broadcast_in_dim.38), channel_id=1, replica_groups={{0,16,32,48,64,80,96,112,128,144,160,176},{8,24,40,56,72,88,104,120,136..., dimensions={0} | all-to-all | bytes 294912 | tf_op jit(solution)/shard_map/all_to_all | solution.py:35
  159.7 9.7 %all_to_all.44 = bf16[4,288,256]{2,1,0:T(8,128)(2,1)S(1)} all-to-all(bf16[4,288,256]{2,1,0:T(8,128)(2,1)S(1)} %broadcast_in_dim.40), channel_id=1, replica_groups={{0,192,384,576},{8,200,392,584},{16,208,400,592},{24,216,408,600},{32,2..., dimensions={0} | all-to-all | bytes 1179648 | tf_op jit(solution)/shard_map/all_to_all | solution.py:35
  169.3 7.5 %collective-permute-start.10 = (bf16[1152,256]{1,0:T(8,128)(2,1)S(1)}, bf16[1152,256]{1,0:T(8,128)(2,1)S(1)}, u32[]{:S(2)}, u32[]{:S(2)}) collective-permute-start(bf16[1152,256]{1,0:T(8,128)(2,1)S(1)} %bitcast.39), channel_id=1, source_target_pairs={{0,8},{8,0},{16,24},{24,16},{32,40},{40,32},{48,56},{56,48},{64,72... | collective-permute-start | bytes 1769480 | tf_op jit(solution)/shard_map/ppermute | solution.py:40
  178.4 2.0 %finish.1 = (f32[2048,256]{1,0:T(8,128)}, f32[1,256]{1,0:T(1,128)}, f32[1,256]{1,0:T(1,128)}) custom-call(s32[4]{0:T(128)S(1)} %pad_add_fusion.place, bf16[1152,256]{1,0:T(8,128)(2,1)S(1)} %bitcast.40, bf16[1152,256]{1,0:T(8,128)(2,1)S(1)} %collective-permute-done.10.other_ref, f32[1,2048]{1,0:T(1,128)S(1)} %bitcast.43, f32[1,2048]{1,0:T(1,128)S(1)} %bitcast.42), custom_call_target="tpu_custom_call" | custom-call | flops 1000000 | bytes 4000000 | tf_op jit(solution)/shard_map/finish/pallas_call | solution.py:375
  (49 shorter events, 8.0 us)
Async XLA Ops:
  0.6 9.1 %copy-start = (bf16[256,2048]{1,0:T(8,128)(2,1)S(1)}, bf16[256,2048]{1,0:T(8,128)(2,1)}, u32[]{:S(2)}) copy-start(bf16[256,2048]{1,0:T(8,128)(2,1)} %param.18) | copy-start | bytes 3145732
  9.7 44.2 %copy-start.8 = (f32[2048]{0:T(1024)S(1)}, f32[2048]{0:T(1024)}, u32[]{:S(2)}) copy-start(f32[2048]{0:T(1024)} %param.20) | copy-start | bytes 24580
  9.7 57.1 %copy-start.1 = (bf16[512,256]{1,0:T(8,128)(2,1)S(1)}, bf16[512,256]{1,0:T(8,128)(2,1)}, u32[]{:S(2)}) copy-start(bf16[512,256]{1,0:T(8,128)(2,1)} %front.1.refs_0_) | copy-start | bytes 786436
  10.5 15.7 %all-to-all-start = ((bf16[8,32,256]{2,1,0:T(8,128)(2,1)}), bf16[8,32,256]{2,1,0:T(8,128)(2,1)S(1)}, u32[]{:S(2)}, u32[]{:S(2)}) async-start(bf16[8,32,256]{2,1,0:T(8,128)(2,1)} %copy.18), calls=%async_computation | async-start | bytes 262144 | tf_op jit(solution)/shard_map/all_to_all | solution.py:423
  18.1 12.7 %collective-permute-start = (bf16[512,256]{1,0:T(8,128)(2,1)}, bf16[512,256]{1,0:T(8,128)(2,1)S(1)}, u32[]{:S(2)}, u32[]{:S(2)}) collective-permute-start(bf16[512,256]{1,0:T(8,128)(2,1)} %front.1.refs_0_), channel_id=1, source_target_pairs={{0,1},{1,2},{2,3},{3,4},{4,5},{5,6},{6,7},{7,0},{8,9},{9,10},{10,1... | collective-permute-start | bytes 786440 | tf_op jit(solution)/shard_map/ppermute | solution.py:165
  21.5 11.6 %collective-permute-start.1 = (bf16[512,256]{1,0:T(8,128)(2,1)}, bf16[512,256]{1,0:T(8,128)(2,1)S(1)}, u32[]{:S(2)}, u32[]{:S(2)}) collective-permute-start(bf16[512,256]{1,0:T(8,128)(2,1)} %front.1.refs_0_), channel_id=1, source_target_pairs={{0,7},{1,0},{2,1},{3,2},{4,3},{5,4},{6,5},{7,6},{8,15},{9,8},{10,9... | collective-permute-start | bytes 786440 | tf_op jit(solution)/shard_map/ppermute | solution.py:165
  27.0 10.7 %all-to-all-start.1 = ((bf16[4,8,32,256]{3,2,1,0:T(8,128)(2,1)}), bf16[4,8,32,256]{3,2,1,0:T(8,128)(2,1)S(1)}, u32[]{:S(2)}, u32[]{:S(2)}) async-start(bf16[4,8,32,256]{3,2,1,0:T(8,128)(2,1)} %broadcast_in_dim.35), calls=%async_computation.1 | async-start | bytes 1048576 | tf_op jit(solution)/shard_map/all_to_all | solution.py:35
  30.8 16.5 %collective-permute-start.2 = (bf16[512,256]{1,0:T(8,128)(2,1)S(1)}, bf16[512,256]{1,0:T(8,128)(2,1)S(1)}, u32[]{:S(2)}, u32[]{:S(2)}) collective-permute-start(bf16[512,256]{1,0:T(8,128)(2,1)S(1)} %collective-permute-done.refs_1_), channel_id=1, source_target_pairs={{0,1},{1,2},{2,3},{3,4},{4,5},{5,6},{6,7},{7,0},{8,9},{9,10},{10,1... | collective-permute-start | bytes 786440 | tf_op jit(solution)/shard_map/ppermute | solution.py:165
  33.1 17.5 %collective-permute-start.3 = (bf16[512,256]{1,0:T(8,128)(2,1)S(1)}, bf16[512,256]{1,0:T(8,128)(2,1)S(1)}, u32[]{:S(2)}, u32[]{:S(2)}) collective-permute-start(bf16[512,256]{1,0:T(8,128)(2,1)S(1)} %collective-permute-done.1.refs_2_), channel_id=1, source_target_pairs={{0,7},{1,0},{2,1},{3,2},{4,3},{5,4},{6,5},{7,6},{8,15},{9,8},{10,9... | collective-permute-start | bytes 786440 | tf_op jit(solution)/shard_map/ppermute | solution.py:165
  37.7 29.1 %collective-permute-start.8 = (bf16[4,8,32,256]{3,2,1,0:T(8,128)(2,1)S(1)}, bf16[4,8,32,256]{3,2,1,0:T(8,128)(2,1)}, u32[]{:S(2)}, u32[]{:S(2)}) collective-permute-start(bf16[4,8,32,256]{3,2,1,0:T(8,128)(2,1)S(1)} %all-to-all-done.1.refs_9_), channel_id=1, source_target_pairs={{0,8},{8,0},{16,24},{24,16},{32,40},{40,32},{48,56},{56,48},{64,72... | collective-permute-start | bytes 1572872 | tf_op jit(solution)/shard_map/ppermute | solution.py:40
  47.3 11.0 %collective-permute-start.4 = (bf16[512,256]{1,0:T(8,128)(2,1)S(1)}, bf16[512,256]{1,0:T(8,128)(2,1)S(1)}, u32[]{:S(2)}, u32[]{:S(2)}) collective-permute-start(bf16[512,256]{1,0:T(8,128)(2,1)S(1)} %collective-permute-done.2.refs_3_), channel_id=1, source_target_pairs={{0,1},{1,2},{2,3},{3,4},{4,5},{5,6},{6,7},{7,0},{8,9},{9,10},{10,1... | collective-permute-start | bytes 786440 | tf_op jit(solution)/shard_map/ppermute | solution.py:165
  50.6 9.8 %collective-permute-start.5 = (bf16[512,256]{1,0:T(8,128)(2,1)S(1)}, bf16[512,256]{1,0:T(8,128)(2,1)S(1)}, u32[]{:S(2)}, u32[]{:S(2)}) collective-permute-start(bf16[512,256]{1,0:T(8,128)(2,1)S(1)} %collective-permute-done.3.refs_4_), channel_id=1, source_target_pairs={{0,7},{1,0},{2,1},{3,2},{4,3},{5,4},{6,5},{7,6},{8,15},{9,8},{10,9... | collective-permute-start | bytes 786440 | tf_op jit(solution)/shard_map/ppermute | solution.py:165
  58.4 7.6 %collective-permute-start.6 = (bf16[256,256]{1,0:T(8,128)(2,1)S(1)}, bf16[256,256]{1,0:T(8,128)(2,1)S(1)}, u32[]{:S(2)}, u32[]{:S(2)}) collective-permute-start(bf16[256,256]{1,0:T(8,128)(2,1)S(1)} %slice.16), channel_id=1, source_target_pairs={{0,1},{1,2},{2,3},{3,4},{4,5},{5,6},{6,7},{7,0},{8,9},{9,10},{10,1... | collective-permute-start | bytes 393224 | tf_op jit(solution)/shard_map/ppermute | solution.py:168
  60.5 6.3 %collective-permute-start.7 = (bf16[256,256]{1,0:T(8,128)(2,1)S(1)}, bf16[256,256]{1,0:T(8,128)(2,1)S(1)}, u32[]{:S(2)}, u32[]{:S(2)}) collective-permute-start(bf16[256,256]{1,0:T(8,128)(2,1)S(1)} %slice.17), channel_id=1, source_target_pairs={{0,7},{1,0},{2,1},{3,2},{4,3},{5,4},{6,5},{7,6},{8,15},{9,8},{10,9... | collective-permute-start | bytes 393224 | tf_op jit(solution)/shard_map/ppermute | solution.py:169
  66.8 2.8 %copy-start.6 = (bf16[256,256]{1,0:T(8,128)(2,1)}, bf16[256,256]{1,0:T(8,128)(2,1)S(1)}, u32[]{:S(2)}) copy-start(bf16[256,256]{1,0:T(8,128)(2,1)S(1)} %collective-permute-done.7.refs_8_) | copy-start | bytes 393220
  69.7 0.8 copy-start.4
  70.5 39.0 %copy-start.10 = (s32[96]{0:T(128)S(1)}, s32[96]{0:T(128)}, u32[]{:S(2)}) copy-start(s32[96]{0:T(128)} %param.13) | copy-start | bytes 1156
  84.0 29.6 %all-to-all-start.3 = ((f32[96,1,128]{2,1,0:T(1,128)}), f32[96,1,128]{2,1,0:T(1,128)}, u32[]{:S(2)}, u32[]{:S(2)}) async-start(f32[96,1,128]{2,1,0:T(1,128)} %reward.1), calls=%async_computation.3 | async-start | bytes 98304 | tf_op jit(solution)/shard_map/all_to_all | solution.py:433
  101.6 1.0 copy-start.5
  102.6 0.9 copy-start.7
  106.0 0.8 copy-start.2
  106.8 7.7 %collective-permute-start.9 = (bf16[1152,256]{1,0:T(8,128)(2,1)}, bf16[1152,256]{1,0:T(8,128)(2,1)S(1)}, u32[]{:S(2)}, u32[]{:S(2)}) collective-permute-start(bf16[1152,256]{1,0:T(8,128)(2,1)} %get-tuple-element.32), channel_id=1, source_target_pairs={{0,8},{8,0},{16,24},{24,16},{32,40},{40,32},{48,56},{56,48},{64,72... | collective-permute-start | bytes 1769480 | tf_op jit(solution)/shard_map/ppermute | solution.py:40
  114.6 1.1 copy-start.3
  116.7 61.7 %copy-start.9 = (f32[2048]{0:T(1024)S(1)}, f32[2048]{0:T(1024)}, u32[]{:S(2)}) copy-start(f32[2048]{0:T(1024)} %param.19) | copy-start | bytes 24580
  169.3 9.1 %collective-permute-start.10 = (bf16[1152,256]{1,0:T(8,128)(2,1)S(1)}, bf16[1152,256]{1,0:T(8,128)(2,1)S(1)}, u32[]{:S(2)}, u32[]{:S(2)}) collective-permute-start(bf16[1152,256]{1,0:T(8,128)(2,1)S(1)} %bitcast.39), channel_id=1, source_target_pairs={{0,8},{8,0},{16,24},{24,16},{32,40},{40,32},{48,56},{56,48},{64,72... | collective-permute-start | bytes 1769480 | tf_op jit(solution)/shard_map/ppermute | solution.py:40

commit v11 on v10

--- a/solution.py
+++ b/solution.py
@@ -12,7 +12,6 @@
 KEY_VALUE_HEADS = 8
 HEAD_SIZE = 64
 NX, NZ, NCORE = 4, 12, 2
-NEAR = NX * NCORE
 
 EPS = 1e-05
 THETA = 500000.0
@@ -180,20 +179,38 @@
     return jnp.concatenate([refs[-2][...], refs[-1][...]], axis=0)
 
 
+def cut_kernel(place, w_ref, out_ref):
+    parts, rows, cols = out_ref.shape
+    mine = pl.ds(pl.multiple_of(place[1] * rows, rows), rows)
+    for g in range(parts):
+        out_ref[g] = w_ref[mine, g * cols : (g + 1) * cols]
+
+
+def cut(place, w_out, n_mp):
+    shape = (n_mp, w_out.shape[0] // NCORE, w_out.shape[1] // n_mp)
+    here = pl.BlockSpec(memory_space=pltpu.VMEM)
+    return pl.pallas_call(
+        cut_kernel,
+        out_shape=jax.ShapeDtypeStruct(shape, BF16),
+        in_specs=[pl.BlockSpec(memory_space=pltpu.SMEM), here],
+        out_specs=here,
+        compiler_params=pltpu.CompilerParams(vmem_limit_bytes=16 * 2**20),
+        cost_estimate=pl.CostEstimate(flops=0, bytes_accessed=1000000, transcendentals=0),
+        name="cut",
+    )(place, w_out)
+
+
 def project_kernel(distances, place, *refs):
     count = len(distances) + 1
     shards = refs[:count]
     mine_ref, other_ref, x_ref, both_ref, resid_ref, stats_ref, w_ref = refs[count:]
-    groups, feat = mine_ref.shape[1], mine_ref.shape[3]
-    for x in range(NX):
-        for g in range(groups):
-            w_ref[g, NCORE * x + place[1]] = mine_ref[x, g]
-            w_ref[g, NCORE * x + 1 - place[1]] = other_ref[x, g]
+    groups, half, feat = mine_ref.shape
+    w_ref[:, pl.ds(pl.multiple_of(place[1] * half, half), half), :] = mine_ref[...]
+    w_ref[:, pl.ds(pl.multiple_of((1 - place[1]) * half, half), half), :] = other_ref[...]
     resid = x_ref[...].astype(F32)
     for i, distance in enumerate(distances):
         group = lax.rem(place[0] + (distance + groups), groups)
-        weight = w_ref[group].reshape(-1, feat)
-        resid = resid + dot(shard_of(shards, i), weight, 1, 0).astype(BF16).astype(F32)
+        resid = resid + dot(shard_of(shards, i), w_ref[group], 1, 0).astype(BF16).astype(F32)
     resid_ref[...] = resid
     squares = dot(jnp.ones((8, feat), F32), resid * resid, 1, 1, lax.Precision.HIGHEST)
     scores = dot(jnp.broadcast_to(both_ref[...], (8, feat)), resid, 1, 1, lax.Precision.HIGHEST)
@@ -202,7 +219,7 @@
 
 
 def project(place, parts, w_mine, w_other, x_cols, both):
-    _, n_mp, piece_rows, feat = w_mine.shape
+    n_mp, half, feat = w_mine.shape
     rows = x_cols.shape[0]
     shards = flatten(parts)
     here = pl.BlockSpec(memory_space=pltpu.VMEM)
@@ -214,7 +231,7 @@
         ),
         in_specs=[pl.BlockSpec(memory_space=pltpu.SMEM)] + [here] * (len(shards) + 4),
         out_specs=(here, here),
-        scratch_shapes=[pltpu.VMEM((n_mp, NEAR, piece_rows, feat), BF16)],
+        scratch_shapes=[pltpu.VMEM((n_mp, NCORE * half, feat), BF16)],
         compiler_params=pltpu.CompilerParams(vmem_limit_bytes=32 * 2**20),
         cost_estimate=pl.CostEstimate(flops=550000000, bytes_accessed=4000000, transcendentals=0),
         name="project",
@@ -309,7 +326,7 @@
     )(place, stats, resid, both, *shards)
 
 
-def weigh_kernel(place, costs_ref, order_ref, keep_ref, got_ref, out_ref, margin_ref, row_ref):
+def weigh_kernel(place, costs_ref, order_ref, keep_ref, got_ref, out_ref, loss_ref, row_ref):
     seqs = costs_ref.shape[0]
     rewards = -costs_ref[...].reshape(seqs, LANES)
     order = order_ref[...]
@@ -325,9 +342,12 @@
     own = jnp.sum(jnp.where(order == me, dreward, 0.0), axis=1, keepdims=True)
     sib = jnp.sum(jnp.where(order == (me ^ 1), dreward, 0.0), axis=1, keepdims=True)
     out_ref[...] = (keep_ref[...].astype(F32) * own + got_ref[...].astype(F32) * sib).astype(BF16)
-    margin_ref[...] = margin
+    each = jnp.maximum(-margin, 0.0) + jnp.log1p(jnp.exp(-jnp.abs(margin)))
+    counted = chosen & (lane < seqs)
+    loss_ref[...] = jnp.sum(jnp.where(counted, each, 0.0), axis=1, keepdims=True)
     at = lax.broadcasted_iota(jnp.int32, (seqs, LANES), 1)
-    row_ref[...] = jnp.sum(jnp.where(seq == at, rewards, 0.0), axis=0, keepdims=True)
+    row = jnp.sum(jnp.where(seq == at, rewards, 0.0), axis=0, keepdims=True)
+    row_ref[...] = row[:, :seqs]
 
 
 def weigh(place, costs, order, keep, got):
@@ -336,14 +356,18 @@
         weigh_kernel,
         out_shape=(
             jax.ShapeDtypeStruct(keep.shape, BF16),
-            jax.ShapeDtypeStruct((1, LANES), F32),
-            jax.ShapeDtypeStruct((1, LANES), F32),
+            jax.ShapeDtypeStruct((1, 1), F32),
+            jax.ShapeDtypeStruct((1, costs.shape[0]), F32),
         ),
         grid_spec=pltpu.PrefetchScalarGridSpec(
             num_scalar_prefetch=1,
             grid=(1,),
             in_specs=[flat(costs), flat(order), flat(keep), flat(got)],
-            out_specs=(flat(keep),) + (pl.BlockSpec((1, LANES), lambda i, s: (0, 0)),) * 2,
+            out_specs=(
+                flat(keep),
+                pl.BlockSpec((1, 1), lambda i, s: (0, 0)),
+                pl.BlockSpec((1, costs.shape[0]), lambda i, s: (0, 0)),
+            ),
         ),
         compiler_params=pltpu.CompilerParams(vmem_limit_bytes=16 * 2**20),
         cost_estimate=pl.CostEstimate(flops=1000000, bytes_accessed=2000000, transcendentals=128),
@@ -416,12 +440,7 @@
     mixed, w_out, hidden_rows, gain_final, w_head = lax.optimization_barrier(
         (mixed, w_out, hidden_rows, gain_final, w_head)
     )
-    piece_rows = w_out.shape[0] // NEAR
-    my_near = (me // (NZ * NCORE)) * NCORE + core
-    w_piece = lax.dynamic_slice_in_dim(w_out, my_near * piece_rows, piece_rows, 0)
-    w_piece = w_piece.reshape(piece_rows, n_mp, feat).swapaxes(0, 1)
-    w_piece = lax.all_to_all(w_piece, "mp", 0, 0, tiled=True)
-    w_mine = swap(jnp.broadcast_to(w_piece[None], (NX,) + w_piece.shape), along_x)
+    w_mine = lax.all_to_all(cut(place, w_out, n_mp), "mp", 0, 0, tiled=True)
     w_other = to_sibling(w_mine)
 
     parts = ring(mixed)
@@ -441,8 +460,7 @@
     got = to_sibling(send)
     seqs = pair_order.shape[0]
     order = jnp.pad(pair_order, (0, LANES - seqs), constant_values=-1)[None]
-    summed, margin, reward_row = weigh(place, costs, order, keep, got)
-    loss = jnp.sum(jax.nn.softplus(-margin[0, :seqs:2]))
+    summed, loss, reward_row = weigh(place, costs, order, keep, got)
 
     got = swap(summed.reshape(NX, NZ * piece, feat), along_x)
     summed = jnp.sum(got.astype(F32), axis=0).astype(BF16)
@@ -453,7 +471,7 @@
     got = got.reshape(half_ext, feat)
     other = to_sibling(got)
     grad_out_proj, grad_head, grad_gain = finish(place, got, other, gain_final, w_head, half)
-    return (loss, reward_row[0, :seqs], grad_out_proj, grad_head[0], grad_gain[0])
+    return (loss[0, 0], reward_row[0], grad_out_proj, grad_head[0], grad_gain[0])
 
 
 def solution(mesh):

time: 182 us -> 184 us (1.011)
  waiting for transfers between devices: 11 us -> 20.4 us
  local copies, waits for them, and re-layouts: 7.95 us -> 2.89 us
  other arithmetic: 2.54 us -> 0.43 us
    ppermute x3, waiting for transfers between devices: 3.74 us -> 12.6 us  [ring(): lax.ppermute(below, 'mp', up)]
    all_to_all x1, starting transfers between devices: 17.6 us -> 22.7 us  [body(): costs = -lax.all_to_all(reward, 'dp', 0, 0, tiled=True)]
    all_to_all x2 -> x1, starting transfers between devices: 11.4 us -> 7.64 us  [body(): w_mine = lax.all_to_all(cut(place, w_out, n_mp), 'mp', 0, 0, tiled=True)]
    unnamed x23 -> x18, local copies, waits for them, and re-layouts: 4.71 us -> 1.84 us
    all_to_all x2 -> x1, waiting for transfers between devices: 1.96 us -> 0.01 us  [body(): w_mine = lax.all_to_all(cut(place, w_out, n_mp), 'mp', 0, 0, tiled=True)]
  transfers between devices with their start and end apart: 14 -> 13, of which waited for: 6 -> 5; matrix products, arithmetic and copies ran while one was open for 3% -> 1% of each run, Pallas kernels for 1% -> 1%
where the time goes in v11:
time: 184 us; the launch traced here: 183 us
  starting transfers between devices  74.9 us (41%)
  blocking collectives  63.8 us (35%)
  waiting for transfers between devices  20.4 us (11%)
  Pallas kernels  18.7 us (10%)
  local copies, waits for them, and re-layouts  2.89 us (2%)
    all_to_all x4, blocking collectives, swap(): lax.all_to_all(parts, 'dp', 0, 0, tiled=True, axis_index_groups=groups)  52 us
    all_to_all x1, starting transfers between devices, body(): costs = -lax.all_to_all(reward, 'dp', 0, 0, tiled=True)  22.7 us
    ppermute x3, starting transfers between devices, to_sibling(): return lax.ppermute(x, 'dp', pairs)  18.6 us
    ppermute x3, waiting for transfers between devices, ring(): lax.ppermute(below, 'mp', up)  12.6 us
    ppermute x3, starting transfers between devices, ring(): lax.ppermute(above, 'mp', down)  12.3 us
    all_to_all x1, blocking collectives, body(): stats = lax.all_to_all(stats, 'mp', 0, 0, tiled=True)  11.8 us
    pallas_call x1, Pallas kernels, front(): pl.pallas_call(front_kernel, out_shape=jax.ShapeDtypeStruct((rows, w_quer...  8.37 us
    all_to_all x1, starting transfers between devices, body(): w_mine = lax.all_to_all(cut(place, w_out, n_mp), 'mp', 0, 0, tiled=True)  7.64 us
  transfers between devices with their start and end apart: 13, of which 5 were waited for; matrix products, arithmetic and copies ran while one was open for 1% of the time, Pallas kernels for 1%

profile of v11, /device:TPU:1, one launch (start us, length us, event | category | flops | bytes accessed | tf_op | source)
XLA Modules:
  0.0 182.8 jit_solution(1400019778021898384)
XLA Ops:
  1.3 8.4 %front.1.refs_0_ = bf16[512,256]{1,0:T(8,128)(2,1)} custom-call(s32[1]{0:T(128)S(6)} %copy.16.lens, bf16[512,2048]{1,0:T(8,128)(2,1)} %x_hbm.1, f32[1,2048]{1,0:T(1,128)} %bitcast.30, bf16[2048,256]{1,0:T(8,128)(2,1)} %wq_hbm.1, bf16[64,2048]{1,0:T(8,128)(2,1)} %bitcast.28, bf16[64,2048]{1,0:T(8,128)(2,1)} %bitcast.29, f32[1,128]{1,0:T(1,128)} %constant.38.clone.freq_ref), custom_call_target="tpu_custom_call" | custom-call | flops 1500000000 | bytes 4000000 | tf_op jit(solution)/shard_map/front/pallas_call | solution.py:134
  9.8 1.4 cut.1
  11.2 7.6 %all-to-all-start = ((bf16[8,128,256]{2,1,0:T(8,128)(2,1)}), bf16[8,128,256]{2,1,0:T(8,128)(2,1)S(1)}, u32[]{:S(2)}, u32[]{:S(2)}) async-start(bf16[8,128,256]{2,1,0:T(8,128)(2,1)} %cut.1), calls=%async_computation | async-start | bytes 1048576 | tf_op jit(solution)/shard_map/all_to_all | solution.py:443
  18.8 3.4 %collective-permute-start = (bf16[512,256]{1,0:T(8,128)(2,1)S(1)}, bf16[512,256]{1,0:T(8,128)(2,1)S(1)}, u32[]{:S(2)}, u32[]{:S(2)}) collective-permute-start(bf16[512,256]{1,0:T(8,128)(2,1)S(1)} %copy-done.1), channel_id=1, source_target_pairs={{0,1},{1,2},{2,3},{3,4},{4,5},{5,6},{6,7},{7,0},{8,9},{9,10},{10,1... | collective-permute-start | bytes 786440 | tf_op jit(solution)/shard_map/ppermute | solution.py:164
  22.2 3.1 %collective-permute-start.1 = (bf16[512,256]{1,0:T(8,128)(2,1)S(1)}, bf16[512,256]{1,0:T(8,128)(2,1)S(1)}, u32[]{:S(2)}, u32[]{:S(2)}) collective-permute-start(bf16[512,256]{1,0:T(8,128)(2,1)S(1)} %copy-done.1), channel_id=1, source_target_pairs={{0,7},{1,0},{2,1},{3,2},{4,3},{5,4},{6,5},{7,6},{8,15},{9,8},{10,9... | collective-permute-start | bytes 786440 | tf_op jit(solution)/shard_map/ppermute | solution.py:164
  25.3 8.6 %collective-permute-done.refs_1_ = bf16[512,256]{1,0:T(8,128)(2,1)S(1)} collective-permute-done((bf16[512,256]{1,0:T(8,128)(2,1)S(1)}, bf16[512,256]{1,0:T(8,128)(2,1)S(1)}, u32[]{:S(2)}, u32[]{:S(2)}) %collective-permute-start) | collective-permute-done | bytes 262176 | tf_op jit(solution)/shard_map/ppermute | solution.py:164
  33.9 1.9 %collective-permute-start.2 = (bf16[512,256]{1,0:T(8,128)(2,1)S(1)}, bf16[512,256]{1,0:T(8,128)(2,1)S(1)}, u32[]{:S(2)}, u32[]{:S(2)}) collective-permute-start(bf16[512,256]{1,0:T(8,128)(2,1)S(1)} %collective-permute-done.refs_1_), channel_id=1, source_target_pairs={{0,1},{1,2},{2,3},{3,4},{4,5},{5,6},{6,7},{7,0},{8,9},{9,10},{10,1... | collective-permute-start | bytes 786440 | tf_op jit(solution)/shard_map/ppermute | solution.py:164
  35.9 4.6 %collective-permute-start.3 = (bf16[512,256]{1,0:T(8,128)(2,1)S(1)}, bf16[512,256]{1,0:T(8,128)(2,1)S(1)}, u32[]{:S(2)}, u32[]{:S(2)}) collective-permute-start(bf16[512,256]{1,0:T(8,128)(2,1)S(1)} %collective-permute-done.1.refs_2_), channel_id=1, source_target_pairs={{0,7},{1,0},{2,1},{3,2},{4,3},{5,4},{6,5},{7,6},{8,15},{9,8},{10,9... | collective-permute-start | bytes 786440 | tf_op jit(solution)/shard_map/ppermute | solution.py:164
  40.5 8.5 %collective-permute-start.8 = (bf16[8,128,256]{2,1,0:T(8,128)(2,1)S(1)}, bf16[8,128,256]{2,1,0:T(8,128)(2,1)S(1)}, u32[]{:S(2)}, u32[]{:S(2)}) collective-permute-start(bf16[8,128,256]{2,1,0:T(8,128)(2,1)S(1)} %all-to-all-done.refs_9_), channel_id=1, source_target_pairs={{0,8},{8,0},{16,24},{24,16},{32,40},{40,32},{48,56},{56,48},{64,72... | collective-permute-start | bytes 1572872 | tf_op jit(solution)/shard_map/ppermute | solution.py:39
  49.0 1.9 %collective-permute-start.4 = (bf16[512,256]{1,0:T(8,128)(2,1)S(1)}, bf16[512,256]{1,0:T(8,128)(2,1)S(1)}, u32[]{:S(2)}, u32[]{:S(2)}) collective-permute-start(bf16[512,256]{1,0:T(8,128)(2,1)S(1)} %collective-permute-done.2.refs_3_), channel_id=1, source_target_pairs={{0,1},{1,2},{2,3},{3,4},{4,5},{5,6},{6,7},{7,0},{8,9},{9,10},{10,1... | collective-permute-start | bytes 786440 | tf_op jit(solution)/shard_map/ppermute | solution.py:164
  51.0 4.6 %collective-permute-start.5 = (bf16[512,256]{1,0:T(8,128)(2,1)S(1)}, bf16[512,256]{1,0:T(8,128)(2,1)S(1)}, u32[]{:S(2)}, u32[]{:S(2)}) collective-permute-start(bf16[512,256]{1,0:T(8,128)(2,1)S(1)} %collective-permute-done.3.refs_4_), channel_id=1, source_target_pairs={{0,7},{1,0},{2,1},{3,2},{4,3},{5,4},{6,5},{7,6},{8,15},{9,8},{10,9... | collective-permute-start | bytes 786440 | tf_op jit(solution)/shard_map/ppermute | solution.py:164
  55.6 4.0 %collective-permute-done.4.refs_5_ = bf16[512,256]{1,0:T(8,128)(2,1)S(1)} collective-permute-done((bf16[512,256]{1,0:T(8,128)(2,1)S(1)}, bf16[512,256]{1,0:T(8,128)(2,1)S(1)}, u32[]{:S(2)}, u32[]{:S(2)}) %collective-permute-start.4) | collective-permute-done | bytes 262176 | tf_op jit(solution)/shard_map/ppermute | solution.py:164
  59.6 1.9 %collective-permute-start.6 = (bf16[256,256]{1,0:T(8,128)(2,1)S(1)}, bf16[256,256]{1,0:T(8,128)(2,1)S(1)}, u32[]{:S(2)}, u32[]{:S(2)}) collective-permute-start(bf16[256,256]{1,0:T(8,128)(2,1)S(1)} %slice.8), channel_id=1, source_target_pairs={{0,1},{1,2},{2,3},{3,4},{4,5},{5,6},{6,7},{7,0},{8,9},{9,10},{10,1... | collective-permute-start | bytes 393224 | tf_op jit(solution)/shard_map/ppermute | solution.py:167
  61.5 4.6 %collective-permute-start.7 = (bf16[256,256]{1,0:T(8,128)(2,1)S(1)}, bf16[256,256]{1,0:T(8,128)(2,1)S(1)}, u32[]{:S(2)}, u32[]{:S(2)}) collective-permute-start(bf16[256,256]{1,0:T(8,128)(2,1)S(1)} %slice.9), channel_id=1, source_target_pairs={{0,7},{1,0},{2,1},{3,2},{4,3},{5,4},{6,5},{7,6},{8,15},{9,8},{10,9... | collective-permute-start | bytes 393224 | tf_op jit(solution)/shard_map/ppermute | solution.py:168
  66.2 1.0 constant_dynamic-slice_fusion.refs_11_
  67.2 0.8 collective-permute-done.7.refs_8_
  68.1 2.2 %project.1 = (f32[512,256]{1,0:T(8,128)S(1)}, f32[8,2,512]{2,1,0:T(2,128)S(1)}) custom-call(s32[4]{0:T(128)S(1)} %pad_add_fusion.place, bf16[512,256]{1,0:T(8,128)(2,1)S(1)} %copy-done.1, bf16[512,256]{1,0:T(8,128)(2,1)S(1)} %collective-permute-done.refs_1_, bf16[512,256]{1,0:T(8,128)(2,1)S(1)} %collective-permute-done.1.refs_2_, ...), custom_call_target="tpu_custom_call" | custom-call | flops 550000000 | bytes 4000000 | tf_op jit(solution)/shard_map/project/pallas_call | solution.py:226
  70.3 11.8 %all_to_all.35.stats_ref = f32[8,2,512]{2,1,0:T(2,128)S(1)} all-to-all(f32[8,2,512]{2,1,0:T(2,128)S(1)} %get-tuple-element.27), channel_id=1, replica_groups=mesh['dp'=96,'mp'=8] {'mp'}, dimensions={0} | all-to-all | bytes 65536 | tf_op jit(solution)/shard_map/all_to_all | solution.py:450
  82.8 22.7 %all-to-all-start.2 = ((f32[96,1,128]{2,1,0:T(1,128)}), f32[96,1,128]{2,1,0:T(1,128)S(1)}, u32[]{:S(2)}, u32[]{:S(2)}) async-start(f32[96,1,128]{2,1,0:T(1,128)} %reward.1), calls=%async_computation.2 | async-start | bytes 98304 | tf_op jit(solution)/shard_map/all_to_all | solution.py:452
  105.5 0.9 copy-done.3
  106.4 0.9 copy-done.5
  107.3 2.4 %gradient.1 = (bf16[1152,256]{1,0:T(8,128)(2,1)}, bf16[1152,256]{1,0:T(8,128)(2,1)S(1)}) custom-call(s32[4]{0:T(128)S(1)} %pad_add_fusion.place, f32[8,2,512]{2,1,0:T(2,128)S(1)} %all_to_all.35.stats_ref, f32[512,256]{1,0:T(8,128)S(1)} %get-tuple-element.30.resid_ref, f32[1,256]{1,0:T(1,128)S(1)} %bitcast.25, bf16[512,256]{1,0:T(8,128)(2,1)S(1)} %copy-done.1, ...), custom_call_target="tpu_custom_call" | custom-call | flops 550000000 | bytes 4000000 | tf_op jit(solution)/shard_map/gradient/pallas_call | solution.py:317
  109.8 2.6 %collective-permute-start.9 = (bf16[1152,256]{1,0:T(8,128)(2,1)}, bf16[1152,256]{1,0:T(8,128)(2,1)S(1)}, u32[]{:S(2)}, u32[]{:S(2)}) collective-permute-start(bf16[1152,256]{1,0:T(8,128)(2,1)} %get-tuple-element.32), channel_id=1, source_target_pairs={{0,8},{8,0},{16,24},{24,16},{32,40},{40,32},{48,56},{56,48},{64,72... | collective-permute-start | bytes 1769480 | tf_op jit(solution)/shard_map/ppermute | solution.py:39
  112.4 5.4 %all-to-all-done.2 = f32[96,1,128]{2,1,0:T(1,128)S(1)} async-done(((f32[96,1,128]{2,1,0:T(1,128)}), f32[96,1,128]{2,1,0:T(1,128)S(1)}, u32[]{:S(2)}, u32[]{:S(2)}) %all-to-all-start.2) | async-done | bytes 49184 | tf_op jit(solution)/shard_map/all_to_all | solution.py:452
  117.9 1.6 weigh.1
  119.5 11.4 %all_to_all.36 = bf16[4,288,256]{2,1,0:T(8,128)(2,1)S(1)} all-to-all(bf16[4,288,256]{2,1,0:T(8,128)(2,1)S(1)} %bitcast.21), channel_id=1, replica_groups={{0,192,384,576},{8,200,392,584},{16,208,400,592},{24,216,408,600},{32,2..., dimensions={0} | all-to-all | bytes 1179648 | tf_op jit(solution)/shard_map/all_to_all | solution.py:34
  131.0 17.8 %all_to_all.37 = bf16[12,24,256]{2,1,0:T(8,128)(2,1)S(1)} all-to-all(bf16[12,24,256]{2,1,0:T(8,128)(2,1)S(1)} %bitcast.26), channel_id=1, replica_groups={{0,16,32,48,64,80,96,112,128,144,160,176},{8,24,40,56,72,88,104,120,136..., dimensions={0} | all-to-all | bytes 294912 | tf_op jit(solution)/shard_map/all_to_all | solution.py:34
  148.8 13.1 %all_to_all.38 = bf16[12,24,256]{2,1,0:T(8,128)(2,1)S(1)} all-to-all(bf16[12,24,256]{2,1,0:T(8,128)(2,1)S(1)} %broadcast_in_dim.31), channel_id=1, replica_groups={{0,16,32,48,64,80,96,112,128,144,160,176},{8,24,40,56,72,88,104,120,136..., dimensions={0} | all-to-all | bytes 294912 | tf_op jit(solution)/shard_map/all_to_all | solution.py:34
  162.0 9.7 %all_to_all.39 = bf16[4,288,256]{2,1,0:T(8,128)(2,1)S(1)} all-to-all(bf16[4,288,256]{2,1,0:T(8,128)(2,1)S(1)} %broadcast_in_dim.33), channel_id=1, replica_groups={{0,192,384,576},{8,200,392,584},{16,208,400,592},{24,216,408,600},{32,2..., dimensions={0} | all-to-all | bytes 1179648 | tf_op jit(solution)/shard_map/all_to_all | solution.py:34
  171.7 7.5 %collective-permute-start.10 = (bf16[1152,256]{1,0:T(8,128)(2,1)S(1)}, bf16[1152,256]{1,0:T(8,128)(2,1)S(1)}, u32[]{:S(2)}, u32[]{:S(2)}) collective-permute-start(bf16[1152,256]{1,0:T(8,128)(2,1)S(1)} %bitcast.19), channel_id=1, source_target_pairs={{0,8},{8,0},{16,24},{24,16},{32,40},{40,32},{48,56},{56,48},{64,72... | collective-permute-start | bytes 1769480 | tf_op jit(solution)/shard_map/ppermute | solution.py:39
  179.2 1.6 collective-permute-done.10.other_ref
  180.8 2.0 %finish.1 = (f32[2048,256]{1,0:T(8,128)}, f32[1,256]{1,0:T(1,128)}, f32[1,256]{1,0:T(1,128)}) custom-call(s32[4]{0:T(128)S(1)} %pad_add_fusion.place, bf16[1152,256]{1,0:T(8,128)(2,1)S(1)} %bitcast.20, bf16[1152,256]{1,0:T(8,128)(2,1)S(1)} %collective-permute-done.10.other_ref, f32[1,2048]{1,0:T(1,128)S(1)} %bitcast.23, f32[1,2048]{1,0:T(1,128)S(1)} %bitcast.22), custom_call_target="tpu_custom_call" | custom-call | flops 1000000 | bytes 4000000 | tf_op jit(solution)/shard_map/finish/pallas_call | solution.py:399
  (37 shorter events, 1.3 us)
Async XLA Ops:
  1.3 8.5 %copy-start = (bf16[256,2048]{1,0:T(8,128)(2,1)S(1)}, bf16[256,2048]{1,0:T(8,128)(2,1)}, u32[]{:S(2)}) copy-start(bf16[256,2048]{1,0:T(8,128)(2,1)} %w_ref) | copy-start | bytes 3145732
  9.7 9.1 %copy-start.1 = (bf16[512,256]{1,0:T(8,128)(2,1)S(1)}, bf16[512,256]{1,0:T(8,128)(2,1)}, u32[]{:S(2)}) copy-start(bf16[512,256]{1,0:T(8,128)(2,1)} %front.1.refs_0_) | copy-start | bytes 786436
  9.7 56.4 %copy-start.6 = (f32[2048]{0:T(1024)S(1)}, f32[2048]{0:T(1024)}, u32[]{:S(2)}) copy-start(f32[2048]{0:T(1024)} %param.20) | copy-start | bytes 24580
  9.7 56.4 %copy-start.7 = (f32[2048]{0:T(1024)S(1)}, f32[2048]{0:T(1024)}, u32[]{:S(2)}) copy-start(f32[2048]{0:T(1024)} %param.19) | copy-start | bytes 24580
  11.2 29.3 %all-to-all-start = ((bf16[8,128,256]{2,1,0:T(8,128)(2,1)}), bf16[8,128,256]{2,1,0:T(8,128)(2,1)S(1)}, u32[]{:S(2)}, u32[]{:S(2)}) async-start(bf16[8,128,256]{2,1,0:T(8,128)(2,1)} %cut.1), calls=%async_computation | async-start | bytes 1048576 | tf_op jit(solution)/shard_map/all_to_all | solution.py:443
  18.8 15.1 %collective-permute-start = (bf16[512,256]{1,0:T(8,128)(2,1)S(1)}, bf16[512,256]{1,0:T(8,128)(2,1)S(1)}, u32[]{:S(2)}, u32[]{:S(2)}) collective-permute-start(bf16[512,256]{1,0:T(8,128)(2,1)S(1)} %copy-done.1), channel_id=1, source_target_pairs={{0,1},{1,2},{2,3},{3,4},{4,5},{5,6},{6,7},{7,0},{8,9},{9,10},{10,1... | collective-permute-start | bytes 786440 | tf_op jit(solution)/shard_map/ppermute | solution.py:164
  22.2 13.7 %collective-permute-start.1 = (bf16[512,256]{1,0:T(8,128)(2,1)S(1)}, bf16[512,256]{1,0:T(8,128)(2,1)S(1)}, u32[]{:S(2)}, u32[]{:S(2)}) collective-permute-start(bf16[512,256]{1,0:T(8,128)(2,1)S(1)} %copy-done.1), channel_id=1, source_target_pairs={{0,7},{1,0},{2,1},{3,2},{4,3},{5,4},{6,5},{7,6},{8,15},{9,8},{10,9... | collective-permute-start | bytes 786440 | tf_op jit(solution)/shard_map/ppermute | solution.py:164
  33.9 15.1 %collective-permute-start.2 = (bf16[512,256]{1,0:T(8,128)(2,1)S(1)}, bf16[512,256]{1,0:T(8,128)(2,1)S(1)}, u32[]{:S(2)}, u32[]{:S(2)}) collective-permute-start(bf16[512,256]{1,0:T(8,128)(2,1)S(1)} %collective-permute-done.refs_1_), channel_id=1, source_target_pairs={{0,1},{1,2},{2,3},{3,4},{4,5},{5,6},{6,7},{7,0},{8,9},{9,10},{10,1... | collective-permute-start | bytes 786440 | tf_op jit(solution)/shard_map/ppermute | solution.py:164
  35.9 15.1 %collective-permute-start.3 = (bf16[512,256]{1,0:T(8,128)(2,1)S(1)}, bf16[512,256]{1,0:T(8,128)(2,1)S(1)}, u32[]{:S(2)}, u32[]{:S(2)}) collective-permute-start(bf16[512,256]{1,0:T(8,128)(2,1)S(1)} %collective-permute-done.1.refs_2_), channel_id=1, source_target_pairs={{0,7},{1,0},{2,1},{3,2},{4,3},{5,4},{6,5},{7,6},{8,15},{9,8},{10,9... | collective-permute-start | bytes 786440 | tf_op jit(solution)/shard_map/ppermute | solution.py:164
  40.5 27.6 %collective-permute-start.8 = (bf16[8,128,256]{2,1,0:T(8,128)(2,1)S(1)}, bf16[8,128,256]{2,1,0:T(8,128)(2,1)S(1)}, u32[]{:S(2)}, u32[]{:S(2)}) collective-permute-start(bf16[8,128,256]{2,1,0:T(8,128)(2,1)S(1)} %all-to-all-done.refs_9_), channel_id=1, source_target_pairs={{0,8},{8,0},{16,24},{24,16},{32,40},{40,32},{48,56},{56,48},{64,72... | collective-permute-start | bytes 1572872 | tf_op jit(solution)/shard_map/ppermute | solution.py:39
  49.0 10.5 %collective-permute-start.4 = (bf16[512,256]{1,0:T(8,128)(2,1)S(1)}, bf16[512,256]{1,0:T(8,128)(2,1)S(1)}, u32[]{:S(2)}, u32[]{:S(2)}) collective-permute-start(bf16[512,256]{1,0:T(8,128)(2,1)S(1)} %collective-permute-done.2.refs_3_), channel_id=1, source_target_pairs={{0,1},{1,2},{2,3},{3,4},{4,5},{5,6},{6,7},{7,0},{8,9},{9,10},{10,1... | collective-permute-start | bytes 786440 | tf_op jit(solution)/shard_map/ppermute | solution.py:164
  51.0 10.5 %collective-permute-start.5 = (bf16[512,256]{1,0:T(8,128)(2,1)S(1)}, bf16[512,256]{1,0:T(8,128)(2,1)S(1)}, u32[]{:S(2)}, u32[]{:S(2)}) collective-permute-start(bf16[512,256]{1,0:T(8,128)(2,1)S(1)} %collective-permute-done.3.refs_4_), channel_id=1, source_target_pairs={{0,7},{1,0},{2,1},{3,2},{4,3},{5,4},{6,5},{7,6},{8,15},{9,8},{10,9... | collective-permute-start | bytes 786440 | tf_op jit(solution)/shard_map/ppermute | solution.py:164
  59.6 7.6 %collective-permute-start.6 = (bf16[256,256]{1,0:T(8,128)(2,1)S(1)}, bf16[256,256]{1,0:T(8,128)(2,1)S(1)}, u32[]{:S(2)}, u32[]{:S(2)}) collective-permute-start(bf16[256,256]{1,0:T(8,128)(2,1)S(1)} %slice.8), channel_id=1, source_target_pairs={{0,1},{1,2},{2,3},{3,4},{4,5},{5,6},{6,7},{7,0},{8,9},{9,10},{10,1... | collective-permute-start | bytes 393224 | tf_op jit(solution)/shard_map/ppermute | solution.py:167
  61.5 6.5 %collective-permute-start.7 = (bf16[256,256]{1,0:T(8,128)(2,1)S(1)}, bf16[256,256]{1,0:T(8,128)(2,1)S(1)}, u32[]{:S(2)}, u32[]{:S(2)}) collective-permute-start(bf16[256,256]{1,0:T(8,128)(2,1)S(1)} %slice.9), channel_id=1, source_target_pairs={{0,7},{1,0},{2,1},{3,2},{4,3},{5,4},{6,5},{7,6},{8,15},{9,8},{10,9... | collective-permute-start | bytes 393224 | tf_op jit(solution)/shard_map/ppermute | solution.py:168
  67.2 3.1 %copy-start.2 = (bf16[256,256]{1,0:T(8,128)(2,1)}, bf16[256,256]{1,0:T(8,128)(2,1)S(1)}, u32[]{:S(2)}) copy-start(bf16[256,256]{1,0:T(8,128)(2,1)S(1)} %collective-permute-done.6.refs_7_) | copy-start | bytes 393220
  68.0 2.3 %copy-start.4 = (bf16[256,256]{1,0:T(8,128)(2,1)}, bf16[256,256]{1,0:T(8,128)(2,1)S(1)}, u32[]{:S(2)}) copy-start(bf16[256,256]{1,0:T(8,128)(2,1)S(1)} %collective-permute-done.7.refs_8_) | copy-start | bytes 393220
  70.3 42.0 %copy-start.8 = (s32[96]{0:T(128)S(1)}, s32[96]{0:T(128)}, u32[]{:S(2)}) copy-start(s32[96]{0:T(128)} %param.13) | copy-start | bytes 1156
  82.8 34.9 %all-to-all-start.2 = ((f32[96,1,128]{2,1,0:T(1,128)}), f32[96,1,128]{2,1,0:T(1,128)S(1)}, u32[]{:S(2)}, u32[]{:S(2)}) async-start(f32[96,1,128]{2,1,0:T(1,128)} %reward.1), calls=%async_computation.2 | async-start | bytes 98304 | tf_op jit(solution)/shard_map/all_to_all | solution.py:452
  105.5 0.9 copy-start.3
  106.4 0.9 copy-start.5
  109.8 8.1 %collective-permute-start.9 = (bf16[1152,256]{1,0:T(8,128)(2,1)}, bf16[1152,256]{1,0:T(8,128)(2,1)S(1)}, u32[]{:S(2)}, u32[]{:S(2)}) collective-permute-start(bf16[1152,256]{1,0:T(8,128)(2,1)} %get-tuple-element.32), channel_id=1, source_target_pairs={{0,8},{8,0},{16,24},{24,16},{32,40},{40,32},{48,56},{56,48},{64,72... | collective-permute-start | bytes 1769480 | tf_op jit(solution)/shard_map/ppermute | solution.py:39
  171.7 9.1 %collective-permute-start.10 = (bf16[1152,256]{1,0:T(8,128)(2,1)S(1)}, bf16[1152,256]{1,0:T(8,128)(2,1)S(1)}, u32[]{:S(2)}, u32[]{:S(2)}) collective-permute-start(bf16[1152,256]{1,0:T(8,128)(2,1)S(1)} %bitcast.19), channel_id=1, source_target_pairs={{0,8},{8,0},{16,24},{24,16},{32,40},{40,32},{48,56},{56,48},{64,72... | collective-permute-start | bytes 1769480 | tf_op jit(solution)/shard_map/ppermute | solution.py:39

commit v12 on v10

--- a/solution.py
+++ b/solution.py
@@ -309,7 +309,7 @@
     )(place, stats, resid, both, *shards)
 
 
-def weigh_kernel(place, costs_ref, order_ref, keep_ref, got_ref, out_ref, margin_ref, row_ref):
+def weigh_kernel(place, costs_ref, order_ref, keep_ref, got_ref, out_ref, loss_ref, row_ref):
     seqs = costs_ref.shape[0]
     rewards = -costs_ref[...].reshape(seqs, LANES)
     order = order_ref[...]
@@ -325,9 +325,12 @@
     own = jnp.sum(jnp.where(order == me, dreward, 0.0), axis=1, keepdims=True)
     sib = jnp.sum(jnp.where(order == (me ^ 1), dreward, 0.0), axis=1, keepdims=True)
     out_ref[...] = (keep_ref[...].astype(F32) * own + got_ref[...].astype(F32) * sib).astype(BF16)
-    margin_ref[...] = margin
+    each = jnp.maximum(-margin, 0.0) + jnp.log1p(jnp.exp(-jnp.abs(margin)))
+    counted = chosen & (lane < seqs)
+    loss_ref[...] = jnp.sum(jnp.where(counted, each, 0.0), axis=1, keepdims=True)
     at = lax.broadcasted_iota(jnp.int32, (seqs, LANES), 1)
-    row_ref[...] = jnp.sum(jnp.where(seq == at, rewards, 0.0), axis=0, keepdims=True)
+    row = jnp.sum(jnp.where(seq == at, rewards, 0.0), axis=0, keepdims=True)
+    row_ref[...] = row[:, :seqs]
 
 
 def weigh(place, costs, order, keep, got):
@@ -336,14 +339,18 @@
         weigh_kernel,
         out_shape=(
             jax.ShapeDtypeStruct(keep.shape, BF16),
-            jax.ShapeDtypeStruct((1, LANES), F32),
-            jax.ShapeDtypeStruct((1, LANES), F32),
+            jax.ShapeDtypeStruct((1, 1), F32),
+            jax.ShapeDtypeStruct((1, costs.shape[0]), F32),
         ),
         grid_spec=pltpu.PrefetchScalarGridSpec(
             num_scalar_prefetch=1,
             grid=(1,),
             in_specs=[flat(costs), flat(order), flat(keep), flat(got)],
-            out_specs=(flat(keep),) + (pl.BlockSpec((1, LANES), lambda i, s: (0, 0)),) * 2,
+            out_specs=(
+                flat(keep),
+                pl.BlockSpec((1, 1), lambda i, s: (0, 0)),
+                pl.BlockSpec((1, costs.shape[0]), lambda i, s: (0, 0)),
+            ),
         ),
         compiler_params=pltpu.CompilerParams(vmem_limit_bytes=16 * 2**20),
         cost_estimate=pl.CostEstimate(flops=1000000, bytes_accessed=2000000, transcendentals=128),
@@ -441,8 +448,7 @@
     got = to_sibling(send)
     seqs = pair_order.shape[0]
     order = jnp.pad(pair_order, (0, LANES - seqs), constant_values=-1)[None]
-    summed, margin, reward_row = weigh(place, costs, order, keep, got)
-    loss = jnp.sum(jax.nn.softplus(-margin[0, :seqs:2]))
+    summed, loss, reward_row = weigh(place, costs, order, keep, got)
 
     got = swap(summed.reshape(NX, NZ * piece, feat), along_x)
     summed = jnp.sum(got.astype(F32), axis=0).astype(BF16)
@@ -453,7 +459,7 @@
     got = got.reshape(half_ext, feat)
     other = to_sibling(got)
     grad_out_proj, grad_head, grad_gain = finish(place, got, other, gain_final, w_head, half)
-    return (loss, reward_row[0, :seqs], grad_out_proj, grad_head[0], grad_gain[0])
+    return (loss[0, 0], reward_row[0], grad_out_proj, grad_head[0], grad_gain[0])
 
 
 def solution(mesh):

time: 182 us -> 182 us (level)
  transfers between devices with their start and end apart: 14 -> 14, of which waited for: 6 -> 6; matrix products, arithmetic and copies ran while one was open for 3% -> 2% of each run, Pallas kernels for 1% -> 1%
where the time goes in v12:
time: 182 us; the launch traced here: 181 us
  starting transfers between devices  74.7 us (41%)
  blocking collectives  65.5 us (36%)
  Pallas kernels  17.8 us (10%)
  waiting for transfers between devices  12.1 us (7%)
  local copies, waits for them, and re-layouts  7.32 us (4%)
  other arithmetic  1.91 us (1%)
    all_to_all x4, blocking collectives, swap(): lax.all_to_all(parts, 'dp', 0, 0, tiled=True, axis_index_groups=groups)  52.7 us
    ppermute x3, starting transfers between devices, to_sibling(): return lax.ppermute(x, 'dp', pairs)  19.7 us
    all_to_all x1, starting transfers between devices, body(): costs = -lax.all_to_all(reward, 'dp', 0, 0, tiled=True)  17.6 us
    all_to_all x1, blocking collectives, body(): stats = lax.all_to_all(stats, 'mp', 0, 0, tiled=True)  12.8 us
    ppermute x3, starting transfers between devices, ring(): lax.ppermute(above, 'mp', down)  10.5 us
    ppermute x3, starting transfers between devices, ring(): lax.ppermute(below, 'mp', up)  8.96 us
    pallas_call x1, Pallas kernels, front(): pl.pallas_call(front_kernel, out_shape=jax.ShapeDtypeStruct((rows, w_quer...  8.27 us
    all_to_all x1, starting transfers between devices, body(): w_piece = lax.all_to_all(w_piece, 'mp', 0, 0, tiled=True)  7.65 us
  transfers between devices with their start and end apart: 14, of which 6 were waited for; matrix products, arithmetic and copies ran while one was open for 2% of the time, Pallas kernels for 1%

profile of v12, /device:TPU:1, one launch (start us, length us, event | category | flops | bytes accessed | tf_op | source)
XLA Modules:
  0.0 181.1 jit_solution(1657756020543558285)
XLA Ops:
  1.4 8.3 %front.1.refs_0_ = bf16[512,256]{1,0:T(8,128)(2,1)} custom-call(s32[1]{0:T(128)S(6)} %copy.20.lens, bf16[512,2048]{1,0:T(8,128)(2,1)} %x_hbm.1, f32[1,2048]{1,0:T(1,128)} %bitcast.36, bf16[2048,256]{1,0:T(8,128)(2,1)} %wq_hbm.1, bf16[64,2048]{1,0:T(8,128)(2,1)} %bitcast.34, bf16[64,2048]{1,0:T(8,128)(2,1)} %bitcast.35, f32[1,128]{1,0:T(1,128)} %constant.48.clone.freq_ref), custom_call_target="tpu_custom_call" | custom-call | flops 1500000000 | bytes 4000000 | tf_op jit(solution)/shard_map/front/pallas_call | solution.py:135
  10.5 7.6 %all-to-all-start = ((bf16[8,32,256]{2,1,0:T(8,128)(2,1)}), bf16[8,32,256]{2,1,0:T(8,128)(2,1)S(1)}, u32[]{:S(2)}, u32[]{:S(2)}) async-start(bf16[8,32,256]{2,1,0:T(8,128)(2,1)} %copy.18), calls=%async_computation | async-start | bytes 262144 | tf_op jit(solution)/shard_map/all_to_all | solution.py:430
  18.1 3.4 %collective-permute-start = (bf16[512,256]{1,0:T(8,128)(2,1)}, bf16[512,256]{1,0:T(8,128)(2,1)S(1)}, u32[]{:S(2)}, u32[]{:S(2)}) collective-permute-start(bf16[512,256]{1,0:T(8,128)(2,1)} %front.1.refs_0_), channel_id=1, source_target_pairs={{0,1},{1,2},{2,3},{3,4},{4,5},{5,6},{6,7},{7,0},{8,9},{9,10},{10,1... | collective-permute-start | bytes 786440 | tf_op jit(solution)/shard_map/ppermute | solution.py:165
  21.5 3.1 %collective-permute-start.1 = (bf16[512,256]{1,0:T(8,128)(2,1)}, bf16[512,256]{1,0:T(8,128)(2,1)S(1)}, u32[]{:S(2)}, u32[]{:S(2)}) collective-permute-start(bf16[512,256]{1,0:T(8,128)(2,1)} %front.1.refs_0_), channel_id=1, source_target_pairs={{0,7},{1,0},{2,1},{3,2},{4,3},{5,4},{6,5},{7,6},{8,15},{9,8},{10,9... | collective-permute-start | bytes 786440 | tf_op jit(solution)/shard_map/ppermute | solution.py:165
  24.6 1.5 all-to-all-done
  27.0 3.8 %all-to-all-start.1 = ((bf16[4,8,32,256]{3,2,1,0:T(8,128)(2,1)}), bf16[4,8,32,256]{3,2,1,0:T(8,128)(2,1)S(1)}, u32[]{:S(2)}, u32[]{:S(2)}) async-start(bf16[4,8,32,256]{3,2,1,0:T(8,128)(2,1)} %broadcast_in_dim.35), calls=%async_computation.1 | async-start | bytes 1048576 | tf_op jit(solution)/shard_map/all_to_all | solution.py:35
  30.8 2.3 %collective-permute-start.2 = (bf16[512,256]{1,0:T(8,128)(2,1)S(1)}, bf16[512,256]{1,0:T(8,128)(2,1)S(1)}, u32[]{:S(2)}, u32[]{:S(2)}) collective-permute-start(bf16[512,256]{1,0:T(8,128)(2,1)S(1)} %collective-permute-done.refs_1_), channel_id=1, source_target_pairs={{0,1},{1,2},{2,3},{3,4},{4,5},{5,6},{6,7},{7,0},{8,9},{9,10},{10,1... | collective-permute-start | bytes 786440 | tf_op jit(solution)/shard_map/ppermute | solution.py:165
  33.1 4.2 %collective-permute-start.3 = (bf16[512,256]{1,0:T(8,128)(2,1)S(1)}, bf16[512,256]{1,0:T(8,128)(2,1)S(1)}, u32[]{:S(2)}, u32[]{:S(2)}) collective-permute-start(bf16[512,256]{1,0:T(8,128)(2,1)S(1)} %collective-permute-done.1.refs_2_), channel_id=1, source_target_pairs={{0,7},{1,0},{2,1},{3,2},{4,3},{5,4},{6,5},{7,6},{8,15},{9,8},{10,9... | collective-permute-start | bytes 786440 | tf_op jit(solution)/shard_map/ppermute | solution.py:165
  37.7 9.6 %collective-permute-start.8 = (bf16[4,8,32,256]{3,2,1,0:T(8,128)(2,1)S(1)}, bf16[4,8,32,256]{3,2,1,0:T(8,128)(2,1)}, u32[]{:S(2)}, u32[]{:S(2)}) collective-permute-start(bf16[4,8,32,256]{3,2,1,0:T(8,128)(2,1)S(1)} %all-to-all-done.1.refs_9_), channel_id=1, source_target_pairs={{0,8},{8,0},{16,24},{24,16},{32,40},{40,32},{48,56},{56,48},{64,72... | collective-permute-start | bytes 1572872 | tf_op jit(solution)/shard_map/ppermute | solution.py:40
  47.3 3.3 %collective-permute-start.4 = (bf16[512,256]{1,0:T(8,128)(2,1)S(1)}, bf16[512,256]{1,0:T(8,128)(2,1)S(1)}, u32[]{:S(2)}, u32[]{:S(2)}) collective-permute-start(bf16[512,256]{1,0:T(8,128)(2,1)S(1)} %collective-permute-done.2.refs_3_), channel_id=1, source_target_pairs={{0,1},{1,2},{2,3},{3,4},{4,5},{5,6},{6,7},{7,0},{8,9},{9,10},{10,1... | collective-permute-start | bytes 786440 | tf_op jit(solution)/shard_map/ppermute | solution.py:165
  50.6 3.2 %collective-permute-start.5 = (bf16[512,256]{1,0:T(8,128)(2,1)S(1)}, bf16[512,256]{1,0:T(8,128)(2,1)S(1)}, u32[]{:S(2)}, u32[]{:S(2)}) collective-permute-start(bf16[512,256]{1,0:T(8,128)(2,1)S(1)} %collective-permute-done.3.refs_4_), channel_id=1, source_target_pairs={{0,7},{1,0},{2,1},{3,2},{4,3},{5,4},{6,5},{7,6},{8,15},{9,8},{10,9... | collective-permute-start | bytes 786440 | tf_op jit(solution)/shard_map/ppermute | solution.py:165
  54.6 3.7 %collective-permute-done.4.refs_5_ = bf16[512,256]{1,0:T(8,128)(2,1)S(1)} collective-permute-done((bf16[512,256]{1,0:T(8,128)(2,1)S(1)}, bf16[512,256]{1,0:T(8,128)(2,1)S(1)}, u32[]{:S(2)}, u32[]{:S(2)}) %collective-permute-start.4) | collective-permute-done | bytes 262176 | tf_op jit(solution)/shard_map/ppermute | solution.py:165
  58.4 2.1 %collective-permute-start.6 = (bf16[256,256]{1,0:T(8,128)(2,1)S(1)}, bf16[256,256]{1,0:T(8,128)(2,1)S(1)}, u32[]{:S(2)}, u32[]{:S(2)}) collective-permute-start(bf16[256,256]{1,0:T(8,128)(2,1)S(1)} %slice.8), channel_id=1, source_target_pairs={{0,1},{1,2},{2,3},{3,4},{4,5},{5,6},{6,7},{7,0},{8,9},{9,10},{10,1... | collective-permute-start | bytes 393224 | tf_op jit(solution)/shard_map/ppermute | solution.py:168
  60.5 4.4 %collective-permute-start.7 = (bf16[256,256]{1,0:T(8,128)(2,1)S(1)}, bf16[256,256]{1,0:T(8,128)(2,1)S(1)}, u32[]{:S(2)}, u32[]{:S(2)}) collective-permute-start(bf16[256,256]{1,0:T(8,128)(2,1)S(1)} %slice.9), channel_id=1, source_target_pairs={{0,7},{1,0},{2,1},{3,2},{4,3},{5,4},{6,5},{7,6},{8,15},{9,8},{10,9... | collective-permute-start | bytes 393224 | tf_op jit(solution)/shard_map/ppermute | solution.py:169
  65.0 1.0 constant_dynamic-slice_fusion.refs_11_
  66.8 2.8 %project.1 = (f32[512,256]{1,0:T(8,128)S(1)}, f32[8,2,512]{2,1,0:T(2,128)S(1)}) custom-call(s32[4]{0:T(128)S(1)} %pad_add_fusion.place, bf16[512,256]{1,0:T(8,128)(2,1)S(1)} %copy-done.1, bf16[512,256]{1,0:T(8,128)(2,1)S(1)} %collective-permute-done.refs_1_, bf16[512,256]{1,0:T(8,128)(2,1)S(1)} %collective-permute-done.1.refs_2_, ...), custom_call_target="tpu_custom_call" | custom-call | flops 550000000 | bytes 4000000 | tf_op jit(solution)/shard_map/project/pallas_call | solution.py:209
  70.5 12.8 %all_to_all.40.stats_ref = f32[8,2,512]{2,1,0:T(2,128)S(1)} all-to-all(f32[8,2,512]{2,1,0:T(2,128)S(1)} %get-tuple-element.27), channel_id=1, replica_groups=mesh['dp'=96,'mp'=8] {'mp'}, dimensions={0} | all-to-all | bytes 65536 | tf_op jit(solution)/shard_map/all_to_all | solution.py:438
  84.0 17.6 %all-to-all-start.3 = ((f32[96,1,128]{2,1,0:T(1,128)}), f32[96,1,128]{2,1,0:T(1,128)}, u32[]{:S(2)}, u32[]{:S(2)}) async-start(f32[96,1,128]{2,1,0:T(1,128)} %reward.1), calls=%async_computation.3 | async-start | bytes 98304 | tf_op jit(solution)/shard_map/all_to_all | solution.py:440
  101.6 1.0 copy-done.5
  102.7 0.9 copy-done.7
  103.6 2.4 %gradient.1 = (bf16[1152,256]{1,0:T(8,128)(2,1)}, bf16[1152,256]{1,0:T(8,128)(2,1)S(1)}) custom-call(s32[4]{0:T(128)S(1)} %pad_add_fusion.place, f32[8,2,512]{2,1,0:T(2,128)S(1)} %all_to_all.40.stats_ref, f32[512,256]{1,0:T(8,128)S(1)} %copy-done.5, f32[1,256]{1,0:T(1,128)S(1)} %bitcast.29, bf16[512,256]{1,0:T(8,128)(2,1)S(1)} %copy-done.1, ...), custom_call_target="tpu_custom_call" | custom-call | flops 550000000 | bytes 4000000 | tf_op jit(solution)/shard_map/gradient/pallas_call | solution.py:300
  106.9 2.6 %collective-permute-start.9 = (bf16[1152,256]{1,0:T(8,128)(2,1)}, bf16[1152,256]{1,0:T(8,128)(2,1)S(1)}, u32[]{:S(2)}, u32[]{:S(2)}) collective-permute-start(bf16[1152,256]{1,0:T(8,128)(2,1)} %get-tuple-element.32), channel_id=1, source_target_pairs={{0,8},{8,0},{16,24},{24,16},{32,40},{40,32},{48,56},{56,48},{64,72... | collective-permute-start | bytes 1769480 | tf_op jit(solution)/shard_map/ppermute | solution.py:40
  109.5 3.9 %all-to-all-done.3 = f32[96,1,128]{2,1,0:T(1,128)} async-done(((f32[96,1,128]{2,1,0:T(1,128)}), f32[96,1,128]{2,1,0:T(1,128)}, u32[]{:S(2)}, u32[]{:S(2)}) %all-to-all-start.3) | async-done | bytes 49184 | tf_op jit(solution)/shard_map/all_to_all | solution.py:440
  114.4 1.1 copy-done.3
  115.5 1.6 weigh.1
  117.1 11.4 %all_to_all.41 = bf16[4,288,256]{2,1,0:T(8,128)(2,1)S(1)} all-to-all(bf16[4,288,256]{2,1,0:T(8,128)(2,1)S(1)} %bitcast.25), channel_id=1, replica_groups={{0,192,384,576},{8,200,392,584},{16,208,400,592},{24,216,408,600},{32,2..., dimensions={0} | all-to-all | bytes 1179648 | tf_op jit(solution)/shard_map/all_to_all | solution.py:35
  128.6 18.5 %all_to_all.42 = bf16[12,24,256]{2,1,0:T(8,128)(2,1)S(1)} all-to-all(bf16[12,24,256]{2,1,0:T(8,128)(2,1)S(1)} %bitcast.30), channel_id=1, replica_groups={{0,16,32,48,64,80,96,112,128,144,160,176},{8,24,40,56,72,88,104,120,136..., dimensions={0} | all-to-all | bytes 294912 | tf_op jit(solution)/shard_map/all_to_all | solution.py:35
  147.2 13.1 %all_to_all.43 = bf16[12,24,256]{2,1,0:T(8,128)(2,1)S(1)} all-to-all(bf16[12,24,256]{2,1,0:T(8,128)(2,1)S(1)} %broadcast_in_dim.38), channel_id=1, replica_groups={{0,16,32,48,64,80,96,112,128,144,160,176},{8,24,40,56,72,88,104,120,136..., dimensions={0} | all-to-all | bytes 294912 | tf_op jit(solution)/shard_map/all_to_all | solution.py:35
  160.3 9.7 %all_to_all.44 = bf16[4,288,256]{2,1,0:T(8,128)(2,1)S(1)} all-to-all(bf16[4,288,256]{2,1,0:T(8,128)(2,1)S(1)} %broadcast_in_dim.40), channel_id=1, replica_groups={{0,192,384,576},{8,200,392,584},{16,208,400,592},{24,216,408,600},{32,2..., dimensions={0} | all-to-all | bytes 1179648 | tf_op jit(solution)/shard_map/all_to_all | solution.py:35
  170.0 7.5 %collective-permute-start.10 = (bf16[1152,256]{1,0:T(8,128)(2,1)S(1)}, bf16[1152,256]{1,0:T(8,128)(2,1)S(1)}, u32[]{:S(2)}, u32[]{:S(2)}) collective-permute-start(bf16[1152,256]{1,0:T(8,128)(2,1)S(1)} %bitcast.23), channel_id=1, source_target_pairs={{0,8},{8,0},{16,24},{24,16},{32,40},{40,32},{48,56},{56,48},{64,72... | collective-permute-start | bytes 1769480 | tf_op jit(solution)/shard_map/ppermute | solution.py:40
  177.5 1.6 collective-permute-done.10.other_ref
  179.1 2.0 %finish.1 = (f32[2048,256]{1,0:T(8,128)}, f32[1,256]{1,0:T(1,128)}, f32[1,256]{1,0:T(1,128)}) custom-call(s32[4]{0:T(128)S(1)} %pad_add_fusion.place, bf16[1152,256]{1,0:T(8,128)(2,1)S(1)} %bitcast.24, bf16[1152,256]{1,0:T(8,128)(2,1)S(1)} %collective-permute-done.10.other_ref, f32[1,2048]{1,0:T(1,128)S(1)} %bitcast.27, f32[1,2048]{1,0:T(1,128)S(1)} %bitcast.26), custom_call_target="tpu_custom_call" | custom-call | flops 1000000 | bytes 4000000 | tf_op jit(solution)/shard_map/finish/pallas_call | solution.py:382
  (46 shorter events, 7.3 us)
Async XLA Ops:
  0.6 9.1 %copy-start = (bf16[256,2048]{1,0:T(8,128)(2,1)S(1)}, bf16[256,2048]{1,0:T(8,128)(2,1)}, u32[]{:S(2)}) copy-start(bf16[256,2048]{1,0:T(8,128)(2,1)} %param.18) | copy-start | bytes 3145732
  9.7 44.1 %copy-start.8 = (f32[2048]{0:T(1024)S(1)}, f32[2048]{0:T(1024)}, u32[]{:S(2)}) copy-start(f32[2048]{0:T(1024)} %param.20) | copy-start | bytes 24580
  9.7 57.1 %copy-start.1 = (bf16[512,256]{1,0:T(8,128)(2,1)S(1)}, bf16[512,256]{1,0:T(8,128)(2,1)}, u32[]{:S(2)}) copy-start(bf16[512,256]{1,0:T(8,128)(2,1)} %front.1.refs_0_) | copy-start | bytes 786436
  10.5 15.7 %all-to-all-start = ((bf16[8,32,256]{2,1,0:T(8,128)(2,1)}), bf16[8,32,256]{2,1,0:T(8,128)(2,1)S(1)}, u32[]{:S(2)}, u32[]{:S(2)}) async-start(bf16[8,32,256]{2,1,0:T(8,128)(2,1)} %copy.18), calls=%async_computation | async-start | bytes 262144 | tf_op jit(solution)/shard_map/all_to_all | solution.py:430
  18.1 12.7 %collective-permute-start = (bf16[512,256]{1,0:T(8,128)(2,1)}, bf16[512,256]{1,0:T(8,128)(2,1)S(1)}, u32[]{:S(2)}, u32[]{:S(2)}) collective-permute-start(bf16[512,256]{1,0:T(8,128)(2,1)} %front.1.refs_0_), channel_id=1, source_target_pairs={{0,1},{1,2},{2,3},{3,4},{4,5},{5,6},{6,7},{7,0},{8,9},{9,10},{10,1... | collective-permute-start | bytes 786440 | tf_op jit(solution)/shard_map/ppermute | solution.py:165
  21.5 11.6 %collective-permute-start.1 = (bf16[512,256]{1,0:T(8,128)(2,1)}, bf16[512,256]{1,0:T(8,128)(2,1)S(1)}, u32[]{:S(2)}, u32[]{:S(2)}) collective-permute-start(bf16[512,256]{1,0:T(8,128)(2,1)} %front.1.refs_0_), channel_id=1, source_target_pairs={{0,7},{1,0},{2,1},{3,2},{4,3},{5,4},{6,5},{7,6},{8,15},{9,8},{10,9... | collective-permute-start | bytes 786440 | tf_op jit(solution)/shard_map/ppermute | solution.py:165
  27.0 10.7 %all-to-all-start.1 = ((bf16[4,8,32,256]{3,2,1,0:T(8,128)(2,1)}), bf16[4,8,32,256]{3,2,1,0:T(8,128)(2,1)S(1)}, u32[]{:S(2)}, u32[]{:S(2)}) async-start(bf16[4,8,32,256]{3,2,1,0:T(8,128)(2,1)} %broadcast_in_dim.35), calls=%async_computation.1 | async-start | bytes 1048576 | tf_op jit(solution)/shard_map/all_to_all | solution.py:35
  30.8 16.5 %collective-permute-start.2 = (bf16[512,256]{1,0:T(8,128)(2,1)S(1)}, bf16[512,256]{1,0:T(8,128)(2,1)S(1)}, u32[]{:S(2)}, u32[]{:S(2)}) collective-permute-start(bf16[512,256]{1,0:T(8,128)(2,1)S(1)} %collective-permute-done.refs_1_), channel_id=1, source_target_pairs={{0,1},{1,2},{2,3},{3,4},{4,5},{5,6},{6,7},{7,0},{8,9},{9,10},{10,1... | collective-permute-start | bytes 786440 | tf_op jit(solution)/shard_map/ppermute | solution.py:165
  33.1 17.5 %collective-permute-start.3 = (bf16[512,256]{1,0:T(8,128)(2,1)S(1)}, bf16[512,256]{1,0:T(8,128)(2,1)S(1)}, u32[]{:S(2)}, u32[]{:S(2)}) collective-permute-start(bf16[512,256]{1,0:T(8,128)(2,1)S(1)} %collective-permute-done.1.refs_2_), channel_id=1, source_target_pairs={{0,7},{1,0},{2,1},{3,2},{4,3},{5,4},{6,5},{7,6},{8,15},{9,8},{10,9... | collective-permute-start | bytes 786440 | tf_op jit(solution)/shard_map/ppermute | solution.py:165
  37.7 29.1 %collective-permute-start.8 = (bf16[4,8,32,256]{3,2,1,0:T(8,128)(2,1)S(1)}, bf16[4,8,32,256]{3,2,1,0:T(8,128)(2,1)}, u32[]{:S(2)}, u32[]{:S(2)}) collective-permute-start(bf16[4,8,32,256]{3,2,1,0:T(8,128)(2,1)S(1)} %all-to-all-done.1.refs_9_), channel_id=1, source_target_pairs={{0,8},{8,0},{16,24},{24,16},{32,40},{40,32},{48,56},{56,48},{64,72... | collective-permute-start | bytes 1572872 | tf_op jit(solution)/shard_map/ppermute | solution.py:40
  47.3 11.0 %collective-permute-start.4 = (bf16[512,256]{1,0:T(8,128)(2,1)S(1)}, bf16[512,256]{1,0:T(8,128)(2,1)S(1)}, u32[]{:S(2)}, u32[]{:S(2)}) collective-permute-start(bf16[512,256]{1,0:T(8,128)(2,1)S(1)} %collective-permute-done.2.refs_3_), channel_id=1, source_target_pairs={{0,1},{1,2},{2,3},{3,4},{4,5},{5,6},{6,7},{7,0},{8,9},{9,10},{10,1... | collective-permute-start | bytes 786440 | tf_op jit(solution)/shard_map/ppermute | solution.py:165
  50.6 9.8 %collective-permute-start.5 = (bf16[512,256]{1,0:T(8,128)(2,1)S(1)}, bf16[512,256]{1,0:T(8,128)(2,1)S(1)}, u32[]{:S(2)}, u32[]{:S(2)}) collective-permute-start(bf16[512,256]{1,0:T(8,128)(2,1)S(1)} %collective-permute-done.3.refs_4_), channel_id=1, source_target_pairs={{0,7},{1,0},{2,1},{3,2},{4,3},{5,4},{6,5},{7,6},{8,15},{9,8},{10,9... | collective-permute-start | bytes 786440 | tf_op jit(solution)/shard_map/ppermute | solution.py:165
  58.4 7.6 %collective-permute-start.6 = (bf16[256,256]{1,0:T(8,128)(2,1)S(1)}, bf16[256,256]{1,0:T(8,128)(2,1)S(1)}, u32[]{:S(2)}, u32[]{:S(2)}) collective-permute-start(bf16[256,256]{1,0:T(8,128)(2,1)S(1)} %slice.8), channel_id=1, source_target_pairs={{0,1},{1,2},{2,3},{3,4},{4,5},{5,6},{6,7},{7,0},{8,9},{9,10},{10,1... | collective-permute-start | bytes 393224 | tf_op jit(solution)/shard_map/ppermute | solution.py:168
  60.5 6.3 %collective-permute-start.7 = (bf16[256,256]{1,0:T(8,128)(2,1)S(1)}, bf16[256,256]{1,0:T(8,128)(2,1)S(1)}, u32[]{:S(2)}, u32[]{:S(2)}) collective-permute-start(bf16[256,256]{1,0:T(8,128)(2,1)S(1)} %slice.9), channel_id=1, source_target_pairs={{0,7},{1,0},{2,1},{3,2},{4,3},{5,4},{6,5},{7,6},{8,15},{9,8},{10,9... | collective-permute-start | bytes 393224 | tf_op jit(solution)/shard_map/ppermute | solution.py:169
  66.8 2.8 %copy-start.6 = (bf16[256,256]{1,0:T(8,128)(2,1)}, bf16[256,256]{1,0:T(8,128)(2,1)S(1)}, u32[]{:S(2)}) copy-start(bf16[256,256]{1,0:T(8,128)(2,1)S(1)} %collective-permute-done.7.refs_8_) | copy-start | bytes 393220
  69.7 0.8 copy-start.4
  70.5 39.1 %copy-start.10 = (s32[96]{0:T(128)S(1)}, s32[96]{0:T(128)}, u32[]{:S(2)}) copy-start(s32[96]{0:T(128)} %param.13) | copy-start | bytes 1156
  84.0 29.4 %all-to-all-start.3 = ((f32[96,1,128]{2,1,0:T(1,128)}), f32[96,1,128]{2,1,0:T(1,128)}, u32[]{:S(2)}, u32[]{:S(2)}) async-start(f32[96,1,128]{2,1,0:T(1,128)} %reward.1), calls=%async_computation.3 | async-start | bytes 98304 | tf_op jit(solution)/shard_map/all_to_all | solution.py:440
  101.6 1.0 copy-start.5
  102.7 0.9 copy-start.7
  106.0 0.9 copy-start.2
  106.9 7.5 %collective-permute-start.9 = (bf16[1152,256]{1,0:T(8,128)(2,1)}, bf16[1152,256]{1,0:T(8,128)(2,1)S(1)}, u32[]{:S(2)}, u32[]{:S(2)}) collective-permute-start(bf16[1152,256]{1,0:T(8,128)(2,1)} %get-tuple-element.32), channel_id=1, source_target_pairs={{0,8},{8,0},{16,24},{24,16},{32,40},{40,32},{48,56},{56,48},{64,72... | collective-permute-start | bytes 1769480 | tf_op jit(solution)/shard_map/ppermute | solution.py:40
  114.4 1.1 copy-start.3
  117.1 62.0 %copy-start.9 = (f32[2048]{0:T(1024)S(1)}, f32[2048]{0:T(1024)}, u32[]{:S(2)}) copy-start(f32[2048]{0:T(1024)} %param.19) | copy-start | bytes 24580
  170.0 9.1 %collective-permute-start.10 = (bf16[1152,256]{1,0:T(8,128)(2,1)S(1)}, bf16[1152,256]{1,0:T(8,128)(2,1)S(1)}, u32[]{:S(2)}, u32[]{:S(2)}) collective-permute-start(bf16[1152,256]{1,0:T(8,128)(2,1)S(1)} %bitcast.23), channel_id=1, source_target_pairs={{0,8},{8,0},{16,24},{24,16},{32,40},{40,32},{48,56},{56,48},{64,72... | collective-permute-start | bytes 1769480 | tf_op jit(solution)/shard_map/ppermute | solution.py:40

commit v13 on v12

--- a/solution.py
+++ b/solution.py
@@ -156,18 +156,20 @@
     )(lengths, hidden_rows, gain, w_query, key_weight, value_weight, jnp.asarray(freq))
 
 
-def ring(x):
+def ring(x, beside):
     n = lax.axis_size("mp")
     up = [(i, (i + 1) % n) for i in range(n)]
     down = [(i, (i - 1) % n) for i in range(n)]
     parts, below, above = [(0, x)], x, x
     for step in range(1, n // 2):
         below, above = lax.ppermute(below, "mp", up), lax.ppermute(above, "mp", down)
+        if step == 1:
+            below, beside = lax.optimization_barrier((below, beside))
         parts += [(-step, below), (step, above)]
     half = x.shape[0] // 2
     first = lax.ppermute(below[:half], "mp", up)
     second = lax.ppermute(above[half:], "mp", down)
-    return parts + [(n // 2, (first, second))]
+    return parts + [(n // 2, (first, second))], beside
 
 
 def flatten(parts):
@@ -427,11 +429,11 @@
     my_near = (me // (NZ * NCORE)) * NCORE + core
     w_piece = lax.dynamic_slice_in_dim(w_out, my_near * piece_rows, piece_rows, 0)
     w_piece = w_piece.reshape(piece_rows, n_mp, feat).swapaxes(0, 1)
+    parts, w_piece = ring(mixed, w_piece)
     w_piece = lax.all_to_all(w_piece, "mp", 0, 0, tiled=True)
     w_mine = swap(jnp.broadcast_to(w_piece[None], (NX,) + w_piece.shape), along_x)
     w_other = to_sibling(w_mine)
 
-    parts = ring(mixed)
     x_cols = lax.dynamic_slice_in_dim(hidden_rows, place[0] * feat, feat, 1)
     both = lax.dynamic_slice_in_dim(gain_final * w_head, place[0] * feat, feat, 0)[None]
     resid, stats = project(place, parts, w_mine, w_other, x_cols, both)

time: 182 us -> 193 us (1.060)
  waiting for transfers between devices: 12.1 us -> 18.4 us
  starting transfers between devices: 74.7 us -> 78.8 us
    ppermute x3, waiting for transfers between devices: 3.74 us -> 9.47 us  [ring(): lax.ppermute(below, 'mp', up)]
    ppermute x3, starting transfers between devices: 10.5 us -> 13.1 us  [ring(): lax.ppermute(above, 'mp', down)]
    unnamed x23 -> x25, local copies, waits for them, and re-layouts: 4.72 us -> 5.48 us
  transfers between devices with their start and end apart: 14 -> 14, of which waited for: 6 -> 7; matrix products, arithmetic and copies ran while one was open for 2% -> 2% of each run, Pallas kernels for 1% -> 1%
where the time goes in v13:
time: 193 us; the launch traced here: 192 us
  starting transfers between devices  78.8 us (41%)
  blocking collectives  64.4 us (33%)
  waiting for transfers between devices  18.4 us (10%)
  Pallas kernels  17.8 us (9%)
  local copies, waits for them, and re-layouts  8.73 us (5%)
    all_to_all x4, blocking collectives, swap(): lax.all_to_all(parts, 'dp', 0, 0, tiled=True, axis_index_groups=groups)  53.3 us
    all_to_all x1, starting transfers between devices, body(): costs = -lax.all_to_all(reward, 'dp', 0, 0, tiled=True)  19.2 us
    ppermute x3, starting transfers between devices, to_sibling(): return lax.ppermute(x, 'dp', pairs)  19.1 us
    ppermute x3, starting transfers between devices, ring(): lax.ppermute(above, 'mp', down)  13.1 us
    all_to_all x1, blocking collectives, body(): stats = lax.all_to_all(stats, 'mp', 0, 0, tiled=True)  11.1 us
    ppermute x3, waiting for transfers between devices, ring(): lax.ppermute(below, 'mp', up)  9.47 us
    ppermute x3, starting transfers between devices, ring(): lax.ppermute(below, 'mp', up)  8.63 us
    pallas_call x1, Pallas kernels, front(): pl.pallas_call(front_kernel, out_shape=jax.ShapeDtypeStruct((rows, w_quer...  8.28 us
  transfers between devices with their start and end apart: 14, of which 7 were waited for; matrix products, arithmetic and copies ran while one was open for 2% of the time, Pallas kernels for 1%

profile of v13, /device:TPU:1, one launch (start us, length us, event | category | flops | bytes accessed | tf_op | source)
XLA Modules:
  0.0 191.8 jit_solution(1534942579875396987)
XLA Ops:
  1.4 8.3 %front.1.refs_0_ = bf16[512,256]{1,0:T(8,128)(2,1)} custom-call(s32[1]{0:T(128)S(6)} %copy.20.lens, bf16[512,2048]{1,0:T(8,128)(2,1)} %x_hbm.1, f32[1,2048]{1,0:T(1,128)} %bitcast.36, bf16[2048,256]{1,0:T(8,128)(2,1)} %wq_hbm.1, bf16[64,2048]{1,0:T(8,128)(2,1)} %bitcast.34, bf16[64,2048]{1,0:T(8,128)(2,1)} %bitcast.35, f32[1,128]{1,0:T(1,128)} %constant.48.clone.freq_ref), custom_call_target="tpu_custom_call" | custom-call | flops 1500000000 | bytes 4000000 | tf_op jit(solution)/shard_map/front/pallas_call | solution.py:135
  9.7 4.2 %collective-permute-start = (bf16[512,256]{1,0:T(8,128)(2,1)}, bf16[512,256]{1,0:T(8,128)(2,1)S(1)}, u32[]{:S(2)}, u32[]{:S(2)}) collective-permute-start(bf16[512,256]{1,0:T(8,128)(2,1)} %front.1.refs_0_), channel_id=1, source_target_pairs={{0,1},{1,2},{2,3},{3,4},{4,5},{5,6},{6,7},{7,0},{8,9},{9,10},{10,1... | collective-permute-start | bytes 786440 | tf_op jit(solution)/shard_map/ppermute | solution.py:165
  14.0 5.7 %collective-permute-done.refs_1_ = bf16[512,256]{1,0:T(8,128)(2,1)S(1)} collective-permute-done((bf16[512,256]{1,0:T(8,128)(2,1)}, bf16[512,256]{1,0:T(8,128)(2,1)S(1)}, u32[]{:S(2)}, u32[]{:S(2)}) %collective-permute-start) | collective-permute-done | bytes 262176 | tf_op jit(solution)/shard_map/ppermute | solution.py:165
  20.4 8.3 %all-to-all-start = ((bf16[8,32,256]{2,1,0:T(8,128)(2,1)}), bf16[8,32,256]{2,1,0:T(8,128)(2,1)S(1)}, u32[]{:S(2)}, u32[]{:S(2)}) async-start(bf16[8,32,256]{2,1,0:T(8,128)(2,1)} %copy.18), calls=%async_computation | async-start | bytes 262144 | tf_op jit(solution)/shard_map/all_to_all | solution.py:433
  28.7 4.6 %collective-permute-start.1 = (bf16[512,256]{1,0:T(8,128)(2,1)}, bf16[512,256]{1,0:T(8,128)(2,1)S(1)}, u32[]{:S(2)}, u32[]{:S(2)}) collective-permute-start(bf16[512,256]{1,0:T(8,128)(2,1)} %front.1.refs_0_), channel_id=1, source_target_pairs={{0,7},{1,0},{2,1},{3,2},{4,3},{5,4},{6,5},{7,6},{8,15},{9,8},{10,9... | collective-permute-start | bytes 786440 | tf_op jit(solution)/shard_map/ppermute | solution.py:165
  33.2 3.4 %all-to-all-done = bf16[8,32,256]{2,1,0:T(8,128)(2,1)S(1)} async-done(((bf16[8,32,256]{2,1,0:T(8,128)(2,1)}), bf16[8,32,256]{2,1,0:T(8,128)(2,1)S(1)}, u32[]{:S(2)}, u32[]{:S(2)}) %all-to-all-start) | async-done | bytes 131104 | tf_op jit(solution)/shard_map/all_to_all | solution.py:433
  37.4 4.0 %all-to-all-start.1 = ((bf16[4,8,32,256]{3,2,1,0:T(8,128)(2,1)}), bf16[4,8,32,256]{3,2,1,0:T(8,128)(2,1)S(1)}, u32[]{:S(2)}, u32[]{:S(2)}) async-start(bf16[4,8,32,256]{3,2,1,0:T(8,128)(2,1)} %broadcast_in_dim.35), calls=%async_computation.1 | async-start | bytes 1048576 | tf_op jit(solution)/shard_map/all_to_all | solution.py:35
  41.4 2.2 %collective-permute-start.2 = (bf16[512,256]{1,0:T(8,128)(2,1)S(1)}, bf16[512,256]{1,0:T(8,128)(2,1)S(1)}, u32[]{:S(2)}, u32[]{:S(2)}) collective-permute-start(bf16[512,256]{1,0:T(8,128)(2,1)S(1)} %collective-permute-done.refs_1_), channel_id=1, source_target_pairs={{0,1},{1,2},{2,3},{3,4},{4,5},{5,6},{6,7},{7,0},{8,9},{9,10},{10,1... | collective-permute-start | bytes 786440 | tf_op jit(solution)/shard_map/ppermute | solution.py:165
  43.7 4.3 %collective-permute-start.3 = (bf16[512,256]{1,0:T(8,128)(2,1)S(1)}, bf16[512,256]{1,0:T(8,128)(2,1)S(1)}, u32[]{:S(2)}, u32[]{:S(2)}) collective-permute-start(bf16[512,256]{1,0:T(8,128)(2,1)S(1)} %collective-permute-done.1.refs_2_), channel_id=1, source_target_pairs={{0,7},{1,0},{2,1},{3,2},{4,3},{5,4},{6,5},{7,6},{8,15},{9,8},{10,9... | collective-permute-start | bytes 786440 | tf_op jit(solution)/shard_map/ppermute | solution.py:165
  48.4 9.0 %collective-permute-start.8 = (bf16[4,8,32,256]{3,2,1,0:T(8,128)(2,1)S(1)}, bf16[4,8,32,256]{3,2,1,0:T(8,128)(2,1)}, u32[]{:S(2)}, u32[]{:S(2)}) collective-permute-start(bf16[4,8,32,256]{3,2,1,0:T(8,128)(2,1)S(1)} %all-to-all-done.1.refs_9_), channel_id=1, source_target_pairs={{0,8},{8,0},{16,24},{24,16},{32,40},{40,32},{48,56},{56,48},{64,72... | collective-permute-start | bytes 1572872 | tf_op jit(solution)/shard_map/ppermute | solution.py:40
  57.4 2.3 %collective-permute-start.4 = (bf16[512,256]{1,0:T(8,128)(2,1)S(1)}, bf16[512,256]{1,0:T(8,128)(2,1)S(1)}, u32[]{:S(2)}, u32[]{:S(2)}) collective-permute-start(bf16[512,256]{1,0:T(8,128)(2,1)S(1)} %collective-permute-done.2.refs_3_), channel_id=1, source_target_pairs={{0,1},{1,2},{2,3},{3,4},{4,5},{5,6},{6,7},{7,0},{8,9},{9,10},{10,1... | collective-permute-start | bytes 786440 | tf_op jit(solution)/shard_map/ppermute | solution.py:165
  59.7 4.2 %collective-permute-start.5 = (bf16[512,256]{1,0:T(8,128)(2,1)S(1)}, bf16[512,256]{1,0:T(8,128)(2,1)S(1)}, u32[]{:S(2)}, u32[]{:S(2)}) collective-permute-start(bf16[512,256]{1,0:T(8,128)(2,1)S(1)} %collective-permute-done.3.refs_4_), channel_id=1, source_target_pairs={{0,7},{1,0},{2,1},{3,2},{4,3},{5,4},{6,5},{7,6},{8,15},{9,8},{10,9... | collective-permute-start | bytes 786440 | tf_op jit(solution)/shard_map/ppermute | solution.py:165
  64.7 3.7 %collective-permute-done.4.refs_5_ = bf16[512,256]{1,0:T(8,128)(2,1)S(1)} collective-permute-done((bf16[512,256]{1,0:T(8,128)(2,1)S(1)}, bf16[512,256]{1,0:T(8,128)(2,1)S(1)}, u32[]{:S(2)}, u32[]{:S(2)}) %collective-permute-start.4) | collective-permute-done | bytes 262176 | tf_op jit(solution)/shard_map/ppermute | solution.py:165
  68.4 1.9 %collective-permute-start.6 = (bf16[256,256]{1,0:T(8,128)(2,1)S(1)}, bf16[256,256]{1,0:T(8,128)(2,1)S(1)}, u32[]{:S(2)}, u32[]{:S(2)}) collective-permute-start(bf16[256,256]{1,0:T(8,128)(2,1)S(1)} %slice.8), channel_id=1, source_target_pairs={{0,1},{1,2},{2,3},{3,4},{4,5},{5,6},{6,7},{7,0},{8,9},{9,10},{10,1... | collective-permute-start | bytes 393224 | tf_op jit(solution)/shard_map/ppermute | solution.py:170
  70.4 4.6 %collective-permute-start.7 = (bf16[256,256]{1,0:T(8,128)(2,1)S(1)}, bf16[256,256]{1,0:T(8,128)(2,1)S(1)}, u32[]{:S(2)}, u32[]{:S(2)}) collective-permute-start(bf16[256,256]{1,0:T(8,128)(2,1)S(1)} %slice.9), channel_id=1, source_target_pairs={{0,7},{1,0},{2,1},{3,2},{4,3},{5,4},{6,5},{7,6},{8,15},{9,8},{10,9... | collective-permute-start | bytes 393224 | tf_op jit(solution)/shard_map/ppermute | solution.py:171
  75.1 1.0 constant_dynamic-slice_fusion.refs_11_
  76.9 2.8 %project.1 = (f32[512,256]{1,0:T(8,128)S(1)}, f32[8,2,512]{2,1,0:T(2,128)S(1)}) custom-call(s32[4]{0:T(128)S(1)} %pad_add_fusion.place, bf16[512,256]{1,0:T(8,128)(2,1)S(1)} %copy-done.1, bf16[512,256]{1,0:T(8,128)(2,1)S(1)} %collective-permute-done.refs_1_, bf16[512,256]{1,0:T(8,128)(2,1)S(1)} %collective-permute-done.1.refs_2_, ...), custom_call_target="tpu_custom_call" | custom-call | flops 550000000 | bytes 4000000 | tf_op jit(solution)/shard_map/project/pallas_call | solution.py:211
  80.5 11.1 %all_to_all.40.stats_ref = f32[8,2,512]{2,1,0:T(2,128)S(1)} all-to-all(f32[8,2,512]{2,1,0:T(2,128)S(1)} %get-tuple-element.31), channel_id=1, replica_groups=mesh['dp'=96,'mp'=8] {'mp'}, dimensions={0} | all-to-all | bytes 65536 | tf_op jit(solution)/shard_map/all_to_all | solution.py:440
  92.4 19.2 %all-to-all-start.3 = ((f32[96,1,128]{2,1,0:T(1,128)}), f32[96,1,128]{2,1,0:T(1,128)}, u32[]{:S(2)}, u32[]{:S(2)}) async-start(f32[96,1,128]{2,1,0:T(1,128)} %reward.1), calls=%async_computation.3 | async-start | bytes 98304 | tf_op jit(solution)/shard_map/all_to_all | solution.py:442
  111.6 1.0 copy-done.5
  114.3 2.4 %gradient.1 = (bf16[1152,256]{1,0:T(8,128)(2,1)}, bf16[1152,256]{1,0:T(8,128)(2,1)S(1)}) custom-call(s32[4]{0:T(128)S(1)} %pad_add_fusion.place, f32[8,2,512]{2,1,0:T(2,128)S(1)} %copy-done.9, f32[512,256]{1,0:T(8,128)S(1)} %copy-done.5, f32[1,256]{1,0:T(1,128)S(1)} %bitcast.29, bf16[512,256]{1,0:T(8,128)(2,1)S(1)} %copy-done.1, ...), custom_call_target="tpu_custom_call" | custom-call | flops 550000000 | bytes 4000000 | tf_op jit(solution)/shard_map/gradient/pallas_call | solution.py:302
  117.6 2.6 %collective-permute-start.9 = (bf16[1152,256]{1,0:T(8,128)(2,1)}, bf16[1152,256]{1,0:T(8,128)(2,1)S(1)}, u32[]{:S(2)}, u32[]{:S(2)}) collective-permute-start(bf16[1152,256]{1,0:T(8,128)(2,1)} %get-tuple-element.36), channel_id=1, source_target_pairs={{0,8},{8,0},{16,24},{24,16},{32,40},{40,32},{48,56},{56,48},{64,72... | collective-permute-start | bytes 1769480 | tf_op jit(solution)/shard_map/ppermute | solution.py:40
  120.9 2.6 %all-to-all-done.3 = f32[96,1,128]{2,1,0:T(1,128)} async-done(((f32[96,1,128]{2,1,0:T(1,128)}), f32[96,1,128]{2,1,0:T(1,128)}, u32[]{:S(2)}, u32[]{:S(2)}) %all-to-all-start.3) | async-done | bytes 49184 | tf_op jit(solution)/shard_map/all_to_all | solution.py:442
  124.6 1.1 copy-done.3
  125.6 1.6 weigh.1
  127.3 12.0 %all_to_all.41 = bf16[4,288,256]{2,1,0:T(8,128)(2,1)S(1)} all-to-all(bf16[4,288,256]{2,1,0:T(8,128)(2,1)S(1)} %bitcast.25), channel_id=1, replica_groups={{0,192,384,576},{8,200,392,584},{16,208,400,592},{24,216,408,600},{32,2..., dimensions={0} | all-to-all | bytes 1179648 | tf_op jit(solution)/shard_map/all_to_all | solution.py:35
  139.3 18.5 %all_to_all.42 = bf16[12,24,256]{2,1,0:T(8,128)(2,1)S(1)} all-to-all(bf16[12,24,256]{2,1,0:T(8,128)(2,1)S(1)} %bitcast.30), channel_id=1, replica_groups={{0,16,32,48,64,80,96,112,128,144,160,176},{8,24,40,56,72,88,104,120,136..., dimensions={0} | all-to-all | bytes 294912 | tf_op jit(solution)/shard_map/all_to_all | solution.py:35
  157.9 13.1 %all_to_all.43 = bf16[12,24,256]{2,1,0:T(8,128)(2,1)S(1)} all-to-all(bf16[12,24,256]{2,1,0:T(8,128)(2,1)S(1)} %broadcast_in_dim.38), channel_id=1, replica_groups={{0,16,32,48,64,80,96,112,128,144,160,176},{8,24,40,56,72,88,104,120,136..., dimensions={0} | all-to-all | bytes 294912 | tf_op jit(solution)/shard_map/all_to_all | solution.py:35
  171.1 9.7 %all_to_all.44 = bf16[4,288,256]{2,1,0:T(8,128)(2,1)S(1)} all-to-all(bf16[4,288,256]{2,1,0:T(8,128)(2,1)S(1)} %broadcast_in_dim.40), channel_id=1, replica_groups={{0,192,384,576},{8,200,392,584},{16,208,400,592},{24,216,408,600},{32,2..., dimensions={0} | all-to-all | bytes 1179648 | tf_op jit(solution)/shard_map/all_to_all | solution.py:35
  180.8 7.5 %collective-permute-start.10 = (bf16[1152,256]{1,0:T(8,128)(2,1)S(1)}, bf16[1152,256]{1,0:T(8,128)(2,1)S(1)}, u32[]{:S(2)}, u32[]{:S(2)}) collective-permute-start(bf16[1152,256]{1,0:T(8,128)(2,1)S(1)} %bitcast.23), channel_id=1, source_target_pairs={{0,8},{8,0},{16,24},{24,16},{32,40},{40,32},{48,56},{56,48},{64,72... | collective-permute-start | bytes 1769480 | tf_op jit(solution)/shard_map/ppermute | solution.py:40
  188.3 1.6 collective-permute-done.10.other_ref
  189.9 2.0 %finish.1 = (f32[2048,256]{1,0:T(8,128)}, f32[1,256]{1,0:T(1,128)}, f32[1,256]{1,0:T(1,128)}) custom-call(s32[4]{0:T(128)S(1)} %pad_add_fusion.place, bf16[1152,256]{1,0:T(8,128)(2,1)S(1)} %bitcast.24, bf16[1152,256]{1,0:T(8,128)(2,1)S(1)} %collective-permute-done.10.other_ref, f32[1,2048]{1,0:T(1,128)S(1)} %bitcast.27, f32[1,2048]{1,0:T(1,128)S(1)} %bitcast.26), custom_call_target="tpu_custom_call" | custom-call | flops 1000000 | bytes 4000000 | tf_op jit(solution)/shard_map/finish/pallas_call | solution.py:384
  (48 shorter events, 9.6 us)
Async XLA Ops:
  0.6 13.3 %copy-start = (bf16[256,2048]{1,0:T(8,128)(2,1)S(1)}, bf16[256,2048]{1,0:T(8,128)(2,1)}, u32[]{:S(2)}) copy-start(bf16[256,2048]{1,0:T(8,128)(2,1)} %param.18) | copy-start | bytes 3145732
  9.7 54.2 %copy-start.10 = (f32[2048]{0:T(1024)S(1)}, f32[2048]{0:T(1024)}, u32[]{:S(2)}) copy-start(f32[2048]{0:T(1024)} %param.20) | copy-start | bytes 24580
  9.7 67.2 %copy-start.1 = (bf16[512,256]{1,0:T(8,128)(2,1)S(1)}, bf16[512,256]{1,0:T(8,128)(2,1)}, u32[]{:S(2)}) copy-start(bf16[512,256]{1,0:T(8,128)(2,1)} %front.1.refs_0_) | copy-start | bytes 786436
  9.7 10.0 %collective-permute-start = (bf16[512,256]{1,0:T(8,128)(2,1)}, bf16[512,256]{1,0:T(8,128)(2,1)S(1)}, u32[]{:S(2)}, u32[]{:S(2)}) collective-permute-start(bf16[512,256]{1,0:T(8,128)(2,1)} %front.1.refs_0_), channel_id=1, source_target_pairs={{0,1},{1,2},{2,3},{3,4},{4,5},{5,6},{6,7},{7,0},{8,9},{9,10},{10,1... | collective-permute-start | bytes 786440 | tf_op jit(solution)/shard_map/ppermute | solution.py:165
  20.4 16.2 %all-to-all-start = ((bf16[8,32,256]{2,1,0:T(8,128)(2,1)}), bf16[8,32,256]{2,1,0:T(8,128)(2,1)S(1)}, u32[]{:S(2)}, u32[]{:S(2)}) async-start(bf16[8,32,256]{2,1,0:T(8,128)(2,1)} %copy.18), calls=%async_computation | async-start | bytes 262144 | tf_op jit(solution)/shard_map/all_to_all | solution.py:433
  28.7 15.0 %collective-permute-start.1 = (bf16[512,256]{1,0:T(8,128)(2,1)}, bf16[512,256]{1,0:T(8,128)(2,1)S(1)}, u32[]{:S(2)}, u32[]{:S(2)}) collective-permute-start(bf16[512,256]{1,0:T(8,128)(2,1)} %front.1.refs_0_), channel_id=1, source_target_pairs={{0,7},{1,0},{2,1},{3,2},{4,3},{5,4},{6,5},{7,6},{8,15},{9,8},{10,9... | collective-permute-start | bytes 786440 | tf_op jit(solution)/shard_map/ppermute | solution.py:165
  37.4 10.9 %all-to-all-start.1 = ((bf16[4,8,32,256]{3,2,1,0:T(8,128)(2,1)}), bf16[4,8,32,256]{3,2,1,0:T(8,128)(2,1)S(1)}, u32[]{:S(2)}, u32[]{:S(2)}) async-start(bf16[4,8,32,256]{3,2,1,0:T(8,128)(2,1)} %broadcast_in_dim.35), calls=%async_computation.1 | async-start | bytes 1048576 | tf_op jit(solution)/shard_map/all_to_all | solution.py:35
  41.4 15.9 %collective-permute-start.2 = (bf16[512,256]{1,0:T(8,128)(2,1)S(1)}, bf16[512,256]{1,0:T(8,128)(2,1)S(1)}, u32[]{:S(2)}, u32[]{:S(2)}) collective-permute-start(bf16[512,256]{1,0:T(8,128)(2,1)S(1)} %collective-permute-done.refs_1_), channel_id=1, source_target_pairs={{0,1},{1,2},{2,3},{3,4},{4,5},{5,6},{6,7},{7,0},{8,9},{9,10},{10,1... | collective-permute-start | bytes 786440 | tf_op jit(solution)/shard_map/ppermute | solution.py:165
  43.7 16.0 %collective-permute-start.3 = (bf16[512,256]{1,0:T(8,128)(2,1)S(1)}, bf16[512,256]{1,0:T(8,128)(2,1)S(1)}, u32[]{:S(2)}, u32[]{:S(2)}) collective-permute-start(bf16[512,256]{1,0:T(8,128)(2,1)S(1)} %collective-permute-done.1.refs_2_), channel_id=1, source_target_pairs={{0,7},{1,0},{2,1},{3,2},{4,3},{5,4},{6,5},{7,6},{8,15},{9,8},{10,9... | collective-permute-start | bytes 786440 | tf_op jit(solution)/shard_map/ppermute | solution.py:165
  48.4 28.5 %collective-permute-start.8 = (bf16[4,8,32,256]{3,2,1,0:T(8,128)(2,1)S(1)}, bf16[4,8,32,256]{3,2,1,0:T(8,128)(2,1)}, u32[]{:S(2)}, u32[]{:S(2)}) collective-permute-start(bf16[4,8,32,256]{3,2,1,0:T(8,128)(2,1)S(1)} %all-to-all-done.1.refs_9_), channel_id=1, source_target_pairs={{0,8},{8,0},{16,24},{24,16},{32,40},{40,32},{48,56},{56,48},{64,72... | collective-permute-start | bytes 1572872 | tf_op jit(solution)/shard_map/ppermute | solution.py:40
  57.4 11.0 %collective-permute-start.4 = (bf16[512,256]{1,0:T(8,128)(2,1)S(1)}, bf16[512,256]{1,0:T(8,128)(2,1)S(1)}, u32[]{:S(2)}, u32[]{:S(2)}) collective-permute-start(bf16[512,256]{1,0:T(8,128)(2,1)S(1)} %collective-permute-done.2.refs_3_), channel_id=1, source_target_pairs={{0,1},{1,2},{2,3},{3,4},{4,5},{5,6},{6,7},{7,0},{8,9},{9,10},{10,1... | collective-permute-start | bytes 786440 | tf_op jit(solution)/shard_map/ppermute | solution.py:165
  59.7 10.7 %collective-permute-start.5 = (bf16[512,256]{1,0:T(8,128)(2,1)S(1)}, bf16[512,256]{1,0:T(8,128)(2,1)S(1)}, u32[]{:S(2)}, u32[]{:S(2)}) collective-permute-start(bf16[512,256]{1,0:T(8,128)(2,1)S(1)} %collective-permute-done.3.refs_4_), channel_id=1, source_target_pairs={{0,7},{1,0},{2,1},{3,2},{4,3},{5,4},{6,5},{7,6},{8,15},{9,8},{10,9... | collective-permute-start | bytes 786440 | tf_op jit(solution)/shard_map/ppermute | solution.py:165
  68.4 7.6 %collective-permute-start.6 = (bf16[256,256]{1,0:T(8,128)(2,1)S(1)}, bf16[256,256]{1,0:T(8,128)(2,1)S(1)}, u32[]{:S(2)}, u32[]{:S(2)}) collective-permute-start(bf16[256,256]{1,0:T(8,128)(2,1)S(1)} %slice.8), channel_id=1, source_target_pairs={{0,1},{1,2},{2,3},{3,4},{4,5},{5,6},{6,7},{7,0},{8,9},{9,10},{10,1... | collective-permute-start | bytes 393224 | tf_op jit(solution)/shard_map/ppermute | solution.py:170
  70.4 6.5 %collective-permute-start.7 = (bf16[256,256]{1,0:T(8,128)(2,1)S(1)}, bf16[256,256]{1,0:T(8,128)(2,1)S(1)}, u32[]{:S(2)}, u32[]{:S(2)}) collective-permute-start(bf16[256,256]{1,0:T(8,128)(2,1)S(1)} %slice.9), channel_id=1, source_target_pairs={{0,7},{1,0},{2,1},{3,2},{4,3},{5,4},{6,5},{7,6},{8,15},{9,8},{10,9... | collective-permute-start | bytes 393224 | tf_op jit(solution)/shard_map/ppermute | solution.py:171
  76.9 2.8 %copy-start.6 = (bf16[256,256]{1,0:T(8,128)(2,1)}, bf16[256,256]{1,0:T(8,128)(2,1)S(1)}, u32[]{:S(2)}) copy-start(bf16[256,256]{1,0:T(8,128)(2,1)S(1)} %collective-permute-done.7.refs_8_) | copy-start | bytes 393220
  79.7 0.8 copy-start.4
  91.6 20.0 %copy-start.8 = (f32[8,2,512]{2,1,0:T(2,128)}, f32[8,2,512]{2,1,0:T(2,128)S(1)}, u32[]{:S(2)}) copy-start(f32[8,2,512]{2,1,0:T(2,128)S(1)} %all_to_all.40.stats_ref) | copy-start | bytes 98308
  92.4 31.2 %all-to-all-start.3 = ((f32[96,1,128]{2,1,0:T(1,128)}), f32[96,1,128]{2,1,0:T(1,128)}, u32[]{:S(2)}, u32[]{:S(2)}) async-start(f32[96,1,128]{2,1,0:T(1,128)} %reward.1), calls=%async_computation.3 | async-start | bytes 98304 | tf_op jit(solution)/shard_map/all_to_all | solution.py:442
  111.6 1.0 copy-start.5
  112.7 0.9 copy-start.7
  113.6 0.8 copy-start.9
  116.8 0.8 copy-start.2
  117.6 6.9 %collective-permute-start.9 = (bf16[1152,256]{1,0:T(8,128)(2,1)}, bf16[1152,256]{1,0:T(8,128)(2,1)S(1)}, u32[]{:S(2)}, u32[]{:S(2)}) collective-permute-start(bf16[1152,256]{1,0:T(8,128)(2,1)} %get-tuple-element.36), channel_id=1, source_target_pairs={{0,8},{8,0},{16,24},{24,16},{32,40},{40,32},{48,56},{56,48},{64,72... | collective-permute-start | bytes 1769480 | tf_op jit(solution)/shard_map/ppermute | solution.py:40
  124.6 1.1 copy-start.3
  127.3 62.6 %copy-start.11 = (f32[2048]{0:T(1024)S(1)}, f32[2048]{0:T(1024)}, u32[]{:S(2)}) copy-start(f32[2048]{0:T(1024)} %param.19) | copy-start | bytes 24580
  180.8 9.1 %collective-permute-start.10 = (bf16[1152,256]{1,0:T(8,128)(2,1)S(1)}, bf16[1152,256]{1,0:T(8,128)(2,1)S(1)}, u32[]{:S(2)}, u32[]{:S(2)}) collective-permute-start(bf16[1152,256]{1,0:T(8,128)(2,1)S(1)} %bitcast.23), channel_id=1, source_target_pairs={{0,8},{8,0},{16,24},{24,16},{32,40},{40,32},{48,56},{56,48},{64,72... | collective-permute-start | bytes 1769480 | tf_op jit(solution)/shard_map/ppermute | solution.py:40
